TPU v7x, 32 devices: a whole 2x2x4 slice. The times are simulated.
32 devices in a mesh: row: 8 (over z, core), col: 4 (over y, x).
Axes of the slice: x: 2, y: 2, z: 4, core: 2. Of those that a mesh axis runs over, the one named last changes fastest.
Arguments:
- start_basis: float32 [32, 16384], P(None, ('row', 'col')), may hold values from -6 to 6
- degrees: float32 [16384], P(('row', 'col')), may hold values from 0.5 to 1.5
- tiles: float32 [1024, 256, 256], P(('row', 'col')), may hold values from -0.046875 to 0.046875
- tile_rows: int32 [8, 128], P('row', 'col'), may hold values from 0 to 7, as said below
- tile_cols: int32 [8, 128], P('row', 'col'), may hold values from 0 to 15
- counts: int32 [8, 4], P('row', 'col'), may hold values from 1 to 31, as said below
Outputs:
- basis: float32 [32, 16384], P(None, ('row', 'col'))
- projected: float32 [32, 32], replicated
Inputs may be any that keep to these rules, and one draw needn't show every extreme that they name: `tile_rows`: the 32 (row, column) pairs of one device are distinct. counts[r, c] + counts[r', c] <= 32 where r' differs from r by 4; equality holds in column 0.
All inputs are finite; a program needn't handle non-finite values.
Results may differ from a plain program's by a relative error of at most 0.0003.
Values sent between devices are 32-bit elements; how exact they have to be, the bound alone decides.
No kernel may reach another device: no remote copies, remote signals or barrier semaphores. Data moves between devices by JAX's collectives and lax.ppermute only.
A program may use at most 64 MiB of HBM per device.

v0:
```python
import jax
import jax.numpy as jnp
from jax import lax
from jax.sharding import PartitionSpec as P

DEGREE = 3


center_shift = 1.0
spread_radius = 1.4
group_width = 8


def tile_products(blocks, tiles, row_local, col_local, live, row_blocks):
    subspace = blocks.shape[0]
    edge = blocks.shape[2]
    block_ids = jnp.arange(row_blocks, dtype=jnp.int32)

    def add_group(index, total):
        start = index * group_width
        group_tiles = lax.dynamic_slice_in_dim(tiles, start, group_width, 0)
        group_rows = lax.dynamic_slice_in_dim(row_local, start, group_width, 0)
        group_cols = lax.dynamic_slice_in_dim(col_local, start, group_width, 0)
        picked = jnp.take(blocks, group_cols, axis=1)
        product = jnp.einsum("kgj,gij->kgi", picked, group_tiles, precision=lax.Precision.HIGHEST)
        valid = start + jnp.arange(group_width, dtype=jnp.int32) < live
        select = ((group_rows[None, :] == block_ids[:, None]) & valid[None, :]).astype(jnp.float32)
        return total + jnp.einsum("ig,kgb->kib", select, product, precision=lax.Precision.HIGHEST)

    initial = jnp.zeros((subspace, row_blocks, edge), jnp.float32)
    return lax.fori_loop(0, (live + group_width - 1) // group_width, add_group, initial)


def inner_products(left, right):
    return jnp.einsum("kn,mn->km", left, right, precision=lax.Precision.HIGHEST)


def body(start_basis, degrees, tiles, tile_rows, tile_cols, counts):
    subspace = start_basis.shape[0]
    edge = tiles.shape[1]
    row_local = tile_rows[0]
    col_local = tile_cols[0]
    live_count = counts[0, 0]
    row_blocks = lax.axis_size("col") * start_basis.shape[1] // edge
    nverts = lax.axis_size("row") * lax.axis_size("col") * start_basis.shape[1]

    def apply_operator(vectors):
        gathered = lax.all_gather(vectors, "row", axis=1, tiled=True)
        blocks = gathered.reshape(subspace, -1, edge)
        partial_value = tile_products(blocks, tiles, row_local, col_local, live_count, row_blocks)
        summed = lax.psum_scatter(
            partial_value.reshape(subspace, -1), "col", scatter_dimension=1, tiled=True
        )
        return degrees[None, :] * vectors - summed

    def shifted(vectors):
        return (apply_operator(vectors) - center_shift * vectors) / spread_radius

    previous = start_basis
    filtered = shifted(start_basis)
    for level in range(DEGREE - 1):
        following = 2.0 * shifted(filtered) - previous
        previous, filtered = (filtered, following)
    gram_matrix = lax.psum(inner_products(filtered, filtered), ("row", "col")) / nverts
    factor = jnp.linalg.cholesky(gram_matrix)
    basis = jax.scipy.linalg.solve_triangular(factor, filtered, lower=True)
    image = apply_operator(basis)
    moment = lax.psum(inner_products(basis, image), ("row", "col")) / nverts
    projected = 0.5 * (moment + moment.T)
    return (basis, projected)


def solution(mesh):
    return jax.shard_map(
        body,
        mesh=mesh,
        in_specs=(
            P(None, ("row", "col")),
            P(("row", "col")),
            P(("row", "col"), None, None),
            P("row", "col"),
            P("row", "col"),
            P("row", "col"),
        ),
        out_specs=(P(None, ("row", "col")), P()),
        check_vma=False,
    )
```

profile of v0, /device:TPU:0, one launch (start us, length us, event | category | flops | bytes accessed | tf_op | source)
XLA Modules:
  0.0 377.9 jit_solution(18313725073773698578)
XLA Ops:
  7.9 16.8 %all_gather.12 = f32[32,4096]{1,0:T(8,128)S(1)} all-gather(f32[32,512]{1,0:T(8,128)} %param.16), channel_id=1, replica_groups=mesh['row'=8,'col'=4] {'row'}, dimensions={1}, use_global_device_ids=true | all-gather | bytes 589824 | tf_op jit(solution)/shard_map/all_gather | solution.py:48
  24.8 6.8 %while.44 = (s32[]{:T(128)}, f32[32,8,256]{2,1,0:T(8,128)S(1)}, s32[]{:T(128)}, f32[32,256,256]{2,1,0:T(8,128)}, s32[32]{0:T(128)}, /*index=5*/f32[32,16,256]{2,...) while((s32[]{:T(128)}, f32[32,8,256]{2,1,0:T(8,128)S(1)}, ...), condition=%wide.region_1.3_spmd.clone, body=%wide.region_0.2_spmd.clone.sunk | while | flops 207750336 | bytes 3936695 | solution.py:31
  24.8 1.4 compare_and_fusion.8
  26.2 0.6 gather_fusion
  26.8 3.6 fusion.122
  30.4 0.7 dynamic_slice.81
  31.1 0.4 fusion.123
  31.6 0.8 copy.40
  32.4 45.6 %reduce-scatter.5.cloned.1.call-done = f32[32,512]{1,0:T(8,128)} async-done(((f32[32,2048]{1,0:T(8,128)}), f32[32,512]{1,0:T(8,128)}) %reduce-scatter.5.cloned.1.call-update) | async-done | bytes 65552 | tf_op jit(solution)/shard_map/reduce_scatter | solution.py:51
  78.0 0.9 fusion.83
  78.9 14.7 %all_gather.13 = f32[32,4096]{1,0:T(8,128)S(1)} all-gather(f32[32,512]{1,0:T(8,128)S(1)} %fusion.83), channel_id=1, replica_groups=mesh['row'=8,'col'=4] {'row'}, dimensions={1}, use_global_device_ids=true | all-gather | bytes 589824 | tf_op jit(solution)/shard_map/all_gather | solution.py:48
  93.7 6.8 %while.45 = (s32[]{:T(128)}, f32[32,8,256]{2,1,0:T(8,128)S(1)}, s32[]{:T(128)}, f32[32,256,256]{2,1,0:T(8,128)}, s32[32]{0:T(128)}, /*index=5*/f32[32,16,256]{2,...) while((s32[]{:T(128)}, f32[32,8,256]{2,1,0:T(8,128)S(1)}, ...), condition=%wide.region_4.6_spmd.clone, body=%wide.region_3.5_spmd.clone.sunk | while | flops 207750336 | bytes 3936695 | solution.py:31
  93.7 1.4 compare_and_fusion.9
  95.1 0.6 gather_fusion.1
  95.7 3.6 fusion.128
  99.3 0.7 dynamic_slice.83
  100.1 0.4 fusion.129
  100.5 0.8 copy.41
  101.4 44.8 %reduce-scatter.7.cloned.1.call-done = f32[32,512]{1,0:T(8,128)} async-done(((f32[32,2048]{1,0:T(8,128)}), f32[32,512]{1,0:T(8,128)}) %reduce-scatter.7.cloned.1.call-update) | async-done | bytes 65552 | tf_op jit(solution)/shard_map/reduce_scatter | solution.py:51
  146.2 0.9 multiply_subtract_fusion.1
  147.1 14.7 %all_gather.14 = f32[32,4096]{1,0:T(8,128)S(1)} all-gather(f32[32,512]{1,0:T(8,128)S(1)} %multiply_subtract_fusion.1), channel_id=1, replica_groups=mesh['row'=8,'col'=4] {'row'}, dimensions={1}, use_global_device_ids=true | all-gather | bytes 589824 | tf_op jit(solution)/shard_map/all_gather | solution.py:48
  161.9 6.8 %while.46 = (s32[]{:T(128)}, f32[32,8,256]{2,1,0:T(8,128)S(1)}, s32[]{:T(128)}, f32[32,256,256]{2,1,0:T(8,128)}, s32[32]{0:T(128)}, /*index=5*/f32[32,16,256]{2,...) while((s32[]{:T(128)}, f32[32,8,256]{2,1,0:T(8,128)S(1)}, ...), condition=%wide.region_7.9_spmd.clone, body=%wide.region_6.8_spmd.clone.sunk | while | flops 207750336 | bytes 3936695 | solution.py:31
  161.9 1.4 compare_and_fusion.10
  163.3 0.6 gather_fusion.2
  163.9 3.6 fusion.134
  167.5 0.7 dynamic_slice.85
  168.2 0.4 fusion.135
  168.7 0.8 copy.42
  169.5 44.9 %reduce-scatter.9.cloned.1.call-done = f32[32,512]{1,0:T(8,128)} async-done(((f32[32,2048]{1,0:T(8,128)}), f32[32,512]{1,0:T(8,128)}) %reduce-scatter.9.cloned.1.call-update) | async-done | bytes 65552 | tf_op jit(solution)/shard_map/reduce_scatter | solution.py:51
  214.4 0.9 multiply_subtract_fusion
  215.5 39.5 %psum.14 = f32[32,32]{0,1:T(8,128)S(1)} all-reduce(f32[32,32]{0,1:T(8,128)S(1)} %fusion.89), channel_id=1, replica_groups=mesh['row'=8,'col'=4] {'row','col'}, use_global_device_ids=true, to_apply=%region_9.11 | all-reduce | flops 1024 | bytes 8192 | tf_op jit(solution)/shard_map/psum | solution.py:64
  255.1 2.9 cholesky.16
  258.1 0.6 compare_reduce_fusion
  258.7 0.7 fusion.85
  259.4 2.4 custom-call.7
  261.8 0.3 fusion.87
  262.1 14.9 %all_gather.15 = f32[32,4096]{1,0:T(8,128)S(1)} all-gather(f32[32,512]{1,0:T(8,128)S(1)} %fusion.87), channel_id=1, replica_groups=mesh['row'=8,'col'=4] {'row'}, dimensions={1}, use_global_device_ids=true | all-gather | bytes 589824 | tf_op jit(solution)/shard_map/all_gather | solution.py:48
  277.1 7.0 %while.47 = (s32[]{:T(128)}, f32[32,8,256]{2,1,0:T(8,128)S(1)}, s32[]{:T(128)}, f32[32,256,256]{2,1,0:T(8,128)}, s32[32]{0:T(128)}, /*index=5*/f32[32,16,256]{2,...) while((s32[]{:T(128)}, f32[32,8,256]{2,1,0:T(8,128)S(1)}, ...), condition=%wide.region_13.15_spmd.clone, body=%wide.region_12.14_spmd.clone.sunk | while | flops 207750336 | bytes 3936695 | solution.py:31
  277.3 1.4 compare_and_fusion.11
  278.7 0.6 gather_fusion.3
  279.3 3.6 fusion.140
  282.9 0.7 dynamic_slice.87
  283.6 0.4 fusion.141
  284.1 0.8 copy.43
  284.9 45.3 %reduce-scatter.11.cloned.1.call-done = f32[32,512]{1,0:T(8,128)} async-done(((f32[32,2048]{1,0:T(8,128)}), f32[32,512]{1,0:T(8,128)}) %reduce-scatter.11.cloned.1.call-update) | async-done | bytes 65552 | tf_op jit(solution)/shard_map/reduce_scatter | solution.py:51
  330.2 1.0 fusion.80
  331.3 39.5 %psum.15 = f32[32,32]{0,1:T(8,128)S(1)} all-reduce(f32[32,32]{0,1:T(8,128)S(1)} %fusion.80), channel_id=1, replica_groups=mesh['row'=8,'col'=4] {'row','col'}, use_global_device_ids=true, to_apply=%region_15.17 | all-reduce | flops 1024 | bytes 8192 | tf_op jit(solution)/shard_map/psum | solution.py:68
  370.8 0.6 fusion.86
  (38 shorter events, 1.0 us)
Async XLA Ops:
  7.2 70.9 %reduce-scatter.5.cloned.1.call-start = ((), (), s32[]{:S(2)}) async-start(), calls=%async_computation.4 | async-start | bytes 327680 | tf_op jit(solution)/shard_map/reduce_scatter | solution.py:51
  24.8 53.3 %copy-start = (f32[32,512]{1,0:T(8,128)S(1)}, f32[32,512]{1,0:T(8,128)}, u32[]{:S(2)}) copy-start(f32[32,512]{1,0:T(8,128)} %param.16) | copy-start | bytes 196612
  24.8 53.3 %copy-start.3 = (f32[512]{0:T(512)S(1)}, f32[512]{0:T(512)}, u32[]{:S(2)}) copy-start(f32[512]{0:T(512)} %param.17) | copy-start | bytes 6148
  32.4 113.8 %reduce-scatter.7.cloned.1.call-start = ((), (), s32[]{:S(2)}) async-start(), calls=%async_computation.5 | async-start | bytes 327680 | tf_op jit(solution)/shard_map/reduce_scatter | solution.py:51
  93.7 52.5 %copy-start.2 = (f32[32,512]{1,0:T(8,128)S(1)}, f32[32,512]{1,0:T(8,128)}, u32[]{:S(2)}) copy-start(f32[32,512]{1,0:T(8,128)} %reduce-scatter.5.cloned.1.call-done) | copy-start | bytes 196612
  101.3 113.1 %reduce-scatter.9.cloned.1.call-start = ((), (), s32[]{:S(2)}) async-start(), calls=%async_computation.6 | async-start | bytes 327680 | tf_op jit(solution)/shard_map/reduce_scatter | solution.py:51
  169.5 160.7 %reduce-scatter.11.cloned.1.call-start = ((), (), s32[]{:S(2)}) async-start(), calls=%async_computation.7 | async-start | bytes 327680 | tf_op jit(solution)/shard_map/reduce_scatter | solution.py:51
  262.1 68.1 %copy-start.1 = (f32[32,512]{1,0:T(8,128)}, f32[32,512]{1,0:T(8,128)S(1)}, u32[]{:S(2)}) copy-start(f32[32,512]{1,0:T(8,128)S(1)} %fusion.87) | copy-start | bytes 196612
Sparse Core Ops, SparseCore 0:
  32.5 45.4 reduce-scatter.4
  101.4 44.7 reduce-scatter.6
  169.6 44.7 reduce-scatter.8
  285.0 45.1 reduce-scatter.10
where the time goes:
time: 379 us; the launch traced here: 378 us
  waiting for transfers between devices  181 us (48%)
  blocking collectives  140 us (37%)
  matrix products  17.7 us (5%)
  other arithmetic  15.5 us (4%)
  between operations  14.6 us (4%)
  local copies, waits for them, and re-layouts  8.8 us (2%)
    reduce_scatter x4, waiting for transfers between devices, apply_operator(): lax.psum_scatter(partial_value.reshape(subspace, -1), 'col', scatter_dime...  181 us
    all_gather x4, blocking collectives, apply_operator(): gathered = lax.all_gather(vectors, 'row', axis=1, tiled=True)  61.1 us
    psum x1, blocking collectives, body(): lax.psum(inner_products(filtered, filtered), ('row', 'col')) / nverts  39.5 us
    psum x1, blocking collectives, body(): moment = lax.psum(inner_products(basis, image), ('row', 'col')) / nverts  39.5 us
    dot_general x4, matrix products, add_group(): jnp.einsum('kgj,gij->kgi', picked, group_tiles, precision=lax.Precision.H...  14.5 us
  transfers between devices with their start and end apart: 4, of which 4 were waited for; matrix products, arithmetic and copies ran while one was open for 0% of the time, Pallas kernels for 0%

commit v1 on v0

v1 whole, which is shorter than its diff:
```python
import functools

import jax
import jax.numpy as jnp
from jax import lax
from jax.experimental import pallas as pl
from jax.experimental.pallas import tpu as pltpu
from jax.sharding import PartitionSpec as P

DEGREE = 3


center_shift = 1.0
spread_radius = 1.4
MIB = 1 << 20

ROWS_BY_ROWS = (((1,), (1,)), ((), ()))


def dot_rows(left, right, precision=None):
    return lax.dot_general(
        left, right, ROWS_BY_ROWS, precision=precision, preferred_element_type=jnp.float32
    )


def split(value):
    high = value.astype(jnp.bfloat16)
    low = (value - high.astype(jnp.float32)).astype(jnp.bfloat16)
    return high, low


def accumulate_tiles(slots, tiles, parts, halves, total):
    subspace = parts[0].shape[0]
    edge = tiles.shape[1]
    per_part = parts[0].shape[1] // edge
    for index, part in enumerate(parts):
        for block in range(per_part):
            high, low = split(part[:, block * edge : (block + 1) * edge])
            halves[index * per_part + block, :subspace] = high
            halves[index * per_part + block, subspace:] = low
    total[...] = jnp.zeros_like(total)
    for slot in range(tiles.shape[0]):
        vectors = halves[slots[1, slot]]
        tile_high, tile_low = split(tiles[slot])
        first = dot_rows(vectors, tile_high)
        second = dot_rows(vectors[:subspace], tile_low)
        total[slots[0, slot]] += first[:subspace] + first[subspace:] + second


def product_kernel(n_row, n_col, slots, tiles, *refs):
    parts, outs = refs[:n_row], refs[n_row : n_row + n_col]
    halves, total = refs[n_row + n_col :]
    accumulate_tiles(slots, tiles, parts, halves, total)
    edge = tiles.shape[1]
    per_part = parts[0].shape[1] // edge
    for index, out in enumerate(outs):
        for block in range(per_part):
            out[:, block * edge : (block + 1) * edge] = total[index * per_part + block]


def moment_kernel(n_row, n_col, slots, tiles, degrees, *refs):
    parts, sides = refs[:n_row], refs[n_row : n_row + n_col - 1]
    out, halves, total = refs[n_row + n_col - 1 :]
    accumulate_tiles(slots, tiles, parts, halves, total)
    edge = tiles.shape[1]
    subspace, width = parts[0].shape
    per_part = width // edge
    own = parts[0][...]
    gram = dot_rows(own, own, lax.Precision.HIGHEST)
    moment = dot_rows(own, own * degrees[...], lax.Precision.HIGHEST)
    for index, side in enumerate((parts[0], *sides)):
        for block in range(per_part):
            left = jnp.concatenate(split(side[:, block * edge : (block + 1) * edge]), 0)
            right = jnp.concatenate(split(total[index * per_part + block]), 0)
            both = dot_rows(left, right)
            both = both[:subspace] + both[subspace:]
            moment -= both[:, :subspace] + both[:, subspace:]
    out[...] = jnp.concatenate([gram, moment], 1)


def finish_kernel(nverts, sums, filtered, basis, projected):
    subspace = filtered.shape[0]
    both = sums[...] * (1.0 / nverts)
    gram, moment = both[:, :subspace], both[:, subspace:]
    row = lax.broadcasted_iota(jnp.int32, (subspace, subspace), 0)
    column = lax.broadcasted_iota(jnp.int32, (subspace, subspace), 1)
    work = jnp.concatenate([gram, (row == column).astype(jnp.float32)], 1)
    wide_row = lax.broadcasted_iota(jnp.int32, (subspace, 2 * subspace), 0)
    scale = jnp.zeros((subspace, 1), jnp.float32)
    for step in range(subspace):
        pivot = work[step : step + 1, step : step + 1]
        scale = jnp.where(wide_row[:, :1] == step, lax.rsqrt(pivot), scale)
        ratio = work[:, step : step + 1] / pivot
        work = jnp.where(wide_row > step, work - ratio * work[step : step + 1, :], work)
    inverse = scale * work[:, subspace:]
    highest = lax.Precision.HIGHEST
    basis[...] = jnp.dot(
        inverse, filtered[...], precision=highest, preferred_element_type=jnp.float32
    )
    half = jnp.dot(inverse, moment, precision=highest, preferred_element_type=jnp.float32)
    whole = dot_rows(half, inverse, highest)
    projected[...] = 0.5 * (whole + whole.T)


def body(n_row, n_col, start_basis, degrees, tiles, tile_rows, tile_cols, counts):
    subspace, width = start_basis.shape
    slots_held, edge = tiles.shape[0], tiles.shape[1]
    per_part = width // edge
    nverts = n_row * n_col * width
    row, col = lax.axis_index("row"), lax.axis_index("col")
    degrees = degrees[None, :]

    row_local, col_local = tile_rows[0], tile_cols[0]
    row_place = ((row_local // per_part) ^ col) * per_part + row_local % per_part
    col_place = ((col_local // per_part) ^ row) * per_part + col_local % per_part
    live = jnp.arange(slots_held, dtype=jnp.int32) < counts[0, 0]
    spare = n_col * per_part
    slots = jnp.stack([jnp.where(live, row_place, spare), col_place])

    def swap(value, axis, size, distance):
        return lax.ppermute(value, axis, [(i, i ^ distance) for i in range(size)])

    def gather_row(value):
        parts = [None] * n_row
        parts[0] = value
        for distance in range(2, n_row, 2):
            parts[distance] = swap(value, "row", n_row, distance)
        for distance in range(0, n_row, 2):
            parts[distance + 1] = swap(parts[distance], "row", n_row, 1)
        return parts

    def gather_col(value):
        return [swap(value, "col", n_col, distance) for distance in range(1, n_col)]

    def vmem(count):
        return [pl.BlockSpec(memory_space=pltpu.VMEM)] * count

    scratch = [
        pltpu.VMEM((n_row * per_part, 2 * subspace, edge), jnp.bfloat16),
        pltpu.VMEM((n_col * per_part + 1, subspace, edge), jnp.float32),
    ]
    slots_spec = pl.BlockSpec(memory_space=pltpu.SMEM)
    params = pltpu.CompilerParams(vmem_limit_bytes=20 * MIB)
    piece = jax.ShapeDtypeStruct((subspace, width), jnp.float32)

    def weights(vectors):
        partial_values = pl.pallas_call(
            functools.partial(product_kernel, n_row, n_col),
            out_shape=[piece] * n_col,
            in_specs=[slots_spec, *vmem(1 + n_row)],
            out_specs=vmem(n_col),
            scratch_shapes=scratch,
            compiler_params=params,
            name="tile_products",
        )(slots, tiles, *gather_row(vectors))
        total = partial_values[0]
        for distance in range(1, n_col):
            total = total + swap(partial_values[distance], "col", n_col, distance)
        return total

    def shifted(vectors):
        return ((degrees - center_shift) * vectors - weights(vectors)) / spread_radius

    previous = start_basis
    filtered = shifted(start_basis)
    for level in range(DEGREE - 1):
        following = 2.0 * shifted(filtered) - previous
        previous, filtered = (filtered, following)

    sums = pl.pallas_call(
        functools.partial(moment_kernel, n_row, n_col),
        out_shape=jax.ShapeDtypeStruct((subspace, 2 * subspace), jnp.float32),
        in_specs=[slots_spec, *vmem(2 + n_row + n_col - 1)],
        out_specs=pl.BlockSpec(memory_space=pltpu.VMEM),
        scratch_shapes=scratch,
        compiler_params=params,
        name="moment",
    )(slots, tiles, degrees, *gather_row(filtered), *gather_col(filtered))
    sums = sums + swap(sums, "row", n_row, 1)
    sums = sum([swap(sums, "row", n_row, distance) for distance in range(2, n_row, 2)], sums)
    sums = sum([swap(sums, "col", n_col, distance) for distance in range(1, n_col)], sums)
    basis, projected = pl.pallas_call(
        functools.partial(finish_kernel, nverts),
        out_shape=[piece, jax.ShapeDtypeStruct((subspace, subspace), jnp.float32)],
        in_specs=vmem(2),
        out_specs=vmem(2),
        compiler_params=params,
        name="finish",
    )(sums, filtered)
    return (basis, projected)


def solution(mesh):
    return jax.shard_map(
        functools.partial(body, mesh.shape["row"], mesh.shape["col"]),
        mesh=mesh,
        in_specs=(
            P(None, ("row", "col")),
            P(("row", "col")),
            P(("row", "col"), None, None),
            P("row", "col"),
            P("row", "col"),
            P("row", "col"),
        ),
        out_specs=(P(None, ("row", "col")), P()),
        check_vma=False,
    )
```

time: 379 us -> 103 us (0.27)
  waiting for transfers between devices: 181 us -> 34.8 us
  blocking collectives: 140 us -> 0 us
  starting transfers between devices: 0.16 us -> 44 us
  matrix products: 17.7 us -> 0 us
  Pallas kernels: 0 us -> 17.3 us
  other arithmetic: 15.5 us -> 0.81 us
  between operations: 14.6 us -> 1.39 us
  local copies, waits for them, and re-layouts: 8.8 us -> 4.23 us
    reduce_scatter x4 -> x0, waiting for transfers between devices: 181 us -> none  [apply_operator(): lax.psum_scatter(partial_value.reshape(subspace, -1), 'col', scatter_dime...]
    psum x2 -> x0, blocking collectives: 78.9 us -> none  [the longest x1 39.5 us: body(): lax.psum(inner_products(filtered, filtered), ('row', 'col')) / nverts]
    all_gather x4 -> x0, blocking collectives: 61.1 us -> none  [apply_operator(): gathered = lax.all_gather(vectors, 'row', axis=1, tiled=True)]
    ppermute x0 -> x47, starting transfers between devices: none -> 44 us  [swap(): return lax.ppermute(value, axis, [(i, i ^ distance) for i in range(size)])]
    ppermute x0 -> x47, waiting for transfers between devices: none -> 34.8 us  [swap(): return lax.ppermute(value, axis, [(i, i ^ distance) for i in range(size)])]
    dot_general x10 -> x0, matrix products: 17.5 us -> none  [the longest x4 14.5 us: add_group(): jnp.einsum('kgj,gij->kgi', picked, group_tiles, precision=lax.Precision.H...]
    pallas_call x0 -> x5, Pallas kernels: none -> 17.3 us  [the longest x3 9.7 us: weights(): pl.pallas_call(functools.partial(product_kernel, n_row, n_col), out_shape...]
    another operation x5 -> x1, other arithmetic: 6.69 us -> 0.01 us  [body(): slots = jnp.stack([jnp.where(live, row_place, spare), col_place])]
  transfers between devices with their start and end apart: 4 -> 47, of which waited for: 4 -> 32; matrix products, arithmetic and copies ran while one was open for 0% -> 1% of each run, Pallas kernels for 0% -> 0%
where the time goes in v1:
time: 103 us; the launch traced here: 102 us
  starting transfers between devices  44 us (43%)
  waiting for transfers between devices  34.8 us (34%)
  Pallas kernels  17.3 us (17%)
  local copies, waits for them, and re-layouts  4.23 us (4%)
  between operations  1.39 us (1%)
    ppermute x47, starting transfers between devices, swap(): return lax.ppermute(value, axis, [(i, i ^ distance) for i in range(size)])  44 us
    ppermute x47, waiting for transfers between devices, swap(): return lax.ppermute(value, axis, [(i, i ^ distance) for i in range(size)])  34.8 us
    pallas_call x3, Pallas kernels, weights(): pl.pallas_call(functools.partial(product_kernel, n_row, n_col), out_shape...  9.7 us
    unnamed x8, local copies, waits for them, and re-layouts  4.23 us
    pallas_call x1, Pallas kernels, body(): pl.pallas_call(functools.partial(finish_kernel, nverts), out_shape=[piece...  3.98 us
    pallas_call x1, Pallas kernels, body(): pl.pallas_call(functools.partial(moment_kernel, n_row, n_col), out_shape=...  3.6 us
  transfers between devices with their start and end apart: 47, of which 32 were waited for; matrix products, arithmetic and copies ran while one was open for 1% of the time, Pallas kernels for 0%

profile of v1, /device:TPU:0, one launch (start us, length us, event | category | flops | bytes accessed | tf_op | source)
XLA Modules:
  0.0 102.5 jit_solution(8825103324426765673)
XLA Ops:
  0.6 5.1 %collective-permute-start.5 = (f32[32,512]{1,0:T(8,128)}, f32[32,512]{1,0:T(8,128)S(1)}, u32[]{:S(2)}, u32[]{:S(2)}) collective-permute-start(f32[32,512]{1,0:T(8,128)} %refs_0_.1), channel_id=1, source_target_pairs={{0,24},{4,28},{8,16},{12,20},{16,8},{20,12},{24,0},{28,4},{1,25},{... | collective-permute-start | bytes 196616 | tf_op jit(solution)/shard_map/ppermute | solution.py:121
  7.7 0.8 collective-permute-done.5.refs_6_
  8.6 3.0 %collective-permute-done.3.refs_4_ = f32[32,512]{1,0:T(8,128)S(1)} collective-permute-done((f32[32,512]{1,0:T(8,128)}, f32[32,512]{1,0:T(8,128)S(1)}, u32[]{:S(2)}, u32[]{:S(2)}) %collective-permute-start.3) | collective-permute-done | bytes 65568 | tf_op jit(solution)/shard_map/ppermute | solution.py:121
  13.0 3.4 %copy-done = f32[32,256,256]{2,1,0:T(8,128)S(1)} copy-done((f32[32,256,256]{2,1,0:T(8,128)S(1)}, f32[32,256,256]{2,1,0:T(8,128)}, u32[]{:S(2)}) %copy-start) | copy-done | bytes 8388632
  16.4 0.8 copy-done.1
  17.2 3.2 %tile_products.3 = (f32[32,512]{1,0:T(8,128)S(1)}, f32[32,512]{1,0:T(8,128)S(1)}, f32[32,512]{1,0:T(8,128)S(1)}, f32[32,512]{1,0:T(8,128)S(1)}) custom-call(s32[2,32]{1,0:T(2,128)S(1)} %pad_add_fusion.slots, f32[32,256,256]{2,1,0:T(8,128)S(1)} %copy-done, f32[32,512]{1,0:T(8,128)S(1)} %copy-done.1, f32[32,512]{1,0:T(8,128)S(1)} %collective-permute-done.refs_1_, ...), custom_call_target="tpu_custom_call" | custom-call | tf_op jit(solution)/shard_map/tile_products/pallas_call | solution.py:147
  20.5 1.6 %collective-permute-start.7 = (f32[32,512]{1,0:T(8,128)S(1)}, f32[32,512]{1,0:T(8,128)S(1)}, u32[]{:S(2)}, u32[]{:S(2)}) collective-permute-start(f32[32,512]{1,0:T(8,128)S(1)} %get-tuple-element.15), channel_id=1, source_target_pairs={{0,1},{1,0},{2,3},{3,2},{4,5},{5,4},{6,7},{7,6},{8,9},{9,8},{10,11... | collective-permute-start | bytes 196616 | tf_op jit(solution)/shard_map/ppermute | solution.py:121
  22.0 1.5 %collective-permute-start.8 = (f32[32,512]{1,0:T(8,128)S(1)}, f32[32,512]{1,0:T(8,128)S(1)}, u32[]{:S(2)}, u32[]{:S(2)}) collective-permute-start(f32[32,512]{1,0:T(8,128)S(1)} %get-tuple-element.16), channel_id=1, source_target_pairs={{0,2},{1,3},{2,0},{3,1},{4,6},{5,7},{6,4},{7,5},{8,10},{9,11},{10,... | collective-permute-start | bytes 196616 | tf_op jit(solution)/shard_map/ppermute | solution.py:121
  24.0 0.8 collective-permute-done.7
  24.9 1.4 %collective-permute-done.8 = f32[32,512]{1,0:T(8,128)S(1)} collective-permute-done((f32[32,512]{1,0:T(8,128)S(1)}, f32[32,512]{1,0:T(8,128)S(1)}, u32[]{:S(2)}, u32[]{:S(2)}) %collective-permute-start.8) | collective-permute-done | bytes 65568 | tf_op jit(solution)/shard_map/ppermute | solution.py:121
  26.3 2.4 %collective-permute-done.9 = f32[32,512]{1,0:T(8,128)S(1)} collective-permute-done((f32[32,512]{1,0:T(8,128)S(1)}, f32[32,512]{1,0:T(8,128)S(1)}, u32[]{:S(2)}, u32[]{:S(2)}) %collective-permute-start.9) | collective-permute-done | bytes 65568 | tf_op jit(solution)/shard_map/ppermute | solution.py:121
  28.7 2.8 %collective-permute-start.15 = (f32[32,512]{1,0:T(8,128)S(1)}, f32[32,512]{1,0:T(8,128)S(1)}, u32[]{:S(2)}, u32[]{:S(2)}) collective-permute-start(f32[32,512]{1,0:T(8,128)S(1)} %get-tuple-element.26.refs_0_), channel_id=1, source_target_pairs={{0,24},{4,28},{8,16},{12,20},{16,8},{20,12},{24,0},{28,4},{1,25},{... | collective-permute-start | bytes 196616 | tf_op jit(solution)/shard_map/ppermute | solution.py:121
  31.5 1.7 %collective-permute-start.11 = (f32[32,512]{1,0:T(8,128)S(1)}, f32[32,512]{1,0:T(8,128)S(1)}, u32[]{:S(2)}, u32[]{:S(2)}) collective-permute-start(f32[32,512]{1,0:T(8,128)S(1)} %get-tuple-element.26.refs_0_), channel_id=1, source_target_pairs={{0,8},{4,12},{8,0},{12,4},{16,24},{20,28},{24,16},{28,20},{1,9},{5... | collective-permute-start | bytes 196616 | tf_op jit(solution)/shard_map/ppermute | solution.py:121
  33.2 2.1 %collective-permute-done.15.refs_6_ = f32[32,512]{1,0:T(8,128)S(1)} collective-permute-done((f32[32,512]{1,0:T(8,128)S(1)}, f32[32,512]{1,0:T(8,128)S(1)}, u32[]{:S(2)}, u32[]{:S(2)}) %collective-permute-start.15) | collective-permute-done | bytes 65568 | tf_op jit(solution)/shard_map/ppermute | solution.py:121
  35.2 1.7 %collective-permute-done.13.refs_4_ = f32[32,512]{1,0:T(8,128)S(1)} collective-permute-done((f32[32,512]{1,0:T(8,128)S(1)}, f32[32,512]{1,0:T(8,128)S(1)}, u32[]{:S(2)}, u32[]{:S(2)}) %collective-permute-start.13) | collective-permute-done | bytes 65568 | tf_op jit(solution)/shard_map/ppermute | solution.py:121
  37.5 0.7 collective-permute-done.14.refs_5_
  38.4 3.2 %tile_products.4 = (f32[32,512]{1,0:T(8,128)S(1)}, f32[32,512]{1,0:T(8,128)S(1)}, f32[32,512]{1,0:T(8,128)S(1)}, f32[32,512]{1,0:T(8,128)S(1)}) custom-call(s32[2,32]{1,0:T(2,128)S(1)} %pad_add_fusion.slots, f32[32,256,256]{2,1,0:T(8,128)S(1)} %copy-done, f32[32,512]{1,0:T(8,128)S(1)} %get-tuple-element.26.refs_0_, ...), custom_call_target="tpu_custom_call" | custom-call | tf_op jit(solution)/shard_map/tile_products/pallas_call | solution.py:147
  42.7 2.4 %collective-permute-start.19 = (f32[32,512]{1,0:T(8,128)S(1)}, f32[32,512]{1,0:T(8,128)S(1)}, u32[]{:S(2)}, u32[]{:S(2)}) collective-permute-start(f32[32,512]{1,0:T(8,128)S(1)} %get-tuple-element.21), channel_id=1, source_target_pairs={{0,3},{1,2},{2,1},{3,0},{4,7},{5,6},{6,5},{7,4},{8,11},{9,10},{10,... | collective-permute-start | bytes 196616 | tf_op jit(solution)/shard_map/ppermute | solution.py:121
  45.2 0.9 collective-permute-done.17
  46.0 1.2 %collective-permute-done.18 = f32[32,512]{1,0:T(8,128)S(1)} collective-permute-done((f32[32,512]{1,0:T(8,128)S(1)}, f32[32,512]{1,0:T(8,128)S(1)}, u32[]{:S(2)}, u32[]{:S(2)}) %collective-permute-start.18) | collective-permute-done | bytes 65568 | tf_op jit(solution)/shard_map/ppermute | solution.py:121
  48.0 2.6 %collective-permute-start.25 = (f32[32,512]{1,0:T(8,128)S(1)}, f32[32,512]{1,0:T(8,128)S(1)}, u32[]{:S(2)}, u32[]{:S(2)}) collective-permute-start(f32[32,512]{1,0:T(8,128)S(1)} %multiply_subtract_fusion.1.refs_0_), channel_id=1, source_target_pairs={{0,24},{4,28},{8,16},{12,20},{16,8},{20,12},{24,0},{28,4},{1,25},{... | collective-permute-start | bytes 196616 | tf_op jit(solution)/shard_map/ppermute | solution.py:121
  50.5 1.9 %collective-permute-start.21 = (f32[32,512]{1,0:T(8,128)S(1)}, f32[32,512]{1,0:T(8,128)S(1)}, u32[]{:S(2)}, u32[]{:S(2)}) collective-permute-start(f32[32,512]{1,0:T(8,128)S(1)} %multiply_subtract_fusion.1.refs_0_), channel_id=1, source_target_pairs={{0,8},{4,12},{8,0},{12,4},{16,24},{20,28},{24,16},{28,20},{1,9},{5... | collective-permute-start | bytes 196616 | tf_op jit(solution)/shard_map/ppermute | solution.py:121
  52.4 2.1 %collective-permute-done.25.refs_6_ = f32[32,512]{1,0:T(8,128)S(1)} collective-permute-done((f32[32,512]{1,0:T(8,128)S(1)}, f32[32,512]{1,0:T(8,128)S(1)}, u32[]{:S(2)}, u32[]{:S(2)}) %collective-permute-start.25) | collective-permute-done | bytes 65568 | tf_op jit(solution)/shard_map/ppermute | solution.py:121
  54.5 1.6 %collective-permute-done.23.refs_4_ = f32[32,512]{1,0:T(8,128)S(1)} collective-permute-done((f32[32,512]{1,0:T(8,128)S(1)}, f32[32,512]{1,0:T(8,128)S(1)}, u32[]{:S(2)}, u32[]{:S(2)}) %collective-permute-start.23) | collective-permute-done | bytes 65568 | tf_op jit(solution)/shard_map/ppermute | solution.py:121
  56.7 0.7 collective-permute-done.24.refs_5_
  57.6 3.2 %tile_products.5 = (f32[32,512]{1,0:T(8,128)S(1)}, f32[32,512]{1,0:T(8,128)S(1)}, f32[32,512]{1,0:T(8,128)S(1)}, f32[32,512]{1,0:T(8,128)S(1)}) custom-call(s32[2,32]{1,0:T(2,128)S(1)} %pad_add_fusion.slots, f32[32,256,256]{2,1,0:T(8,128)S(1)} %copy-done, f32[32,512]{1,0:T(8,128)S(1)} %multiply_subtract_fusion.1.refs_0_, ...), custom_call_target="tpu_custom_call" | custom-call | tf_op jit(solution)/shard_map/tile_products/pallas_call | solution.py:147
  60.8 1.6 %collective-permute-start.27 = (f32[32,512]{1,0:T(8,128)S(1)}, f32[32,512]{1,0:T(8,128)S(1)}, u32[]{:S(2)}, u32[]{:S(2)}) collective-permute-start(f32[32,512]{1,0:T(8,128)S(1)} %get-tuple-element.23), channel_id=1, source_target_pairs={{0,1},{1,0},{2,3},{3,2},{4,5},{5,4},{6,7},{7,6},{8,9},{9,8},{10,11... | collective-permute-start | bytes 196616 | tf_op jit(solution)/shard_map/ppermute | solution.py:121
  62.4 1.6 %collective-permute-start.28 = (f32[32,512]{1,0:T(8,128)S(1)}, f32[32,512]{1,0:T(8,128)S(1)}, u32[]{:S(2)}, u32[]{:S(2)}) collective-permute-start(f32[32,512]{1,0:T(8,128)S(1)} %get-tuple-element.24), channel_id=1, source_target_pairs={{0,2},{1,3},{2,0},{3,1},{4,6},{5,7},{6,4},{7,5},{8,10},{9,11},{10,... | collective-permute-start | bytes 196616 | tf_op jit(solution)/shard_map/ppermute | solution.py:121
  64.4 0.9 collective-permute-done.27
  65.2 1.4 %collective-permute-done.28 = f32[32,512]{1,0:T(8,128)S(1)} collective-permute-done((f32[32,512]{1,0:T(8,128)S(1)}, f32[32,512]{1,0:T(8,128)S(1)}, u32[]{:S(2)}, u32[]{:S(2)}) %collective-permute-start.28) | collective-permute-done | bytes 65568 | tf_op jit(solution)/shard_map/ppermute | solution.py:121
  66.6 2.5 %collective-permute-done.29 = f32[32,512]{1,0:T(8,128)S(1)} collective-permute-done((f32[32,512]{1,0:T(8,128)S(1)}, f32[32,512]{1,0:T(8,128)S(1)}, u32[]{:S(2)}, u32[]{:S(2)}) %collective-permute-start.29) | collective-permute-done | bytes 65568 | tf_op jit(solution)/shard_map/ppermute | solution.py:121
  69.7 1.5 %collective-permute-start.38 = (f32[32,512]{1,0:T(8,128)S(1)}, f32[32,512]{1,0:T(8,128)S(1)}, u32[]{:S(2)}, u32[]{:S(2)}) collective-permute-start(f32[32,512]{1,0:T(8,128)S(1)} %multiply_subtract_fusion.refs_0_.filtered), channel_id=1, source_target_pairs={{0,2},{1,3},{2,0},{3,1},{4,6},{5,7},{6,4},{7,5},{8,10},{9,11},{10,... | collective-permute-start | bytes 196616 | tf_op jit(solution)/shard_map/ppermute | solution.py:121
  71.2 2.2 %collective-permute-start.35 = (f32[32,512]{1,0:T(8,128)S(1)}, f32[32,512]{1,0:T(8,128)S(1)}, u32[]{:S(2)}, u32[]{:S(2)}) collective-permute-start(f32[32,512]{1,0:T(8,128)S(1)} %multiply_subtract_fusion.refs_0_.filtered), channel_id=1, source_target_pairs={{0,24},{4,28},{8,16},{12,20},{16,8},{20,12},{24,0},{28,4},{1,25},{... | collective-permute-start | bytes 196616 | tf_op jit(solution)/shard_map/ppermute | solution.py:121
  73.4 2.2 %collective-permute-start.31 = (f32[32,512]{1,0:T(8,128)S(1)}, f32[32,512]{1,0:T(8,128)S(1)}, u32[]{:S(2)}, u32[]{:S(2)}) collective-permute-start(f32[32,512]{1,0:T(8,128)S(1)} %multiply_subtract_fusion.refs_0_.filtered), channel_id=1, source_target_pairs={{0,8},{4,12},{8,0},{12,4},{16,24},{20,28},{24,16},{28,20},{1,9},{5... | collective-permute-start | bytes 196616 | tf_op jit(solution)/shard_map/ppermute | solution.py:121
  75.6 1.5 %collective-permute-start.37 = (f32[32,512]{1,0:T(8,128)S(1)}, f32[32,512]{1,0:T(8,128)S(1)}, u32[]{:S(2)}, u32[]{:S(2)}) collective-permute-start(f32[32,512]{1,0:T(8,128)S(1)} %multiply_subtract_fusion.refs_0_.filtered), channel_id=1, source_target_pairs={{0,1},{1,0},{2,3},{3,2},{4,5},{5,4},{6,7},{7,6},{8,9},{9,8},{10,11... | collective-permute-start | bytes 196616 | tf_op jit(solution)/shard_map/ppermute | solution.py:121
  77.6 1.1 %collective-permute-done.33.refs_4_ = f32[32,512]{1,0:T(8,128)S(1)} collective-permute-done((f32[32,512]{1,0:T(8,128)S(1)}, f32[32,512]{1,0:T(8,128)S(1)}, u32[]{:S(2)}, u32[]{:S(2)}) %collective-permute-start.33) | collective-permute-done | bytes 65568 | tf_op jit(solution)/shard_map/ppermute | solution.py:121
  80.1 3.6 %moment.1 = f32[32,64]{1,0:T(8,128)S(1)} custom-call(s32[2,32]{1,0:T(2,128)S(1)} %pad_add_fusion.slots, f32[32,256,256]{2,1,0:T(8,128)S(1)} %copy-done, f32[1,512]{1,0:T(1,128)S(1)} %bitcast.3, f32[32,512]{1,0:T(8,128)S(1)} %multiply_subtract_fusion.refs_0_.filtered, f32[32,512]{1,0:T(8,128)S(1)} %collective-permute-done.30.refs_1_, ...), custom_call_target="tpu_custom_call" | custom-call | tf_op jit(solution)/shard_map/moment/pallas_call | solution.py:170
  84.1 0.8 collective-permute-done.40
  84.9 2.2 %collective-permute-start.43 = (f32[32,64]{1,0:T(8,128)S(1)}, f32[32,64]{1,0:T(8,128)S(1)}, u32[]{:S(2)}, u32[]{:S(2)}) collective-permute-start(f32[32,64]{1,0:T(8,128)S(1)} %add.87), channel_id=1, source_target_pairs={{0,24},{4,28},{8,16},{12,20},{16,8},{20,12},{24,0},{28,4},{1,25},{... | collective-permute-start | bytes 24584 | tf_op jit(solution)/shard_map/ppermute | solution.py:121
  87.4 1.9 %collective-permute-start.41 = (f32[32,64]{1,0:T(8,128)S(1)}, f32[32,64]{1,0:T(8,128)S(1)}, u32[]{:S(2)}, u32[]{:S(2)}) collective-permute-start(f32[32,64]{1,0:T(8,128)S(1)} %add.87), channel_id=1, source_target_pairs={{0,8},{4,12},{8,0},{12,4},{16,24},{20,28},{24,16},{28,20},{1,9},{5... | collective-permute-start | bytes 24584 | tf_op jit(solution)/shard_map/ppermute | solution.py:121
  89.3 1.1 %collective-permute-done.43 = f32[32,64]{1,0:T(8,128)S(1)} collective-permute-done((f32[32,64]{1,0:T(8,128)S(1)}, f32[32,64]{1,0:T(8,128)S(1)}, u32[]{:S(2)}, u32[]{:S(2)}) %collective-permute-start.43) | collective-permute-done | bytes 8224 | tf_op jit(solution)/shard_map/ppermute | solution.py:121
  90.5 1.3 %collective-permute-done.42 = f32[32,64]{1,0:T(8,128)S(1)} collective-permute-done((f32[32,64]{1,0:T(8,128)S(1)}, f32[32,64]{1,0:T(8,128)S(1)}, u32[]{:S(2)}, u32[]{:S(2)}) %collective-permute-start.42) | collective-permute-done | bytes 8224 | tf_op jit(solution)/shard_map/ppermute | solution.py:121
  91.8 1.7 %collective-permute-start.46 = (f32[32,64]{1,0:T(8,128)S(1)}, f32[32,64]{1,0:T(8,128)S(1)}, u32[]{:S(2)}, u32[]{:S(2)}) collective-permute-start(f32[32,64]{1,0:T(8,128)S(1)} %add_add_fusion.1), channel_id=1, source_target_pairs={{0,3},{1,2},{2,1},{3,0},{4,7},{5,6},{6,5},{7,4},{8,11},{9,10},{10,... | collective-permute-start | bytes 24584 | tf_op jit(solution)/shard_map/ppermute | solution.py:121
  93.5 1.3 %collective-permute-start.45 = (f32[32,64]{1,0:T(8,128)S(1)}, f32[32,64]{1,0:T(8,128)S(1)}, u32[]{:S(2)}, u32[]{:S(2)}) collective-permute-start(f32[32,64]{1,0:T(8,128)S(1)} %add_add_fusion.1), channel_id=1, source_target_pairs={{0,2},{1,3},{2,0},{3,1},{4,6},{5,7},{6,4},{7,5},{8,10},{9,11},{10,... | collective-permute-start | bytes 24584 | tf_op jit(solution)/shard_map/ppermute | solution.py:121
  95.3 1.1 %collective-permute-done.46 = f32[32,64]{1,0:T(8,128)S(1)} collective-permute-done((f32[32,64]{1,0:T(8,128)S(1)}, f32[32,64]{1,0:T(8,128)S(1)}, u32[]{:S(2)}, u32[]{:S(2)}) %collective-permute-start.46) | collective-permute-done | bytes 8224 | tf_op jit(solution)/shard_map/ppermute | solution.py:121
  96.5 0.8 collective-permute-done.45
  97.2 1.3 %collective-permute-done.44 = f32[32,64]{1,0:T(8,128)S(1)} collective-permute-done((f32[32,64]{1,0:T(8,128)S(1)}, f32[32,64]{1,0:T(8,128)S(1)}, u32[]{:S(2)}, u32[]{:S(2)}) %collective-permute-start.44) | collective-permute-done | bytes 8224 | tf_op jit(solution)/shard_map/ppermute | solution.py:121
  98.5 4.0 %finish.1 = (f32[32,512]{1,0:T(8,128)}, f32[32,32]{1,0:T(8,128)}) custom-call(f32[32,64]{1,0:T(8,128)S(1)} %add_add_fusion.sums, f32[32,512]{1,0:T(8,128)S(1)} %multiply_subtract_fusion.refs_0_.filtered), custom_call_target="tpu_custom_call" | custom-call | tf_op jit(solution)/shard_map/finish/pallas_call | solution.py:182
  (68 shorter events, 10.7 us)
Async XLA Ops:
  0.6 7.9 %collective-permute-start.5 = (f32[32,512]{1,0:T(8,128)}, f32[32,512]{1,0:T(8,128)S(1)}, u32[]{:S(2)}, u32[]{:S(2)}) collective-permute-start(f32[32,512]{1,0:T(8,128)} %refs_0_.1), channel_id=1, source_target_pairs={{0,24},{4,28},{8,16},{12,20},{16,8},{20,12},{24,0},{28,4},{1,25},{... | collective-permute-start | bytes 196616 | tf_op jit(solution)/shard_map/ppermute | solution.py:121
  5.8 5.8 %collective-permute-start.3 = (f32[32,512]{1,0:T(8,128)}, f32[32,512]{1,0:T(8,128)S(1)}, u32[]{:S(2)}, u32[]{:S(2)}) collective-permute-start(f32[32,512]{1,0:T(8,128)} %refs_0_.1), channel_id=1, source_target_pairs={{0,16},{4,20},{8,24},{12,28},{16,0},{20,4},{24,8},{28,12},{1,17},{... | collective-permute-start | bytes 196616 | tf_op jit(solution)/shard_map/ppermute | solution.py:121
  5.8 5.8 %collective-permute-start.1 = (f32[32,512]{1,0:T(8,128)}, f32[32,512]{1,0:T(8,128)S(1)}, u32[]{:S(2)}, u32[]{:S(2)}) collective-permute-start(f32[32,512]{1,0:T(8,128)} %refs_0_.1), channel_id=1, source_target_pairs={{0,8},{4,12},{8,0},{12,4},{16,24},{20,28},{24,16},{28,20},{1,9},{5... | collective-permute-start | bytes 196616 | tf_op jit(solution)/shard_map/ppermute | solution.py:121
  6.4 5.7 %collective-permute-start = (f32[32,512]{1,0:T(8,128)}, f32[32,512]{1,0:T(8,128)S(1)}, u32[]{:S(2)}, u32[]{:S(2)}) collective-permute-start(f32[32,512]{1,0:T(8,128)} %refs_0_.1), channel_id=1, source_target_pairs={{0,4},{4,0},{8,12},{12,8},{16,20},{20,16},{24,28},{28,24},{1,5},{5... | collective-permute-start | bytes 196616 | tf_op jit(solution)/shard_map/ppermute | solution.py:121
  8.6 3.5 %collective-permute-start.6 = (f32[32,512]{1,0:T(8,128)S(1)}, f32[32,512]{1,0:T(8,128)S(1)}, u32[]{:S(2)}, u32[]{:S(2)}) collective-permute-start(f32[32,512]{1,0:T(8,128)S(1)} %collective-permute-done.5.refs_6_), channel_id=1, source_target_pairs={{0,4},{4,0},{8,12},{12,8},{16,20},{20,16},{24,28},{28,24},{1,5},{5... | collective-permute-start | bytes 196616 | tf_op jit(solution)/shard_map/ppermute | solution.py:121
  11.6 1.3 %collective-permute-start.4 = (f32[32,512]{1,0:T(8,128)S(1)}, f32[32,512]{1,0:T(8,128)S(1)}, u32[]{:S(2)}, u32[]{:S(2)}) collective-permute-start(f32[32,512]{1,0:T(8,128)S(1)} %collective-permute-done.3.refs_4_), channel_id=1, source_target_pairs={{0,4},{4,0},{8,12},{12,8},{16,20},{20,16},{24,28},{28,24},{1,5},{5... | collective-permute-start | bytes 196616 | tf_op jit(solution)/shard_map/ppermute | solution.py:121
  11.6 1.4 %collective-permute-start.2 = (f32[32,512]{1,0:T(8,128)S(1)}, f32[32,512]{1,0:T(8,128)S(1)}, u32[]{:S(2)}, u32[]{:S(2)}) collective-permute-start(f32[32,512]{1,0:T(8,128)S(1)} %collective-permute-done.1.refs_2_), channel_id=1, source_target_pairs={{0,4},{4,0},{8,12},{12,8},{16,20},{20,16},{24,28},{28,24},{1,5},{5... | collective-permute-start | bytes 196616 | tf_op jit(solution)/shard_map/ppermute | solution.py:121
  17.2 30.7 %copy-start.2 = (f32[32,512]{1,0:T(8,128)S(1)}, f32[32,512]{1,0:T(8,128)}, u32[]{:S(2)}) copy-start(f32[32,512]{1,0:T(8,128)} %refs_0_.1) | copy-start | bytes 196612
  20.5 4.4 %collective-permute-start.7 = (f32[32,512]{1,0:T(8,128)S(1)}, f32[32,512]{1,0:T(8,128)S(1)}, u32[]{:S(2)}, u32[]{:S(2)}) collective-permute-start(f32[32,512]{1,0:T(8,128)S(1)} %get-tuple-element.15), channel_id=1, source_target_pairs={{0,1},{1,0},{2,3},{3,2},{4,5},{5,4},{6,7},{7,6},{8,9},{9,8},{10,11... | collective-permute-start | bytes 196616 | tf_op jit(solution)/shard_map/ppermute | solution.py:121
  22.0 4.3 %collective-permute-start.8 = (f32[32,512]{1,0:T(8,128)S(1)}, f32[32,512]{1,0:T(8,128)S(1)}, u32[]{:S(2)}, u32[]{:S(2)}) collective-permute-start(f32[32,512]{1,0:T(8,128)S(1)} %get-tuple-element.16), channel_id=1, source_target_pairs={{0,2},{1,3},{2,0},{3,1},{4,6},{5,7},{6,4},{7,5},{8,10},{9,11},{10,... | collective-permute-start | bytes 196616 | tf_op jit(solution)/shard_map/ppermute | solution.py:121
  23.5 5.2 %collective-permute-start.9 = (f32[32,512]{1,0:T(8,128)S(1)}, f32[32,512]{1,0:T(8,128)S(1)}, u32[]{:S(2)}, u32[]{:S(2)}) collective-permute-start(f32[32,512]{1,0:T(8,128)S(1)} %get-tuple-element.17), channel_id=1, source_target_pairs={{0,3},{1,2},{2,1},{3,0},{4,7},{5,6},{6,5},{7,4},{8,11},{9,10},{10,... | collective-permute-start | bytes 196616 | tf_op jit(solution)/shard_map/ppermute | solution.py:121
  28.7 6.5 %collective-permute-start.15 = (f32[32,512]{1,0:T(8,128)S(1)}, f32[32,512]{1,0:T(8,128)S(1)}, u32[]{:S(2)}, u32[]{:S(2)}) collective-permute-start(f32[32,512]{1,0:T(8,128)S(1)} %get-tuple-element.26.refs_0_), channel_id=1, source_target_pairs={{0,24},{4,28},{8,16},{12,20},{16,8},{20,12},{24,0},{28,4},{1,25},{... | collective-permute-start | bytes 196616 | tf_op jit(solution)/shard_map/ppermute | solution.py:121
  31.5 5.4 %collective-permute-start.13 = (f32[32,512]{1,0:T(8,128)S(1)}, f32[32,512]{1,0:T(8,128)S(1)}, u32[]{:S(2)}, u32[]{:S(2)}) collective-permute-start(f32[32,512]{1,0:T(8,128)S(1)} %get-tuple-element.26.refs_0_), channel_id=1, source_target_pairs={{0,16},{4,20},{8,24},{12,28},{16,0},{20,4},{24,8},{28,12},{1,17},{... | collective-permute-start | bytes 196616 | tf_op jit(solution)/shard_map/ppermute | solution.py:121
  31.5 5.4 %collective-permute-start.11 = (f32[32,512]{1,0:T(8,128)S(1)}, f32[32,512]{1,0:T(8,128)S(1)}, u32[]{:S(2)}, u32[]{:S(2)}) collective-permute-start(f32[32,512]{1,0:T(8,128)S(1)} %get-tuple-element.26.refs_0_), channel_id=1, source_target_pairs={{0,8},{4,12},{8,0},{12,4},{16,24},{20,28},{24,16},{28,20},{1,9},{5... | collective-permute-start | bytes 196616 | tf_op jit(solution)/shard_map/ppermute | solution.py:121
  33.2 4.3 %collective-permute-start.10 = (f32[32,512]{1,0:T(8,128)S(1)}, f32[32,512]{1,0:T(8,128)S(1)}, u32[]{:S(2)}, u32[]{:S(2)}) collective-permute-start(f32[32,512]{1,0:T(8,128)S(1)} %get-tuple-element.26.refs_0_), channel_id=1, source_target_pairs={{0,4},{4,0},{8,12},{12,8},{16,20},{20,16},{24,28},{28,24},{1,5},{5... | collective-permute-start | bytes 196616 | tf_op jit(solution)/shard_map/ppermute | solution.py:121
  35.2 2.2 %collective-permute-start.16 = (f32[32,512]{1,0:T(8,128)S(1)}, f32[32,512]{1,0:T(8,128)S(1)}, u32[]{:S(2)}, u32[]{:S(2)}) collective-permute-start(f32[32,512]{1,0:T(8,128)S(1)} %collective-permute-done.15.refs_6_), channel_id=1, source_target_pairs={{0,4},{4,0},{8,12},{12,8},{16,20},{20,16},{24,28},{28,24},{1,5},{5... | collective-permute-start | bytes 196616 | tf_op jit(solution)/shard_map/ppermute | solution.py:121
  37.0 1.3 %collective-permute-start.14 = (f32[32,512]{1,0:T(8,128)S(1)}, f32[32,512]{1,0:T(8,128)S(1)}, u32[]{:S(2)}, u32[]{:S(2)}) collective-permute-start(f32[32,512]{1,0:T(8,128)S(1)} %collective-permute-done.13.refs_4_), channel_id=1, source_target_pairs={{0,4},{4,0},{8,12},{12,8},{16,20},{20,16},{24,28},{28,24},{1,5},{5... | collective-permute-start | bytes 196616 | tf_op jit(solution)/shard_map/ppermute | solution.py:121
  37.0 1.4 %collective-permute-start.12 = (f32[32,512]{1,0:T(8,128)S(1)}, f32[32,512]{1,0:T(8,128)S(1)}, u32[]{:S(2)}, u32[]{:S(2)}) collective-permute-start(f32[32,512]{1,0:T(8,128)S(1)} %collective-permute-done.11.refs_2_), channel_id=1, source_target_pairs={{0,4},{4,0},{8,12},{12,8},{16,20},{20,16},{24,28},{28,24},{1,5},{5... | collective-permute-start | bytes 196616 | tf_op jit(solution)/shard_map/ppermute | solution.py:121
  41.6 4.4 %collective-permute-start.17 = (f32[32,512]{1,0:T(8,128)S(1)}, f32[32,512]{1,0:T(8,128)S(1)}, u32[]{:S(2)}, u32[]{:S(2)}) collective-permute-start(f32[32,512]{1,0:T(8,128)S(1)} %get-tuple-element.19), channel_id=1, source_target_pairs={{0,1},{1,0},{2,3},{3,2},{4,5},{5,4},{6,7},{7,6},{8,9},{9,8},{10,11... | collective-permute-start | bytes 196616 | tf_op jit(solution)/shard_map/ppermute | solution.py:121
  42.2 5.0 %collective-permute-start.18 = (f32[32,512]{1,0:T(8,128)S(1)}, f32[32,512]{1,0:T(8,128)S(1)}, u32[]{:S(2)}, u32[]{:S(2)}) collective-permute-start(f32[32,512]{1,0:T(8,128)S(1)} %get-tuple-element.20), channel_id=1, source_target_pairs={{0,2},{1,3},{2,0},{3,1},{4,6},{5,7},{6,4},{7,5},{8,10},{9,11},{10,... | collective-permute-start | bytes 196616 | tf_op jit(solution)/shard_map/ppermute | solution.py:121
  42.7 5.2 %collective-permute-start.19 = (f32[32,512]{1,0:T(8,128)S(1)}, f32[32,512]{1,0:T(8,128)S(1)}, u32[]{:S(2)}, u32[]{:S(2)}) collective-permute-start(f32[32,512]{1,0:T(8,128)S(1)} %get-tuple-element.21), channel_id=1, source_target_pairs={{0,3},{1,2},{2,1},{3,0},{4,7},{5,6},{6,5},{7,4},{8,11},{9,10},{10,... | collective-permute-start | bytes 196616 | tf_op jit(solution)/shard_map/ppermute | solution.py:121
  48.0 6.6 %collective-permute-start.25 = (f32[32,512]{1,0:T(8,128)S(1)}, f32[32,512]{1,0:T(8,128)S(1)}, u32[]{:S(2)}, u32[]{:S(2)}) collective-permute-start(f32[32,512]{1,0:T(8,128)S(1)} %multiply_subtract_fusion.1.refs_0_), channel_id=1, source_target_pairs={{0,24},{4,28},{8,16},{12,20},{16,8},{20,12},{24,0},{28,4},{1,25},{... | collective-permute-start | bytes 196616 | tf_op jit(solution)/shard_map/ppermute | solution.py:121
  50.5 5.6 %collective-permute-start.23 = (f32[32,512]{1,0:T(8,128)S(1)}, f32[32,512]{1,0:T(8,128)S(1)}, u32[]{:S(2)}, u32[]{:S(2)}) collective-permute-start(f32[32,512]{1,0:T(8,128)S(1)} %multiply_subtract_fusion.1.refs_0_), channel_id=1, source_target_pairs={{0,16},{4,20},{8,24},{12,28},{16,0},{20,4},{24,8},{28,12},{1,17},{... | collective-permute-start | bytes 196616 | tf_op jit(solution)/shard_map/ppermute | solution.py:121
  50.5 5.6 %collective-permute-start.21 = (f32[32,512]{1,0:T(8,128)S(1)}, f32[32,512]{1,0:T(8,128)S(1)}, u32[]{:S(2)}, u32[]{:S(2)}) collective-permute-start(f32[32,512]{1,0:T(8,128)S(1)} %multiply_subtract_fusion.1.refs_0_), channel_id=1, source_target_pairs={{0,8},{4,12},{8,0},{12,4},{16,24},{20,28},{24,16},{28,20},{1,9},{5... | collective-permute-start | bytes 196616 | tf_op jit(solution)/shard_map/ppermute | solution.py:121
  52.4 4.3 %collective-permute-start.20 = (f32[32,512]{1,0:T(8,128)S(1)}, f32[32,512]{1,0:T(8,128)S(1)}, u32[]{:S(2)}, u32[]{:S(2)}) collective-permute-start(f32[32,512]{1,0:T(8,128)S(1)} %multiply_subtract_fusion.1.refs_0_), channel_id=1, source_target_pairs={{0,4},{4,0},{8,12},{12,8},{16,20},{20,16},{24,28},{28,24},{1,5},{5... | collective-permute-start | bytes 196616 | tf_op jit(solution)/shard_map/ppermute | solution.py:121
  54.5 2.2 %collective-permute-start.26 = (f32[32,512]{1,0:T(8,128)S(1)}, f32[32,512]{1,0:T(8,128)S(1)}, u32[]{:S(2)}, u32[]{:S(2)}) collective-permute-start(f32[32,512]{1,0:T(8,128)S(1)} %collective-permute-done.25.refs_6_), channel_id=1, source_target_pairs={{0,4},{4,0},{8,12},{12,8},{16,20},{20,16},{24,28},{28,24},{1,5},{5... | collective-permute-start | bytes 196616 | tf_op jit(solution)/shard_map/ppermute | solution.py:121
  56.1 1.3 %collective-permute-start.24 = (f32[32,512]{1,0:T(8,128)S(1)}, f32[32,512]{1,0:T(8,128)S(1)}, u32[]{:S(2)}, u32[]{:S(2)}) collective-permute-start(f32[32,512]{1,0:T(8,128)S(1)} %collective-permute-done.23.refs_4_), channel_id=1, source_target_pairs={{0,4},{4,0},{8,12},{12,8},{16,20},{20,16},{24,28},{28,24},{1,5},{5... | collective-permute-start | bytes 196616 | tf_op jit(solution)/shard_map/ppermute | solution.py:121
  56.1 1.4 %collective-permute-start.22 = (f32[32,512]{1,0:T(8,128)S(1)}, f32[32,512]{1,0:T(8,128)S(1)}, u32[]{:S(2)}, u32[]{:S(2)}) collective-permute-start(f32[32,512]{1,0:T(8,128)S(1)} %collective-permute-done.21.refs_2_), channel_id=1, source_target_pairs={{0,4},{4,0},{8,12},{12,8},{16,20},{20,16},{24,28},{28,24},{1,5},{5... | collective-permute-start | bytes 196616 | tf_op jit(solution)/shard_map/ppermute | solution.py:121
  60.8 4.4 %collective-permute-start.27 = (f32[32,512]{1,0:T(8,128)S(1)}, f32[32,512]{1,0:T(8,128)S(1)}, u32[]{:S(2)}, u32[]{:S(2)}) collective-permute-start(f32[32,512]{1,0:T(8,128)S(1)} %get-tuple-element.23), channel_id=1, source_target_pairs={{0,1},{1,0},{2,3},{3,2},{4,5},{5,4},{6,7},{7,6},{8,9},{9,8},{10,11... | collective-permute-start | bytes 196616 | tf_op jit(solution)/shard_map/ppermute | solution.py:121
  62.4 4.3 %collective-permute-start.28 = (f32[32,512]{1,0:T(8,128)S(1)}, f32[32,512]{1,0:T(8,128)S(1)}, u32[]{:S(2)}, u32[]{:S(2)}) collective-permute-start(f32[32,512]{1,0:T(8,128)S(1)} %get-tuple-element.24), channel_id=1, source_target_pairs={{0,2},{1,3},{2,0},{3,1},{4,6},{5,7},{6,4},{7,5},{8,10},{9,11},{10,... | collective-permute-start | bytes 196616 | tf_op jit(solution)/shard_map/ppermute | solution.py:121
  63.9 5.2 %collective-permute-start.29 = (f32[32,512]{1,0:T(8,128)S(1)}, f32[32,512]{1,0:T(8,128)S(1)}, u32[]{:S(2)}, u32[]{:S(2)}) collective-permute-start(f32[32,512]{1,0:T(8,128)S(1)} %get-tuple-element.25), channel_id=1, source_target_pairs={{0,3},{1,2},{2,1},{3,0},{4,7},{5,6},{6,5},{7,4},{8,11},{9,10},{10,... | collective-permute-start | bytes 196616 | tf_op jit(solution)/shard_map/ppermute | solution.py:121
  69.1 6.5 %collective-permute-start.39 = (f32[32,512]{1,0:T(8,128)S(1)}, f32[32,512]{1,0:T(8,128)S(1)}, u32[]{:S(2)}, u32[]{:S(2)}) collective-permute-start(f32[32,512]{1,0:T(8,128)S(1)} %multiply_subtract_fusion.refs_0_.filtered), channel_id=1, source_target_pairs={{0,3},{1,2},{2,1},{3,0},{4,7},{5,6},{6,5},{7,4},{8,11},{9,10},{10,... | collective-permute-start | bytes 196616 | tf_op jit(solution)/shard_map/ppermute | solution.py:121
  69.7 7.4 %collective-permute-start.38 = (f32[32,512]{1,0:T(8,128)S(1)}, f32[32,512]{1,0:T(8,128)S(1)}, u32[]{:S(2)}, u32[]{:S(2)}) collective-permute-start(f32[32,512]{1,0:T(8,128)S(1)} %multiply_subtract_fusion.refs_0_.filtered), channel_id=1, source_target_pairs={{0,2},{1,3},{2,0},{3,1},{4,6},{5,7},{6,4},{7,5},{8,10},{9,11},{10,... | collective-permute-start | bytes 196616 | tf_op jit(solution)/shard_map/ppermute | solution.py:121
  71.2 6.1 %collective-permute-start.35 = (f32[32,512]{1,0:T(8,128)S(1)}, f32[32,512]{1,0:T(8,128)S(1)}, u32[]{:S(2)}, u32[]{:S(2)}) collective-permute-start(f32[32,512]{1,0:T(8,128)S(1)} %multiply_subtract_fusion.refs_0_.filtered), channel_id=1, source_target_pairs={{0,24},{4,28},{8,16},{12,20},{16,8},{20,12},{24,0},{28,4},{1,25},{... | collective-permute-start | bytes 196616 | tf_op jit(solution)/shard_map/ppermute | solution.py:121
  73.4 5.3 %collective-permute-start.33 = (f32[32,512]{1,0:T(8,128)S(1)}, f32[32,512]{1,0:T(8,128)S(1)}, u32[]{:S(2)}, u32[]{:S(2)}) collective-permute-start(f32[32,512]{1,0:T(8,128)S(1)} %multiply_subtract_fusion.refs_0_.filtered), channel_id=1, source_target_pairs={{0,16},{4,20},{8,24},{12,28},{16,0},{20,4},{24,8},{28,12},{1,17},{... | collective-permute-start | bytes 196616 | tf_op jit(solution)/shard_map/ppermute | solution.py:121
  73.4 5.3 %collective-permute-start.31 = (f32[32,512]{1,0:T(8,128)S(1)}, f32[32,512]{1,0:T(8,128)S(1)}, u32[]{:S(2)}, u32[]{:S(2)}) collective-permute-start(f32[32,512]{1,0:T(8,128)S(1)} %multiply_subtract_fusion.refs_0_.filtered), channel_id=1, source_target_pairs={{0,8},{4,12},{8,0},{12,4},{16,24},{20,28},{24,16},{28,20},{1,9},{5... | collective-permute-start | bytes 196616 | tf_op jit(solution)/shard_map/ppermute | solution.py:121
  75.6 4.3 %collective-permute-start.37 = (f32[32,512]{1,0:T(8,128)S(1)}, f32[32,512]{1,0:T(8,128)S(1)}, u32[]{:S(2)}, u32[]{:S(2)}) collective-permute-start(f32[32,512]{1,0:T(8,128)S(1)} %multiply_subtract_fusion.refs_0_.filtered), channel_id=1, source_target_pairs={{0,1},{1,0},{2,3},{3,2},{4,5},{5,4},{6,7},{7,6},{8,9},{9,8},{10,11... | collective-permute-start | bytes 196616 | tf_op jit(solution)/shard_map/ppermute | solution.py:121
  77.1 2.8 %collective-permute-start.30 = (f32[32,512]{1,0:T(8,128)S(1)}, f32[32,512]{1,0:T(8,128)S(1)}, u32[]{:S(2)}, u32[]{:S(2)}) collective-permute-start(f32[32,512]{1,0:T(8,128)S(1)} %multiply_subtract_fusion.refs_0_.filtered), channel_id=1, source_target_pairs={{0,4},{4,0},{8,12},{12,8},{16,20},{20,16},{24,28},{28,24},{1,5},{5... | collective-permute-start | bytes 196616 | tf_op jit(solution)/shard_map/ppermute | solution.py:121
  77.3 2.6 %collective-permute-start.36 = (f32[32,512]{1,0:T(8,128)S(1)}, f32[32,512]{1,0:T(8,128)S(1)}, u32[]{:S(2)}, u32[]{:S(2)}) collective-permute-start(f32[32,512]{1,0:T(8,128)S(1)} %collective-permute-done.35.refs_6_), channel_id=1, source_target_pairs={{0,4},{4,0},{8,12},{12,8},{16,20},{20,16},{24,28},{28,24},{1,5},{5... | collective-permute-start | bytes 196616 | tf_op jit(solution)/shard_map/ppermute | solution.py:121
  78.7 1.3 %collective-permute-start.34 = (f32[32,512]{1,0:T(8,128)S(1)}, f32[32,512]{1,0:T(8,128)S(1)}, u32[]{:S(2)}, u32[]{:S(2)}) collective-permute-start(f32[32,512]{1,0:T(8,128)S(1)} %collective-permute-done.33.refs_4_), channel_id=1, source_target_pairs={{0,4},{4,0},{8,12},{12,8},{16,20},{20,16},{24,28},{28,24},{1,5},{5... | collective-permute-start | bytes 196616 | tf_op jit(solution)/shard_map/ppermute | solution.py:121
  78.7 1.4 %collective-permute-start.32 = (f32[32,512]{1,0:T(8,128)S(1)}, f32[32,512]{1,0:T(8,128)S(1)}, u32[]{:S(2)}, u32[]{:S(2)}) collective-permute-start(f32[32,512]{1,0:T(8,128)S(1)} %collective-permute-done.31.refs_2_), channel_id=1, source_target_pairs={{0,4},{4,0},{8,12},{12,8},{16,20},{20,16},{24,28},{28,24},{1,5},{5... | collective-permute-start | bytes 196616 | tf_op jit(solution)/shard_map/ppermute | solution.py:121
  83.7 1.2 %collective-permute-start.40 = (f32[32,64]{1,0:T(8,128)S(1)}, f32[32,64]{1,0:T(8,128)S(1)}, u32[]{:S(2)}, u32[]{:S(2)}) collective-permute-start(f32[32,64]{1,0:T(8,128)S(1)} %moment.1), channel_id=1, source_target_pairs={{0,4},{4,0},{8,12},{12,8},{16,20},{20,16},{24,28},{28,24},{1,5},{5... | collective-permute-start | bytes 24584 | tf_op jit(solution)/shard_map/ppermute | solution.py:121
  84.9 5.5 %collective-permute-start.43 = (f32[32,64]{1,0:T(8,128)S(1)}, f32[32,64]{1,0:T(8,128)S(1)}, u32[]{:S(2)}, u32[]{:S(2)}) collective-permute-start(f32[32,64]{1,0:T(8,128)S(1)} %add.87), channel_id=1, source_target_pairs={{0,24},{4,28},{8,16},{12,20},{16,8},{20,12},{24,0},{28,4},{1,25},{... | collective-permute-start | bytes 24584 | tf_op jit(solution)/shard_map/ppermute | solution.py:121
  87.1 4.6 %collective-permute-start.42 = (f32[32,64]{1,0:T(8,128)S(1)}, f32[32,64]{1,0:T(8,128)S(1)}, u32[]{:S(2)}, u32[]{:S(2)}) collective-permute-start(f32[32,64]{1,0:T(8,128)S(1)} %add.87), channel_id=1, source_target_pairs={{0,16},{4,20},{8,24},{12,28},{16,0},{20,4},{24,8},{28,12},{1,17},{... | collective-permute-start | bytes 24584 | tf_op jit(solution)/shard_map/ppermute | solution.py:121
  87.4 4.4 %collective-permute-start.41 = (f32[32,64]{1,0:T(8,128)S(1)}, f32[32,64]{1,0:T(8,128)S(1)}, u32[]{:S(2)}, u32[]{:S(2)}) collective-permute-start(f32[32,64]{1,0:T(8,128)S(1)} %add.87), channel_id=1, source_target_pairs={{0,8},{4,12},{8,0},{12,4},{16,24},{20,28},{24,16},{28,20},{1,9},{5... | collective-permute-start | bytes 24584 | tf_op jit(solution)/shard_map/ppermute | solution.py:121
  91.8 4.7 %collective-permute-start.46 = (f32[32,64]{1,0:T(8,128)S(1)}, f32[32,64]{1,0:T(8,128)S(1)}, u32[]{:S(2)}, u32[]{:S(2)}) collective-permute-start(f32[32,64]{1,0:T(8,128)S(1)} %add_add_fusion.1), channel_id=1, source_target_pairs={{0,3},{1,2},{2,1},{3,0},{4,7},{5,6},{6,5},{7,4},{8,11},{9,10},{10,... | collective-permute-start | bytes 24584 | tf_op jit(solution)/shard_map/ppermute | solution.py:121
  93.5 3.7 %collective-permute-start.45 = (f32[32,64]{1,0:T(8,128)S(1)}, f32[32,64]{1,0:T(8,128)S(1)}, u32[]{:S(2)}, u32[]{:S(2)}) collective-permute-start(f32[32,64]{1,0:T(8,128)S(1)} %add_add_fusion.1), channel_id=1, source_target_pairs={{0,2},{1,3},{2,0},{3,1},{4,6},{5,7},{6,4},{7,5},{8,10},{9,11},{10,... | collective-permute-start | bytes 24584 | tf_op jit(solution)/shard_map/ppermute | solution.py:121
  94.8 3.7 %collective-permute-start.44 = (f32[32,64]{1,0:T(8,128)S(1)}, f32[32,64]{1,0:T(8,128)S(1)}, u32[]{:S(2)}, u32[]{:S(2)}) collective-permute-start(f32[32,64]{1,0:T(8,128)S(1)} %add_add_fusion.1), channel_id=1, source_target_pairs={{0,1},{1,0},{2,3},{3,2},{4,5},{5,4},{6,7},{7,6},{8,9},{9,8},{10,11... | collective-permute-start | bytes 24584 | tf_op jit(solution)/shard_map/ppermute | solution.py:121
  (3 other events, 27.6 us)

commit v2 on v1

--- a/solution.py
+++ b/solution.py
@@ -29,40 +29,57 @@
     return high, low
 
 
-def accumulate_tiles(slots, tiles, parts, halves, total):
+def stage_kernel(tiles, high, low, arrived, sems):
+    chunks = sems.shape[0]
+    width = tiles.shape[0] // chunks
+    copies = [
+        pltpu.make_async_copy(
+            tiles.at[pl.ds(chunk * width, width)], arrived.at[pl.ds(chunk * width, width)], sems.at[chunk]
+        )
+        for chunk in range(chunks)
+    ]
+    for copy in copies:
+        copy.start()
+    for chunk, copy in enumerate(copies):
+        copy.wait()
+        for slot in range(chunk * width, (chunk + 1) * width):
+            high[slot], low[slot] = split(arrived[slot].T)
+
+
+def accumulate_tiles(slots, high, low, parts, halves, total):
     subspace = parts[0].shape[0]
-    edge = tiles.shape[1]
+    edge = high.shape[1]
     per_part = parts[0].shape[1] // edge
+    places = slots[...]
     for index, part in enumerate(parts):
         for block in range(per_part):
-            high, low = split(part[:, block * edge : (block + 1) * edge])
-            halves[index * per_part + block, :subspace] = high
-            halves[index * per_part + block, subspace:] = low
+            upper, lower = split(part[:, block * edge : (block + 1) * edge])
+            halves[index * per_part + block, :subspace] = upper
+            halves[index * per_part + block, subspace:] = lower
     total[...] = jnp.zeros_like(total)
-    for slot in range(tiles.shape[0]):
-        vectors = halves[slots[1, slot]]
-        tile_high, tile_low = split(tiles[slot])
-        first = dot_rows(vectors, tile_high)
-        second = dot_rows(vectors[:subspace], tile_low)
-        total[slots[0, slot]] += first[:subspace] + first[subspace:] + second
-
-
-def product_kernel(n_row, n_col, slots, tiles, *refs):
+    for slot in range(high.shape[0]):
+        vectors = halves[places[1, slot]]
+        first = jnp.dot(vectors, high[slot], preferred_element_type=jnp.float32)
+        second = jnp.dot(vectors[:subspace], low[slot], preferred_element_type=jnp.float32)
+        total[places[0, slot]] += first[:subspace] + first[subspace:] + second
+
+
+def product_kernel(n_row, n_col, slots, high, low, *refs):
     parts, outs = refs[:n_row], refs[n_row : n_row + n_col]
     halves, total = refs[n_row + n_col :]
-    accumulate_tiles(slots, tiles, parts, halves, total)
-    edge = tiles.shape[1]
+    accumulate_tiles(slots, high, low, parts, halves, total)
+    edge = high.shape[1]
     per_part = parts[0].shape[1] // edge
     for index, out in enumerate(outs):
         for block in range(per_part):
             out[:, block * edge : (block + 1) * edge] = total[index * per_part + block]
 
 
-def moment_kernel(n_row, n_col, slots, tiles, degrees, *refs):
+def moment_kernel(n_row, n_col, slots, high, low, degrees, *refs):
     parts, sides = refs[:n_row], refs[n_row : n_row + n_col - 1]
     out, halves, total = refs[n_row + n_col - 1 :]
-    accumulate_tiles(slots, tiles, parts, halves, total)
-    edge = tiles.shape[1]
+    accumulate_tiles(slots, high, low, parts, halves, total)
+    edge = high.shape[1]
     subspace, width = parts[0].shape
     per_part = width // edge
     own = parts[0][...]
@@ -78,28 +95,40 @@
     out[...] = jnp.concatenate([gram, moment], 1)
 
 
+def eliminate(work, size, panel):
+    row = lax.broadcasted_iota(jnp.int32, work.shape, 0)
+    pivots = jnp.ones_like(work)
+    for first in range(0, size, panel):
+        columns = [
+            jnp.broadcast_to(work[:, index : index + 1], work.shape)
+            for index in range(first, first + panel)
+        ]
+        for index in range(panel):
+            step = first + index
+            pivot = columns[index][step : step + 1, :]
+            pivots = jnp.where(row == step, pivot, pivots)
+            ratio = jnp.where(row > step, columns[index], 0.0) * (1.0 / pivot)
+            work = work - ratio * work[step : step + 1, :]
+            for later in range(index + 1, panel):
+                columns[later] = columns[later] - ratio * columns[later][step : step + 1, :]
+    return work, lax.rsqrt(pivots)
+
+
 def finish_kernel(nverts, sums, filtered, basis, projected):
     subspace = filtered.shape[0]
     both = sums[...] * (1.0 / nverts)
     gram, moment = both[:, :subspace], both[:, subspace:]
+    moment = 0.5 * (moment + moment.T)
     row = lax.broadcasted_iota(jnp.int32, (subspace, subspace), 0)
     column = lax.broadcasted_iota(jnp.int32, (subspace, subspace), 1)
-    work = jnp.concatenate([gram, (row == column).astype(jnp.float32)], 1)
-    wide_row = lax.broadcasted_iota(jnp.int32, (subspace, 2 * subspace), 0)
-    scale = jnp.zeros((subspace, 1), jnp.float32)
-    for step in range(subspace):
-        pivot = work[step : step + 1, step : step + 1]
-        scale = jnp.where(wide_row[:, :1] == step, lax.rsqrt(pivot), scale)
-        ratio = work[:, step : step + 1] / pivot
-        work = jnp.where(wide_row > step, work - ratio * work[step : step + 1, :], work)
-    inverse = scale * work[:, subspace:]
-    highest = lax.Precision.HIGHEST
+    identity = (row == column).astype(jnp.float32)
+    work, scale = eliminate(jnp.concatenate([gram, identity, moment], 1), subspace, 8)
+    work = work * scale
+    inverse, half = work[:, subspace : 2 * subspace], work[:, 2 * subspace :]
+    projected[...] = dot_rows(half, inverse, lax.Precision.HIGHEST)
     basis[...] = jnp.dot(
-        inverse, filtered[...], precision=highest, preferred_element_type=jnp.float32
+        inverse, filtered[...], precision=lax.Precision.HIGHEST, preferred_element_type=jnp.float32
     )
-    half = jnp.dot(inverse, moment, precision=highest, preferred_element_type=jnp.float32)
-    whole = dot_rows(half, inverse, highest)
-    projected[...] = 0.5 * (whole + whole.T)
 
 
 def body(n_row, n_col, start_basis, degrees, tiles, tile_rows, tile_cols, counts):
@@ -139,20 +168,31 @@
         pltpu.VMEM((n_row * per_part, 2 * subspace, edge), jnp.bfloat16),
         pltpu.VMEM((n_col * per_part + 1, subspace, edge), jnp.float32),
     ]
-    slots_spec = pl.BlockSpec(memory_space=pltpu.SMEM)
     params = pltpu.CompilerParams(vmem_limit_bytes=20 * MIB)
     piece = jax.ShapeDtypeStruct((subspace, width), jnp.float32)
+    high, low = pl.pallas_call(
+        stage_kernel,
+        out_shape=[jax.ShapeDtypeStruct(tiles.shape, jnp.bfloat16)] * 2,
+        in_specs=[pl.BlockSpec(memory_space=pltpu.HBM)],
+        out_specs=vmem(2),
+        scratch_shapes=[
+            pltpu.VMEM(tiles.shape, jnp.float32),
+            pltpu.SemaphoreType.DMA((slots_held // 2,)),
+        ],
+        compiler_params=pltpu.CompilerParams(vmem_limit_bytes=42 * MIB),
+        name="stage",
+    )(tiles)
 
     def weights(vectors):
         partial_values = pl.pallas_call(
             functools.partial(product_kernel, n_row, n_col),
             out_shape=[piece] * n_col,
-            in_specs=[slots_spec, *vmem(1 + n_row)],
+            in_specs=vmem(3 + n_row),
             out_specs=vmem(n_col),
             scratch_shapes=scratch,
             compiler_params=params,
             name="tile_products",
-        )(slots, tiles, *gather_row(vectors))
+        )(slots, high, low, *gather_row(vectors))
         total = partial_values[0]
         for distance in range(1, n_col):
             total = total + swap(partial_values[distance], "col", n_col, distance)
@@ -170,12 +210,12 @@
     sums = pl.pallas_call(
         functools.partial(moment_kernel, n_row, n_col),
         out_shape=jax.ShapeDtypeStruct((subspace, 2 * subspace), jnp.float32),
-        in_specs=[slots_spec, *vmem(2 + n_row + n_col - 1)],
+        in_specs=vmem(4 + n_row + n_col - 1),
         out_specs=pl.BlockSpec(memory_space=pltpu.VMEM),
         scratch_shapes=scratch,
         compiler_params=params,
         name="moment",
-    )(slots, tiles, degrees, *gather_row(filtered), *gather_col(filtered))
+    )(slots, high, low, degrees, *gather_row(filtered), *gather_col(filtered))
     sums = sums + swap(sums, "row", n_row, 1)
     sums = sum([swap(sums, "row", n_row, distance) for distance in range(2, n_row, 2)], sums)
     sums = sum([swap(sums, "col", n_col, distance) for distance in range(1, n_col)], sums)

time: 103 us -> 91 us (0.88)
  Pallas kernels: 17.3 us -> 12.7 us
  local copies, waits for them, and re-layouts: 4.23 us -> 0.01 us
  waiting for transfers between devices: 34.8 us -> 31.4 us
    pallas_call x3, Pallas kernels: 9.7 us -> 4.29 us  [weights(): pl.pallas_call(functools.partial(product_kernel, n_row, n_col), out_shape...]
    pallas_call x0 -> x1, Pallas kernels: none -> 4.54 us  [body(): pl.pallas_call(stage_kernel, out_shape=[jax.ShapeDtypeStruct(tiles.shape,...]
    unnamed x8 -> x4, local copies, waits for them, and re-layouts: 4.23 us -> 0.01 us
    ppermute x47, waiting for transfers between devices: 34.8 us -> 31.4 us  [swap(): return lax.ppermute(value, axis, [(i, i ^ distance) for i in range(size)])]
    pallas_call x1, Pallas kernels: 3.98 us -> 2.08 us  [body(): pl.pallas_call(functools.partial(finish_kernel, nverts), out_shape=[piece...]
    pallas_call x1, Pallas kernels: 3.6 us -> 1.76 us  [body(): pl.pallas_call(functools.partial(moment_kernel, n_row, n_col), out_shape=...]
  transfers between devices with their start and end apart: 47 -> 47, of which waited for: 32 -> 31; matrix products, arithmetic and copies ran while one was open for 1% -> 1% of each run, Pallas kernels for 0% -> 5%
where the time goes in v2:
time: 91 us; the launch traced here: 90.8 us
  starting transfers between devices  44.5 us (49%)
  waiting for transfers between devices  31.4 us (35%)
  Pallas kernels  12.7 us (14%)
  between operations  1.4 us (2%)
    ppermute x47, starting transfers between devices, swap(): return lax.ppermute(value, axis, [(i, i ^ distance) for i in range(size)])  44.5 us
    ppermute x47, waiting for transfers between devices, swap(): return lax.ppermute(value, axis, [(i, i ^ distance) for i in range(size)])  31.4 us
    pallas_call x1, Pallas kernels, body(): pl.pallas_call(stage_kernel, out_shape=[jax.ShapeDtypeStruct(tiles.shape,...  4.54 us
    pallas_call x3, Pallas kernels, weights(): pl.pallas_call(functools.partial(product_kernel, n_row, n_col), out_shape...  4.29 us
    pallas_call x1, Pallas kernels, body(): pl.pallas_call(functools.partial(finish_kernel, nverts), out_shape=[piece...  2.08 us
  transfers between devices with their start and end apart: 47, of which 31 were waited for; matrix products, arithmetic and copies ran while one was open for 1% of the time, Pallas kernels for 5%

profile of v2, /device:TPU:0, one launch (start us, length us, event | category | flops | bytes accessed | tf_op | source)
XLA Modules:
  0.0 90.8 jit_solution(12987662602071559745)
XLA Ops:
  0.6 5.1 %collective-permute-start.5 = (f32[32,512]{1,0:T(8,128)}, f32[32,512]{1,0:T(8,128)S(1)}, u32[]{:S(2)}, u32[]{:S(2)}) collective-permute-start(f32[32,512]{1,0:T(8,128)} %refs_0_.1), channel_id=1, source_target_pairs={{0,24},{4,28},{8,16},{12,20},{16,8},{20,12},{24,0},{28,4},{1,25},{... | collective-permute-start | bytes 196616 | tf_op jit(solution)/shard_map/ppermute | solution.py:150
  7.0 0.7 compare_select_fusion
  7.7 4.5 %stage.1 = (bf16[32,256,256]{2,1,0:T(8,128)(2,1)S(1)}, bf16[32,256,256]{2,1,0:T(8,128)(2,1)S(1)}) custom-call(f32[32,256,256]{2,1,0:T(8,128)} %tiles.1), custom_call_target="tpu_custom_call" | custom-call | tf_op jit(solution)/shard_map/stage/pallas_call | solution.py:173
  14.3 1.4 %tile_products.3 = (f32[32,512]{1,0:T(8,128)S(1)}, f32[32,512]{1,0:T(8,128)S(1)}, f32[32,512]{1,0:T(8,128)S(1)}, f32[32,512]{1,0:T(8,128)S(1)}) custom-call(s32[2,32]{1,0:T(2,128)S(1)} %pad_add_fusion.slots, bf16[32,256,256]{2,1,0:T(8,128)(2,1)S(1)} %get-tuple-element.16.high, bf16[32,256,256]{2,1,0:T(8,128)(2,1)S(1)} %get-tuple-element.17.low, ...), custom_call_target="tpu_custom_call" | custom-call | tf_op jit(solution)/shard_map/tile_products/pallas_call | solution.py:187
  15.7 1.7 %collective-permute-start.7 = (f32[32,512]{1,0:T(8,128)S(1)}, f32[32,512]{1,0:T(8,128)S(1)}, u32[]{:S(2)}, u32[]{:S(2)}) collective-permute-start(f32[32,512]{1,0:T(8,128)S(1)} %get-tuple-element.19), channel_id=1, source_target_pairs={{0,1},{1,0},{2,3},{3,2},{4,5},{5,4},{6,7},{7,6},{8,9},{9,8},{10,11... | collective-permute-start | bytes 196616 | tf_op jit(solution)/shard_map/ppermute | solution.py:150
  17.4 1.5 %collective-permute-start.8 = (f32[32,512]{1,0:T(8,128)S(1)}, f32[32,512]{1,0:T(8,128)S(1)}, u32[]{:S(2)}, u32[]{:S(2)}) collective-permute-start(f32[32,512]{1,0:T(8,128)S(1)} %get-tuple-element.20), channel_id=1, source_target_pairs={{0,2},{1,3},{2,0},{3,1},{4,6},{5,7},{6,4},{7,5},{8,10},{9,11},{10,... | collective-permute-start | bytes 196616 | tf_op jit(solution)/shard_map/ppermute | solution.py:150
  19.3 0.9 collective-permute-done.7
  20.2 1.5 %collective-permute-done.8 = f32[32,512]{1,0:T(8,128)S(1)} collective-permute-done((f32[32,512]{1,0:T(8,128)S(1)}, f32[32,512]{1,0:T(8,128)S(1)}, u32[]{:S(2)}, u32[]{:S(2)}) %collective-permute-start.8) | collective-permute-done | bytes 65568 | tf_op jit(solution)/shard_map/ppermute | solution.py:150
  21.7 2.4 %collective-permute-done.9 = f32[32,512]{1,0:T(8,128)S(1)} collective-permute-done((f32[32,512]{1,0:T(8,128)S(1)}, f32[32,512]{1,0:T(8,128)S(1)}, u32[]{:S(2)}, u32[]{:S(2)}) %collective-permute-start.9) | collective-permute-done | bytes 65568 | tf_op jit(solution)/shard_map/ppermute | solution.py:150
  24.2 3.7 %collective-permute-start.15 = (f32[32,512]{1,0:T(8,128)S(1)}, f32[32,512]{1,0:T(8,128)S(1)}, u32[]{:S(2)}, u32[]{:S(2)}) collective-permute-start(f32[32,512]{1,0:T(8,128)S(1)} %get-tuple-element.30.refs_0_), channel_id=1, source_target_pairs={{0,24},{4,28},{8,16},{12,20},{16,8},{20,12},{24,0},{28,4},{1,25},{... | collective-permute-start | bytes 196616 | tf_op jit(solution)/shard_map/ppermute | solution.py:150
  27.8 0.8 collective-permute-start.11
  28.6 1.8 %collective-permute-done.15.refs_6_ = f32[32,512]{1,0:T(8,128)S(1)} collective-permute-done((f32[32,512]{1,0:T(8,128)S(1)}, f32[32,512]{1,0:T(8,128)S(1)}, u32[]{:S(2)}, u32[]{:S(2)}) %collective-permute-start.15) | collective-permute-done | bytes 65568 | tf_op jit(solution)/shard_map/ppermute | solution.py:150
  30.4 2.6 %collective-permute-done.13.refs_4_ = f32[32,512]{1,0:T(8,128)S(1)} collective-permute-done((f32[32,512]{1,0:T(8,128)S(1)}, f32[32,512]{1,0:T(8,128)S(1)}, u32[]{:S(2)}, u32[]{:S(2)}) %collective-permute-start.13) | collective-permute-done | bytes 65568 | tf_op jit(solution)/shard_map/ppermute | solution.py:150
  33.5 0.7 collective-permute-done.14.refs_5_
  34.4 1.4 %tile_products.4 = (f32[32,512]{1,0:T(8,128)S(1)}, f32[32,512]{1,0:T(8,128)S(1)}, f32[32,512]{1,0:T(8,128)S(1)}, f32[32,512]{1,0:T(8,128)S(1)}) custom-call(s32[2,32]{1,0:T(2,128)S(1)} %pad_add_fusion.slots, bf16[32,256,256]{2,1,0:T(8,128)(2,1)S(1)} %get-tuple-element.16.high, bf16[32,256,256]{2,1,0:T(8,128)(2,1)S(1)} %get-tuple-element.17.low, ...), custom_call_target="tpu_custom_call" | custom-call | tf_op jit(solution)/shard_map/tile_products/pallas_call | solution.py:187
  37.0 2.4 %collective-permute-start.19 = (f32[32,512]{1,0:T(8,128)S(1)}, f32[32,512]{1,0:T(8,128)S(1)}, u32[]{:S(2)}, u32[]{:S(2)}) collective-permute-start(f32[32,512]{1,0:T(8,128)S(1)} %get-tuple-element.25), channel_id=1, source_target_pairs={{0,3},{1,2},{2,1},{3,0},{4,7},{5,6},{6,5},{7,4},{8,11},{9,10},{10,... | collective-permute-start | bytes 196616 | tf_op jit(solution)/shard_map/ppermute | solution.py:150
  39.4 0.9 collective-permute-done.17
  40.3 1.1 %collective-permute-done.18 = f32[32,512]{1,0:T(8,128)S(1)} collective-permute-done((f32[32,512]{1,0:T(8,128)S(1)}, f32[32,512]{1,0:T(8,128)S(1)}, u32[]{:S(2)}, u32[]{:S(2)}) %collective-permute-start.18) | collective-permute-done | bytes 65568 | tf_op jit(solution)/shard_map/ppermute | solution.py:150
  41.4 0.7 collective-permute-done.19
  42.2 2.1 %collective-permute-start.25 = (f32[32,512]{1,0:T(8,128)S(1)}, f32[32,512]{1,0:T(8,128)S(1)}, u32[]{:S(2)}, u32[]{:S(2)}) collective-permute-start(f32[32,512]{1,0:T(8,128)S(1)} %multiply_subtract_fusion.1.refs_0_), channel_id=1, source_target_pairs={{0,24},{4,28},{8,16},{12,20},{16,8},{20,12},{24,0},{28,4},{1,25},{... | collective-permute-start | bytes 196616 | tf_op jit(solution)/shard_map/ppermute | solution.py:150
  44.3 2.3 %collective-permute-start.21 = (f32[32,512]{1,0:T(8,128)S(1)}, f32[32,512]{1,0:T(8,128)S(1)}, u32[]{:S(2)}, u32[]{:S(2)}) collective-permute-start(f32[32,512]{1,0:T(8,128)S(1)} %multiply_subtract_fusion.1.refs_0_), channel_id=1, source_target_pairs={{0,8},{4,12},{8,0},{12,4},{16,24},{20,28},{24,16},{28,20},{1,9},{5... | collective-permute-start | bytes 196616 | tf_op jit(solution)/shard_map/ppermute | solution.py:150
  46.6 2.3 %collective-permute-done.25.refs_6_ = f32[32,512]{1,0:T(8,128)S(1)} collective-permute-done((f32[32,512]{1,0:T(8,128)S(1)}, f32[32,512]{1,0:T(8,128)S(1)}, u32[]{:S(2)}, u32[]{:S(2)}) %collective-permute-start.25) | collective-permute-done | bytes 65568 | tf_op jit(solution)/shard_map/ppermute | solution.py:150
  48.9 1.4 %collective-permute-done.23.refs_4_ = f32[32,512]{1,0:T(8,128)S(1)} collective-permute-done((f32[32,512]{1,0:T(8,128)S(1)}, f32[32,512]{1,0:T(8,128)S(1)}, u32[]{:S(2)}, u32[]{:S(2)}) %collective-permute-start.23) | collective-permute-done | bytes 65568 | tf_op jit(solution)/shard_map/ppermute | solution.py:150
  50.8 0.7 collective-permute-done.24.refs_5_
  51.7 1.4 %tile_products.5 = (f32[32,512]{1,0:T(8,128)S(1)}, f32[32,512]{1,0:T(8,128)S(1)}, f32[32,512]{1,0:T(8,128)S(1)}, f32[32,512]{1,0:T(8,128)S(1)}) custom-call(s32[2,32]{1,0:T(2,128)S(1)} %pad_add_fusion.slots, bf16[32,256,256]{2,1,0:T(8,128)(2,1)S(1)} %get-tuple-element.16.high, bf16[32,256,256]{2,1,0:T(8,128)(2,1)S(1)} %get-tuple-element.17.low, ...), custom_call_target="tpu_custom_call" | custom-call | tf_op jit(solution)/shard_map/tile_products/pallas_call | solution.py:187
  53.1 1.6 %collective-permute-start.27 = (f32[32,512]{1,0:T(8,128)S(1)}, f32[32,512]{1,0:T(8,128)S(1)}, u32[]{:S(2)}, u32[]{:S(2)}) collective-permute-start(f32[32,512]{1,0:T(8,128)S(1)} %get-tuple-element.27), channel_id=1, source_target_pairs={{0,1},{1,0},{2,3},{3,2},{4,5},{5,4},{6,7},{7,6},{8,9},{9,8},{10,11... | collective-permute-start | bytes 196616 | tf_op jit(solution)/shard_map/ppermute | solution.py:150
  54.7 1.4 %collective-permute-start.28 = (f32[32,512]{1,0:T(8,128)S(1)}, f32[32,512]{1,0:T(8,128)S(1)}, u32[]{:S(2)}, u32[]{:S(2)}) collective-permute-start(f32[32,512]{1,0:T(8,128)S(1)} %get-tuple-element.28), channel_id=1, source_target_pairs={{0,2},{1,3},{2,0},{3,1},{4,6},{5,7},{6,4},{7,5},{8,10},{9,11},{10,... | collective-permute-start | bytes 196616 | tf_op jit(solution)/shard_map/ppermute | solution.py:150
  56.7 0.9 collective-permute-done.27
  57.5 1.4 %collective-permute-done.28 = f32[32,512]{1,0:T(8,128)S(1)} collective-permute-done((f32[32,512]{1,0:T(8,128)S(1)}, f32[32,512]{1,0:T(8,128)S(1)}, u32[]{:S(2)}, u32[]{:S(2)}) %collective-permute-start.28) | collective-permute-done | bytes 65568 | tf_op jit(solution)/shard_map/ppermute | solution.py:150
  59.0 2.3 %collective-permute-done.29 = f32[32,512]{1,0:T(8,128)S(1)} collective-permute-done((f32[32,512]{1,0:T(8,128)S(1)}, f32[32,512]{1,0:T(8,128)S(1)}, u32[]{:S(2)}, u32[]{:S(2)}) %collective-permute-start.29) | collective-permute-done | bytes 65568 | tf_op jit(solution)/shard_map/ppermute | solution.py:150
  62.0 1.4 %collective-permute-start.38 = (f32[32,512]{1,0:T(8,128)S(1)}, f32[32,512]{1,0:T(8,128)S(1)}, u32[]{:S(2)}, u32[]{:S(2)}) collective-permute-start(f32[32,512]{1,0:T(8,128)S(1)} %multiply_subtract_fusion.refs_0_.filtered), channel_id=1, source_target_pairs={{0,2},{1,3},{2,0},{3,1},{4,6},{5,7},{6,4},{7,5},{8,10},{9,11},{10,... | collective-permute-start | bytes 196616 | tf_op jit(solution)/shard_map/ppermute | solution.py:150
  63.4 2.1 %collective-permute-start.35 = (f32[32,512]{1,0:T(8,128)S(1)}, f32[32,512]{1,0:T(8,128)S(1)}, u32[]{:S(2)}, u32[]{:S(2)}) collective-permute-start(f32[32,512]{1,0:T(8,128)S(1)} %multiply_subtract_fusion.refs_0_.filtered), channel_id=1, source_target_pairs={{0,24},{4,28},{8,16},{12,20},{16,8},{20,12},{24,0},{28,4},{1,25},{... | collective-permute-start | bytes 196616 | tf_op jit(solution)/shard_map/ppermute | solution.py:150
  65.4 2.3 %collective-permute-start.31 = (f32[32,512]{1,0:T(8,128)S(1)}, f32[32,512]{1,0:T(8,128)S(1)}, u32[]{:S(2)}, u32[]{:S(2)}) collective-permute-start(f32[32,512]{1,0:T(8,128)S(1)} %multiply_subtract_fusion.refs_0_.filtered), channel_id=1, source_target_pairs={{0,8},{4,12},{8,0},{12,4},{16,24},{20,28},{24,16},{28,20},{1,9},{5... | collective-permute-start | bytes 196616 | tf_op jit(solution)/shard_map/ppermute | solution.py:150
  67.8 1.5 %collective-permute-start.37 = (f32[32,512]{1,0:T(8,128)S(1)}, f32[32,512]{1,0:T(8,128)S(1)}, u32[]{:S(2)}, u32[]{:S(2)}) collective-permute-start(f32[32,512]{1,0:T(8,128)S(1)} %multiply_subtract_fusion.refs_0_.filtered), channel_id=1, source_target_pairs={{0,1},{1,0},{2,3},{3,2},{4,5},{5,4},{6,7},{7,6},{8,9},{9,8},{10,11... | collective-permute-start | bytes 196616 | tf_op jit(solution)/shard_map/ppermute | solution.py:150
  69.8 1.1 %collective-permute-done.33.refs_4_ = f32[32,512]{1,0:T(8,128)S(1)} collective-permute-done((f32[32,512]{1,0:T(8,128)S(1)}, f32[32,512]{1,0:T(8,128)S(1)}, u32[]{:S(2)}, u32[]{:S(2)}) %collective-permute-start.33) | collective-permute-done | bytes 65568 | tf_op jit(solution)/shard_map/ppermute | solution.py:150
  71.4 0.7 collective-permute-done.37.refs_8_
  72.3 1.8 %moment.1 = f32[32,64]{1,0:T(8,128)S(1)} custom-call(s32[2,32]{1,0:T(2,128)S(1)} %pad_add_fusion.slots, bf16[32,256,256]{2,1,0:T(8,128)(2,1)S(1)} %get-tuple-element.16.high, bf16[32,256,256]{2,1,0:T(8,128)(2,1)S(1)} %get-tuple-element.17.low, f32[1,512]{1,0:T(1,128)S(1)} %bitcast.3, f32[32,512]{1,0:T(8,128)S(1)} %multiply_subtract_fusion.refs_0_.filtered, ...), custom_call_target="tpu_custom_call" | custom-call | tf_op jit(solution)/shard_map/moment/pallas_call | solution.py:210
  74.4 0.8 collective-permute-done.40
  75.2 2.1 %collective-permute-start.43 = (f32[32,64]{1,0:T(8,128)S(1)}, f32[32,64]{1,0:T(8,128)S(1)}, u32[]{:S(2)}, u32[]{:S(2)}) collective-permute-start(f32[32,64]{1,0:T(8,128)S(1)} %add.87), channel_id=1, source_target_pairs={{0,24},{4,28},{8,16},{12,20},{16,8},{20,12},{24,0},{28,4},{1,25},{... | collective-permute-start | bytes 24584 | tf_op jit(solution)/shard_map/ppermute | solution.py:150
  77.7 1.9 %collective-permute-start.41 = (f32[32,64]{1,0:T(8,128)S(1)}, f32[32,64]{1,0:T(8,128)S(1)}, u32[]{:S(2)}, u32[]{:S(2)}) collective-permute-start(f32[32,64]{1,0:T(8,128)S(1)} %add.87), channel_id=1, source_target_pairs={{0,8},{4,12},{8,0},{12,4},{16,24},{20,28},{24,16},{28,20},{1,9},{5... | collective-permute-start | bytes 24584 | tf_op jit(solution)/shard_map/ppermute | solution.py:150
  79.6 1.1 %collective-permute-done.43 = f32[32,64]{1,0:T(8,128)S(1)} collective-permute-done((f32[32,64]{1,0:T(8,128)S(1)}, f32[32,64]{1,0:T(8,128)S(1)}, u32[]{:S(2)}, u32[]{:S(2)}) %collective-permute-start.43) | collective-permute-done | bytes 8224 | tf_op jit(solution)/shard_map/ppermute | solution.py:150
  80.8 1.2 %collective-permute-done.42 = f32[32,64]{1,0:T(8,128)S(1)} collective-permute-done((f32[32,64]{1,0:T(8,128)S(1)}, f32[32,64]{1,0:T(8,128)S(1)}, u32[]{:S(2)}, u32[]{:S(2)}) %collective-permute-start.42) | collective-permute-done | bytes 8224 | tf_op jit(solution)/shard_map/ppermute | solution.py:150
  81.9 1.7 %collective-permute-start.46 = (f32[32,64]{1,0:T(8,128)S(1)}, f32[32,64]{1,0:T(8,128)S(1)}, u32[]{:S(2)}, u32[]{:S(2)}) collective-permute-start(f32[32,64]{1,0:T(8,128)S(1)} %add_add_fusion.1), channel_id=1, source_target_pairs={{0,3},{1,2},{2,1},{3,0},{4,7},{5,6},{6,5},{7,4},{8,11},{9,10},{10,... | collective-permute-start | bytes 24584 | tf_op jit(solution)/shard_map/ppermute | solution.py:150
  83.6 1.4 %collective-permute-start.45 = (f32[32,64]{1,0:T(8,128)S(1)}, f32[32,64]{1,0:T(8,128)S(1)}, u32[]{:S(2)}, u32[]{:S(2)}) collective-permute-start(f32[32,64]{1,0:T(8,128)S(1)} %add_add_fusion.1), channel_id=1, source_target_pairs={{0,2},{1,3},{2,0},{3,1},{4,6},{5,7},{6,4},{7,5},{8,10},{9,11},{10,... | collective-permute-start | bytes 24584 | tf_op jit(solution)/shard_map/ppermute | solution.py:150
  85.5 1.1 %collective-permute-done.46 = f32[32,64]{1,0:T(8,128)S(1)} collective-permute-done((f32[32,64]{1,0:T(8,128)S(1)}, f32[32,64]{1,0:T(8,128)S(1)}, u32[]{:S(2)}, u32[]{:S(2)}) %collective-permute-start.46) | collective-permute-done | bytes 8224 | tf_op jit(solution)/shard_map/ppermute | solution.py:150
  86.6 0.7 collective-permute-done.45
  87.3 1.4 %collective-permute-done.44 = f32[32,64]{1,0:T(8,128)S(1)} collective-permute-done((f32[32,64]{1,0:T(8,128)S(1)}, f32[32,64]{1,0:T(8,128)S(1)}, u32[]{:S(2)}, u32[]{:S(2)}) %collective-permute-start.44) | collective-permute-done | bytes 8224 | tf_op jit(solution)/shard_map/ppermute | solution.py:150
  88.7 2.1 %finish.1 = (f32[32,512]{1,0:T(8,128)}, f32[32,32]{1,0:T(8,128)}) custom-call(f32[32,64]{1,0:T(8,128)S(1)} %add_add_fusion.sums, f32[32,512]{1,0:T(8,128)S(1)} %multiply_subtract_fusion.refs_0_.filtered), custom_call_target="tpu_custom_call" | custom-call | tf_op jit(solution)/shard_map/finish/pallas_call | solution.py:222
  (65 shorter events, 9.4 us)
Async XLA Ops:
  0.6 11.7 %collective-permute-start.5 = (f32[32,512]{1,0:T(8,128)}, f32[32,512]{1,0:T(8,128)S(1)}, u32[]{:S(2)}, u32[]{:S(2)}) collective-permute-start(f32[32,512]{1,0:T(8,128)} %refs_0_.1), channel_id=1, source_target_pairs={{0,24},{4,28},{8,16},{12,20},{16,8},{20,12},{24,0},{28,4},{1,25},{... | collective-permute-start | bytes 196616 | tf_op jit(solution)/shard_map/ppermute | solution.py:150
  5.7 7.1 %collective-permute-start.3 = (f32[32,512]{1,0:T(8,128)}, f32[32,512]{1,0:T(8,128)S(1)}, u32[]{:S(2)}, u32[]{:S(2)}) collective-permute-start(f32[32,512]{1,0:T(8,128)} %refs_0_.1), channel_id=1, source_target_pairs={{0,16},{4,20},{8,24},{12,28},{16,0},{20,4},{24,8},{28,12},{1,17},{... | collective-permute-start | bytes 196616 | tf_op jit(solution)/shard_map/ppermute | solution.py:150
  5.7 7.2 %collective-permute-start.1 = (f32[32,512]{1,0:T(8,128)}, f32[32,512]{1,0:T(8,128)S(1)}, u32[]{:S(2)}, u32[]{:S(2)}) collective-permute-start(f32[32,512]{1,0:T(8,128)} %refs_0_.1), channel_id=1, source_target_pairs={{0,8},{4,12},{8,0},{12,4},{16,24},{20,28},{24,16},{28,20},{1,9},{5... | collective-permute-start | bytes 196616 | tf_op jit(solution)/shard_map/ppermute | solution.py:150
  6.4 7.0 %collective-permute-start = (f32[32,512]{1,0:T(8,128)}, f32[32,512]{1,0:T(8,128)S(1)}, u32[]{:S(2)}, u32[]{:S(2)}) collective-permute-start(f32[32,512]{1,0:T(8,128)} %refs_0_.1), channel_id=1, source_target_pairs={{0,4},{4,0},{8,12},{12,8},{16,20},{20,16},{24,28},{28,24},{1,5},{5... | collective-permute-start | bytes 196616 | tf_op jit(solution)/shard_map/ppermute | solution.py:150
  7.7 6.6 %copy-start = (f32[32,512]{1,0:T(8,128)S(1)}, f32[32,512]{1,0:T(8,128)}, u32[]{:S(2)}) copy-start(f32[32,512]{1,0:T(8,128)} %refs_0_.1) | copy-start | bytes 196612
  12.3 1.5 %collective-permute-start.6 = (f32[32,512]{1,0:T(8,128)S(1)}, f32[32,512]{1,0:T(8,128)S(1)}, u32[]{:S(2)}, u32[]{:S(2)}) collective-permute-start(f32[32,512]{1,0:T(8,128)S(1)} %collective-permute-done.5.refs_6_), channel_id=1, source_target_pairs={{0,4},{4,0},{8,12},{12,8},{16,20},{20,16},{24,28},{28,24},{1,5},{5... | collective-permute-start | bytes 196616 | tf_op jit(solution)/shard_map/ppermute | solution.py:150
  12.9 1.3 %collective-permute-start.4 = (f32[32,512]{1,0:T(8,128)S(1)}, f32[32,512]{1,0:T(8,128)S(1)}, u32[]{:S(2)}, u32[]{:S(2)}) collective-permute-start(f32[32,512]{1,0:T(8,128)S(1)} %collective-permute-done.3.refs_4_), channel_id=1, source_target_pairs={{0,4},{4,0},{8,12},{12,8},{16,20},{20,16},{24,28},{28,24},{1,5},{5... | collective-permute-start | bytes 196616 | tf_op jit(solution)/shard_map/ppermute | solution.py:150
  13.0 1.3 %collective-permute-start.2 = (f32[32,512]{1,0:T(8,128)S(1)}, f32[32,512]{1,0:T(8,128)S(1)}, u32[]{:S(2)}, u32[]{:S(2)}) collective-permute-start(f32[32,512]{1,0:T(8,128)S(1)} %collective-permute-done.1.refs_2_), channel_id=1, source_target_pairs={{0,4},{4,0},{8,12},{12,8},{16,20},{20,16},{24,28},{28,24},{1,5},{5... | collective-permute-start | bytes 196616 | tf_op jit(solution)/shard_map/ppermute | solution.py:150
  15.7 4.4 %collective-permute-start.7 = (f32[32,512]{1,0:T(8,128)S(1)}, f32[32,512]{1,0:T(8,128)S(1)}, u32[]{:S(2)}, u32[]{:S(2)}) collective-permute-start(f32[32,512]{1,0:T(8,128)S(1)} %get-tuple-element.19), channel_id=1, source_target_pairs={{0,1},{1,0},{2,3},{3,2},{4,5},{5,4},{6,7},{7,6},{8,9},{9,8},{10,11... | collective-permute-start | bytes 196616 | tf_op jit(solution)/shard_map/ppermute | solution.py:150
  17.4 4.3 %collective-permute-start.8 = (f32[32,512]{1,0:T(8,128)S(1)}, f32[32,512]{1,0:T(8,128)S(1)}, u32[]{:S(2)}, u32[]{:S(2)}) collective-permute-start(f32[32,512]{1,0:T(8,128)S(1)} %get-tuple-element.20), channel_id=1, source_target_pairs={{0,2},{1,3},{2,0},{3,1},{4,6},{5,7},{6,4},{7,5},{8,10},{9,11},{10,... | collective-permute-start | bytes 196616 | tf_op jit(solution)/shard_map/ppermute | solution.py:150
  19.0 5.2 %collective-permute-start.9 = (f32[32,512]{1,0:T(8,128)S(1)}, f32[32,512]{1,0:T(8,128)S(1)}, u32[]{:S(2)}, u32[]{:S(2)}) collective-permute-start(f32[32,512]{1,0:T(8,128)S(1)} %get-tuple-element.21), channel_id=1, source_target_pairs={{0,3},{1,2},{2,1},{3,0},{4,7},{5,6},{6,5},{7,4},{8,11},{9,10},{10,... | collective-permute-start | bytes 196616 | tf_op jit(solution)/shard_map/ppermute | solution.py:150
  24.2 6.2 %collective-permute-start.15 = (f32[32,512]{1,0:T(8,128)S(1)}, f32[32,512]{1,0:T(8,128)S(1)}, u32[]{:S(2)}, u32[]{:S(2)}) collective-permute-start(f32[32,512]{1,0:T(8,128)S(1)} %get-tuple-element.30.refs_0_), channel_id=1, source_target_pairs={{0,24},{4,28},{8,16},{12,20},{16,8},{20,12},{24,0},{28,4},{1,25},{... | collective-permute-start | bytes 196616 | tf_op jit(solution)/shard_map/ppermute | solution.py:150
  27.8 5.2 %collective-permute-start.13 = (f32[32,512]{1,0:T(8,128)S(1)}, f32[32,512]{1,0:T(8,128)S(1)}, u32[]{:S(2)}, u32[]{:S(2)}) collective-permute-start(f32[32,512]{1,0:T(8,128)S(1)} %get-tuple-element.30.refs_0_), channel_id=1, source_target_pairs={{0,16},{4,20},{8,24},{12,28},{16,0},{20,4},{24,8},{28,12},{1,17},{... | collective-permute-start | bytes 196616 | tf_op jit(solution)/shard_map/ppermute | solution.py:150
  27.8 5.2 %collective-permute-start.11 = (f32[32,512]{1,0:T(8,128)S(1)}, f32[32,512]{1,0:T(8,128)S(1)}, u32[]{:S(2)}, u32[]{:S(2)}) collective-permute-start(f32[32,512]{1,0:T(8,128)S(1)} %get-tuple-element.30.refs_0_), channel_id=1, source_target_pairs={{0,8},{4,12},{8,0},{12,4},{16,24},{20,28},{24,16},{28,20},{1,9},{5... | collective-permute-start | bytes 196616 | tf_op jit(solution)/shard_map/ppermute | solution.py:150
  28.6 4.9 %collective-permute-start.10 = (f32[32,512]{1,0:T(8,128)S(1)}, f32[32,512]{1,0:T(8,128)S(1)}, u32[]{:S(2)}, u32[]{:S(2)}) collective-permute-start(f32[32,512]{1,0:T(8,128)S(1)} %get-tuple-element.30.refs_0_), channel_id=1, source_target_pairs={{0,4},{4,0},{8,12},{12,8},{16,20},{20,16},{24,28},{28,24},{1,5},{5... | collective-permute-start | bytes 196616 | tf_op jit(solution)/shard_map/ppermute | solution.py:150
  30.4 3.1 %collective-permute-start.16 = (f32[32,512]{1,0:T(8,128)S(1)}, f32[32,512]{1,0:T(8,128)S(1)}, u32[]{:S(2)}, u32[]{:S(2)}) collective-permute-start(f32[32,512]{1,0:T(8,128)S(1)} %collective-permute-done.15.refs_6_), channel_id=1, source_target_pairs={{0,4},{4,0},{8,12},{12,8},{16,20},{20,16},{24,28},{28,24},{1,5},{5... | collective-permute-start | bytes 196616 | tf_op jit(solution)/shard_map/ppermute | solution.py:150
  33.0 1.3 %collective-permute-start.14 = (f32[32,512]{1,0:T(8,128)S(1)}, f32[32,512]{1,0:T(8,128)S(1)}, u32[]{:S(2)}, u32[]{:S(2)}) collective-permute-start(f32[32,512]{1,0:T(8,128)S(1)} %collective-permute-done.13.refs_4_), channel_id=1, source_target_pairs={{0,4},{4,0},{8,12},{12,8},{16,20},{20,16},{24,28},{28,24},{1,5},{5... | collective-permute-start | bytes 196616 | tf_op jit(solution)/shard_map/ppermute | solution.py:150
  33.0 1.4 %collective-permute-start.12 = (f32[32,512]{1,0:T(8,128)S(1)}, f32[32,512]{1,0:T(8,128)S(1)}, u32[]{:S(2)}, u32[]{:S(2)}) collective-permute-start(f32[32,512]{1,0:T(8,128)S(1)} %collective-permute-done.11.refs_2_), channel_id=1, source_target_pairs={{0,4},{4,0},{8,12},{12,8},{16,20},{20,16},{24,28},{28,24},{1,5},{5... | collective-permute-start | bytes 196616 | tf_op jit(solution)/shard_map/ppermute | solution.py:150
  35.8 4.4 %collective-permute-start.17 = (f32[32,512]{1,0:T(8,128)S(1)}, f32[32,512]{1,0:T(8,128)S(1)}, u32[]{:S(2)}, u32[]{:S(2)}) collective-permute-start(f32[32,512]{1,0:T(8,128)S(1)} %get-tuple-element.23), channel_id=1, source_target_pairs={{0,1},{1,0},{2,3},{3,2},{4,5},{5,4},{6,7},{7,6},{8,9},{9,8},{10,11... | collective-permute-start | bytes 196616 | tf_op jit(solution)/shard_map/ppermute | solution.py:150
  36.4 5.0 %collective-permute-start.18 = (f32[32,512]{1,0:T(8,128)S(1)}, f32[32,512]{1,0:T(8,128)S(1)}, u32[]{:S(2)}, u32[]{:S(2)}) collective-permute-start(f32[32,512]{1,0:T(8,128)S(1)} %get-tuple-element.24), channel_id=1, source_target_pairs={{0,2},{1,3},{2,0},{3,1},{4,6},{5,7},{6,4},{7,5},{8,10},{9,11},{10,... | collective-permute-start | bytes 196616 | tf_op jit(solution)/shard_map/ppermute | solution.py:150
  37.0 5.2 %collective-permute-start.19 = (f32[32,512]{1,0:T(8,128)S(1)}, f32[32,512]{1,0:T(8,128)S(1)}, u32[]{:S(2)}, u32[]{:S(2)}) collective-permute-start(f32[32,512]{1,0:T(8,128)S(1)} %get-tuple-element.25), channel_id=1, source_target_pairs={{0,3},{1,2},{2,1},{3,0},{4,7},{5,6},{6,5},{7,4},{8,11},{9,10},{10,... | collective-permute-start | bytes 196616 | tf_op jit(solution)/shard_map/ppermute | solution.py:150
  42.2 6.8 %collective-permute-start.25 = (f32[32,512]{1,0:T(8,128)S(1)}, f32[32,512]{1,0:T(8,128)S(1)}, u32[]{:S(2)}, u32[]{:S(2)}) collective-permute-start(f32[32,512]{1,0:T(8,128)S(1)} %multiply_subtract_fusion.1.refs_0_), channel_id=1, source_target_pairs={{0,24},{4,28},{8,16},{12,20},{16,8},{20,12},{24,0},{28,4},{1,25},{... | collective-permute-start | bytes 196616 | tf_op jit(solution)/shard_map/ppermute | solution.py:150
  44.3 6.0 %collective-permute-start.23 = (f32[32,512]{1,0:T(8,128)S(1)}, f32[32,512]{1,0:T(8,128)S(1)}, u32[]{:S(2)}, u32[]{:S(2)}) collective-permute-start(f32[32,512]{1,0:T(8,128)S(1)} %multiply_subtract_fusion.1.refs_0_), channel_id=1, source_target_pairs={{0,16},{4,20},{8,24},{12,28},{16,0},{20,4},{24,8},{28,12},{1,17},{... | collective-permute-start | bytes 196616 | tf_op jit(solution)/shard_map/ppermute | solution.py:150
  44.3 6.0 %collective-permute-start.21 = (f32[32,512]{1,0:T(8,128)S(1)}, f32[32,512]{1,0:T(8,128)S(1)}, u32[]{:S(2)}, u32[]{:S(2)}) collective-permute-start(f32[32,512]{1,0:T(8,128)S(1)} %multiply_subtract_fusion.1.refs_0_), channel_id=1, source_target_pairs={{0,8},{4,12},{8,0},{12,4},{16,24},{20,28},{24,16},{28,20},{1,9},{5... | collective-permute-start | bytes 196616 | tf_op jit(solution)/shard_map/ppermute | solution.py:150
  46.6 4.2 %collective-permute-start.20 = (f32[32,512]{1,0:T(8,128)S(1)}, f32[32,512]{1,0:T(8,128)S(1)}, u32[]{:S(2)}, u32[]{:S(2)}) collective-permute-start(f32[32,512]{1,0:T(8,128)S(1)} %multiply_subtract_fusion.1.refs_0_), channel_id=1, source_target_pairs={{0,4},{4,0},{8,12},{12,8},{16,20},{20,16},{24,28},{28,24},{1,5},{5... | collective-permute-start | bytes 196616 | tf_op jit(solution)/shard_map/ppermute | solution.py:150
  48.9 1.9 %collective-permute-start.26 = (f32[32,512]{1,0:T(8,128)S(1)}, f32[32,512]{1,0:T(8,128)S(1)}, u32[]{:S(2)}, u32[]{:S(2)}) collective-permute-start(f32[32,512]{1,0:T(8,128)S(1)} %collective-permute-done.25.refs_6_), channel_id=1, source_target_pairs={{0,4},{4,0},{8,12},{12,8},{16,20},{20,16},{24,28},{28,24},{1,5},{5... | collective-permute-start | bytes 196616 | tf_op jit(solution)/shard_map/ppermute | solution.py:150
  50.3 1.3 %collective-permute-start.24 = (f32[32,512]{1,0:T(8,128)S(1)}, f32[32,512]{1,0:T(8,128)S(1)}, u32[]{:S(2)}, u32[]{:S(2)}) collective-permute-start(f32[32,512]{1,0:T(8,128)S(1)} %collective-permute-done.23.refs_4_), channel_id=1, source_target_pairs={{0,4},{4,0},{8,12},{12,8},{16,20},{20,16},{24,28},{28,24},{1,5},{5... | collective-permute-start | bytes 196616 | tf_op jit(solution)/shard_map/ppermute | solution.py:150
  50.3 1.4 %collective-permute-start.22 = (f32[32,512]{1,0:T(8,128)S(1)}, f32[32,512]{1,0:T(8,128)S(1)}, u32[]{:S(2)}, u32[]{:S(2)}) collective-permute-start(f32[32,512]{1,0:T(8,128)S(1)} %collective-permute-done.21.refs_2_), channel_id=1, source_target_pairs={{0,4},{4,0},{8,12},{12,8},{16,20},{20,16},{24,28},{28,24},{1,5},{5... | collective-permute-start | bytes 196616 | tf_op jit(solution)/shard_map/ppermute | solution.py:150
  53.1 4.4 %collective-permute-start.27 = (f32[32,512]{1,0:T(8,128)S(1)}, f32[32,512]{1,0:T(8,128)S(1)}, u32[]{:S(2)}, u32[]{:S(2)}) collective-permute-start(f32[32,512]{1,0:T(8,128)S(1)} %get-tuple-element.27), channel_id=1, source_target_pairs={{0,1},{1,0},{2,3},{3,2},{4,5},{5,4},{6,7},{7,6},{8,9},{9,8},{10,11... | collective-permute-start | bytes 196616 | tf_op jit(solution)/shard_map/ppermute | solution.py:150
  54.7 4.3 %collective-permute-start.28 = (f32[32,512]{1,0:T(8,128)S(1)}, f32[32,512]{1,0:T(8,128)S(1)}, u32[]{:S(2)}, u32[]{:S(2)}) collective-permute-start(f32[32,512]{1,0:T(8,128)S(1)} %get-tuple-element.28), channel_id=1, source_target_pairs={{0,2},{1,3},{2,0},{3,1},{4,6},{5,7},{6,4},{7,5},{8,10},{9,11},{10,... | collective-permute-start | bytes 196616 | tf_op jit(solution)/shard_map/ppermute | solution.py:150
  56.1 5.2 %collective-permute-start.29 = (f32[32,512]{1,0:T(8,128)S(1)}, f32[32,512]{1,0:T(8,128)S(1)}, u32[]{:S(2)}, u32[]{:S(2)}) collective-permute-start(f32[32,512]{1,0:T(8,128)S(1)} %get-tuple-element.29), channel_id=1, source_target_pairs={{0,3},{1,2},{2,1},{3,0},{4,7},{5,6},{6,5},{7,4},{8,11},{9,10},{10,... | collective-permute-start | bytes 196616 | tf_op jit(solution)/shard_map/ppermute | solution.py:150
  61.3 6.5 %collective-permute-start.39 = (f32[32,512]{1,0:T(8,128)S(1)}, f32[32,512]{1,0:T(8,128)S(1)}, u32[]{:S(2)}, u32[]{:S(2)}) collective-permute-start(f32[32,512]{1,0:T(8,128)S(1)} %multiply_subtract_fusion.refs_0_.filtered), channel_id=1, source_target_pairs={{0,3},{1,2},{2,1},{3,0},{4,7},{5,6},{6,5},{7,4},{8,11},{9,10},{10,... | collective-permute-start | bytes 196616 | tf_op jit(solution)/shard_map/ppermute | solution.py:150
  62.0 7.3 %collective-permute-start.38 = (f32[32,512]{1,0:T(8,128)S(1)}, f32[32,512]{1,0:T(8,128)S(1)}, u32[]{:S(2)}, u32[]{:S(2)}) collective-permute-start(f32[32,512]{1,0:T(8,128)S(1)} %multiply_subtract_fusion.refs_0_.filtered), channel_id=1, source_target_pairs={{0,2},{1,3},{2,0},{3,1},{4,6},{5,7},{6,4},{7,5},{8,10},{9,11},{10,... | collective-permute-start | bytes 196616 | tf_op jit(solution)/shard_map/ppermute | solution.py:150
  63.4 6.1 %collective-permute-start.35 = (f32[32,512]{1,0:T(8,128)S(1)}, f32[32,512]{1,0:T(8,128)S(1)}, u32[]{:S(2)}, u32[]{:S(2)}) collective-permute-start(f32[32,512]{1,0:T(8,128)S(1)} %multiply_subtract_fusion.refs_0_.filtered), channel_id=1, source_target_pairs={{0,24},{4,28},{8,16},{12,20},{16,8},{20,12},{24,0},{28,4},{1,25},{... | collective-permute-start | bytes 196616 | tf_op jit(solution)/shard_map/ppermute | solution.py:150
  65.4 5.4 %collective-permute-start.33 = (f32[32,512]{1,0:T(8,128)S(1)}, f32[32,512]{1,0:T(8,128)S(1)}, u32[]{:S(2)}, u32[]{:S(2)}) collective-permute-start(f32[32,512]{1,0:T(8,128)S(1)} %multiply_subtract_fusion.refs_0_.filtered), channel_id=1, source_target_pairs={{0,16},{4,20},{8,24},{12,28},{16,0},{20,4},{24,8},{28,12},{1,17},{... | collective-permute-start | bytes 196616 | tf_op jit(solution)/shard_map/ppermute | solution.py:150
  65.4 5.4 %collective-permute-start.31 = (f32[32,512]{1,0:T(8,128)S(1)}, f32[32,512]{1,0:T(8,128)S(1)}, u32[]{:S(2)}, u32[]{:S(2)}) collective-permute-start(f32[32,512]{1,0:T(8,128)S(1)} %multiply_subtract_fusion.refs_0_.filtered), channel_id=1, source_target_pairs={{0,8},{4,12},{8,0},{12,4},{16,24},{20,28},{24,16},{28,20},{1,9},{5... | collective-permute-start | bytes 196616 | tf_op jit(solution)/shard_map/ppermute | solution.py:150
  67.8 4.3 %collective-permute-start.37 = (f32[32,512]{1,0:T(8,128)S(1)}, f32[32,512]{1,0:T(8,128)S(1)}, u32[]{:S(2)}, u32[]{:S(2)}) collective-permute-start(f32[32,512]{1,0:T(8,128)S(1)} %multiply_subtract_fusion.refs_0_.filtered), channel_id=1, source_target_pairs={{0,1},{1,0},{2,3},{3,2},{4,5},{5,4},{6,7},{7,6},{8,9},{9,8},{10,11... | collective-permute-start | bytes 196616 | tf_op jit(solution)/shard_map/ppermute | solution.py:150
  69.3 2.8 %collective-permute-start.30 = (f32[32,512]{1,0:T(8,128)S(1)}, f32[32,512]{1,0:T(8,128)S(1)}, u32[]{:S(2)}, u32[]{:S(2)}) collective-permute-start(f32[32,512]{1,0:T(8,128)S(1)} %multiply_subtract_fusion.refs_0_.filtered), channel_id=1, source_target_pairs={{0,4},{4,0},{8,12},{12,8},{16,20},{20,16},{24,28},{28,24},{1,5},{5... | collective-permute-start | bytes 196616 | tf_op jit(solution)/shard_map/ppermute | solution.py:150
  69.4 2.6 %collective-permute-start.36 = (f32[32,512]{1,0:T(8,128)S(1)}, f32[32,512]{1,0:T(8,128)S(1)}, u32[]{:S(2)}, u32[]{:S(2)}) collective-permute-start(f32[32,512]{1,0:T(8,128)S(1)} %collective-permute-done.35.refs_6_), channel_id=1, source_target_pairs={{0,4},{4,0},{8,12},{12,8},{16,20},{20,16},{24,28},{28,24},{1,5},{5... | collective-permute-start | bytes 196616 | tf_op jit(solution)/shard_map/ppermute | solution.py:150
  70.8 1.3 %collective-permute-start.34 = (f32[32,512]{1,0:T(8,128)S(1)}, f32[32,512]{1,0:T(8,128)S(1)}, u32[]{:S(2)}, u32[]{:S(2)}) collective-permute-start(f32[32,512]{1,0:T(8,128)S(1)} %collective-permute-done.33.refs_4_), channel_id=1, source_target_pairs={{0,4},{4,0},{8,12},{12,8},{16,20},{20,16},{24,28},{28,24},{1,5},{5... | collective-permute-start | bytes 196616 | tf_op jit(solution)/shard_map/ppermute | solution.py:150
  70.8 1.4 %collective-permute-start.32 = (f32[32,512]{1,0:T(8,128)S(1)}, f32[32,512]{1,0:T(8,128)S(1)}, u32[]{:S(2)}, u32[]{:S(2)}) collective-permute-start(f32[32,512]{1,0:T(8,128)S(1)} %collective-permute-done.31.refs_2_), channel_id=1, source_target_pairs={{0,4},{4,0},{8,12},{12,8},{16,20},{20,16},{24,28},{28,24},{1,5},{5... | collective-permute-start | bytes 196616 | tf_op jit(solution)/shard_map/ppermute | solution.py:150
  74.0 1.2 %collective-permute-start.40 = (f32[32,64]{1,0:T(8,128)S(1)}, f32[32,64]{1,0:T(8,128)S(1)}, u32[]{:S(2)}, u32[]{:S(2)}) collective-permute-start(f32[32,64]{1,0:T(8,128)S(1)} %moment.1), channel_id=1, source_target_pairs={{0,4},{4,0},{8,12},{12,8},{16,20},{20,16},{24,28},{28,24},{1,5},{5... | collective-permute-start | bytes 24584 | tf_op jit(solution)/shard_map/ppermute | solution.py:150
  75.2 5.5 %collective-permute-start.43 = (f32[32,64]{1,0:T(8,128)S(1)}, f32[32,64]{1,0:T(8,128)S(1)}, u32[]{:S(2)}, u32[]{:S(2)}) collective-permute-start(f32[32,64]{1,0:T(8,128)S(1)} %add.87), channel_id=1, source_target_pairs={{0,24},{4,28},{8,16},{12,20},{16,8},{20,12},{24,0},{28,4},{1,25},{... | collective-permute-start | bytes 24584 | tf_op jit(solution)/shard_map/ppermute | solution.py:150
  77.3 4.6 %collective-permute-start.42 = (f32[32,64]{1,0:T(8,128)S(1)}, f32[32,64]{1,0:T(8,128)S(1)}, u32[]{:S(2)}, u32[]{:S(2)}) collective-permute-start(f32[32,64]{1,0:T(8,128)S(1)} %add.87), channel_id=1, source_target_pairs={{0,16},{4,20},{8,24},{12,28},{16,0},{20,4},{24,8},{28,12},{1,17},{... | collective-permute-start | bytes 24584 | tf_op jit(solution)/shard_map/ppermute | solution.py:150
  77.7 4.2 %collective-permute-start.41 = (f32[32,64]{1,0:T(8,128)S(1)}, f32[32,64]{1,0:T(8,128)S(1)}, u32[]{:S(2)}, u32[]{:S(2)}) collective-permute-start(f32[32,64]{1,0:T(8,128)S(1)} %add.87), channel_id=1, source_target_pairs={{0,8},{4,12},{8,0},{12,4},{16,24},{20,28},{24,16},{28,20},{1,9},{5... | collective-permute-start | bytes 24584 | tf_op jit(solution)/shard_map/ppermute | solution.py:150
  81.9 4.7 %collective-permute-start.46 = (f32[32,64]{1,0:T(8,128)S(1)}, f32[32,64]{1,0:T(8,128)S(1)}, u32[]{:S(2)}, u32[]{:S(2)}) collective-permute-start(f32[32,64]{1,0:T(8,128)S(1)} %add_add_fusion.1), channel_id=1, source_target_pairs={{0,3},{1,2},{2,1},{3,0},{4,7},{5,6},{6,5},{7,4},{8,11},{9,10},{10,... | collective-permute-start | bytes 24584 | tf_op jit(solution)/shard_map/ppermute | solution.py:150
  83.6 3.7 %collective-permute-start.45 = (f32[32,64]{1,0:T(8,128)S(1)}, f32[32,64]{1,0:T(8,128)S(1)}, u32[]{:S(2)}, u32[]{:S(2)}) collective-permute-start(f32[32,64]{1,0:T(8,128)S(1)} %add_add_fusion.1), channel_id=1, source_target_pairs={{0,2},{1,3},{2,0},{3,1},{4,6},{5,7},{6,4},{7,5},{8,10},{9,11},{10,... | collective-permute-start | bytes 24584 | tf_op jit(solution)/shard_map/ppermute | solution.py:150
  84.9 3.7 %collective-permute-start.44 = (f32[32,64]{1,0:T(8,128)S(1)}, f32[32,64]{1,0:T(8,128)S(1)}, u32[]{:S(2)}, u32[]{:S(2)}) collective-permute-start(f32[32,64]{1,0:T(8,128)S(1)} %add_add_fusion.1), channel_id=1, source_target_pairs={{0,1},{1,0},{2,3},{3,2},{4,5},{5,4},{6,7},{7,6},{8,9},{9,8},{10,11... | collective-permute-start | bytes 24584 | tf_op jit(solution)/shard_map/ppermute | solution.py:150
  (1 other events, 5.0 us)

commit v3 on v2

--- a/solution.py
+++ b/solution.py
@@ -27,6 +27,18 @@
     high = value.astype(jnp.bfloat16)
     low = (value - high.astype(jnp.float32)).astype(jnp.bfloat16)
     return high, low
+
+
+def place_slots(n_col, per_part, rows, columns, counts):
+    shift = per_part.bit_length() - 1
+    row = rows[...] ^ (lax.axis_index("col") << shift)
+    column = columns[...] ^ (lax.axis_index("row") << shift)
+    live = lax.broadcasted_iota(jnp.int32, row.shape, 1) < counts[...]
+    return jnp.concatenate([jnp.where(live, row, n_col * per_part), column], 0)
+
+
+def place_kernel(n_col, per_part, rows, columns, counts, places):
+    places[...] = place_slots(n_col, per_part, rows, columns, counts)
 
 
 def stage_kernel(tiles, high, low, arrived, sems):
@@ -75,23 +87,26 @@
             out[:, block * edge : (block + 1) * edge] = total[index * per_part + block]
 
 
-def moment_kernel(n_row, n_col, slots, high, low, degrees, *refs):
-    parts, sides = refs[:n_row], refs[n_row : n_row + n_col - 1]
-    out, halves, total = refs[n_row + n_col - 1 :]
-    accumulate_tiles(slots, high, low, parts, halves, total)
-    edge = high.shape[1]
-    subspace, width = parts[0].shape
-    per_part = width // edge
+def moment_kernel(n_row, n_col, degrees, *refs):
+    parts, sides, products = refs[:n_row], refs[n_row : n_row + n_col - 1], refs[n_row + n_col - 1 : -1]
+    out = refs[-1]
+    subspace = parts[0].shape[0]
+
+    def quarters(left, right):
+        both = dot_rows(left, right)
+        both = both[:subspace] + both[subspace:]
+        return both[:, :subspace] + both[:, subspace:]
+
     own = parts[0][...]
-    gram = dot_rows(own, own, lax.Precision.HIGHEST)
     moment = dot_rows(own, own * degrees[...], lax.Precision.HIGHEST)
-    for index, side in enumerate((parts[0], *sides)):
-        for block in range(per_part):
-            left = jnp.concatenate(split(side[:, block * edge : (block + 1) * edge]), 0)
-            right = jnp.concatenate(split(total[index * per_part + block]), 0)
-            both = dot_rows(left, right)
-            both = both[:subspace] + both[subspace:]
-            moment -= both[:, :subspace] + both[:, subspace:]
+    gram = jnp.zeros_like(moment)
+    for part in parts:
+        both = jnp.concatenate(split(part[...]), 0)
+        gram += quarters(both, both)
+    for side, product in zip((parts[0], *sides), products):
+        moment -= quarters(
+            jnp.concatenate(split(side[...]), 0), jnp.concatenate(split(product[...]), 0)
+        )
     out[...] = jnp.concatenate([gram, moment], 1)
 
 
@@ -114,21 +129,30 @@
     return work, lax.rsqrt(pivots)
 
 
-def finish_kernel(nverts, sums, filtered, basis, projected):
+def factor_kernel(nverts, sums, filtered, inverse, basis):
     subspace = filtered.shape[0]
-    both = sums[...] * (1.0 / nverts)
-    gram, moment = both[:, :subspace], both[:, subspace:]
-    moment = 0.5 * (moment + moment.T)
+    gram = sums[:, :subspace] * (1.0 / nverts)
     row = lax.broadcasted_iota(jnp.int32, (subspace, subspace), 0)
     column = lax.broadcasted_iota(jnp.int32, (subspace, subspace), 1)
     identity = (row == column).astype(jnp.float32)
-    work, scale = eliminate(jnp.concatenate([gram, identity, moment], 1), subspace, 8)
-    work = work * scale
-    inverse, half = work[:, subspace : 2 * subspace], work[:, 2 * subspace :]
-    projected[...] = dot_rows(half, inverse, lax.Precision.HIGHEST)
+    work, scale = eliminate(jnp.concatenate([gram, identity], 1), subspace, 8)
+    solved = (work * scale)[:, subspace:]
+    inverse[...] = solved
     basis[...] = jnp.dot(
-        inverse, filtered[...], precision=lax.Precision.HIGHEST, preferred_element_type=jnp.float32
-    )
+        solved, filtered[...], precision=lax.Precision.HIGHEST, preferred_element_type=jnp.float32
+    )
+
+
+def project_kernel(nverts, sums, inverse, projected):
+    subspace = inverse.shape[0]
+    moment = sums[:, subspace:] * (0.5 / nverts)
+    half = jnp.dot(
+        inverse[...],
+        moment + moment.T,
+        precision=lax.Precision.HIGHEST,
+        preferred_element_type=jnp.float32,
+    )
+    projected[...] = dot_rows(half, inverse[...], lax.Precision.HIGHEST)
 
 
 def body(n_row, n_col, start_basis, degrees, tiles, tile_rows, tile_cols, counts):
@@ -136,27 +160,21 @@
     slots_held, edge = tiles.shape[0], tiles.shape[1]
     per_part = width // edge
     nverts = n_row * n_col * width
-    row, col = lax.axis_index("row"), lax.axis_index("col")
     degrees = degrees[None, :]
-
-    row_local, col_local = tile_rows[0], tile_cols[0]
-    row_place = ((row_local // per_part) ^ col) * per_part + row_local % per_part
-    col_place = ((col_local // per_part) ^ row) * per_part + col_local % per_part
-    live = jnp.arange(slots_held, dtype=jnp.int32) < counts[0, 0]
-    spare = n_col * per_part
-    slots = jnp.stack([jnp.where(live, row_place, spare), col_place])
 
     def swap(value, axis, size, distance):
         return lax.ppermute(value, axis, [(i, i ^ distance) for i in range(size)])
 
-    def gather_row(value):
+    def gather_row(value, behind=None):
         parts = [None] * n_row
         parts[0] = value
         for distance in range(2, n_row, 2):
             parts[distance] = swap(value, "row", n_row, distance)
+        if behind is not None:
+            parts[2::2], behind = lax.optimization_barrier((parts[2::2], behind))
         for distance in range(0, n_row, 2):
             parts[distance + 1] = swap(parts[distance], "row", n_row, 1)
-        return parts
+        return parts if behind is None else (parts, behind)
 
     def gather_col(value):
         return [swap(value, "col", n_col, distance) for distance in range(1, n_col)]
@@ -170,6 +188,14 @@
     ]
     params = pltpu.CompilerParams(vmem_limit_bytes=20 * MIB)
     piece = jax.ShapeDtypeStruct((subspace, width), jnp.float32)
+    slots = pl.pallas_call(
+        functools.partial(place_kernel, n_col, per_part),
+        out_shape=jax.ShapeDtypeStruct((2, slots_held), jnp.int32),
+        in_specs=vmem(3),
+        out_specs=pl.BlockSpec(memory_space=pltpu.VMEM),
+        compiler_params=params,
+        name="places",
+    )(tile_rows, tile_cols, counts)
     high, low = pl.pallas_call(
         stage_kernel,
         out_shape=[jax.ShapeDtypeStruct(tiles.shape, jnp.bfloat16)] * 2,
@@ -183,8 +209,10 @@
         name="stage",
     )(tiles)
 
-    def weights(vectors):
-        partial_values = pl.pallas_call(
+    parts, (slots, high, low) = gather_row(start_basis, (slots, high, low))
+
+    def products(parts):
+        return pl.pallas_call(
             functools.partial(product_kernel, n_row, n_col),
             out_shape=[piece] * n_col,
             in_specs=vmem(3 + n_row),
@@ -192,41 +220,59 @@
             scratch_shapes=scratch,
             compiler_params=params,
             name="tile_products",
-        )(slots, high, low, *gather_row(vectors))
+        )(slots, high, low, *parts)
+
+    def weights(parts):
+        partial_values = products(parts)
         total = partial_values[0]
-        for distance in range(1, n_col):
+        for distance in reversed(range(1, n_col)):
             total = total + swap(partial_values[distance], "col", n_col, distance)
         return total
 
-    def shifted(vectors):
-        return ((degrees - center_shift) * vectors - weights(vectors)) / spread_radius
+    def shifted(vectors, parts=None):
+        parts = gather_row(vectors) if parts is None else parts
+        return ((degrees - center_shift) * vectors - weights(parts)) / spread_radius
 
     previous = start_basis
-    filtered = shifted(start_basis)
+    filtered = shifted(start_basis, parts)
     for level in range(DEGREE - 1):
         following = 2.0 * shifted(filtered) - previous
         previous, filtered = (filtered, following)
 
+    parts = gather_row(filtered)
+    beside = filtered
+    sides = gather_col(beside)
+    sides, parts[n_row // 2 + 1] = lax.optimization_barrier((sides, parts[n_row // 2 + 1]))
+    pieces = products(parts)
     sums = pl.pallas_call(
         functools.partial(moment_kernel, n_row, n_col),
         out_shape=jax.ShapeDtypeStruct((subspace, 2 * subspace), jnp.float32),
-        in_specs=vmem(4 + n_row + n_col - 1),
+        in_specs=vmem(n_row + 2 * n_col),
         out_specs=pl.BlockSpec(memory_space=pltpu.VMEM),
-        scratch_shapes=scratch,
         compiler_params=params,
         name="moment",
-    )(slots, high, low, degrees, *gather_row(filtered), *gather_col(filtered))
-    sums = sums + swap(sums, "row", n_row, 1)
-    sums = sum([swap(sums, "row", n_row, distance) for distance in range(2, n_row, 2)], sums)
+    )(degrees, *parts, *sides, *pieces)
     sums = sum([swap(sums, "col", n_col, distance) for distance in range(1, n_col)], sums)
-    basis, projected = pl.pallas_call(
-        functools.partial(finish_kernel, nverts),
-        out_shape=[piece, jax.ShapeDtypeStruct((subspace, subspace), jnp.float32)],
+    inverse, basis = pl.pallas_call(
+        functools.partial(factor_kernel, nverts),
+        out_shape=[jax.ShapeDtypeStruct((subspace, subspace), jnp.float32), piece],
         in_specs=vmem(2),
         out_specs=vmem(2),
         compiler_params=params,
-        name="finish",
+        name="factor",
     )(sums, filtered)
+    arrived = [swap(sums, "row", n_row, distance) for distance in range(2, n_row, 2)]
+    arrived, inverse = lax.optimization_barrier((arrived, inverse))
+    sums = sum(arrived, sums)
+    sums = sums + swap(sums, "row", n_row, 1)
+    projected = pl.pallas_call(
+        functools.partial(project_kernel, nverts),
+        out_shape=jax.ShapeDtypeStruct((subspace, subspace), jnp.float32),
+        in_specs=vmem(2),
+        out_specs=pl.BlockSpec(memory_space=pltpu.VMEM),
+        compiler_params=params,
+        name="project",
+    )(sums, inverse)
     return (basis, projected)
 
 

time: 91 us -> 88.9 us (0.977)
  waiting for transfers between devices: 31.4 us -> 29.1 us
  Pallas kernels: 12.7 us -> 13.8 us
    pallas_call x4 -> x7, Pallas kernels: 6.37 us -> 8.71 us  [the longest x4 5.73 us: products(): pl.pallas_call(functools.partial(product_kernel, n_row, n_col), out_shape...]
    ppermute x47, waiting for transfers between devices: 31.4 us -> 29.1 us  [swap(): return lax.ppermute(value, axis, [(i, i ^ distance) for i in range(size)])]
    pallas_call x1, Pallas kernels: 1.76 us -> 0.55 us  [body(): pl.pallas_call(functools.partial(moment_kernel, n_row, n_col), out_shape=...]
  transfers between devices with their start and end apart: 47 -> 47, of which waited for: 31 -> 28; matrix products, arithmetic and copies ran while one was open for 1% -> 0% of each run, Pallas kernels for 5% -> 7%
where the time goes in v3:
time: 88.9 us; the launch traced here: 88.8 us
  starting transfers between devices  44.2 us (50%)
  waiting for transfers between devices  29.1 us (33%)
  Pallas kernels  13.8 us (16%)
  between operations  1.46 us (2%)
    ppermute x47, starting transfers between devices, swap(): return lax.ppermute(value, axis, [(i, i ^ distance) for i in range(size)])  44.2 us
    ppermute x47, waiting for transfers between devices, swap(): return lax.ppermute(value, axis, [(i, i ^ distance) for i in range(size)])  29.1 us
    pallas_call x4, Pallas kernels, products(): pl.pallas_call(functools.partial(product_kernel, n_row, n_col), out_shape...  5.73 us
    pallas_call x1, Pallas kernels, body(): pl.pallas_call(stage_kernel, out_shape=[jax.ShapeDtypeStruct(tiles.shape,...  4.53 us
  transfers between devices with their start and end apart: 47, of which 28 were waited for; matrix products, arithmetic and copies ran while one was open for 0% of the time, Pallas kernels for 7%

profile of v3, /device:TPU:0, one launch (start us, length us, event | category | flops | bytes accessed | tf_op | source)
XLA Modules:
  0.0 88.8 jit_solution(15032128352009713081)
XLA Ops:
  0.6 5.1 %collective-permute-start.2 = (f32[32,512]{1,0:T(8,128)}, f32[32,512]{1,0:T(8,128)S(1)}, u32[]{:S(2)}, u32[]{:S(2)}) collective-permute-start(f32[32,512]{1,0:T(8,128)} %refs_0_.1), channel_id=1, source_target_pairs={{0,24},{4,28},{8,16},{12,20},{16,8},{20,12},{24,0},{28,4},{1,25},{... | collective-permute-start | bytes 196616 | tf_op jit(solution)/shard_map/ppermute | solution.py:166
  5.7 0.6 collective-permute-start
  7.1 4.5 %stage.1 = (bf16[32,256,256]{2,1,0:T(8,128)(2,1)S(1)}, bf16[32,256,256]{2,1,0:T(8,128)(2,1)S(1)}) custom-call(f32[32,256,256]{2,1,0:T(8,128)} %tiles.1), custom_call_target="tpu_custom_call" | custom-call | tf_op jit(solution)/shard_map/stage/pallas_call | solution.py:199
  13.7 1.4 %tile_products.4 = (f32[32,512]{1,0:T(8,128)S(1)}, f32[32,512]{1,0:T(8,128)S(1)}, f32[32,512]{1,0:T(8,128)S(1)}, f32[32,512]{1,0:T(8,128)S(1)}) custom-call(s32[2,32]{1,0:T(2,128)S(1)} %places.1.slots, bf16[32,256,256]{2,1,0:T(8,128)(2,1)S(1)} %get-tuple-element.39.high, bf16[32,256,256]{2,1,0:T(8,128)(2,1)S(1)} %get-tuple-element.40.low, ...), custom_call_target="tpu_custom_call" | custom-call | tf_op jit(solution)/shard_map/tile_products/pallas_call | solution.py:215
  15.2 2.7 %collective-permute-start.7 = (f32[32,512]{1,0:T(8,128)S(1)}, f32[32,512]{1,0:T(8,128)S(1)}, u32[]{:S(2)}, u32[]{:S(2)}) collective-permute-start(f32[32,512]{1,0:T(8,128)S(1)} %get-tuple-element.45), channel_id=1, source_target_pairs={{0,3},{1,2},{2,1},{3,0},{4,7},{5,6},{6,5},{7,4},{8,11},{9,10},{10,... | collective-permute-start | bytes 196616 | tf_op jit(solution)/shard_map/ppermute | solution.py:166
  18.7 1.8 %collective-permute-done.7 = f32[32,512]{1,0:T(8,128)S(1)} collective-permute-done((f32[32,512]{1,0:T(8,128)S(1)}, f32[32,512]{1,0:T(8,128)S(1)}, u32[]{:S(2)}, u32[]{:S(2)}) %collective-permute-start.7) | collective-permute-done | bytes 65568 | tf_op jit(solution)/shard_map/ppermute | solution.py:166
  20.5 1.6 %collective-permute-done.8 = f32[32,512]{1,0:T(8,128)S(1)} collective-permute-done((f32[32,512]{1,0:T(8,128)S(1)}, f32[32,512]{1,0:T(8,128)S(1)}, u32[]{:S(2)}, u32[]{:S(2)}) %collective-permute-start.8) | collective-permute-done | bytes 65568 | tf_op jit(solution)/shard_map/ppermute | solution.py:166
  22.6 3.7 %collective-permute-start.15 = (f32[32,512]{1,0:T(8,128)S(1)}, f32[32,512]{1,0:T(8,128)S(1)}, u32[]{:S(2)}, u32[]{:S(2)}) collective-permute-start(f32[32,512]{1,0:T(8,128)S(1)} %get-tuple-element.70.refs_0_), channel_id=1, source_target_pairs={{0,24},{4,28},{8,16},{12,20},{16,8},{20,12},{24,0},{28,4},{1,25},{... | collective-permute-start | bytes 196616 | tf_op jit(solution)/shard_map/ppermute | solution.py:166
  26.3 0.8 collective-permute-start.11
  27.1 1.8 %collective-permute-done.15.refs_6_ = f32[32,512]{1,0:T(8,128)S(1)} collective-permute-done((f32[32,512]{1,0:T(8,128)S(1)}, f32[32,512]{1,0:T(8,128)S(1)}, u32[]{:S(2)}, u32[]{:S(2)}) %collective-permute-start.15) | collective-permute-done | bytes 65568 | tf_op jit(solution)/shard_map/ppermute | solution.py:166
  28.9 2.6 %collective-permute-done.13.refs_4_ = f32[32,512]{1,0:T(8,128)S(1)} collective-permute-done((f32[32,512]{1,0:T(8,128)S(1)}, f32[32,512]{1,0:T(8,128)S(1)}, u32[]{:S(2)}, u32[]{:S(2)}) %collective-permute-start.13) | collective-permute-done | bytes 65568 | tf_op jit(solution)/shard_map/ppermute | solution.py:166
  32.0 0.7 collective-permute-done.14.refs_5_
  32.9 1.4 %tile_products.5 = (f32[32,512]{1,0:T(8,128)S(1)}, f32[32,512]{1,0:T(8,128)S(1)}, f32[32,512]{1,0:T(8,128)S(1)}, f32[32,512]{1,0:T(8,128)S(1)}) custom-call(s32[2,32]{1,0:T(2,128)S(1)} %places.1.slots, bf16[32,256,256]{2,1,0:T(8,128)(2,1)S(1)} %get-tuple-element.39.high, bf16[32,256,256]{2,1,0:T(8,128)(2,1)S(1)} %get-tuple-element.40.low, ...), custom_call_target="tpu_custom_call" | custom-call | tf_op jit(solution)/shard_map/tile_products/pallas_call | solution.py:215
  34.4 1.6 %collective-permute-start.17 = (f32[32,512]{1,0:T(8,128)S(1)}, f32[32,512]{1,0:T(8,128)S(1)}, u32[]{:S(2)}, u32[]{:S(2)}) collective-permute-start(f32[32,512]{1,0:T(8,128)S(1)} %get-tuple-element.49), channel_id=1, source_target_pairs={{0,3},{1,2},{2,1},{3,0},{4,7},{5,6},{6,5},{7,4},{8,11},{9,10},{10,... | collective-permute-start | bytes 196616 | tf_op jit(solution)/shard_map/ppermute | solution.py:166
  35.9 1.4 %collective-permute-start.18 = (f32[32,512]{1,0:T(8,128)S(1)}, f32[32,512]{1,0:T(8,128)S(1)}, u32[]{:S(2)}, u32[]{:S(2)}) collective-permute-start(f32[32,512]{1,0:T(8,128)S(1)} %get-tuple-element.50), channel_id=1, source_target_pairs={{0,2},{1,3},{2,0},{3,1},{4,6},{5,7},{6,4},{7,5},{8,10},{9,11},{10,... | collective-permute-start | bytes 196616 | tf_op jit(solution)/shard_map/ppermute | solution.py:166
  37.3 0.6 collective-permute-start.19
  37.9 1.9 %collective-permute-done.17 = f32[32,512]{1,0:T(8,128)S(1)} collective-permute-done((f32[32,512]{1,0:T(8,128)S(1)}, f32[32,512]{1,0:T(8,128)S(1)}, u32[]{:S(2)}, u32[]{:S(2)}) %collective-permute-start.17) | collective-permute-done | bytes 65568 | tf_op jit(solution)/shard_map/ppermute | solution.py:166
  39.8 1.3 %collective-permute-done.18 = f32[32,512]{1,0:T(8,128)S(1)} collective-permute-done((f32[32,512]{1,0:T(8,128)S(1)}, f32[32,512]{1,0:T(8,128)S(1)}, u32[]{:S(2)}, u32[]{:S(2)}) %collective-permute-start.18) | collective-permute-done | bytes 65568 | tf_op jit(solution)/shard_map/ppermute | solution.py:166
  41.6 2.3 %collective-permute-start.25 = (f32[32,512]{1,0:T(8,128)S(1)}, f32[32,512]{1,0:T(8,128)S(1)}, u32[]{:S(2)}, u32[]{:S(2)}) collective-permute-start(f32[32,512]{1,0:T(8,128)S(1)} %multiply_subtract_fusion.1.refs_0_), channel_id=1, source_target_pairs={{0,24},{4,28},{8,16},{12,20},{16,8},{20,12},{24,0},{28,4},{1,25},{... | collective-permute-start | bytes 196616 | tf_op jit(solution)/shard_map/ppermute | solution.py:166
  44.2 1.9 %collective-permute-start.21 = (f32[32,512]{1,0:T(8,128)S(1)}, f32[32,512]{1,0:T(8,128)S(1)}, u32[]{:S(2)}, u32[]{:S(2)}) collective-permute-start(f32[32,512]{1,0:T(8,128)S(1)} %multiply_subtract_fusion.1.refs_0_), channel_id=1, source_target_pairs={{0,8},{4,12},{8,0},{12,4},{16,24},{20,28},{24,16},{28,20},{1,9},{5... | collective-permute-start | bytes 196616 | tf_op jit(solution)/shard_map/ppermute | solution.py:166
  46.1 1.7 %collective-permute-done.25.refs_6_ = f32[32,512]{1,0:T(8,128)S(1)} collective-permute-done((f32[32,512]{1,0:T(8,128)S(1)}, f32[32,512]{1,0:T(8,128)S(1)}, u32[]{:S(2)}, u32[]{:S(2)}) %collective-permute-start.25) | collective-permute-done | bytes 65568 | tf_op jit(solution)/shard_map/ppermute | solution.py:166
  47.8 2.7 %collective-permute-done.23.refs_4_ = f32[32,512]{1,0:T(8,128)S(1)} collective-permute-done((f32[32,512]{1,0:T(8,128)S(1)}, f32[32,512]{1,0:T(8,128)S(1)}, u32[]{:S(2)}, u32[]{:S(2)}) %collective-permute-start.23) | collective-permute-done | bytes 65568 | tf_op jit(solution)/shard_map/ppermute | solution.py:166
  51.1 0.7 collective-permute-done.24.refs_5_
  52.0 1.4 %tile_products.6 = (f32[32,512]{1,0:T(8,128)S(1)}, f32[32,512]{1,0:T(8,128)S(1)}, f32[32,512]{1,0:T(8,128)S(1)}, f32[32,512]{1,0:T(8,128)S(1)}) custom-call(s32[2,32]{1,0:T(2,128)S(1)} %places.1.slots, bf16[32,256,256]{2,1,0:T(8,128)(2,1)S(1)} %get-tuple-element.39.high, bf16[32,256,256]{2,1,0:T(8,128)(2,1)S(1)} %get-tuple-element.40.low, ...), custom_call_target="tpu_custom_call" | custom-call | tf_op jit(solution)/shard_map/tile_products/pallas_call | solution.py:215
  53.4 1.6 %collective-permute-start.27 = (f32[32,512]{1,0:T(8,128)S(1)}, f32[32,512]{1,0:T(8,128)S(1)}, u32[]{:S(2)}, u32[]{:S(2)}) collective-permute-start(f32[32,512]{1,0:T(8,128)S(1)} %get-tuple-element.53), channel_id=1, source_target_pairs={{0,3},{1,2},{2,1},{3,0},{4,7},{5,6},{6,5},{7,4},{8,11},{9,10},{10,... | collective-permute-start | bytes 196616 | tf_op jit(solution)/shard_map/ppermute | solution.py:166
  55.0 0.8 collective-permute-start.28
  55.7 1.2 %collective-permute-start.29 = (f32[32,512]{1,0:T(8,128)S(1)}, f32[32,512]{1,0:T(8,128)S(1)}, u32[]{:S(2)}, u32[]{:S(2)}) collective-permute-start(f32[32,512]{1,0:T(8,128)S(1)} %get-tuple-element.55), channel_id=1, source_target_pairs={{0,1},{1,0},{2,3},{3,2},{4,5},{5,4},{6,7},{7,6},{8,9},{9,8},{10,11... | collective-permute-start | bytes 196616 | tf_op jit(solution)/shard_map/ppermute | solution.py:166
  56.9 1.9 %collective-permute-done.27 = f32[32,512]{1,0:T(8,128)S(1)} collective-permute-done((f32[32,512]{1,0:T(8,128)S(1)}, f32[32,512]{1,0:T(8,128)S(1)}, u32[]{:S(2)}, u32[]{:S(2)}) %collective-permute-start.27) | collective-permute-done | bytes 65568 | tf_op jit(solution)/shard_map/ppermute | solution.py:166
  58.8 1.3 %collective-permute-done.28 = f32[32,512]{1,0:T(8,128)S(1)} collective-permute-done((f32[32,512]{1,0:T(8,128)S(1)}, f32[32,512]{1,0:T(8,128)S(1)}, u32[]{:S(2)}, u32[]{:S(2)}) %collective-permute-start.28) | collective-permute-done | bytes 65568 | tf_op jit(solution)/shard_map/ppermute | solution.py:166
  60.2 2.1 %collective-permute-start.38 = (f32[32,512]{1,0:T(8,128)S(1)}, f32[32,512]{1,0:T(8,128)S(1)}, u32[]{:S(2)}, u32[]{:S(2)}) collective-permute-start(f32[32,512]{1,0:T(8,128)S(1)} %multiply_subtract_fusion.refs_0_.filtered), channel_id=1, source_target_pairs={{0,24},{4,28},{8,16},{12,20},{16,8},{20,12},{24,0},{28,4},{1,25},{... | collective-permute-start | bytes 196616 | tf_op jit(solution)/shard_map/ppermute | solution.py:166
  62.2 1.6 %collective-permute-start.36 = (f32[32,512]{1,0:T(8,128)S(1)}, f32[32,512]{1,0:T(8,128)S(1)}, u32[]{:S(2)}, u32[]{:S(2)}) collective-permute-start(f32[32,512]{1,0:T(8,128)S(1)} %multiply_subtract_fusion.refs_0_.filtered), channel_id=1, source_target_pairs={{0,3},{1,2},{2,1},{3,0},{4,7},{5,6},{6,5},{7,4},{8,11},{9,10},{10,... | collective-permute-start | bytes 196616 | tf_op jit(solution)/shard_map/ppermute | solution.py:166
  63.9 0.8 collective-permute-start.35
  64.7 2.5 %collective-permute-start.31 = (f32[32,512]{1,0:T(8,128)S(1)}, f32[32,512]{1,0:T(8,128)S(1)}, u32[]{:S(2)}, u32[]{:S(2)}) collective-permute-start(f32[32,512]{1,0:T(8,128)S(1)} %multiply_subtract_fusion.refs_0_.filtered), channel_id=1, source_target_pairs={{0,8},{4,12},{8,0},{12,4},{16,24},{20,28},{24,16},{28,20},{1,9},{5... | collective-permute-start | bytes 196616 | tf_op jit(solution)/shard_map/ppermute | solution.py:166
  67.2 0.9 %collective-permute-start.34 = (f32[32,512]{1,0:T(8,128)S(1)}, f32[32,512]{1,0:T(8,128)S(1)}, u32[]{:S(2)}, u32[]{:S(2)}) collective-permute-start(f32[32,512]{1,0:T(8,128)S(1)} %multiply_subtract_fusion.refs_0_.filtered), channel_id=1, source_target_pairs={{0,1},{1,0},{2,3},{3,2},{4,5},{5,4},{6,7},{7,6},{8,9},{9,8},{10,11... | collective-permute-start | bytes 196616 | tf_op jit(solution)/shard_map/ppermute | solution.py:166
  68.1 0.8 collective-permute-done.33.refs_4_
  69.9 1.5 %collective-permute-done.34.refs_8_ = f32[32,512]{1,0:T(8,128)S(1)} collective-permute-done((f32[32,512]{1,0:T(8,128)S(1)}, f32[32,512]{1,0:T(8,128)S(1)}, u32[]{:S(2)}, u32[]{:S(2)}) %collective-permute-start.34) | collective-permute-done | bytes 65568 | tf_op jit(solution)/shard_map/ppermute | solution.py:166
  71.5 1.4 %tile_products.7 = (f32[32,512]{1,0:T(8,128)S(1)}, f32[32,512]{1,0:T(8,128)S(1)}, f32[32,512]{1,0:T(8,128)S(1)}, f32[32,512]{1,0:T(8,128)S(1)}) custom-call(s32[2,32]{1,0:T(2,128)S(1)} %places.1.slots, bf16[32,256,256]{2,1,0:T(8,128)(2,1)S(1)} %get-tuple-element.39.high, bf16[32,256,256]{2,1,0:T(8,128)(2,1)S(1)} %get-tuple-element.40.low, ...), custom_call_target="tpu_custom_call" | custom-call | tf_op jit(solution)/shard_map/tile_products/pallas_call | solution.py:215
  73.5 1.5 %collective-permute-start.42 = (f32[32,64]{1,0:T(8,128)S(1)}, f32[32,64]{1,0:T(8,128)S(1)}, u32[]{:S(2)}, u32[]{:S(2)}) collective-permute-start(f32[32,64]{1,0:T(8,128)S(1)} %moment.1), channel_id=1, source_target_pairs={{0,3},{1,2},{2,1},{3,0},{4,7},{5,6},{6,5},{7,4},{8,11},{9,10},{10,... | collective-permute-start | bytes 24584 | tf_op jit(solution)/shard_map/ppermute | solution.py:166
  75.0 0.9 %collective-permute-start.41 = (f32[32,64]{1,0:T(8,128)S(1)}, f32[32,64]{1,0:T(8,128)S(1)}, u32[]{:S(2)}, u32[]{:S(2)}) collective-permute-start(f32[32,64]{1,0:T(8,128)S(1)} %moment.1), channel_id=1, source_target_pairs={{0,2},{1,3},{2,0},{3,1},{4,6},{5,7},{6,4},{7,5},{8,10},{9,11},{10,... | collective-permute-start | bytes 24584 | tf_op jit(solution)/shard_map/ppermute | solution.py:166
  75.9 1.1 %collective-permute-start.40 = (f32[32,64]{1,0:T(8,128)S(1)}, f32[32,64]{1,0:T(8,128)S(1)}, u32[]{:S(2)}, u32[]{:S(2)}) collective-permute-start(f32[32,64]{1,0:T(8,128)S(1)} %moment.1), channel_id=1, source_target_pairs={{0,1},{1,0},{2,3},{3,2},{4,5},{5,4},{6,7},{7,6},{8,9},{9,8},{10,11... | collective-permute-start | bytes 24584 | tf_op jit(solution)/shard_map/ppermute | solution.py:166
  77.0 1.1 %collective-permute-done.42 = f32[32,64]{1,0:T(8,128)S(1)} collective-permute-done((f32[32,64]{1,0:T(8,128)S(1)}, f32[32,64]{1,0:T(8,128)S(1)}, u32[]{:S(2)}, u32[]{:S(2)}) %collective-permute-start.42) | collective-permute-done | bytes 8224 | tf_op jit(solution)/shard_map/ppermute | solution.py:166
  78.7 0.9 %collective-permute-done.40 = f32[32,64]{1,0:T(8,128)S(1)} collective-permute-done((f32[32,64]{1,0:T(8,128)S(1)}, f32[32,64]{1,0:T(8,128)S(1)}, u32[]{:S(2)}, u32[]{:S(2)}) %collective-permute-start.40) | collective-permute-done | bytes 8224 | tf_op jit(solution)/shard_map/ppermute | solution.py:166
  79.6 2.0 %collective-permute-start.45 = (f32[32,64]{1,0:T(8,128)S(1)}, f32[32,64]{1,0:T(8,128)S(1)}, u32[]{:S(2)}, u32[]{:S(2)}) collective-permute-start(f32[32,64]{1,0:T(8,128)S(1)} %add_add_fusion.1.sums), channel_id=1, source_target_pairs={{0,24},{4,28},{8,16},{12,20},{16,8},{20,12},{24,0},{28,4},{1,25},{... | collective-permute-start | bytes 24584 | tf_op jit(solution)/shard_map/ppermute | solution.py:166
  81.7 0.7 collective-permute-start.44
  82.3 1.7 %collective-permute-start.43 = (f32[32,64]{1,0:T(8,128)S(1)}, f32[32,64]{1,0:T(8,128)S(1)}, u32[]{:S(2)}, u32[]{:S(2)}) collective-permute-start(f32[32,64]{1,0:T(8,128)S(1)} %add_add_fusion.1.sums), channel_id=1, source_target_pairs={{0,8},{4,12},{8,0},{12,4},{16,24},{20,28},{24,16},{28,20},{1,9},{5... | collective-permute-start | bytes 24584 | tf_op jit(solution)/shard_map/ppermute | solution.py:166
  84.0 1.7 %factor.1 = (f32[32,32]{1,0:T(8,128)S(1)}, f32[32,512]{1,0:T(8,128)}) custom-call(f32[32,64]{1,0:T(8,128)S(1)} %add_add_fusion.1.sums, f32[32,512]{1,0:T(8,128)S(1)} %multiply_subtract_fusion.refs_0_.filtered), custom_call_target="tpu_custom_call" | custom-call | tf_op jit(solution)/shard_map/factor/pallas_call | solution.py:256
  86.4 1.2 %collective-permute-done.46 = f32[32,64]{1,0:T(8,128)S(1)} collective-permute-done((f32[32,64]{1,0:T(8,128)S(1)}, f32[32,64]{1,0:T(8,128)S(1)}, u32[]{:S(2)}, u32[]{:S(2)}) %collective-permute-start.46) | collective-permute-done | bytes 8224 | tf_op jit(solution)/shard_map/ppermute | solution.py:166
  87.6 1.2 %project.1 = f32[32,32]{1,0:T(8,128)} custom-call(f32[32,64]{1,0:T(8,128)S(1)} %add.65.sums, f32[32,32]{1,0:T(8,128)S(1)} %get-tuple-element.69.inverse), custom_call_target="tpu_custom_call" | custom-call | tf_op jit(solution)/shard_map/project/pallas_call | solution.py:268
  (70 shorter events, 8.5 us)
Async XLA Ops:
  0.6 11.1 %collective-permute-start.2 = (f32[32,512]{1,0:T(8,128)}, f32[32,512]{1,0:T(8,128)S(1)}, u32[]{:S(2)}, u32[]{:S(2)}) collective-permute-start(f32[32,512]{1,0:T(8,128)} %refs_0_.1), channel_id=1, source_target_pairs={{0,24},{4,28},{8,16},{12,20},{16,8},{20,12},{24,0},{28,4},{1,25},{... | collective-permute-start | bytes 196616 | tf_op jit(solution)/shard_map/ppermute | solution.py:166
  5.7 6.0 %collective-permute-start.1 = (f32[32,512]{1,0:T(8,128)}, f32[32,512]{1,0:T(8,128)S(1)}, u32[]{:S(2)}, u32[]{:S(2)}) collective-permute-start(f32[32,512]{1,0:T(8,128)} %refs_0_.1), channel_id=1, source_target_pairs={{0,16},{4,20},{8,24},{12,28},{16,0},{20,4},{24,8},{28,12},{1,17},{... | collective-permute-start | bytes 196616 | tf_op jit(solution)/shard_map/ppermute | solution.py:166
  5.7 6.0 %collective-permute-start = (f32[32,512]{1,0:T(8,128)}, f32[32,512]{1,0:T(8,128)S(1)}, u32[]{:S(2)}, u32[]{:S(2)}) collective-permute-start(f32[32,512]{1,0:T(8,128)} %refs_0_.1), channel_id=1, source_target_pairs={{0,8},{4,12},{8,0},{12,4},{16,24},{20,28},{24,16},{28,20},{1,9},{5... | collective-permute-start | bytes 196616 | tf_op jit(solution)/shard_map/ppermute | solution.py:166
  6.4 6.4 %collective-permute-start.3 = (f32[32,512]{1,0:T(8,128)}, f32[32,512]{1,0:T(8,128)S(1)}, u32[]{:S(2)}, u32[]{:S(2)}) collective-permute-start(f32[32,512]{1,0:T(8,128)} %refs_0_.1), channel_id=1, source_target_pairs={{0,4},{4,0},{8,12},{12,8},{16,20},{20,16},{24,28},{28,24},{1,5},{5... | collective-permute-start | bytes 196616 | tf_op jit(solution)/shard_map/ppermute | solution.py:166
  11.7 7.0 %copy-start.1 = (f32[512]{0:T(512)S(1)}, f32[512]{0:T(512)}, u32[]{:S(2)}) copy-start(f32[512]{0:T(512)} %param.7) | copy-start | bytes 6148
  11.7 1.5 %collective-permute-start.4 = (f32[32,512]{1,0:T(8,128)S(1)}, f32[32,512]{1,0:T(8,128)S(1)}, u32[]{:S(2)}, u32[]{:S(2)}) collective-permute-start(f32[32,512]{1,0:T(8,128)S(1)} %collective-permute-done.refs_2_), channel_id=1, source_target_pairs={{0,4},{4,0},{8,12},{12,8},{16,20},{20,16},{24,28},{28,24},{1,5},{5... | collective-permute-start | bytes 196616 | tf_op jit(solution)/shard_map/ppermute | solution.py:166
  12.3 1.3 %collective-permute-start.5 = (f32[32,512]{1,0:T(8,128)S(1)}, f32[32,512]{1,0:T(8,128)S(1)}, u32[]{:S(2)}, u32[]{:S(2)}) collective-permute-start(f32[32,512]{1,0:T(8,128)S(1)} %collective-permute-done.1.refs_4_), channel_id=1, source_target_pairs={{0,4},{4,0},{8,12},{12,8},{16,20},{20,16},{24,28},{28,24},{1,5},{5... | collective-permute-start | bytes 196616 | tf_op jit(solution)/shard_map/ppermute | solution.py:166
  12.4 1.3 %collective-permute-start.6 = (f32[32,512]{1,0:T(8,128)S(1)}, f32[32,512]{1,0:T(8,128)S(1)}, u32[]{:S(2)}, u32[]{:S(2)}) collective-permute-start(f32[32,512]{1,0:T(8,128)S(1)} %collective-permute-done.2.refs_6_), channel_id=1, source_target_pairs={{0,4},{4,0},{8,12},{12,8},{16,20},{20,16},{24,28},{28,24},{1,5},{5... | collective-permute-start | bytes 196616 | tf_op jit(solution)/shard_map/ppermute | solution.py:166
  15.2 5.3 %collective-permute-start.7 = (f32[32,512]{1,0:T(8,128)S(1)}, f32[32,512]{1,0:T(8,128)S(1)}, u32[]{:S(2)}, u32[]{:S(2)}) collective-permute-start(f32[32,512]{1,0:T(8,128)S(1)} %get-tuple-element.45), channel_id=1, source_target_pairs={{0,3},{1,2},{2,1},{3,0},{4,7},{5,6},{6,5},{7,4},{8,11},{9,10},{10,... | collective-permute-start | bytes 196616 | tf_op jit(solution)/shard_map/ppermute | solution.py:166
  17.8 4.3 %collective-permute-start.8 = (f32[32,512]{1,0:T(8,128)S(1)}, f32[32,512]{1,0:T(8,128)S(1)}, u32[]{:S(2)}, u32[]{:S(2)}) collective-permute-start(f32[32,512]{1,0:T(8,128)S(1)} %get-tuple-element.46), channel_id=1, source_target_pairs={{0,2},{1,3},{2,0},{3,1},{4,6},{5,7},{6,4},{7,5},{8,10},{9,11},{10,... | collective-permute-start | bytes 196616 | tf_op jit(solution)/shard_map/ppermute | solution.py:166
  18.3 4.3 %collective-permute-start.9 = (f32[32,512]{1,0:T(8,128)S(1)}, f32[32,512]{1,0:T(8,128)S(1)}, u32[]{:S(2)}, u32[]{:S(2)}) collective-permute-start(f32[32,512]{1,0:T(8,128)S(1)} %get-tuple-element.47), channel_id=1, source_target_pairs={{0,1},{1,0},{2,3},{3,2},{4,5},{5,4},{6,7},{7,6},{8,9},{9,8},{10,11... | collective-permute-start | bytes 196616 | tf_op jit(solution)/shard_map/ppermute | solution.py:166
  22.6 6.2 %collective-permute-start.15 = (f32[32,512]{1,0:T(8,128)S(1)}, f32[32,512]{1,0:T(8,128)S(1)}, u32[]{:S(2)}, u32[]{:S(2)}) collective-permute-start(f32[32,512]{1,0:T(8,128)S(1)} %get-tuple-element.70.refs_0_), channel_id=1, source_target_pairs={{0,24},{4,28},{8,16},{12,20},{16,8},{20,12},{24,0},{28,4},{1,25},{... | collective-permute-start | bytes 196616 | tf_op jit(solution)/shard_map/ppermute | solution.py:166
  26.3 5.2 %collective-permute-start.13 = (f32[32,512]{1,0:T(8,128)S(1)}, f32[32,512]{1,0:T(8,128)S(1)}, u32[]{:S(2)}, u32[]{:S(2)}) collective-permute-start(f32[32,512]{1,0:T(8,128)S(1)} %get-tuple-element.70.refs_0_), channel_id=1, source_target_pairs={{0,16},{4,20},{8,24},{12,28},{16,0},{20,4},{24,8},{28,12},{1,17},{... | collective-permute-start | bytes 196616 | tf_op jit(solution)/shard_map/ppermute | solution.py:166
  26.3 5.3 %collective-permute-start.11 = (f32[32,512]{1,0:T(8,128)S(1)}, f32[32,512]{1,0:T(8,128)S(1)}, u32[]{:S(2)}, u32[]{:S(2)}) collective-permute-start(f32[32,512]{1,0:T(8,128)S(1)} %get-tuple-element.70.refs_0_), channel_id=1, source_target_pairs={{0,8},{4,12},{8,0},{12,4},{16,24},{20,28},{24,16},{28,20},{1,9},{5... | collective-permute-start | bytes 196616 | tf_op jit(solution)/shard_map/ppermute | solution.py:166
  27.1 5.0 %collective-permute-start.10 = (f32[32,512]{1,0:T(8,128)S(1)}, f32[32,512]{1,0:T(8,128)S(1)}, u32[]{:S(2)}, u32[]{:S(2)}) collective-permute-start(f32[32,512]{1,0:T(8,128)S(1)} %get-tuple-element.70.refs_0_), channel_id=1, source_target_pairs={{0,4},{4,0},{8,12},{12,8},{16,20},{20,16},{24,28},{28,24},{1,5},{5... | collective-permute-start | bytes 196616 | tf_op jit(solution)/shard_map/ppermute | solution.py:166
  28.9 3.2 %collective-permute-start.16 = (f32[32,512]{1,0:T(8,128)S(1)}, f32[32,512]{1,0:T(8,128)S(1)}, u32[]{:S(2)}, u32[]{:S(2)}) collective-permute-start(f32[32,512]{1,0:T(8,128)S(1)} %collective-permute-done.15.refs_6_), channel_id=1, source_target_pairs={{0,4},{4,0},{8,12},{12,8},{16,20},{20,16},{24,28},{28,24},{1,5},{5... | collective-permute-start | bytes 196616 | tf_op jit(solution)/shard_map/ppermute | solution.py:166
  31.5 1.3 %collective-permute-start.14 = (f32[32,512]{1,0:T(8,128)S(1)}, f32[32,512]{1,0:T(8,128)S(1)}, u32[]{:S(2)}, u32[]{:S(2)}) collective-permute-start(f32[32,512]{1,0:T(8,128)S(1)} %collective-permute-done.13.refs_4_), channel_id=1, source_target_pairs={{0,4},{4,0},{8,12},{12,8},{16,20},{20,16},{24,28},{28,24},{1,5},{5... | collective-permute-start | bytes 196616 | tf_op jit(solution)/shard_map/ppermute | solution.py:166
  31.6 1.3 %collective-permute-start.12 = (f32[32,512]{1,0:T(8,128)S(1)}, f32[32,512]{1,0:T(8,128)S(1)}, u32[]{:S(2)}, u32[]{:S(2)}) collective-permute-start(f32[32,512]{1,0:T(8,128)S(1)} %collective-permute-done.11.refs_2_), channel_id=1, source_target_pairs={{0,4},{4,0},{8,12},{12,8},{16,20},{20,16},{24,28},{28,24},{1,5},{5... | collective-permute-start | bytes 196616 | tf_op jit(solution)/shard_map/ppermute | solution.py:166
  34.4 5.4 %collective-permute-start.17 = (f32[32,512]{1,0:T(8,128)S(1)}, f32[32,512]{1,0:T(8,128)S(1)}, u32[]{:S(2)}, u32[]{:S(2)}) collective-permute-start(f32[32,512]{1,0:T(8,128)S(1)} %get-tuple-element.49), channel_id=1, source_target_pairs={{0,3},{1,2},{2,1},{3,0},{4,7},{5,6},{6,5},{7,4},{8,11},{9,10},{10,... | collective-permute-start | bytes 196616 | tf_op jit(solution)/shard_map/ppermute | solution.py:166
  35.9 5.2 %collective-permute-start.18 = (f32[32,512]{1,0:T(8,128)S(1)}, f32[32,512]{1,0:T(8,128)S(1)}, u32[]{:S(2)}, u32[]{:S(2)}) collective-permute-start(f32[32,512]{1,0:T(8,128)S(1)} %get-tuple-element.50), channel_id=1, source_target_pairs={{0,2},{1,3},{2,0},{3,1},{4,6},{5,7},{6,4},{7,5},{8,10},{9,11},{10,... | collective-permute-start | bytes 196616 | tf_op jit(solution)/shard_map/ppermute | solution.py:166
  37.3 4.3 %collective-permute-start.19 = (f32[32,512]{1,0:T(8,128)S(1)}, f32[32,512]{1,0:T(8,128)S(1)}, u32[]{:S(2)}, u32[]{:S(2)}) collective-permute-start(f32[32,512]{1,0:T(8,128)S(1)} %get-tuple-element.51), channel_id=1, source_target_pairs={{0,1},{1,0},{2,3},{3,2},{4,5},{5,4},{6,7},{7,6},{8,9},{9,8},{10,11... | collective-permute-start | bytes 196616 | tf_op jit(solution)/shard_map/ppermute | solution.py:166
  41.6 6.2 %collective-permute-start.25 = (f32[32,512]{1,0:T(8,128)S(1)}, f32[32,512]{1,0:T(8,128)S(1)}, u32[]{:S(2)}, u32[]{:S(2)}) collective-permute-start(f32[32,512]{1,0:T(8,128)S(1)} %multiply_subtract_fusion.1.refs_0_), channel_id=1, source_target_pairs={{0,24},{4,28},{8,16},{12,20},{16,8},{20,12},{24,0},{28,4},{1,25},{... | collective-permute-start | bytes 196616 | tf_op jit(solution)/shard_map/ppermute | solution.py:166
  43.9 6.6 %collective-permute-start.23 = (f32[32,512]{1,0:T(8,128)S(1)}, f32[32,512]{1,0:T(8,128)S(1)}, u32[]{:S(2)}, u32[]{:S(2)}) collective-permute-start(f32[32,512]{1,0:T(8,128)S(1)} %multiply_subtract_fusion.1.refs_0_), channel_id=1, source_target_pairs={{0,16},{4,20},{8,24},{12,28},{16,0},{20,4},{24,8},{28,12},{1,17},{... | collective-permute-start | bytes 196616 | tf_op jit(solution)/shard_map/ppermute | solution.py:166
  44.2 6.4 %collective-permute-start.21 = (f32[32,512]{1,0:T(8,128)S(1)}, f32[32,512]{1,0:T(8,128)S(1)}, u32[]{:S(2)}, u32[]{:S(2)}) collective-permute-start(f32[32,512]{1,0:T(8,128)S(1)} %multiply_subtract_fusion.1.refs_0_), channel_id=1, source_target_pairs={{0,8},{4,12},{8,0},{12,4},{16,24},{20,28},{24,16},{28,20},{1,9},{5... | collective-permute-start | bytes 196616 | tf_op jit(solution)/shard_map/ppermute | solution.py:166
  46.1 5.0 %collective-permute-start.20 = (f32[32,512]{1,0:T(8,128)S(1)}, f32[32,512]{1,0:T(8,128)S(1)}, u32[]{:S(2)}, u32[]{:S(2)}) collective-permute-start(f32[32,512]{1,0:T(8,128)S(1)} %multiply_subtract_fusion.1.refs_0_), channel_id=1, source_target_pairs={{0,4},{4,0},{8,12},{12,8},{16,20},{20,16},{24,28},{28,24},{1,5},{5... | collective-permute-start | bytes 196616 | tf_op jit(solution)/shard_map/ppermute | solution.py:166
  47.8 3.2 %collective-permute-start.26 = (f32[32,512]{1,0:T(8,128)S(1)}, f32[32,512]{1,0:T(8,128)S(1)}, u32[]{:S(2)}, u32[]{:S(2)}) collective-permute-start(f32[32,512]{1,0:T(8,128)S(1)} %collective-permute-done.25.refs_6_), channel_id=1, source_target_pairs={{0,4},{4,0},{8,12},{12,8},{16,20},{20,16},{24,28},{28,24},{1,5},{5... | collective-permute-start | bytes 196616 | tf_op jit(solution)/shard_map/ppermute | solution.py:166
  50.5 1.3 %collective-permute-start.24 = (f32[32,512]{1,0:T(8,128)S(1)}, f32[32,512]{1,0:T(8,128)S(1)}, u32[]{:S(2)}, u32[]{:S(2)}) collective-permute-start(f32[32,512]{1,0:T(8,128)S(1)} %collective-permute-done.23.refs_4_), channel_id=1, source_target_pairs={{0,4},{4,0},{8,12},{12,8},{16,20},{20,16},{24,28},{28,24},{1,5},{5... | collective-permute-start | bytes 196616 | tf_op jit(solution)/shard_map/ppermute | solution.py:166
  50.5 1.4 %collective-permute-start.22 = (f32[32,512]{1,0:T(8,128)S(1)}, f32[32,512]{1,0:T(8,128)S(1)}, u32[]{:S(2)}, u32[]{:S(2)}) collective-permute-start(f32[32,512]{1,0:T(8,128)S(1)} %collective-permute-done.21.refs_2_), channel_id=1, source_target_pairs={{0,4},{4,0},{8,12},{12,8},{16,20},{20,16},{24,28},{28,24},{1,5},{5... | collective-permute-start | bytes 196616 | tf_op jit(solution)/shard_map/ppermute | solution.py:166
  53.4 5.4 %collective-permute-start.27 = (f32[32,512]{1,0:T(8,128)S(1)}, f32[32,512]{1,0:T(8,128)S(1)}, u32[]{:S(2)}, u32[]{:S(2)}) collective-permute-start(f32[32,512]{1,0:T(8,128)S(1)} %get-tuple-element.53), channel_id=1, source_target_pairs={{0,3},{1,2},{2,1},{3,0},{4,7},{5,6},{6,5},{7,4},{8,11},{9,10},{10,... | collective-permute-start | bytes 196616 | tf_op jit(solution)/shard_map/ppermute | solution.py:166
  55.0 5.2 %collective-permute-start.28 = (f32[32,512]{1,0:T(8,128)S(1)}, f32[32,512]{1,0:T(8,128)S(1)}, u32[]{:S(2)}, u32[]{:S(2)}) collective-permute-start(f32[32,512]{1,0:T(8,128)S(1)} %get-tuple-element.54), channel_id=1, source_target_pairs={{0,2},{1,3},{2,0},{3,1},{4,6},{5,7},{6,4},{7,5},{8,10},{9,11},{10,... | collective-permute-start | bytes 196616 | tf_op jit(solution)/shard_map/ppermute | solution.py:166
  55.7 4.4 %collective-permute-start.29 = (f32[32,512]{1,0:T(8,128)S(1)}, f32[32,512]{1,0:T(8,128)S(1)}, u32[]{:S(2)}, u32[]{:S(2)}) collective-permute-start(f32[32,512]{1,0:T(8,128)S(1)} %get-tuple-element.55), channel_id=1, source_target_pairs={{0,1},{1,0},{2,3},{3,2},{4,5},{5,4},{6,7},{7,6},{8,9},{9,8},{10,11... | collective-permute-start | bytes 196616 | tf_op jit(solution)/shard_map/ppermute | solution.py:166
  60.2 7.0 %collective-permute-start.38 = (f32[32,512]{1,0:T(8,128)S(1)}, f32[32,512]{1,0:T(8,128)S(1)}, u32[]{:S(2)}, u32[]{:S(2)}) collective-permute-start(f32[32,512]{1,0:T(8,128)S(1)} %multiply_subtract_fusion.refs_0_.filtered), channel_id=1, source_target_pairs={{0,24},{4,28},{8,16},{12,20},{16,8},{20,12},{24,0},{28,4},{1,25},{... | collective-permute-start | bytes 196616 | tf_op jit(solution)/shard_map/ppermute | solution.py:166
  62.2 6.6 %collective-permute-start.33 = (f32[32,512]{1,0:T(8,128)S(1)}, f32[32,512]{1,0:T(8,128)S(1)}, u32[]{:S(2)}, u32[]{:S(2)}) collective-permute-start(f32[32,512]{1,0:T(8,128)S(1)} %multiply_subtract_fusion.refs_0_.filtered), channel_id=1, source_target_pairs={{0,16},{4,20},{8,24},{12,28},{16,0},{20,4},{24,8},{28,12},{1,17},{... | collective-permute-start | bytes 196616 | tf_op jit(solution)/shard_map/ppermute | solution.py:166
  62.2 6.6 %collective-permute-start.36 = (f32[32,512]{1,0:T(8,128)S(1)}, f32[32,512]{1,0:T(8,128)S(1)}, u32[]{:S(2)}, u32[]{:S(2)}) collective-permute-start(f32[32,512]{1,0:T(8,128)S(1)} %multiply_subtract_fusion.refs_0_.filtered), channel_id=1, source_target_pairs={{0,3},{1,2},{2,1},{3,0},{4,7},{5,6},{6,5},{7,4},{8,11},{9,10},{10,... | collective-permute-start | bytes 196616 | tf_op jit(solution)/shard_map/ppermute | solution.py:166
  63.9 5.5 %collective-permute-start.35 = (f32[32,512]{1,0:T(8,128)S(1)}, f32[32,512]{1,0:T(8,128)S(1)}, u32[]{:S(2)}, u32[]{:S(2)}) collective-permute-start(f32[32,512]{1,0:T(8,128)S(1)} %multiply_subtract_fusion.refs_0_.filtered), channel_id=1, source_target_pairs={{0,2},{1,3},{2,0},{3,1},{4,6},{5,7},{6,4},{7,5},{8,10},{9,11},{10,... | collective-permute-start | bytes 196616 | tf_op jit(solution)/shard_map/ppermute | solution.py:166
  64.7 4.9 %collective-permute-start.31 = (f32[32,512]{1,0:T(8,128)S(1)}, f32[32,512]{1,0:T(8,128)S(1)}, u32[]{:S(2)}, u32[]{:S(2)}) collective-permute-start(f32[32,512]{1,0:T(8,128)S(1)} %multiply_subtract_fusion.refs_0_.filtered), channel_id=1, source_target_pairs={{0,8},{4,12},{8,0},{12,4},{16,24},{20,28},{24,16},{28,20},{1,9},{5... | collective-permute-start | bytes 196616 | tf_op jit(solution)/shard_map/ppermute | solution.py:166
  67.2 4.3 %collective-permute-start.34 = (f32[32,512]{1,0:T(8,128)S(1)}, f32[32,512]{1,0:T(8,128)S(1)}, u32[]{:S(2)}, u32[]{:S(2)}) collective-permute-start(f32[32,512]{1,0:T(8,128)S(1)} %multiply_subtract_fusion.refs_0_.filtered), channel_id=1, source_target_pairs={{0,1},{1,0},{2,3},{3,2},{4,5},{5,4},{6,7},{7,6},{8,9},{9,8},{10,11... | collective-permute-start | bytes 196616 | tf_op jit(solution)/shard_map/ppermute | solution.py:166
  68.9 2.6 %collective-permute-start.37 = (f32[32,512]{1,0:T(8,128)S(1)}, f32[32,512]{1,0:T(8,128)S(1)}, u32[]{:S(2)}, u32[]{:S(2)}) collective-permute-start(f32[32,512]{1,0:T(8,128)S(1)} %collective-permute-done.33.refs_4_), channel_id=1, source_target_pairs={{0,4},{4,0},{8,12},{12,8},{16,20},{20,16},{24,28},{28,24},{1,5},{5... | collective-permute-start | bytes 196616 | tf_op jit(solution)/shard_map/ppermute | solution.py:166
  68.9 2.6 %collective-permute-start.30 = (f32[32,512]{1,0:T(8,128)S(1)}, f32[32,512]{1,0:T(8,128)S(1)}, u32[]{:S(2)}, u32[]{:S(2)}) collective-permute-start(f32[32,512]{1,0:T(8,128)S(1)} %multiply_subtract_fusion.refs_0_.filtered), channel_id=1, source_target_pairs={{0,4},{4,0},{8,12},{12,8},{16,20},{20,16},{24,28},{28,24},{1,5},{5... | collective-permute-start | bytes 196616 | tf_op jit(solution)/shard_map/ppermute | solution.py:166
  69.4 2.1 %collective-permute-start.39 = (f32[32,512]{1,0:T(8,128)S(1)}, f32[32,512]{1,0:T(8,128)S(1)}, u32[]{:S(2)}, u32[]{:S(2)}) collective-permute-start(f32[32,512]{1,0:T(8,128)S(1)} %collective-permute-done.38.refs_6_), channel_id=1, source_target_pairs={{0,4},{4,0},{8,12},{12,8},{16,20},{20,16},{24,28},{28,24},{1,5},{5... | collective-permute-start | bytes 196616 | tf_op jit(solution)/shard_map/ppermute | solution.py:166
  69.6 1.9 %collective-permute-start.32 = (f32[32,512]{1,0:T(8,128)S(1)}, f32[32,512]{1,0:T(8,128)S(1)}, u32[]{:S(2)}, u32[]{:S(2)}) collective-permute-start(f32[32,512]{1,0:T(8,128)S(1)} %collective-permute-done.31.refs_2_), channel_id=1, source_target_pairs={{0,4},{4,0},{8,12},{12,8},{16,20},{20,16},{24,28},{28,24},{1,5},{5... | collective-permute-start | bytes 196616 | tf_op jit(solution)/shard_map/ppermute | solution.py:166
  73.5 4.7 %collective-permute-start.42 = (f32[32,64]{1,0:T(8,128)S(1)}, f32[32,64]{1,0:T(8,128)S(1)}, u32[]{:S(2)}, u32[]{:S(2)}) collective-permute-start(f32[32,64]{1,0:T(8,128)S(1)} %moment.1), channel_id=1, source_target_pairs={{0,3},{1,2},{2,1},{3,0},{4,7},{5,6},{6,5},{7,4},{8,11},{9,10},{10,... | collective-permute-start | bytes 24584 | tf_op jit(solution)/shard_map/ppermute | solution.py:166
  75.0 3.7 %collective-permute-start.41 = (f32[32,64]{1,0:T(8,128)S(1)}, f32[32,64]{1,0:T(8,128)S(1)}, u32[]{:S(2)}, u32[]{:S(2)}) collective-permute-start(f32[32,64]{1,0:T(8,128)S(1)} %moment.1), channel_id=1, source_target_pairs={{0,2},{1,3},{2,0},{3,1},{4,6},{5,7},{6,4},{7,5},{8,10},{9,11},{10,... | collective-permute-start | bytes 24584 | tf_op jit(solution)/shard_map/ppermute | solution.py:166
  75.9 3.7 %collective-permute-start.40 = (f32[32,64]{1,0:T(8,128)S(1)}, f32[32,64]{1,0:T(8,128)S(1)}, u32[]{:S(2)}, u32[]{:S(2)}) collective-permute-start(f32[32,64]{1,0:T(8,128)S(1)} %moment.1), channel_id=1, source_target_pairs={{0,1},{1,0},{2,3},{3,2},{4,5},{5,4},{6,7},{7,6},{8,9},{9,8},{10,11... | collective-permute-start | bytes 24584 | tf_op jit(solution)/shard_map/ppermute | solution.py:166
  79.6 6.1 %collective-permute-start.45 = (f32[32,64]{1,0:T(8,128)S(1)}, f32[32,64]{1,0:T(8,128)S(1)}, u32[]{:S(2)}, u32[]{:S(2)}) collective-permute-start(f32[32,64]{1,0:T(8,128)S(1)} %add_add_fusion.1.sums), channel_id=1, source_target_pairs={{0,24},{4,28},{8,16},{12,20},{16,8},{20,12},{24,0},{28,4},{1,25},{... | collective-permute-start | bytes 24584 | tf_op jit(solution)/shard_map/ppermute | solution.py:166
  81.7 4.6 %collective-permute-start.44 = (f32[32,64]{1,0:T(8,128)S(1)}, f32[32,64]{1,0:T(8,128)S(1)}, u32[]{:S(2)}, u32[]{:S(2)}) collective-permute-start(f32[32,64]{1,0:T(8,128)S(1)} %add_add_fusion.1.sums), channel_id=1, source_target_pairs={{0,16},{4,20},{8,24},{12,28},{16,0},{20,4},{24,8},{28,12},{1,17},{... | collective-permute-start | bytes 24584 | tf_op jit(solution)/shard_map/ppermute | solution.py:166
  82.3 4.0 %collective-permute-start.43 = (f32[32,64]{1,0:T(8,128)S(1)}, f32[32,64]{1,0:T(8,128)S(1)}, u32[]{:S(2)}, u32[]{:S(2)}) collective-permute-start(f32[32,64]{1,0:T(8,128)S(1)} %add_add_fusion.1.sums), channel_id=1, source_target_pairs={{0,8},{4,12},{8,0},{12,4},{16,24},{20,28},{24,16},{28,20},{1,9},{5... | collective-permute-start | bytes 24584 | tf_op jit(solution)/shard_map/ppermute | solution.py:166
  86.3 1.2 %collective-permute-start.46 = (f32[32,64]{1,0:T(8,128)S(1)}, f32[32,64]{1,0:T(8,128)S(1)}, u32[]{:S(2)}, u32[]{:S(2)}) collective-permute-start(f32[32,64]{1,0:T(8,128)S(1)} %add_add_fusion), channel_id=1, source_target_pairs={{0,4},{4,0},{8,12},{12,8},{16,20},{20,16},{24,28},{28,24},{1,5},{5... | collective-permute-start | bytes 24584 | tf_op jit(solution)/shard_map/ppermute | solution.py:166
  (3 other events, 15.8 us)

commit v4 on v3

--- a/solution.py
+++ b/solution.py
@@ -188,14 +188,6 @@
     ]
     params = pltpu.CompilerParams(vmem_limit_bytes=20 * MIB)
     piece = jax.ShapeDtypeStruct((subspace, width), jnp.float32)
-    slots = pl.pallas_call(
-        functools.partial(place_kernel, n_col, per_part),
-        out_shape=jax.ShapeDtypeStruct((2, slots_held), jnp.int32),
-        in_specs=vmem(3),
-        out_specs=pl.BlockSpec(memory_space=pltpu.VMEM),
-        compiler_params=params,
-        name="places",
-    )(tile_rows, tile_cols, counts)
     high, low = pl.pallas_call(
         stage_kernel,
         out_shape=[jax.ShapeDtypeStruct(tiles.shape, jnp.bfloat16)] * 2,
@@ -209,7 +201,16 @@
         name="stage",
     )(tiles)
 
-    parts, (slots, high, low) = gather_row(start_basis, (slots, high, low))
+    parts, (high, low) = gather_row(start_basis, (high, low))
+    parts[2], counts = lax.optimization_barrier((parts[2], counts))
+    slots = pl.pallas_call(
+        functools.partial(place_kernel, n_col, per_part),
+        out_shape=jax.ShapeDtypeStruct((2, slots_held), jnp.int32),
+        in_specs=vmem(3),
+        out_specs=pl.BlockSpec(memory_space=pltpu.VMEM),
+        compiler_params=params,
+        name="places",
+    )(tile_rows, tile_cols, counts)
 
     def products(parts):
         return pl.pallas_call(

time: 88.9 us -> 88.1 us (level)
  no operation moved by 1% of the time
where the time goes in v4:
time: 88.1 us; the launch traced here: 88 us
  starting transfers between devices  43.6 us (49%)
  waiting for transfers between devices  29 us (33%)
  Pallas kernels  13.8 us (16%)
  between operations  1.45 us (2%)
    ppermute x47, starting transfers between devices, swap(): return lax.ppermute(value, axis, [(i, i ^ distance) for i in range(size)])  43.6 us
    ppermute x47, waiting for transfers between devices, swap(): return lax.ppermute(value, axis, [(i, i ^ distance) for i in range(size)])  29 us
    pallas_call x4, Pallas kernels, products(): pl.pallas_call(functools.partial(product_kernel, n_row, n_col), out_shape...  5.73 us
    pallas_call x1, Pallas kernels, body(): pl.pallas_call(stage_kernel, out_shape=[jax.ShapeDtypeStruct(tiles.shape,...  4.5 us
  transfers between devices with their start and end apart: 47, of which 28 were waited for; matrix products, arithmetic and copies ran while one was open for 0% of the time, Pallas kernels for 7%

profile of v4, /device:TPU:0, one launch (start us, length us, event | category | flops | bytes accessed | tf_op | source)
XLA Modules:
  0.0 88.0 jit_solution(16577127242437960002)
XLA Ops:
  0.7 5.1 %collective-permute-start.2 = (f32[32,512]{1,0:T(8,128)}, f32[32,512]{1,0:T(8,128)S(1)}, u32[]{:S(2)}, u32[]{:S(2)}) collective-permute-start(f32[32,512]{1,0:T(8,128)} %refs_0_.1), channel_id=1, source_target_pairs={{0,24},{4,28},{8,16},{12,20},{16,8},{20,12},{24,0},{28,4},{1,25},{... | collective-permute-start | bytes 196616 | tf_op jit(solution)/shard_map/ppermute | solution.py:166
  5.8 0.6 collective-permute-start
  6.4 4.5 %stage.1 = (bf16[32,256,256]{2,1,0:T(8,128)(2,1)S(1)}, bf16[32,256,256]{2,1,0:T(8,128)(2,1)S(1)}) custom-call(f32[32,256,256]{2,1,0:T(8,128)} %tiles.1), custom_call_target="tpu_custom_call" | custom-call | tf_op jit(solution)/shard_map/stage/pallas_call | solution.py:191
  10.9 0.6 collective-permute-done.1.refs_4_
  13.4 1.4 %tile_products.4 = (f32[32,512]{1,0:T(8,128)S(1)}, f32[32,512]{1,0:T(8,128)S(1)}, f32[32,512]{1,0:T(8,128)S(1)}, f32[32,512]{1,0:T(8,128)S(1)}) custom-call(s32[2,32]{1,0:T(2,128)S(1)} %places.1.slots, bf16[32,256,256]{2,1,0:T(8,128)(2,1)S(1)} %get-tuple-element.41.high, bf16[32,256,256]{2,1,0:T(8,128)(2,1)S(1)} %get-tuple-element.42.low, ...), custom_call_target="tpu_custom_call" | custom-call | tf_op jit(solution)/shard_map/tile_products/pallas_call | solution.py:216
  14.8 2.5 %collective-permute-start.7 = (f32[32,512]{1,0:T(8,128)S(1)}, f32[32,512]{1,0:T(8,128)S(1)}, u32[]{:S(2)}, u32[]{:S(2)}) collective-permute-start(f32[32,512]{1,0:T(8,128)S(1)} %get-tuple-element.47), channel_id=1, source_target_pairs={{0,3},{1,2},{2,1},{3,0},{4,7},{5,6},{6,5},{7,4},{8,11},{9,10},{10,... | collective-permute-start | bytes 196616 | tf_op jit(solution)/shard_map/ppermute | solution.py:166
  18.4 1.7 %collective-permute-done.7 = f32[32,512]{1,0:T(8,128)S(1)} collective-permute-done((f32[32,512]{1,0:T(8,128)S(1)}, f32[32,512]{1,0:T(8,128)S(1)}, u32[]{:S(2)}, u32[]{:S(2)}) %collective-permute-start.7) | collective-permute-done | bytes 65568 | tf_op jit(solution)/shard_map/ppermute | solution.py:166
  20.1 1.5 %collective-permute-done.8 = f32[32,512]{1,0:T(8,128)S(1)} collective-permute-done((f32[32,512]{1,0:T(8,128)S(1)}, f32[32,512]{1,0:T(8,128)S(1)}, u32[]{:S(2)}, u32[]{:S(2)}) %collective-permute-start.8) | collective-permute-done | bytes 65568 | tf_op jit(solution)/shard_map/ppermute | solution.py:166
  22.1 3.4 %collective-permute-start.15 = (f32[32,512]{1,0:T(8,128)S(1)}, f32[32,512]{1,0:T(8,128)S(1)}, u32[]{:S(2)}, u32[]{:S(2)}) collective-permute-start(f32[32,512]{1,0:T(8,128)S(1)} %get-tuple-element.72.refs_0_), channel_id=1, source_target_pairs={{0,24},{4,28},{8,16},{12,20},{16,8},{20,12},{24,0},{28,4},{1,25},{... | collective-permute-start | bytes 196616 | tf_op jit(solution)/shard_map/ppermute | solution.py:166
  25.5 1.1 %collective-permute-start.11 = (f32[32,512]{1,0:T(8,128)S(1)}, f32[32,512]{1,0:T(8,128)S(1)}, u32[]{:S(2)}, u32[]{:S(2)}) collective-permute-start(f32[32,512]{1,0:T(8,128)S(1)} %get-tuple-element.72.refs_0_), channel_id=1, source_target_pairs={{0,8},{4,12},{8,0},{12,4},{16,24},{20,28},{24,16},{28,20},{1,9},{5... | collective-permute-start | bytes 196616 | tf_op jit(solution)/shard_map/ppermute | solution.py:166
  26.6 1.8 %collective-permute-done.15.refs_6_ = f32[32,512]{1,0:T(8,128)S(1)} collective-permute-done((f32[32,512]{1,0:T(8,128)S(1)}, f32[32,512]{1,0:T(8,128)S(1)}, u32[]{:S(2)}, u32[]{:S(2)}) %collective-permute-start.15) | collective-permute-done | bytes 65568 | tf_op jit(solution)/shard_map/ppermute | solution.py:166
  28.4 2.4 %collective-permute-done.13.refs_4_ = f32[32,512]{1,0:T(8,128)S(1)} collective-permute-done((f32[32,512]{1,0:T(8,128)S(1)}, f32[32,512]{1,0:T(8,128)S(1)}, u32[]{:S(2)}, u32[]{:S(2)}) %collective-permute-start.13) | collective-permute-done | bytes 65568 | tf_op jit(solution)/shard_map/ppermute | solution.py:166
  31.3 0.7 collective-permute-done.14.refs_5_
  32.2 1.4 %tile_products.5 = (f32[32,512]{1,0:T(8,128)S(1)}, f32[32,512]{1,0:T(8,128)S(1)}, f32[32,512]{1,0:T(8,128)S(1)}, f32[32,512]{1,0:T(8,128)S(1)}) custom-call(s32[2,32]{1,0:T(2,128)S(1)} %places.1.slots, bf16[32,256,256]{2,1,0:T(8,128)(2,1)S(1)} %get-tuple-element.41.high, bf16[32,256,256]{2,1,0:T(8,128)(2,1)S(1)} %get-tuple-element.42.low, ...), custom_call_target="tpu_custom_call" | custom-call | tf_op jit(solution)/shard_map/tile_products/pallas_call | solution.py:216
  33.6 1.6 %collective-permute-start.17 = (f32[32,512]{1,0:T(8,128)S(1)}, f32[32,512]{1,0:T(8,128)S(1)}, u32[]{:S(2)}, u32[]{:S(2)}) collective-permute-start(f32[32,512]{1,0:T(8,128)S(1)} %get-tuple-element.51), channel_id=1, source_target_pairs={{0,3},{1,2},{2,1},{3,0},{4,7},{5,6},{6,5},{7,4},{8,11},{9,10},{10,... | collective-permute-start | bytes 196616 | tf_op jit(solution)/shard_map/ppermute | solution.py:166
  35.2 1.4 %collective-permute-start.18 = (f32[32,512]{1,0:T(8,128)S(1)}, f32[32,512]{1,0:T(8,128)S(1)}, u32[]{:S(2)}, u32[]{:S(2)}) collective-permute-start(f32[32,512]{1,0:T(8,128)S(1)} %get-tuple-element.52), channel_id=1, source_target_pairs={{0,2},{1,3},{2,0},{3,1},{4,6},{5,7},{6,4},{7,5},{8,10},{9,11},{10,... | collective-permute-start | bytes 196616 | tf_op jit(solution)/shard_map/ppermute | solution.py:166
  37.2 1.9 %collective-permute-done.17 = f32[32,512]{1,0:T(8,128)S(1)} collective-permute-done((f32[32,512]{1,0:T(8,128)S(1)}, f32[32,512]{1,0:T(8,128)S(1)}, u32[]{:S(2)}, u32[]{:S(2)}) %collective-permute-start.17) | collective-permute-done | bytes 65568 | tf_op jit(solution)/shard_map/ppermute | solution.py:166
  39.0 1.3 %collective-permute-done.18 = f32[32,512]{1,0:T(8,128)S(1)} collective-permute-done((f32[32,512]{1,0:T(8,128)S(1)}, f32[32,512]{1,0:T(8,128)S(1)}, u32[]{:S(2)}, u32[]{:S(2)}) %collective-permute-start.18) | collective-permute-done | bytes 65568 | tf_op jit(solution)/shard_map/ppermute | solution.py:166
  40.8 2.3 %collective-permute-start.25 = (f32[32,512]{1,0:T(8,128)S(1)}, f32[32,512]{1,0:T(8,128)S(1)}, u32[]{:S(2)}, u32[]{:S(2)}) collective-permute-start(f32[32,512]{1,0:T(8,128)S(1)} %multiply_subtract_fusion.1.refs_0_), channel_id=1, source_target_pairs={{0,24},{4,28},{8,16},{12,20},{16,8},{20,12},{24,0},{28,4},{1,25},{... | collective-permute-start | bytes 196616 | tf_op jit(solution)/shard_map/ppermute | solution.py:166
  43.4 1.9 %collective-permute-start.21 = (f32[32,512]{1,0:T(8,128)S(1)}, f32[32,512]{1,0:T(8,128)S(1)}, u32[]{:S(2)}, u32[]{:S(2)}) collective-permute-start(f32[32,512]{1,0:T(8,128)S(1)} %multiply_subtract_fusion.1.refs_0_), channel_id=1, source_target_pairs={{0,8},{4,12},{8,0},{12,4},{16,24},{20,28},{24,16},{28,20},{1,9},{5... | collective-permute-start | bytes 196616 | tf_op jit(solution)/shard_map/ppermute | solution.py:166
  45.3 1.7 %collective-permute-done.25.refs_6_ = f32[32,512]{1,0:T(8,128)S(1)} collective-permute-done((f32[32,512]{1,0:T(8,128)S(1)}, f32[32,512]{1,0:T(8,128)S(1)}, u32[]{:S(2)}, u32[]{:S(2)}) %collective-permute-start.25) | collective-permute-done | bytes 65568 | tf_op jit(solution)/shard_map/ppermute | solution.py:166
  47.1 2.7 %collective-permute-done.23.refs_4_ = f32[32,512]{1,0:T(8,128)S(1)} collective-permute-done((f32[32,512]{1,0:T(8,128)S(1)}, f32[32,512]{1,0:T(8,128)S(1)}, u32[]{:S(2)}, u32[]{:S(2)}) %collective-permute-start.23) | collective-permute-done | bytes 65568 | tf_op jit(solution)/shard_map/ppermute | solution.py:166
  50.3 0.7 collective-permute-done.24.refs_5_
  51.2 1.4 %tile_products.6 = (f32[32,512]{1,0:T(8,128)S(1)}, f32[32,512]{1,0:T(8,128)S(1)}, f32[32,512]{1,0:T(8,128)S(1)}, f32[32,512]{1,0:T(8,128)S(1)}) custom-call(s32[2,32]{1,0:T(2,128)S(1)} %places.1.slots, bf16[32,256,256]{2,1,0:T(8,128)(2,1)S(1)} %get-tuple-element.41.high, bf16[32,256,256]{2,1,0:T(8,128)(2,1)S(1)} %get-tuple-element.42.low, ...), custom_call_target="tpu_custom_call" | custom-call | tf_op jit(solution)/shard_map/tile_products/pallas_call | solution.py:216
  52.6 1.6 %collective-permute-start.27 = (f32[32,512]{1,0:T(8,128)S(1)}, f32[32,512]{1,0:T(8,128)S(1)}, u32[]{:S(2)}, u32[]{:S(2)}) collective-permute-start(f32[32,512]{1,0:T(8,128)S(1)} %get-tuple-element.55), channel_id=1, source_target_pairs={{0,3},{1,2},{2,1},{3,0},{4,7},{5,6},{6,5},{7,4},{8,11},{9,10},{10,... | collective-permute-start | bytes 196616 | tf_op jit(solution)/shard_map/ppermute | solution.py:166
  54.2 0.8 collective-permute-start.28
  54.9 1.2 %collective-permute-start.29 = (f32[32,512]{1,0:T(8,128)S(1)}, f32[32,512]{1,0:T(8,128)S(1)}, u32[]{:S(2)}, u32[]{:S(2)}) collective-permute-start(f32[32,512]{1,0:T(8,128)S(1)} %get-tuple-element.57), channel_id=1, source_target_pairs={{0,1},{1,0},{2,3},{3,2},{4,5},{5,4},{6,7},{7,6},{8,9},{9,8},{10,11... | collective-permute-start | bytes 196616 | tf_op jit(solution)/shard_map/ppermute | solution.py:166
  56.2 1.9 %collective-permute-done.27 = f32[32,512]{1,0:T(8,128)S(1)} collective-permute-done((f32[32,512]{1,0:T(8,128)S(1)}, f32[32,512]{1,0:T(8,128)S(1)}, u32[]{:S(2)}, u32[]{:S(2)}) %collective-permute-start.27) | collective-permute-done | bytes 65568 | tf_op jit(solution)/shard_map/ppermute | solution.py:166
  58.0 1.3 %collective-permute-done.28 = f32[32,512]{1,0:T(8,128)S(1)} collective-permute-done((f32[32,512]{1,0:T(8,128)S(1)}, f32[32,512]{1,0:T(8,128)S(1)}, u32[]{:S(2)}, u32[]{:S(2)}) %collective-permute-start.28) | collective-permute-done | bytes 65568 | tf_op jit(solution)/shard_map/ppermute | solution.py:166
  59.4 2.1 %collective-permute-start.38 = (f32[32,512]{1,0:T(8,128)S(1)}, f32[32,512]{1,0:T(8,128)S(1)}, u32[]{:S(2)}, u32[]{:S(2)}) collective-permute-start(f32[32,512]{1,0:T(8,128)S(1)} %multiply_subtract_fusion.refs_0_.filtered), channel_id=1, source_target_pairs={{0,24},{4,28},{8,16},{12,20},{16,8},{20,12},{24,0},{28,4},{1,25},{... | collective-permute-start | bytes 196616 | tf_op jit(solution)/shard_map/ppermute | solution.py:166
  61.5 1.6 %collective-permute-start.36 = (f32[32,512]{1,0:T(8,128)S(1)}, f32[32,512]{1,0:T(8,128)S(1)}, u32[]{:S(2)}, u32[]{:S(2)}) collective-permute-start(f32[32,512]{1,0:T(8,128)S(1)} %multiply_subtract_fusion.refs_0_.filtered), channel_id=1, source_target_pairs={{0,3},{1,2},{2,1},{3,0},{4,7},{5,6},{6,5},{7,4},{8,11},{9,10},{10,... | collective-permute-start | bytes 196616 | tf_op jit(solution)/shard_map/ppermute | solution.py:166
  63.1 0.8 collective-permute-start.35
  63.9 2.5 %collective-permute-start.31 = (f32[32,512]{1,0:T(8,128)S(1)}, f32[32,512]{1,0:T(8,128)S(1)}, u32[]{:S(2)}, u32[]{:S(2)}) collective-permute-start(f32[32,512]{1,0:T(8,128)S(1)} %multiply_subtract_fusion.refs_0_.filtered), channel_id=1, source_target_pairs={{0,8},{4,12},{8,0},{12,4},{16,24},{20,28},{24,16},{28,20},{1,9},{5... | collective-permute-start | bytes 196616 | tf_op jit(solution)/shard_map/ppermute | solution.py:166
  66.4 0.9 %collective-permute-start.34 = (f32[32,512]{1,0:T(8,128)S(1)}, f32[32,512]{1,0:T(8,128)S(1)}, u32[]{:S(2)}, u32[]{:S(2)}) collective-permute-start(f32[32,512]{1,0:T(8,128)S(1)} %multiply_subtract_fusion.refs_0_.filtered), channel_id=1, source_target_pairs={{0,1},{1,0},{2,3},{3,2},{4,5},{5,4},{6,7},{7,6},{8,9},{9,8},{10,11... | collective-permute-start | bytes 196616 | tf_op jit(solution)/shard_map/ppermute | solution.py:166
  67.3 0.8 collective-permute-done.33.refs_4_
  69.1 1.5 %collective-permute-done.34.refs_8_ = f32[32,512]{1,0:T(8,128)S(1)} collective-permute-done((f32[32,512]{1,0:T(8,128)S(1)}, f32[32,512]{1,0:T(8,128)S(1)}, u32[]{:S(2)}, u32[]{:S(2)}) %collective-permute-start.34) | collective-permute-done | bytes 65568 | tf_op jit(solution)/shard_map/ppermute | solution.py:166
  70.7 1.4 %tile_products.7 = (f32[32,512]{1,0:T(8,128)S(1)}, f32[32,512]{1,0:T(8,128)S(1)}, f32[32,512]{1,0:T(8,128)S(1)}, f32[32,512]{1,0:T(8,128)S(1)}) custom-call(s32[2,32]{1,0:T(2,128)S(1)} %places.1.slots, bf16[32,256,256]{2,1,0:T(8,128)(2,1)S(1)} %get-tuple-element.41.high, bf16[32,256,256]{2,1,0:T(8,128)(2,1)S(1)} %get-tuple-element.42.low, ...), custom_call_target="tpu_custom_call" | custom-call | tf_op jit(solution)/shard_map/tile_products/pallas_call | solution.py:216
  72.7 1.5 %collective-permute-start.42 = (f32[32,64]{1,0:T(8,128)S(1)}, f32[32,64]{1,0:T(8,128)S(1)}, u32[]{:S(2)}, u32[]{:S(2)}) collective-permute-start(f32[32,64]{1,0:T(8,128)S(1)} %moment.1), channel_id=1, source_target_pairs={{0,3},{1,2},{2,1},{3,0},{4,7},{5,6},{6,5},{7,4},{8,11},{9,10},{10,... | collective-permute-start | bytes 24584 | tf_op jit(solution)/shard_map/ppermute | solution.py:166
  74.2 0.9 %collective-permute-start.41 = (f32[32,64]{1,0:T(8,128)S(1)}, f32[32,64]{1,0:T(8,128)S(1)}, u32[]{:S(2)}, u32[]{:S(2)}) collective-permute-start(f32[32,64]{1,0:T(8,128)S(1)} %moment.1), channel_id=1, source_target_pairs={{0,2},{1,3},{2,0},{3,1},{4,6},{5,7},{6,4},{7,5},{8,10},{9,11},{10,... | collective-permute-start | bytes 24584 | tf_op jit(solution)/shard_map/ppermute | solution.py:166
  75.1 1.1 %collective-permute-start.40 = (f32[32,64]{1,0:T(8,128)S(1)}, f32[32,64]{1,0:T(8,128)S(1)}, u32[]{:S(2)}, u32[]{:S(2)}) collective-permute-start(f32[32,64]{1,0:T(8,128)S(1)} %moment.1), channel_id=1, source_target_pairs={{0,1},{1,0},{2,3},{3,2},{4,5},{5,4},{6,7},{7,6},{8,9},{9,8},{10,11... | collective-permute-start | bytes 24584 | tf_op jit(solution)/shard_map/ppermute | solution.py:166
  76.2 1.1 %collective-permute-done.42 = f32[32,64]{1,0:T(8,128)S(1)} collective-permute-done((f32[32,64]{1,0:T(8,128)S(1)}, f32[32,64]{1,0:T(8,128)S(1)}, u32[]{:S(2)}, u32[]{:S(2)}) %collective-permute-start.42) | collective-permute-done | bytes 8224 | tf_op jit(solution)/shard_map/ppermute | solution.py:166
  78.0 0.9 %collective-permute-done.40 = f32[32,64]{1,0:T(8,128)S(1)} collective-permute-done((f32[32,64]{1,0:T(8,128)S(1)}, f32[32,64]{1,0:T(8,128)S(1)}, u32[]{:S(2)}, u32[]{:S(2)}) %collective-permute-start.40) | collective-permute-done | bytes 8224 | tf_op jit(solution)/shard_map/ppermute | solution.py:166
  78.9 2.0 %collective-permute-start.45 = (f32[32,64]{1,0:T(8,128)S(1)}, f32[32,64]{1,0:T(8,128)S(1)}, u32[]{:S(2)}, u32[]{:S(2)}) collective-permute-start(f32[32,64]{1,0:T(8,128)S(1)} %add_add_fusion.1.sums), channel_id=1, source_target_pairs={{0,24},{4,28},{8,16},{12,20},{16,8},{20,12},{24,0},{28,4},{1,25},{... | collective-permute-start | bytes 24584 | tf_op jit(solution)/shard_map/ppermute | solution.py:166
  80.9 0.7 collective-permute-start.44
  81.5 1.7 %collective-permute-start.43 = (f32[32,64]{1,0:T(8,128)S(1)}, f32[32,64]{1,0:T(8,128)S(1)}, u32[]{:S(2)}, u32[]{:S(2)}) collective-permute-start(f32[32,64]{1,0:T(8,128)S(1)} %add_add_fusion.1.sums), channel_id=1, source_target_pairs={{0,8},{4,12},{8,0},{12,4},{16,24},{20,28},{24,16},{28,20},{1,9},{5... | collective-permute-start | bytes 24584 | tf_op jit(solution)/shard_map/ppermute | solution.py:166
  83.2 1.7 %factor.1 = (f32[32,32]{1,0:T(8,128)S(1)}, f32[32,512]{1,0:T(8,128)}) custom-call(f32[32,64]{1,0:T(8,128)S(1)} %add_add_fusion.1.sums, f32[32,512]{1,0:T(8,128)S(1)} %multiply_subtract_fusion.refs_0_.filtered), custom_call_target="tpu_custom_call" | custom-call | tf_op jit(solution)/shard_map/factor/pallas_call | solution.py:257
  85.6 1.2 %collective-permute-done.46 = f32[32,64]{1,0:T(8,128)S(1)} collective-permute-done((f32[32,64]{1,0:T(8,128)S(1)}, f32[32,64]{1,0:T(8,128)S(1)}, u32[]{:S(2)}, u32[]{:S(2)}) %collective-permute-start.46) | collective-permute-done | bytes 8224 | tf_op jit(solution)/shard_map/ppermute | solution.py:166
  86.8 1.2 %project.1 = f32[32,32]{1,0:T(8,128)} custom-call(f32[32,64]{1,0:T(8,128)S(1)} %add.65.sums, f32[32,32]{1,0:T(8,128)S(1)} %get-tuple-element.71.inverse), custom_call_target="tpu_custom_call" | custom-call | tf_op jit(solution)/shard_map/project/pallas_call | solution.py:269
  (70 shorter events, 8.3 us)
Async XLA Ops:
  0.6 12.7 %copy-start = (f32[32,512]{1,0:T(8,128)S(1)}, f32[32,512]{1,0:T(8,128)}, u32[]{:S(2)}) copy-start(f32[32,512]{1,0:T(8,128)} %refs_0_.1) | copy-start | bytes 196612
  0.7 10.3 %collective-permute-start.2 = (f32[32,512]{1,0:T(8,128)}, f32[32,512]{1,0:T(8,128)S(1)}, u32[]{:S(2)}, u32[]{:S(2)}) collective-permute-start(f32[32,512]{1,0:T(8,128)} %refs_0_.1), channel_id=1, source_target_pairs={{0,24},{4,28},{8,16},{12,20},{16,8},{20,12},{24,0},{28,4},{1,25},{... | collective-permute-start | bytes 196616 | tf_op jit(solution)/shard_map/ppermute | solution.py:166
  5.8 5.8 %collective-permute-start.1 = (f32[32,512]{1,0:T(8,128)}, f32[32,512]{1,0:T(8,128)S(1)}, u32[]{:S(2)}, u32[]{:S(2)}) collective-permute-start(f32[32,512]{1,0:T(8,128)} %refs_0_.1), channel_id=1, source_target_pairs={{0,16},{4,20},{8,24},{12,28},{16,0},{20,4},{24,8},{28,12},{1,17},{... | collective-permute-start | bytes 196616 | tf_op jit(solution)/shard_map/ppermute | solution.py:166
  5.8 5.8 %collective-permute-start = (f32[32,512]{1,0:T(8,128)}, f32[32,512]{1,0:T(8,128)S(1)}, u32[]{:S(2)}, u32[]{:S(2)}) collective-permute-start(f32[32,512]{1,0:T(8,128)} %refs_0_.1), channel_id=1, source_target_pairs={{0,8},{4,12},{8,0},{12,4},{16,24},{20,28},{24,16},{28,20},{1,9},{5... | collective-permute-start | bytes 196616 | tf_op jit(solution)/shard_map/ppermute | solution.py:166
  6.4 6.4 %collective-permute-start.3 = (f32[32,512]{1,0:T(8,128)}, f32[32,512]{1,0:T(8,128)S(1)}, u32[]{:S(2)}, u32[]{:S(2)}) collective-permute-start(f32[32,512]{1,0:T(8,128)} %refs_0_.1), channel_id=1, source_target_pairs={{0,4},{4,0},{8,12},{12,8},{16,20},{20,16},{24,28},{28,24},{1,5},{5... | collective-permute-start | bytes 196616 | tf_op jit(solution)/shard_map/ppermute | solution.py:166
  11.6 1.3 %collective-permute-start.4 = (f32[32,512]{1,0:T(8,128)S(1)}, f32[32,512]{1,0:T(8,128)S(1)}, u32[]{:S(2)}, u32[]{:S(2)}) collective-permute-start(f32[32,512]{1,0:T(8,128)S(1)} %collective-permute-done.refs_2_), channel_id=1, source_target_pairs={{0,4},{4,0},{8,12},{12,8},{16,20},{20,16},{24,28},{28,24},{1,5},{5... | collective-permute-start | bytes 196616 | tf_op jit(solution)/shard_map/ppermute | solution.py:166
  11.6 1.4 %collective-permute-start.5 = (f32[32,512]{1,0:T(8,128)S(1)}, f32[32,512]{1,0:T(8,128)S(1)}, u32[]{:S(2)}, u32[]{:S(2)}) collective-permute-start(f32[32,512]{1,0:T(8,128)S(1)} %collective-permute-done.1.refs_4_), channel_id=1, source_target_pairs={{0,4},{4,0},{8,12},{12,8},{16,20},{20,16},{24,28},{28,24},{1,5},{5... | collective-permute-start | bytes 196616 | tf_op jit(solution)/shard_map/ppermute | solution.py:166
  12.1 1.3 %collective-permute-start.6 = (f32[32,512]{1,0:T(8,128)S(1)}, f32[32,512]{1,0:T(8,128)S(1)}, u32[]{:S(2)}, u32[]{:S(2)}) collective-permute-start(f32[32,512]{1,0:T(8,128)S(1)} %collective-permute-done.2.refs_6_), channel_id=1, source_target_pairs={{0,4},{4,0},{8,12},{12,8},{16,20},{20,16},{24,28},{28,24},{1,5},{5... | collective-permute-start | bytes 196616 | tf_op jit(solution)/shard_map/ppermute | solution.py:166
  14.8 5.3 %collective-permute-start.7 = (f32[32,512]{1,0:T(8,128)S(1)}, f32[32,512]{1,0:T(8,128)S(1)}, u32[]{:S(2)}, u32[]{:S(2)}) collective-permute-start(f32[32,512]{1,0:T(8,128)S(1)} %get-tuple-element.47), channel_id=1, source_target_pairs={{0,3},{1,2},{2,1},{3,0},{4,7},{5,6},{6,5},{7,4},{8,11},{9,10},{10,... | collective-permute-start | bytes 196616 | tf_op jit(solution)/shard_map/ppermute | solution.py:166
  17.3 4.3 %collective-permute-start.8 = (f32[32,512]{1,0:T(8,128)S(1)}, f32[32,512]{1,0:T(8,128)S(1)}, u32[]{:S(2)}, u32[]{:S(2)}) collective-permute-start(f32[32,512]{1,0:T(8,128)S(1)} %get-tuple-element.48), channel_id=1, source_target_pairs={{0,2},{1,3},{2,0},{3,1},{4,6},{5,7},{6,4},{7,5},{8,10},{9,11},{10,... | collective-permute-start | bytes 196616 | tf_op jit(solution)/shard_map/ppermute | solution.py:166
  17.8 4.3 %collective-permute-start.9 = (f32[32,512]{1,0:T(8,128)S(1)}, f32[32,512]{1,0:T(8,128)S(1)}, u32[]{:S(2)}, u32[]{:S(2)}) collective-permute-start(f32[32,512]{1,0:T(8,128)S(1)} %get-tuple-element.49), channel_id=1, source_target_pairs={{0,1},{1,0},{2,3},{3,2},{4,5},{5,4},{6,7},{7,6},{8,9},{9,8},{10,11... | collective-permute-start | bytes 196616 | tf_op jit(solution)/shard_map/ppermute | solution.py:166
  22.1 6.2 %collective-permute-start.15 = (f32[32,512]{1,0:T(8,128)S(1)}, f32[32,512]{1,0:T(8,128)S(1)}, u32[]{:S(2)}, u32[]{:S(2)}) collective-permute-start(f32[32,512]{1,0:T(8,128)S(1)} %get-tuple-element.72.refs_0_), channel_id=1, source_target_pairs={{0,24},{4,28},{8,16},{12,20},{16,8},{20,12},{24,0},{28,4},{1,25},{... | collective-permute-start | bytes 196616 | tf_op jit(solution)/shard_map/ppermute | solution.py:166
  25.5 5.2 %collective-permute-start.13 = (f32[32,512]{1,0:T(8,128)S(1)}, f32[32,512]{1,0:T(8,128)S(1)}, u32[]{:S(2)}, u32[]{:S(2)}) collective-permute-start(f32[32,512]{1,0:T(8,128)S(1)} %get-tuple-element.72.refs_0_), channel_id=1, source_target_pairs={{0,16},{4,20},{8,24},{12,28},{16,0},{20,4},{24,8},{28,12},{1,17},{... | collective-permute-start | bytes 196616 | tf_op jit(solution)/shard_map/ppermute | solution.py:166
  25.5 5.3 %collective-permute-start.11 = (f32[32,512]{1,0:T(8,128)S(1)}, f32[32,512]{1,0:T(8,128)S(1)}, u32[]{:S(2)}, u32[]{:S(2)}) collective-permute-start(f32[32,512]{1,0:T(8,128)S(1)} %get-tuple-element.72.refs_0_), channel_id=1, source_target_pairs={{0,8},{4,12},{8,0},{12,4},{16,24},{20,28},{24,16},{28,20},{1,9},{5... | collective-permute-start | bytes 196616 | tf_op jit(solution)/shard_map/ppermute | solution.py:166
  26.6 4.7 %collective-permute-start.10 = (f32[32,512]{1,0:T(8,128)S(1)}, f32[32,512]{1,0:T(8,128)S(1)}, u32[]{:S(2)}, u32[]{:S(2)}) collective-permute-start(f32[32,512]{1,0:T(8,128)S(1)} %get-tuple-element.72.refs_0_), channel_id=1, source_target_pairs={{0,4},{4,0},{8,12},{12,8},{16,20},{20,16},{24,28},{28,24},{1,5},{5... | collective-permute-start | bytes 196616 | tf_op jit(solution)/shard_map/ppermute | solution.py:166
  28.3 2.9 %collective-permute-start.16 = (f32[32,512]{1,0:T(8,128)S(1)}, f32[32,512]{1,0:T(8,128)S(1)}, u32[]{:S(2)}, u32[]{:S(2)}) collective-permute-start(f32[32,512]{1,0:T(8,128)S(1)} %collective-permute-done.15.refs_6_), channel_id=1, source_target_pairs={{0,4},{4,0},{8,12},{12,8},{16,20},{20,16},{24,28},{28,24},{1,5},{5... | collective-permute-start | bytes 196616 | tf_op jit(solution)/shard_map/ppermute | solution.py:166
  30.7 1.3 %collective-permute-start.14 = (f32[32,512]{1,0:T(8,128)S(1)}, f32[32,512]{1,0:T(8,128)S(1)}, u32[]{:S(2)}, u32[]{:S(2)}) collective-permute-start(f32[32,512]{1,0:T(8,128)S(1)} %collective-permute-done.13.refs_4_), channel_id=1, source_target_pairs={{0,4},{4,0},{8,12},{12,8},{16,20},{20,16},{24,28},{28,24},{1,5},{5... | collective-permute-start | bytes 196616 | tf_op jit(solution)/shard_map/ppermute | solution.py:166
  30.9 1.3 %collective-permute-start.12 = (f32[32,512]{1,0:T(8,128)S(1)}, f32[32,512]{1,0:T(8,128)S(1)}, u32[]{:S(2)}, u32[]{:S(2)}) collective-permute-start(f32[32,512]{1,0:T(8,128)S(1)} %collective-permute-done.11.refs_2_), channel_id=1, source_target_pairs={{0,4},{4,0},{8,12},{12,8},{16,20},{20,16},{24,28},{28,24},{1,5},{5... | collective-permute-start | bytes 196616 | tf_op jit(solution)/shard_map/ppermute | solution.py:166
  33.6 5.4 %collective-permute-start.17 = (f32[32,512]{1,0:T(8,128)S(1)}, f32[32,512]{1,0:T(8,128)S(1)}, u32[]{:S(2)}, u32[]{:S(2)}) collective-permute-start(f32[32,512]{1,0:T(8,128)S(1)} %get-tuple-element.51), channel_id=1, source_target_pairs={{0,3},{1,2},{2,1},{3,0},{4,7},{5,6},{6,5},{7,4},{8,11},{9,10},{10,... | collective-permute-start | bytes 196616 | tf_op jit(solution)/shard_map/ppermute | solution.py:166
  35.2 5.2 %collective-permute-start.18 = (f32[32,512]{1,0:T(8,128)S(1)}, f32[32,512]{1,0:T(8,128)S(1)}, u32[]{:S(2)}, u32[]{:S(2)}) collective-permute-start(f32[32,512]{1,0:T(8,128)S(1)} %get-tuple-element.52), channel_id=1, source_target_pairs={{0,2},{1,3},{2,0},{3,1},{4,6},{5,7},{6,4},{7,5},{8,10},{9,11},{10,... | collective-permute-start | bytes 196616 | tf_op jit(solution)/shard_map/ppermute | solution.py:166
  36.5 4.3 %collective-permute-start.19 = (f32[32,512]{1,0:T(8,128)S(1)}, f32[32,512]{1,0:T(8,128)S(1)}, u32[]{:S(2)}, u32[]{:S(2)}) collective-permute-start(f32[32,512]{1,0:T(8,128)S(1)} %get-tuple-element.53), channel_id=1, source_target_pairs={{0,1},{1,0},{2,3},{3,2},{4,5},{5,4},{6,7},{7,6},{8,9},{9,8},{10,11... | collective-permute-start | bytes 196616 | tf_op jit(solution)/shard_map/ppermute | solution.py:166
  40.8 6.2 %collective-permute-start.25 = (f32[32,512]{1,0:T(8,128)S(1)}, f32[32,512]{1,0:T(8,128)S(1)}, u32[]{:S(2)}, u32[]{:S(2)}) collective-permute-start(f32[32,512]{1,0:T(8,128)S(1)} %multiply_subtract_fusion.1.refs_0_), channel_id=1, source_target_pairs={{0,24},{4,28},{8,16},{12,20},{16,8},{20,12},{24,0},{28,4},{1,25},{... | collective-permute-start | bytes 196616 | tf_op jit(solution)/shard_map/ppermute | solution.py:166
  43.2 6.6 %collective-permute-start.23 = (f32[32,512]{1,0:T(8,128)S(1)}, f32[32,512]{1,0:T(8,128)S(1)}, u32[]{:S(2)}, u32[]{:S(2)}) collective-permute-start(f32[32,512]{1,0:T(8,128)S(1)} %multiply_subtract_fusion.1.refs_0_), channel_id=1, source_target_pairs={{0,16},{4,20},{8,24},{12,28},{16,0},{20,4},{24,8},{28,12},{1,17},{... | collective-permute-start | bytes 196616 | tf_op jit(solution)/shard_map/ppermute | solution.py:166
  43.4 6.4 %collective-permute-start.21 = (f32[32,512]{1,0:T(8,128)S(1)}, f32[32,512]{1,0:T(8,128)S(1)}, u32[]{:S(2)}, u32[]{:S(2)}) collective-permute-start(f32[32,512]{1,0:T(8,128)S(1)} %multiply_subtract_fusion.1.refs_0_), channel_id=1, source_target_pairs={{0,8},{4,12},{8,0},{12,4},{16,24},{20,28},{24,16},{28,20},{1,9},{5... | collective-permute-start | bytes 196616 | tf_op jit(solution)/shard_map/ppermute | solution.py:166
  45.3 5.0 %collective-permute-start.20 = (f32[32,512]{1,0:T(8,128)S(1)}, f32[32,512]{1,0:T(8,128)S(1)}, u32[]{:S(2)}, u32[]{:S(2)}) collective-permute-start(f32[32,512]{1,0:T(8,128)S(1)} %multiply_subtract_fusion.1.refs_0_), channel_id=1, source_target_pairs={{0,4},{4,0},{8,12},{12,8},{16,20},{20,16},{24,28},{28,24},{1,5},{5... | collective-permute-start | bytes 196616 | tf_op jit(solution)/shard_map/ppermute | solution.py:166
  47.1 3.2 %collective-permute-start.26 = (f32[32,512]{1,0:T(8,128)S(1)}, f32[32,512]{1,0:T(8,128)S(1)}, u32[]{:S(2)}, u32[]{:S(2)}) collective-permute-start(f32[32,512]{1,0:T(8,128)S(1)} %collective-permute-done.25.refs_6_), channel_id=1, source_target_pairs={{0,4},{4,0},{8,12},{12,8},{16,20},{20,16},{24,28},{28,24},{1,5},{5... | collective-permute-start | bytes 196616 | tf_op jit(solution)/shard_map/ppermute | solution.py:166
  49.8 1.3 %collective-permute-start.24 = (f32[32,512]{1,0:T(8,128)S(1)}, f32[32,512]{1,0:T(8,128)S(1)}, u32[]{:S(2)}, u32[]{:S(2)}) collective-permute-start(f32[32,512]{1,0:T(8,128)S(1)} %collective-permute-done.23.refs_4_), channel_id=1, source_target_pairs={{0,4},{4,0},{8,12},{12,8},{16,20},{20,16},{24,28},{28,24},{1,5},{5... | collective-permute-start | bytes 196616 | tf_op jit(solution)/shard_map/ppermute | solution.py:166
  49.8 1.4 %collective-permute-start.22 = (f32[32,512]{1,0:T(8,128)S(1)}, f32[32,512]{1,0:T(8,128)S(1)}, u32[]{:S(2)}, u32[]{:S(2)}) collective-permute-start(f32[32,512]{1,0:T(8,128)S(1)} %collective-permute-done.21.refs_2_), channel_id=1, source_target_pairs={{0,4},{4,0},{8,12},{12,8},{16,20},{20,16},{24,28},{28,24},{1,5},{5... | collective-permute-start | bytes 196616 | tf_op jit(solution)/shard_map/ppermute | solution.py:166
  52.6 5.4 %collective-permute-start.27 = (f32[32,512]{1,0:T(8,128)S(1)}, f32[32,512]{1,0:T(8,128)S(1)}, u32[]{:S(2)}, u32[]{:S(2)}) collective-permute-start(f32[32,512]{1,0:T(8,128)S(1)} %get-tuple-element.55), channel_id=1, source_target_pairs={{0,3},{1,2},{2,1},{3,0},{4,7},{5,6},{6,5},{7,4},{8,11},{9,10},{10,... | collective-permute-start | bytes 196616 | tf_op jit(solution)/shard_map/ppermute | solution.py:166
  54.2 5.2 %collective-permute-start.28 = (f32[32,512]{1,0:T(8,128)S(1)}, f32[32,512]{1,0:T(8,128)S(1)}, u32[]{:S(2)}, u32[]{:S(2)}) collective-permute-start(f32[32,512]{1,0:T(8,128)S(1)} %get-tuple-element.56), channel_id=1, source_target_pairs={{0,2},{1,3},{2,0},{3,1},{4,6},{5,7},{6,4},{7,5},{8,10},{9,11},{10,... | collective-permute-start | bytes 196616 | tf_op jit(solution)/shard_map/ppermute | solution.py:166
  54.9 4.4 %collective-permute-start.29 = (f32[32,512]{1,0:T(8,128)S(1)}, f32[32,512]{1,0:T(8,128)S(1)}, u32[]{:S(2)}, u32[]{:S(2)}) collective-permute-start(f32[32,512]{1,0:T(8,128)S(1)} %get-tuple-element.57), channel_id=1, source_target_pairs={{0,1},{1,0},{2,3},{3,2},{4,5},{5,4},{6,7},{7,6},{8,9},{9,8},{10,11... | collective-permute-start | bytes 196616 | tf_op jit(solution)/shard_map/ppermute | solution.py:166
  59.4 7.0 %collective-permute-start.38 = (f32[32,512]{1,0:T(8,128)S(1)}, f32[32,512]{1,0:T(8,128)S(1)}, u32[]{:S(2)}, u32[]{:S(2)}) collective-permute-start(f32[32,512]{1,0:T(8,128)S(1)} %multiply_subtract_fusion.refs_0_.filtered), channel_id=1, source_target_pairs={{0,24},{4,28},{8,16},{12,20},{16,8},{20,12},{24,0},{28,4},{1,25},{... | collective-permute-start | bytes 196616 | tf_op jit(solution)/shard_map/ppermute | solution.py:166
  61.5 6.6 %collective-permute-start.33 = (f32[32,512]{1,0:T(8,128)S(1)}, f32[32,512]{1,0:T(8,128)S(1)}, u32[]{:S(2)}, u32[]{:S(2)}) collective-permute-start(f32[32,512]{1,0:T(8,128)S(1)} %multiply_subtract_fusion.refs_0_.filtered), channel_id=1, source_target_pairs={{0,16},{4,20},{8,24},{12,28},{16,0},{20,4},{24,8},{28,12},{1,17},{... | collective-permute-start | bytes 196616 | tf_op jit(solution)/shard_map/ppermute | solution.py:166
  61.5 6.6 %collective-permute-start.36 = (f32[32,512]{1,0:T(8,128)S(1)}, f32[32,512]{1,0:T(8,128)S(1)}, u32[]{:S(2)}, u32[]{:S(2)}) collective-permute-start(f32[32,512]{1,0:T(8,128)S(1)} %multiply_subtract_fusion.refs_0_.filtered), channel_id=1, source_target_pairs={{0,3},{1,2},{2,1},{3,0},{4,7},{5,6},{6,5},{7,4},{8,11},{9,10},{10,... | collective-permute-start | bytes 196616 | tf_op jit(solution)/shard_map/ppermute | solution.py:166
  63.1 5.5 %collective-permute-start.35 = (f32[32,512]{1,0:T(8,128)S(1)}, f32[32,512]{1,0:T(8,128)S(1)}, u32[]{:S(2)}, u32[]{:S(2)}) collective-permute-start(f32[32,512]{1,0:T(8,128)S(1)} %multiply_subtract_fusion.refs_0_.filtered), channel_id=1, source_target_pairs={{0,2},{1,3},{2,0},{3,1},{4,6},{5,7},{6,4},{7,5},{8,10},{9,11},{10,... | collective-permute-start | bytes 196616 | tf_op jit(solution)/shard_map/ppermute | solution.py:166
  63.9 4.9 %collective-permute-start.31 = (f32[32,512]{1,0:T(8,128)S(1)}, f32[32,512]{1,0:T(8,128)S(1)}, u32[]{:S(2)}, u32[]{:S(2)}) collective-permute-start(f32[32,512]{1,0:T(8,128)S(1)} %multiply_subtract_fusion.refs_0_.filtered), channel_id=1, source_target_pairs={{0,8},{4,12},{8,0},{12,4},{16,24},{20,28},{24,16},{28,20},{1,9},{5... | collective-permute-start | bytes 196616 | tf_op jit(solution)/shard_map/ppermute | solution.py:166
  66.4 4.3 %collective-permute-start.34 = (f32[32,512]{1,0:T(8,128)S(1)}, f32[32,512]{1,0:T(8,128)S(1)}, u32[]{:S(2)}, u32[]{:S(2)}) collective-permute-start(f32[32,512]{1,0:T(8,128)S(1)} %multiply_subtract_fusion.refs_0_.filtered), channel_id=1, source_target_pairs={{0,1},{1,0},{2,3},{3,2},{4,5},{5,4},{6,7},{7,6},{8,9},{9,8},{10,11... | collective-permute-start | bytes 196616 | tf_op jit(solution)/shard_map/ppermute | solution.py:166
  68.1 2.6 %collective-permute-start.37 = (f32[32,512]{1,0:T(8,128)S(1)}, f32[32,512]{1,0:T(8,128)S(1)}, u32[]{:S(2)}, u32[]{:S(2)}) collective-permute-start(f32[32,512]{1,0:T(8,128)S(1)} %collective-permute-done.33.refs_4_), channel_id=1, source_target_pairs={{0,4},{4,0},{8,12},{12,8},{16,20},{20,16},{24,28},{28,24},{1,5},{5... | collective-permute-start | bytes 196616 | tf_op jit(solution)/shard_map/ppermute | solution.py:166
  68.1 2.6 %collective-permute-start.30 = (f32[32,512]{1,0:T(8,128)S(1)}, f32[32,512]{1,0:T(8,128)S(1)}, u32[]{:S(2)}, u32[]{:S(2)}) collective-permute-start(f32[32,512]{1,0:T(8,128)S(1)} %multiply_subtract_fusion.refs_0_.filtered), channel_id=1, source_target_pairs={{0,4},{4,0},{8,12},{12,8},{16,20},{20,16},{24,28},{28,24},{1,5},{5... | collective-permute-start | bytes 196616 | tf_op jit(solution)/shard_map/ppermute | solution.py:166
  68.6 2.1 %collective-permute-start.39 = (f32[32,512]{1,0:T(8,128)S(1)}, f32[32,512]{1,0:T(8,128)S(1)}, u32[]{:S(2)}, u32[]{:S(2)}) collective-permute-start(f32[32,512]{1,0:T(8,128)S(1)} %collective-permute-done.38.refs_6_), channel_id=1, source_target_pairs={{0,4},{4,0},{8,12},{12,8},{16,20},{20,16},{24,28},{28,24},{1,5},{5... | collective-permute-start | bytes 196616 | tf_op jit(solution)/shard_map/ppermute | solution.py:166
  68.8 1.9 %collective-permute-start.32 = (f32[32,512]{1,0:T(8,128)S(1)}, f32[32,512]{1,0:T(8,128)S(1)}, u32[]{:S(2)}, u32[]{:S(2)}) collective-permute-start(f32[32,512]{1,0:T(8,128)S(1)} %collective-permute-done.31.refs_2_), channel_id=1, source_target_pairs={{0,4},{4,0},{8,12},{12,8},{16,20},{20,16},{24,28},{28,24},{1,5},{5... | collective-permute-start | bytes 196616 | tf_op jit(solution)/shard_map/ppermute | solution.py:166
  72.7 4.7 %collective-permute-start.42 = (f32[32,64]{1,0:T(8,128)S(1)}, f32[32,64]{1,0:T(8,128)S(1)}, u32[]{:S(2)}, u32[]{:S(2)}) collective-permute-start(f32[32,64]{1,0:T(8,128)S(1)} %moment.1), channel_id=1, source_target_pairs={{0,3},{1,2},{2,1},{3,0},{4,7},{5,6},{6,5},{7,4},{8,11},{9,10},{10,... | collective-permute-start | bytes 24584 | tf_op jit(solution)/shard_map/ppermute | solution.py:166
  74.2 3.7 %collective-permute-start.41 = (f32[32,64]{1,0:T(8,128)S(1)}, f32[32,64]{1,0:T(8,128)S(1)}, u32[]{:S(2)}, u32[]{:S(2)}) collective-permute-start(f32[32,64]{1,0:T(8,128)S(1)} %moment.1), channel_id=1, source_target_pairs={{0,2},{1,3},{2,0},{3,1},{4,6},{5,7},{6,4},{7,5},{8,10},{9,11},{10,... | collective-permute-start | bytes 24584 | tf_op jit(solution)/shard_map/ppermute | solution.py:166
  75.1 3.7 %collective-permute-start.40 = (f32[32,64]{1,0:T(8,128)S(1)}, f32[32,64]{1,0:T(8,128)S(1)}, u32[]{:S(2)}, u32[]{:S(2)}) collective-permute-start(f32[32,64]{1,0:T(8,128)S(1)} %moment.1), channel_id=1, source_target_pairs={{0,1},{1,0},{2,3},{3,2},{4,5},{5,4},{6,7},{7,6},{8,9},{9,8},{10,11... | collective-permute-start | bytes 24584 | tf_op jit(solution)/shard_map/ppermute | solution.py:166
  78.9 6.1 %collective-permute-start.45 = (f32[32,64]{1,0:T(8,128)S(1)}, f32[32,64]{1,0:T(8,128)S(1)}, u32[]{:S(2)}, u32[]{:S(2)}) collective-permute-start(f32[32,64]{1,0:T(8,128)S(1)} %add_add_fusion.1.sums), channel_id=1, source_target_pairs={{0,24},{4,28},{8,16},{12,20},{16,8},{20,12},{24,0},{28,4},{1,25},{... | collective-permute-start | bytes 24584 | tf_op jit(solution)/shard_map/ppermute | solution.py:166
  80.9 4.6 %collective-permute-start.44 = (f32[32,64]{1,0:T(8,128)S(1)}, f32[32,64]{1,0:T(8,128)S(1)}, u32[]{:S(2)}, u32[]{:S(2)}) collective-permute-start(f32[32,64]{1,0:T(8,128)S(1)} %add_add_fusion.1.sums), channel_id=1, source_target_pairs={{0,16},{4,20},{8,24},{12,28},{16,0},{20,4},{24,8},{28,12},{1,17},{... | collective-permute-start | bytes 24584 | tf_op jit(solution)/shard_map/ppermute | solution.py:166
  81.5 4.0 %collective-permute-start.43 = (f32[32,64]{1,0:T(8,128)S(1)}, f32[32,64]{1,0:T(8,128)S(1)}, u32[]{:S(2)}, u32[]{:S(2)}) collective-permute-start(f32[32,64]{1,0:T(8,128)S(1)} %add_add_fusion.1.sums), channel_id=1, source_target_pairs={{0,8},{4,12},{8,0},{12,4},{16,24},{20,28},{24,16},{28,20},{1,9},{5... | collective-permute-start | bytes 24584 | tf_op jit(solution)/shard_map/ppermute | solution.py:166
  85.5 1.2 %collective-permute-start.46 = (f32[32,64]{1,0:T(8,128)S(1)}, f32[32,64]{1,0:T(8,128)S(1)}, u32[]{:S(2)}, u32[]{:S(2)}) collective-permute-start(f32[32,64]{1,0:T(8,128)S(1)} %add_add_fusion), channel_id=1, source_target_pairs={{0,4},{4,0},{8,12},{12,8},{16,20},{20,16},{24,28},{28,24},{1,5},{5... | collective-permute-start | bytes 24584 | tf_op jit(solution)/shard_map/ppermute | solution.py:166
  (3 other events, 29.7 us)

commit v5 on v4

--- a/solution.py
+++ b/solution.py
@@ -177,7 +177,11 @@
         return parts if behind is None else (parts, behind)
 
     def gather_col(value):
-        return [swap(value, "col", n_col, distance) for distance in range(1, n_col)]
+        held, distance = [value], 1
+        while distance < n_col:
+            held = held + [swap(part, "col", n_col, distance) for part in held]
+            distance *= 2
+        return held[1:]
 
     def vmem(count):
         return [pl.BlockSpec(memory_space=pltpu.VMEM)] * count

time: 88.1 us -> 87.4 us (level)
  starting transfers between devices: 43.6 us -> 42.4 us
    ppermute x47, starting transfers between devices: 43.6 us -> 42.4 us  [swap(): return lax.ppermute(value, axis, [(i, i ^ distance) for i in range(size)])]
  transfers between devices with their start and end apart: 47 -> 47, of which waited for: 28 -> 30; matrix products, arithmetic and copies ran while one was open for 0% -> 0% of each run, Pallas kernels for 7% -> 7%
where the time goes in v5:
time: 87.4 us; the launch traced here: 87.2 us
  starting transfers between devices  42.4 us (49%)
  waiting for transfers between devices  29.5 us (34%)
  Pallas kernels  13.8 us (16%)
  between operations  1.44 us (2%)
    ppermute x47, starting transfers between devices, swap(): return lax.ppermute(value, axis, [(i, i ^ distance) for i in range(size)])  42.4 us
    ppermute x47, waiting for transfers between devices, swap(): return lax.ppermute(value, axis, [(i, i ^ distance) for i in range(size)])  29.5 us
    pallas_call x4, Pallas kernels, products(): pl.pallas_call(functools.partial(product_kernel, n_row, n_col), out_shape...  5.72 us
    pallas_call x1, Pallas kernels, body(): pl.pallas_call(stage_kernel, out_shape=[jax.ShapeDtypeStruct(tiles.shape,...  4.5 us
  transfers between devices with their start and end apart: 47, of which 30 were waited for; matrix products, arithmetic and copies ran while one was open for 0% of the time, Pallas kernels for 7%

profile of v5, /device:TPU:0, one launch (start us, length us, event | category | flops | bytes accessed | tf_op | source)
XLA Modules:
  0.0 87.2 jit_solution(2832296501879770210)
XLA Ops:
  0.7 5.1 %collective-permute-start.2 = (f32[32,512]{1,0:T(8,128)}, f32[32,512]{1,0:T(8,128)S(1)}, u32[]{:S(2)}, u32[]{:S(2)}) collective-permute-start(f32[32,512]{1,0:T(8,128)} %refs_0_.1), channel_id=1, source_target_pairs={{0,24},{4,28},{8,16},{12,20},{16,8},{20,12},{24,0},{28,4},{1,25},{... | collective-permute-start | bytes 196616 | tf_op jit(solution)/shard_map/ppermute | solution.py:166
  5.8 0.6 collective-permute-start
  6.4 4.5 %stage.1 = (bf16[32,256,256]{2,1,0:T(8,128)(2,1)S(1)}, bf16[32,256,256]{2,1,0:T(8,128)(2,1)S(1)}) custom-call(f32[32,256,256]{2,1,0:T(8,128)} %tiles.1), custom_call_target="tpu_custom_call" | custom-call | tf_op jit(solution)/shard_map/stage/pallas_call | solution.py:195
  10.9 0.6 collective-permute-done.1.refs_4_
  13.4 1.4 %tile_products.4 = (f32[32,512]{1,0:T(8,128)S(1)}, f32[32,512]{1,0:T(8,128)S(1)}, f32[32,512]{1,0:T(8,128)S(1)}, f32[32,512]{1,0:T(8,128)S(1)}) custom-call(s32[2,32]{1,0:T(2,128)S(1)} %places.1.slots, bf16[32,256,256]{2,1,0:T(8,128)(2,1)S(1)} %get-tuple-element.41.high, bf16[32,256,256]{2,1,0:T(8,128)(2,1)S(1)} %get-tuple-element.42.low, ...), custom_call_target="tpu_custom_call" | custom-call | tf_op jit(solution)/shard_map/tile_products/pallas_call | solution.py:220
  14.8 2.5 %collective-permute-start.7 = (f32[32,512]{1,0:T(8,128)S(1)}, f32[32,512]{1,0:T(8,128)S(1)}, u32[]{:S(2)}, u32[]{:S(2)}) collective-permute-start(f32[32,512]{1,0:T(8,128)S(1)} %get-tuple-element.47), channel_id=1, source_target_pairs={{0,3},{1,2},{2,1},{3,0},{4,7},{5,6},{6,5},{7,4},{8,11},{9,10},{10,... | collective-permute-start | bytes 196616 | tf_op jit(solution)/shard_map/ppermute | solution.py:166
  18.4 1.7 %collective-permute-done.7 = f32[32,512]{1,0:T(8,128)S(1)} collective-permute-done((f32[32,512]{1,0:T(8,128)S(1)}, f32[32,512]{1,0:T(8,128)S(1)}, u32[]{:S(2)}, u32[]{:S(2)}) %collective-permute-start.7) | collective-permute-done | bytes 65568 | tf_op jit(solution)/shard_map/ppermute | solution.py:166
  20.1 1.5 %collective-permute-done.8 = f32[32,512]{1,0:T(8,128)S(1)} collective-permute-done((f32[32,512]{1,0:T(8,128)S(1)}, f32[32,512]{1,0:T(8,128)S(1)}, u32[]{:S(2)}, u32[]{:S(2)}) %collective-permute-start.8) | collective-permute-done | bytes 65568 | tf_op jit(solution)/shard_map/ppermute | solution.py:166
  22.1 3.4 %collective-permute-start.15 = (f32[32,512]{1,0:T(8,128)S(1)}, f32[32,512]{1,0:T(8,128)S(1)}, u32[]{:S(2)}, u32[]{:S(2)}) collective-permute-start(f32[32,512]{1,0:T(8,128)S(1)} %get-tuple-element.72.refs_0_), channel_id=1, source_target_pairs={{0,24},{4,28},{8,16},{12,20},{16,8},{20,12},{24,0},{28,4},{1,25},{... | collective-permute-start | bytes 196616 | tf_op jit(solution)/shard_map/ppermute | solution.py:166
  25.5 1.1 %collective-permute-start.11 = (f32[32,512]{1,0:T(8,128)S(1)}, f32[32,512]{1,0:T(8,128)S(1)}, u32[]{:S(2)}, u32[]{:S(2)}) collective-permute-start(f32[32,512]{1,0:T(8,128)S(1)} %get-tuple-element.72.refs_0_), channel_id=1, source_target_pairs={{0,8},{4,12},{8,0},{12,4},{16,24},{20,28},{24,16},{28,20},{1,9},{5... | collective-permute-start | bytes 196616 | tf_op jit(solution)/shard_map/ppermute | solution.py:166
  26.6 1.8 %collective-permute-done.15.refs_6_ = f32[32,512]{1,0:T(8,128)S(1)} collective-permute-done((f32[32,512]{1,0:T(8,128)S(1)}, f32[32,512]{1,0:T(8,128)S(1)}, u32[]{:S(2)}, u32[]{:S(2)}) %collective-permute-start.15) | collective-permute-done | bytes 65568 | tf_op jit(solution)/shard_map/ppermute | solution.py:166
  28.4 2.4 %collective-permute-done.13.refs_4_ = f32[32,512]{1,0:T(8,128)S(1)} collective-permute-done((f32[32,512]{1,0:T(8,128)S(1)}, f32[32,512]{1,0:T(8,128)S(1)}, u32[]{:S(2)}, u32[]{:S(2)}) %collective-permute-start.13) | collective-permute-done | bytes 65568 | tf_op jit(solution)/shard_map/ppermute | solution.py:166
  31.3 0.7 collective-permute-done.14.refs_5_
  32.2 1.4 %tile_products.5 = (f32[32,512]{1,0:T(8,128)S(1)}, f32[32,512]{1,0:T(8,128)S(1)}, f32[32,512]{1,0:T(8,128)S(1)}, f32[32,512]{1,0:T(8,128)S(1)}) custom-call(s32[2,32]{1,0:T(2,128)S(1)} %places.1.slots, bf16[32,256,256]{2,1,0:T(8,128)(2,1)S(1)} %get-tuple-element.41.high, bf16[32,256,256]{2,1,0:T(8,128)(2,1)S(1)} %get-tuple-element.42.low, ...), custom_call_target="tpu_custom_call" | custom-call | tf_op jit(solution)/shard_map/tile_products/pallas_call | solution.py:220
  33.6 1.6 %collective-permute-start.17 = (f32[32,512]{1,0:T(8,128)S(1)}, f32[32,512]{1,0:T(8,128)S(1)}, u32[]{:S(2)}, u32[]{:S(2)}) collective-permute-start(f32[32,512]{1,0:T(8,128)S(1)} %get-tuple-element.51), channel_id=1, source_target_pairs={{0,3},{1,2},{2,1},{3,0},{4,7},{5,6},{6,5},{7,4},{8,11},{9,10},{10,... | collective-permute-start | bytes 196616 | tf_op jit(solution)/shard_map/ppermute | solution.py:166
  35.2 1.4 %collective-permute-start.18 = (f32[32,512]{1,0:T(8,128)S(1)}, f32[32,512]{1,0:T(8,128)S(1)}, u32[]{:S(2)}, u32[]{:S(2)}) collective-permute-start(f32[32,512]{1,0:T(8,128)S(1)} %get-tuple-element.52), channel_id=1, source_target_pairs={{0,2},{1,3},{2,0},{3,1},{4,6},{5,7},{6,4},{7,5},{8,10},{9,11},{10,... | collective-permute-start | bytes 196616 | tf_op jit(solution)/shard_map/ppermute | solution.py:166
  36.5 0.6 collective-permute-start.19
  37.2 1.9 %collective-permute-done.17 = f32[32,512]{1,0:T(8,128)S(1)} collective-permute-done((f32[32,512]{1,0:T(8,128)S(1)}, f32[32,512]{1,0:T(8,128)S(1)}, u32[]{:S(2)}, u32[]{:S(2)}) %collective-permute-start.17) | collective-permute-done | bytes 65568 | tf_op jit(solution)/shard_map/ppermute | solution.py:166
  39.0 1.3 %collective-permute-done.18 = f32[32,512]{1,0:T(8,128)S(1)} collective-permute-done((f32[32,512]{1,0:T(8,128)S(1)}, f32[32,512]{1,0:T(8,128)S(1)}, u32[]{:S(2)}, u32[]{:S(2)}) %collective-permute-start.18) | collective-permute-done | bytes 65568 | tf_op jit(solution)/shard_map/ppermute | solution.py:166
  40.8 2.3 %collective-permute-start.25 = (f32[32,512]{1,0:T(8,128)S(1)}, f32[32,512]{1,0:T(8,128)S(1)}, u32[]{:S(2)}, u32[]{:S(2)}) collective-permute-start(f32[32,512]{1,0:T(8,128)S(1)} %multiply_subtract_fusion.1.refs_0_), channel_id=1, source_target_pairs={{0,24},{4,28},{8,16},{12,20},{16,8},{20,12},{24,0},{28,4},{1,25},{... | collective-permute-start | bytes 196616 | tf_op jit(solution)/shard_map/ppermute | solution.py:166
  43.4 1.9 %collective-permute-start.21 = (f32[32,512]{1,0:T(8,128)S(1)}, f32[32,512]{1,0:T(8,128)S(1)}, u32[]{:S(2)}, u32[]{:S(2)}) collective-permute-start(f32[32,512]{1,0:T(8,128)S(1)} %multiply_subtract_fusion.1.refs_0_), channel_id=1, source_target_pairs={{0,8},{4,12},{8,0},{12,4},{16,24},{20,28},{24,16},{28,20},{1,9},{5... | collective-permute-start | bytes 196616 | tf_op jit(solution)/shard_map/ppermute | solution.py:166
  45.3 1.7 %collective-permute-done.25.refs_6_ = f32[32,512]{1,0:T(8,128)S(1)} collective-permute-done((f32[32,512]{1,0:T(8,128)S(1)}, f32[32,512]{1,0:T(8,128)S(1)}, u32[]{:S(2)}, u32[]{:S(2)}) %collective-permute-start.25) | collective-permute-done | bytes 65568 | tf_op jit(solution)/shard_map/ppermute | solution.py:166
  47.1 2.7 %collective-permute-done.23.refs_4_ = f32[32,512]{1,0:T(8,128)S(1)} collective-permute-done((f32[32,512]{1,0:T(8,128)S(1)}, f32[32,512]{1,0:T(8,128)S(1)}, u32[]{:S(2)}, u32[]{:S(2)}) %collective-permute-start.23) | collective-permute-done | bytes 65568 | tf_op jit(solution)/shard_map/ppermute | solution.py:166
  50.3 0.7 collective-permute-done.24.refs_5_
  51.2 1.4 %tile_products.6 = (f32[32,512]{1,0:T(8,128)S(1)}, f32[32,512]{1,0:T(8,128)S(1)}, f32[32,512]{1,0:T(8,128)S(1)}, f32[32,512]{1,0:T(8,128)S(1)}) custom-call(s32[2,32]{1,0:T(2,128)S(1)} %places.1.slots, bf16[32,256,256]{2,1,0:T(8,128)(2,1)S(1)} %get-tuple-element.41.high, bf16[32,256,256]{2,1,0:T(8,128)(2,1)S(1)} %get-tuple-element.42.low, ...), custom_call_target="tpu_custom_call" | custom-call | tf_op jit(solution)/shard_map/tile_products/pallas_call | solution.py:220
  52.6 1.6 %collective-permute-start.27 = (f32[32,512]{1,0:T(8,128)S(1)}, f32[32,512]{1,0:T(8,128)S(1)}, u32[]{:S(2)}, u32[]{:S(2)}) collective-permute-start(f32[32,512]{1,0:T(8,128)S(1)} %get-tuple-element.55), channel_id=1, source_target_pairs={{0,3},{1,2},{2,1},{3,0},{4,7},{5,6},{6,5},{7,4},{8,11},{9,10},{10,... | collective-permute-start | bytes 196616 | tf_op jit(solution)/shard_map/ppermute | solution.py:166
  54.2 0.8 collective-permute-start.28
  54.9 1.2 %collective-permute-start.29 = (f32[32,512]{1,0:T(8,128)S(1)}, f32[32,512]{1,0:T(8,128)S(1)}, u32[]{:S(2)}, u32[]{:S(2)}) collective-permute-start(f32[32,512]{1,0:T(8,128)S(1)} %get-tuple-element.57), channel_id=1, source_target_pairs={{0,1},{1,0},{2,3},{3,2},{4,5},{5,4},{6,7},{7,6},{8,9},{9,8},{10,11... | collective-permute-start | bytes 196616 | tf_op jit(solution)/shard_map/ppermute | solution.py:166
  56.2 1.9 %collective-permute-done.27 = f32[32,512]{1,0:T(8,128)S(1)} collective-permute-done((f32[32,512]{1,0:T(8,128)S(1)}, f32[32,512]{1,0:T(8,128)S(1)}, u32[]{:S(2)}, u32[]{:S(2)}) %collective-permute-start.27) | collective-permute-done | bytes 65568 | tf_op jit(solution)/shard_map/ppermute | solution.py:166
  58.0 1.3 %collective-permute-done.28 = f32[32,512]{1,0:T(8,128)S(1)} collective-permute-done((f32[32,512]{1,0:T(8,128)S(1)}, f32[32,512]{1,0:T(8,128)S(1)}, u32[]{:S(2)}, u32[]{:S(2)}) %collective-permute-start.28) | collective-permute-done | bytes 65568 | tf_op jit(solution)/shard_map/ppermute | solution.py:166
  59.4 1.2 %collective-permute-start.34 = (f32[32,512]{1,0:T(8,128)S(1)}, f32[32,512]{1,0:T(8,128)S(1)}, u32[]{:S(2)}, u32[]{:S(2)}) collective-permute-start(f32[32,512]{1,0:T(8,128)S(1)} %multiply_subtract_fusion.refs_0_.filtered), channel_id=1, source_target_pairs={{0,1},{1,0},{2,3},{3,2},{4,5},{5,4},{6,7},{7,6},{8,9},{9,8},{10,11... | collective-permute-start | bytes 196616 | tf_op jit(solution)/shard_map/ppermute | solution.py:166
  61.0 2.0 %collective-permute-start.38 = (f32[32,512]{1,0:T(8,128)S(1)}, f32[32,512]{1,0:T(8,128)S(1)}, u32[]{:S(2)}, u32[]{:S(2)}) collective-permute-start(f32[32,512]{1,0:T(8,128)S(1)} %multiply_subtract_fusion.refs_0_.filtered), channel_id=1, source_target_pairs={{0,24},{4,28},{8,16},{12,20},{16,8},{20,12},{24,0},{28,4},{1,25},{... | collective-permute-start | bytes 196616 | tf_op jit(solution)/shard_map/ppermute | solution.py:166
  63.0 0.8 collective-permute-start.35
  63.8 1.2 %collective-permute-start.31 = (f32[32,512]{1,0:T(8,128)S(1)}, f32[32,512]{1,0:T(8,128)S(1)}, u32[]{:S(2)}, u32[]{:S(2)}) collective-permute-start(f32[32,512]{1,0:T(8,128)S(1)} %multiply_subtract_fusion.refs_0_.filtered), channel_id=1, source_target_pairs={{0,8},{4,12},{8,0},{12,4},{16,24},{20,28},{24,16},{28,20},{1,9},{5... | collective-permute-start | bytes 196616 | tf_op jit(solution)/shard_map/ppermute | solution.py:166
  65.0 1.1 %collective-permute-start.36 = (f32[32,512]{1,0:T(8,128)S(1)}, f32[32,512]{1,0:T(8,128)S(1)}, u32[]{:S(2)}, u32[]{:S(2)}) collective-permute-start(f32[32,512]{1,0:T(8,128)S(1)} %collective-permute-done.34.refs_8_), channel_id=1, source_target_pairs={{0,2},{1,3},{2,0},{3,1},{4,6},{5,7},{6,4},{7,5},{8,10},{9,11},{10,... | collective-permute-start | bytes 196616 | tf_op jit(solution)/shard_map/ppermute | solution.py:166
  66.1 1.9 %collective-permute-done.33.refs_4_ = f32[32,512]{1,0:T(8,128)S(1)} collective-permute-done((f32[32,512]{1,0:T(8,128)S(1)}, f32[32,512]{1,0:T(8,128)S(1)}, u32[]{:S(2)}, u32[]{:S(2)}) %collective-permute-start.33) | collective-permute-done | bytes 65568 | tf_op jit(solution)/shard_map/ppermute | solution.py:166
  69.9 1.4 %tile_products.7 = (f32[32,512]{1,0:T(8,128)S(1)}, f32[32,512]{1,0:T(8,128)S(1)}, f32[32,512]{1,0:T(8,128)S(1)}, f32[32,512]{1,0:T(8,128)S(1)}) custom-call(s32[2,32]{1,0:T(2,128)S(1)} %places.1.slots, bf16[32,256,256]{2,1,0:T(8,128)(2,1)S(1)} %get-tuple-element.41.high, bf16[32,256,256]{2,1,0:T(8,128)(2,1)S(1)} %get-tuple-element.42.low, ...), custom_call_target="tpu_custom_call" | custom-call | tf_op jit(solution)/shard_map/tile_products/pallas_call | solution.py:220
  71.9 1.5 %collective-permute-start.42 = (f32[32,64]{1,0:T(8,128)S(1)}, f32[32,64]{1,0:T(8,128)S(1)}, u32[]{:S(2)}, u32[]{:S(2)}) collective-permute-start(f32[32,64]{1,0:T(8,128)S(1)} %moment.1), channel_id=1, source_target_pairs={{0,3},{1,2},{2,1},{3,0},{4,7},{5,6},{6,5},{7,4},{8,11},{9,10},{10,... | collective-permute-start | bytes 24584 | tf_op jit(solution)/shard_map/ppermute | solution.py:166
  73.4 1.0 %collective-permute-start.41 = (f32[32,64]{1,0:T(8,128)S(1)}, f32[32,64]{1,0:T(8,128)S(1)}, u32[]{:S(2)}, u32[]{:S(2)}) collective-permute-start(f32[32,64]{1,0:T(8,128)S(1)} %moment.1), channel_id=1, source_target_pairs={{0,2},{1,3},{2,0},{3,1},{4,6},{5,7},{6,4},{7,5},{8,10},{9,11},{10,... | collective-permute-start | bytes 24584 | tf_op jit(solution)/shard_map/ppermute | solution.py:166
  74.3 1.1 %collective-permute-start.40 = (f32[32,64]{1,0:T(8,128)S(1)}, f32[32,64]{1,0:T(8,128)S(1)}, u32[]{:S(2)}, u32[]{:S(2)}) collective-permute-start(f32[32,64]{1,0:T(8,128)S(1)} %moment.1), channel_id=1, source_target_pairs={{0,1},{1,0},{2,3},{3,2},{4,5},{5,4},{6,7},{7,6},{8,9},{9,8},{10,11... | collective-permute-start | bytes 24584 | tf_op jit(solution)/shard_map/ppermute | solution.py:166
  75.4 1.1 %collective-permute-done.42 = f32[32,64]{1,0:T(8,128)S(1)} collective-permute-done((f32[32,64]{1,0:T(8,128)S(1)}, f32[32,64]{1,0:T(8,128)S(1)}, u32[]{:S(2)}, u32[]{:S(2)}) %collective-permute-start.42) | collective-permute-done | bytes 8224 | tf_op jit(solution)/shard_map/ppermute | solution.py:166
  77.1 1.0 %collective-permute-done.40 = f32[32,64]{1,0:T(8,128)S(1)} collective-permute-done((f32[32,64]{1,0:T(8,128)S(1)}, f32[32,64]{1,0:T(8,128)S(1)}, u32[]{:S(2)}, u32[]{:S(2)}) %collective-permute-start.40) | collective-permute-done | bytes 8224 | tf_op jit(solution)/shard_map/ppermute | solution.py:166
  78.1 2.0 %collective-permute-start.45 = (f32[32,64]{1,0:T(8,128)S(1)}, f32[32,64]{1,0:T(8,128)S(1)}, u32[]{:S(2)}, u32[]{:S(2)}) collective-permute-start(f32[32,64]{1,0:T(8,128)S(1)} %add_add_fusion.1.sums), channel_id=1, source_target_pairs={{0,24},{4,28},{8,16},{12,20},{16,8},{20,12},{24,0},{28,4},{1,25},{... | collective-permute-start | bytes 24584 | tf_op jit(solution)/shard_map/ppermute | solution.py:166
  80.7 1.8 %collective-permute-start.43 = (f32[32,64]{1,0:T(8,128)S(1)}, f32[32,64]{1,0:T(8,128)S(1)}, u32[]{:S(2)}, u32[]{:S(2)}) collective-permute-start(f32[32,64]{1,0:T(8,128)S(1)} %add_add_fusion.1.sums), channel_id=1, source_target_pairs={{0,8},{4,12},{8,0},{12,4},{16,24},{20,28},{24,16},{28,20},{1,9},{5... | collective-permute-start | bytes 24584 | tf_op jit(solution)/shard_map/ppermute | solution.py:166
  82.5 1.7 %factor.1 = (f32[32,32]{1,0:T(8,128)S(1)}, f32[32,512]{1,0:T(8,128)}) custom-call(f32[32,64]{1,0:T(8,128)S(1)} %add_add_fusion.1.sums, f32[32,512]{1,0:T(8,128)S(1)} %multiply_subtract_fusion.refs_0_.filtered), custom_call_target="tpu_custom_call" | custom-call | tf_op jit(solution)/shard_map/factor/pallas_call | solution.py:261
  84.2 0.6 collective-permute-done.44
  84.9 1.2 %collective-permute-done.46 = f32[32,64]{1,0:T(8,128)S(1)} collective-permute-done((f32[32,64]{1,0:T(8,128)S(1)}, f32[32,64]{1,0:T(8,128)S(1)}, u32[]{:S(2)}, u32[]{:S(2)}) %collective-permute-start.46) | collective-permute-done | bytes 8224 | tf_op jit(solution)/shard_map/ppermute | solution.py:166
  86.0 1.2 %project.1 = f32[32,32]{1,0:T(8,128)} custom-call(f32[32,64]{1,0:T(8,128)S(1)} %add.65.sums, f32[32,32]{1,0:T(8,128)S(1)} %get-tuple-element.71.inverse), custom_call_target="tpu_custom_call" | custom-call | tf_op jit(solution)/shard_map/project/pallas_call | solution.py:273
  (70 shorter events, 8.9 us)
Async XLA Ops:
  0.6 12.7 %copy-start = (f32[32,512]{1,0:T(8,128)S(1)}, f32[32,512]{1,0:T(8,128)}, u32[]{:S(2)}) copy-start(f32[32,512]{1,0:T(8,128)} %refs_0_.1) | copy-start | bytes 196612
  0.7 10.3 %collective-permute-start.2 = (f32[32,512]{1,0:T(8,128)}, f32[32,512]{1,0:T(8,128)S(1)}, u32[]{:S(2)}, u32[]{:S(2)}) collective-permute-start(f32[32,512]{1,0:T(8,128)} %refs_0_.1), channel_id=1, source_target_pairs={{0,24},{4,28},{8,16},{12,20},{16,8},{20,12},{24,0},{28,4},{1,25},{... | collective-permute-start | bytes 196616 | tf_op jit(solution)/shard_map/ppermute | solution.py:166
  5.8 5.8 %collective-permute-start.1 = (f32[32,512]{1,0:T(8,128)}, f32[32,512]{1,0:T(8,128)S(1)}, u32[]{:S(2)}, u32[]{:S(2)}) collective-permute-start(f32[32,512]{1,0:T(8,128)} %refs_0_.1), channel_id=1, source_target_pairs={{0,16},{4,20},{8,24},{12,28},{16,0},{20,4},{24,8},{28,12},{1,17},{... | collective-permute-start | bytes 196616 | tf_op jit(solution)/shard_map/ppermute | solution.py:166
  5.8 5.8 %collective-permute-start = (f32[32,512]{1,0:T(8,128)}, f32[32,512]{1,0:T(8,128)S(1)}, u32[]{:S(2)}, u32[]{:S(2)}) collective-permute-start(f32[32,512]{1,0:T(8,128)} %refs_0_.1), channel_id=1, source_target_pairs={{0,8},{4,12},{8,0},{12,4},{16,24},{20,28},{24,16},{28,20},{1,9},{5... | collective-permute-start | bytes 196616 | tf_op jit(solution)/shard_map/ppermute | solution.py:166
  6.4 6.4 %collective-permute-start.3 = (f32[32,512]{1,0:T(8,128)}, f32[32,512]{1,0:T(8,128)S(1)}, u32[]{:S(2)}, u32[]{:S(2)}) collective-permute-start(f32[32,512]{1,0:T(8,128)} %refs_0_.1), channel_id=1, source_target_pairs={{0,4},{4,0},{8,12},{12,8},{16,20},{20,16},{24,28},{28,24},{1,5},{5... | collective-permute-start | bytes 196616 | tf_op jit(solution)/shard_map/ppermute | solution.py:166
  11.6 1.3 %collective-permute-start.4 = (f32[32,512]{1,0:T(8,128)S(1)}, f32[32,512]{1,0:T(8,128)S(1)}, u32[]{:S(2)}, u32[]{:S(2)}) collective-permute-start(f32[32,512]{1,0:T(8,128)S(1)} %collective-permute-done.refs_2_), channel_id=1, source_target_pairs={{0,4},{4,0},{8,12},{12,8},{16,20},{20,16},{24,28},{28,24},{1,5},{5... | collective-permute-start | bytes 196616 | tf_op jit(solution)/shard_map/ppermute | solution.py:166
  11.6 1.4 %collective-permute-start.5 = (f32[32,512]{1,0:T(8,128)S(1)}, f32[32,512]{1,0:T(8,128)S(1)}, u32[]{:S(2)}, u32[]{:S(2)}) collective-permute-start(f32[32,512]{1,0:T(8,128)S(1)} %collective-permute-done.1.refs_4_), channel_id=1, source_target_pairs={{0,4},{4,0},{8,12},{12,8},{16,20},{20,16},{24,28},{28,24},{1,5},{5... | collective-permute-start | bytes 196616 | tf_op jit(solution)/shard_map/ppermute | solution.py:166
  12.1 1.3 %collective-permute-start.6 = (f32[32,512]{1,0:T(8,128)S(1)}, f32[32,512]{1,0:T(8,128)S(1)}, u32[]{:S(2)}, u32[]{:S(2)}) collective-permute-start(f32[32,512]{1,0:T(8,128)S(1)} %collective-permute-done.2.refs_6_), channel_id=1, source_target_pairs={{0,4},{4,0},{8,12},{12,8},{16,20},{20,16},{24,28},{28,24},{1,5},{5... | collective-permute-start | bytes 196616 | tf_op jit(solution)/shard_map/ppermute | solution.py:166
  14.8 5.3 %collective-permute-start.7 = (f32[32,512]{1,0:T(8,128)S(1)}, f32[32,512]{1,0:T(8,128)S(1)}, u32[]{:S(2)}, u32[]{:S(2)}) collective-permute-start(f32[32,512]{1,0:T(8,128)S(1)} %get-tuple-element.47), channel_id=1, source_target_pairs={{0,3},{1,2},{2,1},{3,0},{4,7},{5,6},{6,5},{7,4},{8,11},{9,10},{10,... | collective-permute-start | bytes 196616 | tf_op jit(solution)/shard_map/ppermute | solution.py:166
  17.3 4.3 %collective-permute-start.8 = (f32[32,512]{1,0:T(8,128)S(1)}, f32[32,512]{1,0:T(8,128)S(1)}, u32[]{:S(2)}, u32[]{:S(2)}) collective-permute-start(f32[32,512]{1,0:T(8,128)S(1)} %get-tuple-element.48), channel_id=1, source_target_pairs={{0,2},{1,3},{2,0},{3,1},{4,6},{5,7},{6,4},{7,5},{8,10},{9,11},{10,... | collective-permute-start | bytes 196616 | tf_op jit(solution)/shard_map/ppermute | solution.py:166
  17.8 4.3 %collective-permute-start.9 = (f32[32,512]{1,0:T(8,128)S(1)}, f32[32,512]{1,0:T(8,128)S(1)}, u32[]{:S(2)}, u32[]{:S(2)}) collective-permute-start(f32[32,512]{1,0:T(8,128)S(1)} %get-tuple-element.49), channel_id=1, source_target_pairs={{0,1},{1,0},{2,3},{3,2},{4,5},{5,4},{6,7},{7,6},{8,9},{9,8},{10,11... | collective-permute-start | bytes 196616 | tf_op jit(solution)/shard_map/ppermute | solution.py:166
  22.1 6.2 %collective-permute-start.15 = (f32[32,512]{1,0:T(8,128)S(1)}, f32[32,512]{1,0:T(8,128)S(1)}, u32[]{:S(2)}, u32[]{:S(2)}) collective-permute-start(f32[32,512]{1,0:T(8,128)S(1)} %get-tuple-element.72.refs_0_), channel_id=1, source_target_pairs={{0,24},{4,28},{8,16},{12,20},{16,8},{20,12},{24,0},{28,4},{1,25},{... | collective-permute-start | bytes 196616 | tf_op jit(solution)/shard_map/ppermute | solution.py:166
  25.5 5.2 %collective-permute-start.13 = (f32[32,512]{1,0:T(8,128)S(1)}, f32[32,512]{1,0:T(8,128)S(1)}, u32[]{:S(2)}, u32[]{:S(2)}) collective-permute-start(f32[32,512]{1,0:T(8,128)S(1)} %get-tuple-element.72.refs_0_), channel_id=1, source_target_pairs={{0,16},{4,20},{8,24},{12,28},{16,0},{20,4},{24,8},{28,12},{1,17},{... | collective-permute-start | bytes 196616 | tf_op jit(solution)/shard_map/ppermute | solution.py:166
  25.5 5.3 %collective-permute-start.11 = (f32[32,512]{1,0:T(8,128)S(1)}, f32[32,512]{1,0:T(8,128)S(1)}, u32[]{:S(2)}, u32[]{:S(2)}) collective-permute-start(f32[32,512]{1,0:T(8,128)S(1)} %get-tuple-element.72.refs_0_), channel_id=1, source_target_pairs={{0,8},{4,12},{8,0},{12,4},{16,24},{20,28},{24,16},{28,20},{1,9},{5... | collective-permute-start | bytes 196616 | tf_op jit(solution)/shard_map/ppermute | solution.py:166
  26.6 4.7 %collective-permute-start.10 = (f32[32,512]{1,0:T(8,128)S(1)}, f32[32,512]{1,0:T(8,128)S(1)}, u32[]{:S(2)}, u32[]{:S(2)}) collective-permute-start(f32[32,512]{1,0:T(8,128)S(1)} %get-tuple-element.72.refs_0_), channel_id=1, source_target_pairs={{0,4},{4,0},{8,12},{12,8},{16,20},{20,16},{24,28},{28,24},{1,5},{5... | collective-permute-start | bytes 196616 | tf_op jit(solution)/shard_map/ppermute | solution.py:166
  28.4 2.9 %collective-permute-start.16 = (f32[32,512]{1,0:T(8,128)S(1)}, f32[32,512]{1,0:T(8,128)S(1)}, u32[]{:S(2)}, u32[]{:S(2)}) collective-permute-start(f32[32,512]{1,0:T(8,128)S(1)} %collective-permute-done.15.refs_6_), channel_id=1, source_target_pairs={{0,4},{4,0},{8,12},{12,8},{16,20},{20,16},{24,28},{28,24},{1,5},{5... | collective-permute-start | bytes 196616 | tf_op jit(solution)/shard_map/ppermute | solution.py:166
  30.7 1.3 %collective-permute-start.14 = (f32[32,512]{1,0:T(8,128)S(1)}, f32[32,512]{1,0:T(8,128)S(1)}, u32[]{:S(2)}, u32[]{:S(2)}) collective-permute-start(f32[32,512]{1,0:T(8,128)S(1)} %collective-permute-done.13.refs_4_), channel_id=1, source_target_pairs={{0,4},{4,0},{8,12},{12,8},{16,20},{20,16},{24,28},{28,24},{1,5},{5... | collective-permute-start | bytes 196616 | tf_op jit(solution)/shard_map/ppermute | solution.py:166
  30.9 1.3 %collective-permute-start.12 = (f32[32,512]{1,0:T(8,128)S(1)}, f32[32,512]{1,0:T(8,128)S(1)}, u32[]{:S(2)}, u32[]{:S(2)}) collective-permute-start(f32[32,512]{1,0:T(8,128)S(1)} %collective-permute-done.11.refs_2_), channel_id=1, source_target_pairs={{0,4},{4,0},{8,12},{12,8},{16,20},{20,16},{24,28},{28,24},{1,5},{5... | collective-permute-start | bytes 196616 | tf_op jit(solution)/shard_map/ppermute | solution.py:166
  33.6 5.4 %collective-permute-start.17 = (f32[32,512]{1,0:T(8,128)S(1)}, f32[32,512]{1,0:T(8,128)S(1)}, u32[]{:S(2)}, u32[]{:S(2)}) collective-permute-start(f32[32,512]{1,0:T(8,128)S(1)} %get-tuple-element.51), channel_id=1, source_target_pairs={{0,3},{1,2},{2,1},{3,0},{4,7},{5,6},{6,5},{7,4},{8,11},{9,10},{10,... | collective-permute-start | bytes 196616 | tf_op jit(solution)/shard_map/ppermute | solution.py:166
  35.2 5.2 %collective-permute-start.18 = (f32[32,512]{1,0:T(8,128)S(1)}, f32[32,512]{1,0:T(8,128)S(1)}, u32[]{:S(2)}, u32[]{:S(2)}) collective-permute-start(f32[32,512]{1,0:T(8,128)S(1)} %get-tuple-element.52), channel_id=1, source_target_pairs={{0,2},{1,3},{2,0},{3,1},{4,6},{5,7},{6,4},{7,5},{8,10},{9,11},{10,... | collective-permute-start | bytes 196616 | tf_op jit(solution)/shard_map/ppermute | solution.py:166
  36.5 4.3 %collective-permute-start.19 = (f32[32,512]{1,0:T(8,128)S(1)}, f32[32,512]{1,0:T(8,128)S(1)}, u32[]{:S(2)}, u32[]{:S(2)}) collective-permute-start(f32[32,512]{1,0:T(8,128)S(1)} %get-tuple-element.53), channel_id=1, source_target_pairs={{0,1},{1,0},{2,3},{3,2},{4,5},{5,4},{6,7},{7,6},{8,9},{9,8},{10,11... | collective-permute-start | bytes 196616 | tf_op jit(solution)/shard_map/ppermute | solution.py:166
  40.8 6.2 %collective-permute-start.25 = (f32[32,512]{1,0:T(8,128)S(1)}, f32[32,512]{1,0:T(8,128)S(1)}, u32[]{:S(2)}, u32[]{:S(2)}) collective-permute-start(f32[32,512]{1,0:T(8,128)S(1)} %multiply_subtract_fusion.1.refs_0_), channel_id=1, source_target_pairs={{0,24},{4,28},{8,16},{12,20},{16,8},{20,12},{24,0},{28,4},{1,25},{... | collective-permute-start | bytes 196616 | tf_op jit(solution)/shard_map/ppermute | solution.py:166
  43.2 6.6 %collective-permute-start.23 = (f32[32,512]{1,0:T(8,128)S(1)}, f32[32,512]{1,0:T(8,128)S(1)}, u32[]{:S(2)}, u32[]{:S(2)}) collective-permute-start(f32[32,512]{1,0:T(8,128)S(1)} %multiply_subtract_fusion.1.refs_0_), channel_id=1, source_target_pairs={{0,16},{4,20},{8,24},{12,28},{16,0},{20,4},{24,8},{28,12},{1,17},{... | collective-permute-start | bytes 196616 | tf_op jit(solution)/shard_map/ppermute | solution.py:166
  43.4 6.4 %collective-permute-start.21 = (f32[32,512]{1,0:T(8,128)S(1)}, f32[32,512]{1,0:T(8,128)S(1)}, u32[]{:S(2)}, u32[]{:S(2)}) collective-permute-start(f32[32,512]{1,0:T(8,128)S(1)} %multiply_subtract_fusion.1.refs_0_), channel_id=1, source_target_pairs={{0,8},{4,12},{8,0},{12,4},{16,24},{20,28},{24,16},{28,20},{1,9},{5... | collective-permute-start | bytes 196616 | tf_op jit(solution)/shard_map/ppermute | solution.py:166
  45.3 5.0 %collective-permute-start.20 = (f32[32,512]{1,0:T(8,128)S(1)}, f32[32,512]{1,0:T(8,128)S(1)}, u32[]{:S(2)}, u32[]{:S(2)}) collective-permute-start(f32[32,512]{1,0:T(8,128)S(1)} %multiply_subtract_fusion.1.refs_0_), channel_id=1, source_target_pairs={{0,4},{4,0},{8,12},{12,8},{16,20},{20,16},{24,28},{28,24},{1,5},{5... | collective-permute-start | bytes 196616 | tf_op jit(solution)/shard_map/ppermute | solution.py:166
  47.1 3.2 %collective-permute-start.26 = (f32[32,512]{1,0:T(8,128)S(1)}, f32[32,512]{1,0:T(8,128)S(1)}, u32[]{:S(2)}, u32[]{:S(2)}) collective-permute-start(f32[32,512]{1,0:T(8,128)S(1)} %collective-permute-done.25.refs_6_), channel_id=1, source_target_pairs={{0,4},{4,0},{8,12},{12,8},{16,20},{20,16},{24,28},{28,24},{1,5},{5... | collective-permute-start | bytes 196616 | tf_op jit(solution)/shard_map/ppermute | solution.py:166
  49.8 1.3 %collective-permute-start.24 = (f32[32,512]{1,0:T(8,128)S(1)}, f32[32,512]{1,0:T(8,128)S(1)}, u32[]{:S(2)}, u32[]{:S(2)}) collective-permute-start(f32[32,512]{1,0:T(8,128)S(1)} %collective-permute-done.23.refs_4_), channel_id=1, source_target_pairs={{0,4},{4,0},{8,12},{12,8},{16,20},{20,16},{24,28},{28,24},{1,5},{5... | collective-permute-start | bytes 196616 | tf_op jit(solution)/shard_map/ppermute | solution.py:166
  49.8 1.4 %collective-permute-start.22 = (f32[32,512]{1,0:T(8,128)S(1)}, f32[32,512]{1,0:T(8,128)S(1)}, u32[]{:S(2)}, u32[]{:S(2)}) collective-permute-start(f32[32,512]{1,0:T(8,128)S(1)} %collective-permute-done.21.refs_2_), channel_id=1, source_target_pairs={{0,4},{4,0},{8,12},{12,8},{16,20},{20,16},{24,28},{28,24},{1,5},{5... | collective-permute-start | bytes 196616 | tf_op jit(solution)/shard_map/ppermute | solution.py:166
  52.6 5.4 %collective-permute-start.27 = (f32[32,512]{1,0:T(8,128)S(1)}, f32[32,512]{1,0:T(8,128)S(1)}, u32[]{:S(2)}, u32[]{:S(2)}) collective-permute-start(f32[32,512]{1,0:T(8,128)S(1)} %get-tuple-element.55), channel_id=1, source_target_pairs={{0,3},{1,2},{2,1},{3,0},{4,7},{5,6},{6,5},{7,4},{8,11},{9,10},{10,... | collective-permute-start | bytes 196616 | tf_op jit(solution)/shard_map/ppermute | solution.py:166
  54.2 5.2 %collective-permute-start.28 = (f32[32,512]{1,0:T(8,128)S(1)}, f32[32,512]{1,0:T(8,128)S(1)}, u32[]{:S(2)}, u32[]{:S(2)}) collective-permute-start(f32[32,512]{1,0:T(8,128)S(1)} %get-tuple-element.56), channel_id=1, source_target_pairs={{0,2},{1,3},{2,0},{3,1},{4,6},{5,7},{6,4},{7,5},{8,10},{9,11},{10,... | collective-permute-start | bytes 196616 | tf_op jit(solution)/shard_map/ppermute | solution.py:166
  54.9 4.4 %collective-permute-start.29 = (f32[32,512]{1,0:T(8,128)S(1)}, f32[32,512]{1,0:T(8,128)S(1)}, u32[]{:S(2)}, u32[]{:S(2)}) collective-permute-start(f32[32,512]{1,0:T(8,128)S(1)} %get-tuple-element.57), channel_id=1, source_target_pairs={{0,1},{1,0},{2,3},{3,2},{4,5},{5,4},{6,7},{7,6},{8,9},{9,8},{10,11... | collective-permute-start | bytes 196616 | tf_op jit(solution)/shard_map/ppermute | solution.py:166
  59.4 5.6 %collective-permute-start.34 = (f32[32,512]{1,0:T(8,128)S(1)}, f32[32,512]{1,0:T(8,128)S(1)}, u32[]{:S(2)}, u32[]{:S(2)}) collective-permute-start(f32[32,512]{1,0:T(8,128)S(1)} %multiply_subtract_fusion.refs_0_.filtered), channel_id=1, source_target_pairs={{0,1},{1,0},{2,3},{3,2},{4,5},{5,4},{6,7},{7,6},{8,9},{9,8},{10,11... | collective-permute-start | bytes 196616 | tf_op jit(solution)/shard_map/ppermute | solution.py:166
  60.5 7.4 %collective-permute-start.33 = (f32[32,512]{1,0:T(8,128)S(1)}, f32[32,512]{1,0:T(8,128)S(1)}, u32[]{:S(2)}, u32[]{:S(2)}) collective-permute-start(f32[32,512]{1,0:T(8,128)S(1)} %multiply_subtract_fusion.refs_0_.filtered), channel_id=1, source_target_pairs={{0,16},{4,20},{8,24},{12,28},{16,0},{20,4},{24,8},{28,12},{1,17},{... | collective-permute-start | bytes 196616 | tf_op jit(solution)/shard_map/ppermute | solution.py:166
  61.0 7.0 %collective-permute-start.38 = (f32[32,512]{1,0:T(8,128)S(1)}, f32[32,512]{1,0:T(8,128)S(1)}, u32[]{:S(2)}, u32[]{:S(2)}) collective-permute-start(f32[32,512]{1,0:T(8,128)S(1)} %multiply_subtract_fusion.refs_0_.filtered), channel_id=1, source_target_pairs={{0,24},{4,28},{8,16},{12,20},{16,8},{20,12},{24,0},{28,4},{1,25},{... | collective-permute-start | bytes 196616 | tf_op jit(solution)/shard_map/ppermute | solution.py:166
  63.0 5.5 %collective-permute-start.35 = (f32[32,512]{1,0:T(8,128)S(1)}, f32[32,512]{1,0:T(8,128)S(1)}, u32[]{:S(2)}, u32[]{:S(2)}) collective-permute-start(f32[32,512]{1,0:T(8,128)S(1)} %multiply_subtract_fusion.refs_0_.filtered), channel_id=1, source_target_pairs={{0,2},{1,3},{2,0},{3,1},{4,6},{5,7},{6,4},{7,5},{8,10},{9,11},{10,... | collective-permute-start | bytes 196616 | tf_op jit(solution)/shard_map/ppermute | solution.py:166
  63.8 4.8 %collective-permute-start.31 = (f32[32,512]{1,0:T(8,128)S(1)}, f32[32,512]{1,0:T(8,128)S(1)}, u32[]{:S(2)}, u32[]{:S(2)}) collective-permute-start(f32[32,512]{1,0:T(8,128)S(1)} %multiply_subtract_fusion.refs_0_.filtered), channel_id=1, source_target_pairs={{0,8},{4,12},{8,0},{12,4},{16,24},{20,28},{24,16},{28,20},{1,9},{5... | collective-permute-start | bytes 196616 | tf_op jit(solution)/shard_map/ppermute | solution.py:166
  65.0 4.3 %collective-permute-start.36 = (f32[32,512]{1,0:T(8,128)S(1)}, f32[32,512]{1,0:T(8,128)S(1)}, u32[]{:S(2)}, u32[]{:S(2)}) collective-permute-start(f32[32,512]{1,0:T(8,128)S(1)} %collective-permute-done.34.refs_8_), channel_id=1, source_target_pairs={{0,2},{1,3},{2,0},{3,1},{4,6},{5,7},{6,4},{7,5},{8,10},{9,11},{10,... | collective-permute-start | bytes 196616 | tf_op jit(solution)/shard_map/ppermute | solution.py:166
  68.0 1.3 %collective-permute-start.37 = (f32[32,512]{1,0:T(8,128)S(1)}, f32[32,512]{1,0:T(8,128)S(1)}, u32[]{:S(2)}, u32[]{:S(2)}) collective-permute-start(f32[32,512]{1,0:T(8,128)S(1)} %collective-permute-done.33.refs_4_), channel_id=1, source_target_pairs={{0,4},{4,0},{8,12},{12,8},{16,20},{20,16},{24,28},{28,24},{1,5},{5... | collective-permute-start | bytes 196616 | tf_op jit(solution)/shard_map/ppermute | solution.py:166
  68.0 1.4 %collective-permute-start.30 = (f32[32,512]{1,0:T(8,128)S(1)}, f32[32,512]{1,0:T(8,128)S(1)}, u32[]{:S(2)}, u32[]{:S(2)}) collective-permute-start(f32[32,512]{1,0:T(8,128)S(1)} %multiply_subtract_fusion.refs_0_.filtered), channel_id=1, source_target_pairs={{0,4},{4,0},{8,12},{12,8},{16,20},{20,16},{24,28},{28,24},{1,5},{5... | collective-permute-start | bytes 196616 | tf_op jit(solution)/shard_map/ppermute | solution.py:166
  68.5 1.3 %collective-permute-start.39 = (f32[32,512]{1,0:T(8,128)S(1)}, f32[32,512]{1,0:T(8,128)S(1)}, u32[]{:S(2)}, u32[]{:S(2)}) collective-permute-start(f32[32,512]{1,0:T(8,128)S(1)} %collective-permute-done.38.refs_6_), channel_id=1, source_target_pairs={{0,4},{4,0},{8,12},{12,8},{16,20},{20,16},{24,28},{28,24},{1,5},{5... | collective-permute-start | bytes 196616 | tf_op jit(solution)/shard_map/ppermute | solution.py:166
  68.6 1.3 %collective-permute-start.32 = (f32[32,512]{1,0:T(8,128)S(1)}, f32[32,512]{1,0:T(8,128)S(1)}, u32[]{:S(2)}, u32[]{:S(2)}) collective-permute-start(f32[32,512]{1,0:T(8,128)S(1)} %collective-permute-done.31.refs_2_), channel_id=1, source_target_pairs={{0,4},{4,0},{8,12},{12,8},{16,20},{20,16},{24,28},{28,24},{1,5},{5... | collective-permute-start | bytes 196616 | tf_op jit(solution)/shard_map/ppermute | solution.py:166
  71.9 4.7 %collective-permute-start.42 = (f32[32,64]{1,0:T(8,128)S(1)}, f32[32,64]{1,0:T(8,128)S(1)}, u32[]{:S(2)}, u32[]{:S(2)}) collective-permute-start(f32[32,64]{1,0:T(8,128)S(1)} %moment.1), channel_id=1, source_target_pairs={{0,3},{1,2},{2,1},{3,0},{4,7},{5,6},{6,5},{7,4},{8,11},{9,10},{10,... | collective-permute-start | bytes 24584 | tf_op jit(solution)/shard_map/ppermute | solution.py:166
  73.4 3.7 %collective-permute-start.41 = (f32[32,64]{1,0:T(8,128)S(1)}, f32[32,64]{1,0:T(8,128)S(1)}, u32[]{:S(2)}, u32[]{:S(2)}) collective-permute-start(f32[32,64]{1,0:T(8,128)S(1)} %moment.1), channel_id=1, source_target_pairs={{0,2},{1,3},{2,0},{3,1},{4,6},{5,7},{6,4},{7,5},{8,10},{9,11},{10,... | collective-permute-start | bytes 24584 | tf_op jit(solution)/shard_map/ppermute | solution.py:166
  74.3 3.7 %collective-permute-start.40 = (f32[32,64]{1,0:T(8,128)S(1)}, f32[32,64]{1,0:T(8,128)S(1)}, u32[]{:S(2)}, u32[]{:S(2)}) collective-permute-start(f32[32,64]{1,0:T(8,128)S(1)} %moment.1), channel_id=1, source_target_pairs={{0,1},{1,0},{2,3},{3,2},{4,5},{5,4},{6,7},{7,6},{8,9},{9,8},{10,11... | collective-permute-start | bytes 24584 | tf_op jit(solution)/shard_map/ppermute | solution.py:166
  78.1 6.1 %collective-permute-start.45 = (f32[32,64]{1,0:T(8,128)S(1)}, f32[32,64]{1,0:T(8,128)S(1)}, u32[]{:S(2)}, u32[]{:S(2)}) collective-permute-start(f32[32,64]{1,0:T(8,128)S(1)} %add_add_fusion.1.sums), channel_id=1, source_target_pairs={{0,24},{4,28},{8,16},{12,20},{16,8},{20,12},{24,0},{28,4},{1,25},{... | collective-permute-start | bytes 24584 | tf_op jit(solution)/shard_map/ppermute | solution.py:166
  80.1 4.6 %collective-permute-start.44 = (f32[32,64]{1,0:T(8,128)S(1)}, f32[32,64]{1,0:T(8,128)S(1)}, u32[]{:S(2)}, u32[]{:S(2)}) collective-permute-start(f32[32,64]{1,0:T(8,128)S(1)} %add_add_fusion.1.sums), channel_id=1, source_target_pairs={{0,16},{4,20},{8,24},{12,28},{16,0},{20,4},{24,8},{28,12},{1,17},{... | collective-permute-start | bytes 24584 | tf_op jit(solution)/shard_map/ppermute | solution.py:166
  80.7 4.1 %collective-permute-start.43 = (f32[32,64]{1,0:T(8,128)S(1)}, f32[32,64]{1,0:T(8,128)S(1)}, u32[]{:S(2)}, u32[]{:S(2)}) collective-permute-start(f32[32,64]{1,0:T(8,128)S(1)} %add_add_fusion.1.sums), channel_id=1, source_target_pairs={{0,8},{4,12},{8,0},{12,4},{16,24},{20,28},{24,16},{28,20},{1,9},{5... | collective-permute-start | bytes 24584 | tf_op jit(solution)/shard_map/ppermute | solution.py:166
  84.8 1.2 %collective-permute-start.46 = (f32[32,64]{1,0:T(8,128)S(1)}, f32[32,64]{1,0:T(8,128)S(1)}, u32[]{:S(2)}, u32[]{:S(2)}) collective-permute-start(f32[32,64]{1,0:T(8,128)S(1)} %add_add_fusion), channel_id=1, source_target_pairs={{0,4},{4,0},{8,12},{12,8},{16,20},{20,16},{24,28},{28,24},{1,5},{5... | collective-permute-start | bytes 24584 | tf_op jit(solution)/shard_map/ppermute | solution.py:166
  (3 other events, 29.7 us)

commit v6 on v5

--- a/solution.py
+++ b/solution.py
@@ -55,7 +55,8 @@
     for chunk, copy in enumerate(copies):
         copy.wait()
         for slot in range(chunk * width, (chunk + 1) * width):
-            high[slot], low[slot] = split(arrived[slot].T)
+            upper, lower = split(arrived[slot])
+            high[slot], low[slot] = upper.T, lower.T
 
 
 def accumulate_tiles(slots, high, low, parts, halves, total):
@@ -199,7 +200,7 @@
         out_specs=vmem(2),
         scratch_shapes=[
             pltpu.VMEM(tiles.shape, jnp.float32),
-            pltpu.SemaphoreType.DMA((slots_held // 2,)),
+            pltpu.SemaphoreType.DMA((slots_held // 8,)),
         ],
         compiler_params=pltpu.CompilerParams(vmem_limit_bytes=42 * MIB),
         name="stage",

time: 87.4 us -> 87.1 us (level)
  transfers between devices with their start and end apart: 47 -> 47, of which waited for: 30 -> 29; matrix products, arithmetic and copies ran while one was open for 0% -> 0% of each run, Pallas kernels for 7% -> 7%
where the time goes in v6:
time: 87.1 us; the launch traced here: 87 us
  starting transfers between devices  42.5 us (49%)
  waiting for transfers between devices  29.5 us (34%)
  Pallas kernels  13.4 us (15%)
  between operations  1.44 us (2%)
    ppermute x47, starting transfers between devices, swap(): return lax.ppermute(value, axis, [(i, i ^ distance) for i in range(size)])  42.5 us
    ppermute x47, waiting for transfers between devices, swap(): return lax.ppermute(value, axis, [(i, i ^ distance) for i in range(size)])  29.5 us
    pallas_call x4, Pallas kernels, products(): pl.pallas_call(functools.partial(product_kernel, n_row, n_col), out_shape...  5.72 us
    pallas_call x1, Pallas kernels, body(): pl.pallas_call(stage_kernel, out_shape=[jax.ShapeDtypeStruct(tiles.shape,...  4.1 us
  transfers between devices with their start and end apart: 47, of which 29 were waited for; matrix products, arithmetic and copies ran while one was open for 0% of the time, Pallas kernels for 7%

profile of v6, /device:TPU:0, one launch (start us, length us, event | category | flops | bytes accessed | tf_op | source)
XLA Modules:
  0.0 87.0 jit_solution(7673433992712435991)
XLA Ops:
  0.7 5.1 %collective-permute-start.2 = (f32[32,512]{1,0:T(8,128)}, f32[32,512]{1,0:T(8,128)S(1)}, u32[]{:S(2)}, u32[]{:S(2)}) collective-permute-start(f32[32,512]{1,0:T(8,128)} %refs_0_.1), channel_id=1, source_target_pairs={{0,24},{4,28},{8,16},{12,20},{16,8},{20,12},{24,0},{28,4},{1,25},{... | collective-permute-start | bytes 196616 | tf_op jit(solution)/shard_map/ppermute | solution.py:167
  6.4 4.1 %stage.1 = (bf16[32,256,256]{2,1,0:T(8,128)(2,1)S(1)}, bf16[32,256,256]{2,1,0:T(8,128)(2,1)S(1)}) custom-call(f32[32,256,256]{2,1,0:T(8,128)} %tiles.1), custom_call_target="tpu_custom_call" | custom-call | tf_op jit(solution)/shard_map/stage/pallas_call | solution.py:196
  10.5 1.1 %collective-permute-done.1.refs_4_ = f32[32,512]{1,0:T(8,128)S(1)} collective-permute-done((f32[32,512]{1,0:T(8,128)}, f32[32,512]{1,0:T(8,128)S(1)}, u32[]{:S(2)}, u32[]{:S(2)}) %collective-permute-start.1) | collective-permute-done | bytes 65568 | tf_op jit(solution)/shard_map/ppermute | solution.py:167
  13.4 1.4 %tile_products.4 = (f32[32,512]{1,0:T(8,128)S(1)}, f32[32,512]{1,0:T(8,128)S(1)}, f32[32,512]{1,0:T(8,128)S(1)}, f32[32,512]{1,0:T(8,128)S(1)}) custom-call(s32[2,32]{1,0:T(2,128)S(1)} %places.1.slots, bf16[32,256,256]{2,1,0:T(8,128)(2,1)S(1)} %get-tuple-element.41.high, bf16[32,256,256]{2,1,0:T(8,128)(2,1)S(1)} %get-tuple-element.42.low, ...), custom_call_target="tpu_custom_call" | custom-call | tf_op jit(solution)/shard_map/tile_products/pallas_call | solution.py:221
  14.8 2.5 %collective-permute-start.7 = (f32[32,512]{1,0:T(8,128)S(1)}, f32[32,512]{1,0:T(8,128)S(1)}, u32[]{:S(2)}, u32[]{:S(2)}) collective-permute-start(f32[32,512]{1,0:T(8,128)S(1)} %get-tuple-element.47), channel_id=1, source_target_pairs={{0,3},{1,2},{2,1},{3,0},{4,7},{5,6},{6,5},{7,4},{8,11},{9,10},{10,... | collective-permute-start | bytes 196616 | tf_op jit(solution)/shard_map/ppermute | solution.py:167
  18.4 1.7 %collective-permute-done.7 = f32[32,512]{1,0:T(8,128)S(1)} collective-permute-done((f32[32,512]{1,0:T(8,128)S(1)}, f32[32,512]{1,0:T(8,128)S(1)}, u32[]{:S(2)}, u32[]{:S(2)}) %collective-permute-start.7) | collective-permute-done | bytes 65568 | tf_op jit(solution)/shard_map/ppermute | solution.py:167
  20.1 1.5 %collective-permute-done.8 = f32[32,512]{1,0:T(8,128)S(1)} collective-permute-done((f32[32,512]{1,0:T(8,128)S(1)}, f32[32,512]{1,0:T(8,128)S(1)}, u32[]{:S(2)}, u32[]{:S(2)}) %collective-permute-start.8) | collective-permute-done | bytes 65568 | tf_op jit(solution)/shard_map/ppermute | solution.py:167
  22.1 3.0 %collective-permute-start.15 = (f32[32,512]{1,0:T(8,128)S(1)}, f32[32,512]{1,0:T(8,128)S(1)}, u32[]{:S(2)}, u32[]{:S(2)}) collective-permute-start(f32[32,512]{1,0:T(8,128)S(1)} %get-tuple-element.72.refs_0_), channel_id=1, source_target_pairs={{0,24},{4,28},{8,16},{12,20},{16,8},{20,12},{24,0},{28,4},{1,25},{... | collective-permute-start | bytes 196616 | tf_op jit(solution)/shard_map/ppermute | solution.py:167
  25.1 1.5 %collective-permute-start.11 = (f32[32,512]{1,0:T(8,128)S(1)}, f32[32,512]{1,0:T(8,128)S(1)}, u32[]{:S(2)}, u32[]{:S(2)}) collective-permute-start(f32[32,512]{1,0:T(8,128)S(1)} %get-tuple-element.72.refs_0_), channel_id=1, source_target_pairs={{0,8},{4,12},{8,0},{12,4},{16,24},{20,28},{24,16},{28,20},{1,9},{5... | collective-permute-start | bytes 196616 | tf_op jit(solution)/shard_map/ppermute | solution.py:167
  26.6 1.8 %collective-permute-done.15.refs_6_ = f32[32,512]{1,0:T(8,128)S(1)} collective-permute-done((f32[32,512]{1,0:T(8,128)S(1)}, f32[32,512]{1,0:T(8,128)S(1)}, u32[]{:S(2)}, u32[]{:S(2)}) %collective-permute-start.15) | collective-permute-done | bytes 65568 | tf_op jit(solution)/shard_map/ppermute | solution.py:167
  28.4 2.0 %collective-permute-done.13.refs_4_ = f32[32,512]{1,0:T(8,128)S(1)} collective-permute-done((f32[32,512]{1,0:T(8,128)S(1)}, f32[32,512]{1,0:T(8,128)S(1)}, u32[]{:S(2)}, u32[]{:S(2)}) %collective-permute-start.13) | collective-permute-done | bytes 65568 | tf_op jit(solution)/shard_map/ppermute | solution.py:167
  30.9 0.7 collective-permute-done.14.refs_5_
  31.8 1.4 %tile_products.5 = (f32[32,512]{1,0:T(8,128)S(1)}, f32[32,512]{1,0:T(8,128)S(1)}, f32[32,512]{1,0:T(8,128)S(1)}, f32[32,512]{1,0:T(8,128)S(1)}) custom-call(s32[2,32]{1,0:T(2,128)S(1)} %places.1.slots, bf16[32,256,256]{2,1,0:T(8,128)(2,1)S(1)} %get-tuple-element.41.high, bf16[32,256,256]{2,1,0:T(8,128)(2,1)S(1)} %get-tuple-element.42.low, ...), custom_call_target="tpu_custom_call" | custom-call | tf_op jit(solution)/shard_map/tile_products/pallas_call | solution.py:221
  33.2 1.6 %collective-permute-start.17 = (f32[32,512]{1,0:T(8,128)S(1)}, f32[32,512]{1,0:T(8,128)S(1)}, u32[]{:S(2)}, u32[]{:S(2)}) collective-permute-start(f32[32,512]{1,0:T(8,128)S(1)} %get-tuple-element.51), channel_id=1, source_target_pairs={{0,3},{1,2},{2,1},{3,0},{4,7},{5,6},{6,5},{7,4},{8,11},{9,10},{10,... | collective-permute-start | bytes 196616 | tf_op jit(solution)/shard_map/ppermute | solution.py:167
  34.8 1.5 %collective-permute-start.18 = (f32[32,512]{1,0:T(8,128)S(1)}, f32[32,512]{1,0:T(8,128)S(1)}, u32[]{:S(2)}, u32[]{:S(2)}) collective-permute-start(f32[32,512]{1,0:T(8,128)S(1)} %get-tuple-element.52), channel_id=1, source_target_pairs={{0,2},{1,3},{2,0},{3,1},{4,6},{5,7},{6,4},{7,5},{8,10},{9,11},{10,... | collective-permute-start | bytes 196616 | tf_op jit(solution)/shard_map/ppermute | solution.py:167
  36.8 1.9 %collective-permute-done.17 = f32[32,512]{1,0:T(8,128)S(1)} collective-permute-done((f32[32,512]{1,0:T(8,128)S(1)}, f32[32,512]{1,0:T(8,128)S(1)}, u32[]{:S(2)}, u32[]{:S(2)}) %collective-permute-start.17) | collective-permute-done | bytes 65568 | tf_op jit(solution)/shard_map/ppermute | solution.py:167
  38.7 1.3 %collective-permute-done.18 = f32[32,512]{1,0:T(8,128)S(1)} collective-permute-done((f32[32,512]{1,0:T(8,128)S(1)}, f32[32,512]{1,0:T(8,128)S(1)}, u32[]{:S(2)}, u32[]{:S(2)}) %collective-permute-start.18) | collective-permute-done | bytes 65568 | tf_op jit(solution)/shard_map/ppermute | solution.py:167
  40.0 0.7 collective-permute-done.19
  40.7 2.2 %collective-permute-start.25 = (f32[32,512]{1,0:T(8,128)S(1)}, f32[32,512]{1,0:T(8,128)S(1)}, u32[]{:S(2)}, u32[]{:S(2)}) collective-permute-start(f32[32,512]{1,0:T(8,128)S(1)} %multiply_subtract_fusion.1.refs_0_), channel_id=1, source_target_pairs={{0,24},{4,28},{8,16},{12,20},{16,8},{20,12},{24,0},{28,4},{1,25},{... | collective-permute-start | bytes 196616 | tf_op jit(solution)/shard_map/ppermute | solution.py:167
  43.0 2.1 %collective-permute-start.21 = (f32[32,512]{1,0:T(8,128)S(1)}, f32[32,512]{1,0:T(8,128)S(1)}, u32[]{:S(2)}, u32[]{:S(2)}) collective-permute-start(f32[32,512]{1,0:T(8,128)S(1)} %multiply_subtract_fusion.1.refs_0_), channel_id=1, source_target_pairs={{0,8},{4,12},{8,0},{12,4},{16,24},{20,28},{24,16},{28,20},{1,9},{5... | collective-permute-start | bytes 196616 | tf_op jit(solution)/shard_map/ppermute | solution.py:167
  45.1 1.7 %collective-permute-done.25.refs_6_ = f32[32,512]{1,0:T(8,128)S(1)} collective-permute-done((f32[32,512]{1,0:T(8,128)S(1)}, f32[32,512]{1,0:T(8,128)S(1)}, u32[]{:S(2)}, u32[]{:S(2)}) %collective-permute-start.25) | collective-permute-done | bytes 65568 | tf_op jit(solution)/shard_map/ppermute | solution.py:167
  46.8 2.5 %collective-permute-done.23.refs_4_ = f32[32,512]{1,0:T(8,128)S(1)} collective-permute-done((f32[32,512]{1,0:T(8,128)S(1)}, f32[32,512]{1,0:T(8,128)S(1)}, u32[]{:S(2)}, u32[]{:S(2)}) %collective-permute-start.23) | collective-permute-done | bytes 65568 | tf_op jit(solution)/shard_map/ppermute | solution.py:167
  49.9 0.7 collective-permute-done.24.refs_5_
  50.8 1.4 %tile_products.6 = (f32[32,512]{1,0:T(8,128)S(1)}, f32[32,512]{1,0:T(8,128)S(1)}, f32[32,512]{1,0:T(8,128)S(1)}, f32[32,512]{1,0:T(8,128)S(1)}) custom-call(s32[2,32]{1,0:T(2,128)S(1)} %places.1.slots, bf16[32,256,256]{2,1,0:T(8,128)(2,1)S(1)} %get-tuple-element.41.high, bf16[32,256,256]{2,1,0:T(8,128)(2,1)S(1)} %get-tuple-element.42.low, ...), custom_call_target="tpu_custom_call" | custom-call | tf_op jit(solution)/shard_map/tile_products/pallas_call | solution.py:221
  52.2 1.6 %collective-permute-start.27 = (f32[32,512]{1,0:T(8,128)S(1)}, f32[32,512]{1,0:T(8,128)S(1)}, u32[]{:S(2)}, u32[]{:S(2)}) collective-permute-start(f32[32,512]{1,0:T(8,128)S(1)} %get-tuple-element.55), channel_id=1, source_target_pairs={{0,3},{1,2},{2,1},{3,0},{4,7},{5,6},{6,5},{7,4},{8,11},{9,10},{10,... | collective-permute-start | bytes 196616 | tf_op jit(solution)/shard_map/ppermute | solution.py:167
  53.8 0.8 collective-permute-start.28
  54.6 1.2 %collective-permute-start.29 = (f32[32,512]{1,0:T(8,128)S(1)}, f32[32,512]{1,0:T(8,128)S(1)}, u32[]{:S(2)}, u32[]{:S(2)}) collective-permute-start(f32[32,512]{1,0:T(8,128)S(1)} %get-tuple-element.57), channel_id=1, source_target_pairs={{0,1},{1,0},{2,3},{3,2},{4,5},{5,4},{6,7},{7,6},{8,9},{9,8},{10,11... | collective-permute-start | bytes 196616 | tf_op jit(solution)/shard_map/ppermute | solution.py:167
  55.8 1.9 %collective-permute-done.27 = f32[32,512]{1,0:T(8,128)S(1)} collective-permute-done((f32[32,512]{1,0:T(8,128)S(1)}, f32[32,512]{1,0:T(8,128)S(1)}, u32[]{:S(2)}, u32[]{:S(2)}) %collective-permute-start.27) | collective-permute-done | bytes 65568 | tf_op jit(solution)/shard_map/ppermute | solution.py:167
  57.7 1.3 %collective-permute-done.28 = f32[32,512]{1,0:T(8,128)S(1)} collective-permute-done((f32[32,512]{1,0:T(8,128)S(1)}, f32[32,512]{1,0:T(8,128)S(1)}, u32[]{:S(2)}, u32[]{:S(2)}) %collective-permute-start.28) | collective-permute-done | bytes 65568 | tf_op jit(solution)/shard_map/ppermute | solution.py:167
  59.0 1.2 %collective-permute-start.34 = (f32[32,512]{1,0:T(8,128)S(1)}, f32[32,512]{1,0:T(8,128)S(1)}, u32[]{:S(2)}, u32[]{:S(2)}) collective-permute-start(f32[32,512]{1,0:T(8,128)S(1)} %multiply_subtract_fusion.refs_0_.filtered), channel_id=1, source_target_pairs={{0,1},{1,0},{2,3},{3,2},{4,5},{5,4},{6,7},{7,6},{8,9},{9,8},{10,11... | collective-permute-start | bytes 196616 | tf_op jit(solution)/shard_map/ppermute | solution.py:167
  60.7 1.9 %collective-permute-start.38 = (f32[32,512]{1,0:T(8,128)S(1)}, f32[32,512]{1,0:T(8,128)S(1)}, u32[]{:S(2)}, u32[]{:S(2)}) collective-permute-start(f32[32,512]{1,0:T(8,128)S(1)} %multiply_subtract_fusion.refs_0_.filtered), channel_id=1, source_target_pairs={{0,24},{4,28},{8,16},{12,20},{16,8},{20,12},{24,0},{28,4},{1,25},{... | collective-permute-start | bytes 196616 | tf_op jit(solution)/shard_map/ppermute | solution.py:167
  62.6 1.0 %collective-permute-start.35 = (f32[32,512]{1,0:T(8,128)S(1)}, f32[32,512]{1,0:T(8,128)S(1)}, u32[]{:S(2)}, u32[]{:S(2)}) collective-permute-start(f32[32,512]{1,0:T(8,128)S(1)} %multiply_subtract_fusion.refs_0_.filtered), channel_id=1, source_target_pairs={{0,2},{1,3},{2,0},{3,1},{4,6},{5,7},{6,4},{7,5},{8,10},{9,11},{10,... | collective-permute-start | bytes 196616 | tf_op jit(solution)/shard_map/ppermute | solution.py:167
  63.6 1.1 %collective-permute-start.31 = (f32[32,512]{1,0:T(8,128)S(1)}, f32[32,512]{1,0:T(8,128)S(1)}, u32[]{:S(2)}, u32[]{:S(2)}) collective-permute-start(f32[32,512]{1,0:T(8,128)S(1)} %multiply_subtract_fusion.refs_0_.filtered), channel_id=1, source_target_pairs={{0,8},{4,12},{8,0},{12,4},{16,24},{20,28},{24,16},{28,20},{1,9},{5... | collective-permute-start | bytes 196616 | tf_op jit(solution)/shard_map/ppermute | solution.py:167
  64.8 0.9 %collective-permute-start.36 = (f32[32,512]{1,0:T(8,128)S(1)}, f32[32,512]{1,0:T(8,128)S(1)}, u32[]{:S(2)}, u32[]{:S(2)}) collective-permute-start(f32[32,512]{1,0:T(8,128)S(1)} %collective-permute-done.34.refs_8_), channel_id=1, source_target_pairs={{0,2},{1,3},{2,0},{3,1},{4,6},{5,7},{6,4},{7,5},{8,10},{9,11},{10,... | collective-permute-start | bytes 196616 | tf_op jit(solution)/shard_map/ppermute | solution.py:167
  65.7 1.9 %collective-permute-done.33.refs_4_ = f32[32,512]{1,0:T(8,128)S(1)} collective-permute-done((f32[32,512]{1,0:T(8,128)S(1)}, f32[32,512]{1,0:T(8,128)S(1)}, u32[]{:S(2)}, u32[]{:S(2)}) %collective-permute-start.33) | collective-permute-done | bytes 65568 | tf_op jit(solution)/shard_map/ppermute | solution.py:167
  69.5 1.4 %tile_products.7 = (f32[32,512]{1,0:T(8,128)S(1)}, f32[32,512]{1,0:T(8,128)S(1)}, f32[32,512]{1,0:T(8,128)S(1)}, f32[32,512]{1,0:T(8,128)S(1)}) custom-call(s32[2,32]{1,0:T(2,128)S(1)} %places.1.slots, bf16[32,256,256]{2,1,0:T(8,128)(2,1)S(1)} %get-tuple-element.41.high, bf16[32,256,256]{2,1,0:T(8,128)(2,1)S(1)} %get-tuple-element.42.low, ...), custom_call_target="tpu_custom_call" | custom-call | tf_op jit(solution)/shard_map/tile_products/pallas_call | solution.py:221
  71.5 1.7 %collective-permute-start.42 = (f32[32,64]{1,0:T(8,128)S(1)}, f32[32,64]{1,0:T(8,128)S(1)}, u32[]{:S(2)}, u32[]{:S(2)}) collective-permute-start(f32[32,64]{1,0:T(8,128)S(1)} %moment.1), channel_id=1, source_target_pairs={{0,3},{1,2},{2,1},{3,0},{4,7},{5,6},{6,5},{7,4},{8,11},{9,10},{10,... | collective-permute-start | bytes 24584 | tf_op jit(solution)/shard_map/ppermute | solution.py:167
  73.2 0.8 collective-permute-start.41
  74.0 1.0 %collective-permute-start.40 = (f32[32,64]{1,0:T(8,128)S(1)}, f32[32,64]{1,0:T(8,128)S(1)}, u32[]{:S(2)}, u32[]{:S(2)}) collective-permute-start(f32[32,64]{1,0:T(8,128)S(1)} %moment.1), channel_id=1, source_target_pairs={{0,1},{1,0},{2,3},{3,2},{4,5},{5,4},{6,7},{7,6},{8,9},{9,8},{10,11... | collective-permute-start | bytes 24584 | tf_op jit(solution)/shard_map/ppermute | solution.py:167
  75.0 1.2 %collective-permute-done.42 = f32[32,64]{1,0:T(8,128)S(1)} collective-permute-done((f32[32,64]{1,0:T(8,128)S(1)}, f32[32,64]{1,0:T(8,128)S(1)}, u32[]{:S(2)}, u32[]{:S(2)}) %collective-permute-start.42) | collective-permute-done | bytes 8224 | tf_op jit(solution)/shard_map/ppermute | solution.py:167
  76.2 0.7 collective-permute-done.41
  76.9 0.8 collective-permute-done.40
  77.7 2.1 %collective-permute-start.45 = (f32[32,64]{1,0:T(8,128)S(1)}, f32[32,64]{1,0:T(8,128)S(1)}, u32[]{:S(2)}, u32[]{:S(2)}) collective-permute-start(f32[32,64]{1,0:T(8,128)S(1)} %add_add_fusion.1.sums), channel_id=1, source_target_pairs={{0,24},{4,28},{8,16},{12,20},{16,8},{20,12},{24,0},{28,4},{1,25},{... | collective-permute-start | bytes 24584 | tf_op jit(solution)/shard_map/ppermute | solution.py:167
  80.3 1.8 %collective-permute-start.43 = (f32[32,64]{1,0:T(8,128)S(1)}, f32[32,64]{1,0:T(8,128)S(1)}, u32[]{:S(2)}, u32[]{:S(2)}) collective-permute-start(f32[32,64]{1,0:T(8,128)S(1)} %add_add_fusion.1.sums), channel_id=1, source_target_pairs={{0,8},{4,12},{8,0},{12,4},{16,24},{20,28},{24,16},{28,20},{1,9},{5... | collective-permute-start | bytes 24584 | tf_op jit(solution)/shard_map/ppermute | solution.py:167
  82.1 1.7 %factor.1 = (f32[32,32]{1,0:T(8,128)S(1)}, f32[32,512]{1,0:T(8,128)}) custom-call(f32[32,64]{1,0:T(8,128)S(1)} %add_add_fusion.1.sums, f32[32,512]{1,0:T(8,128)S(1)} %multiply_subtract_fusion.refs_0_.filtered), custom_call_target="tpu_custom_call" | custom-call | tf_op jit(solution)/shard_map/factor/pallas_call | solution.py:262
  83.8 0.7 collective-permute-done.44
  84.6 1.2 %collective-permute-done.46 = f32[32,64]{1,0:T(8,128)S(1)} collective-permute-done((f32[32,64]{1,0:T(8,128)S(1)}, f32[32,64]{1,0:T(8,128)S(1)}, u32[]{:S(2)}, u32[]{:S(2)}) %collective-permute-start.46) | collective-permute-done | bytes 8224 | tf_op jit(solution)/shard_map/ppermute | solution.py:167
  85.8 1.2 %project.1 = f32[32,32]{1,0:T(8,128)} custom-call(f32[32,64]{1,0:T(8,128)S(1)} %add.65.sums, f32[32,32]{1,0:T(8,128)S(1)} %get-tuple-element.71.inverse), custom_call_target="tpu_custom_call" | custom-call | tf_op jit(solution)/shard_map/project/pallas_call | solution.py:274
  (70 shorter events, 8.8 us)
Async XLA Ops:
  0.6 12.7 %copy-start = (f32[32,512]{1,0:T(8,128)S(1)}, f32[32,512]{1,0:T(8,128)}, u32[]{:S(2)}) copy-start(f32[32,512]{1,0:T(8,128)} %refs_0_.1) | copy-start | bytes 196612
  0.7 9.9 %collective-permute-start.2 = (f32[32,512]{1,0:T(8,128)}, f32[32,512]{1,0:T(8,128)S(1)}, u32[]{:S(2)}, u32[]{:S(2)}) collective-permute-start(f32[32,512]{1,0:T(8,128)} %refs_0_.1), channel_id=1, source_target_pairs={{0,24},{4,28},{8,16},{12,20},{16,8},{20,12},{24,0},{28,4},{1,25},{... | collective-permute-start | bytes 196616 | tf_op jit(solution)/shard_map/ppermute | solution.py:167
  5.8 5.8 %collective-permute-start.1 = (f32[32,512]{1,0:T(8,128)}, f32[32,512]{1,0:T(8,128)S(1)}, u32[]{:S(2)}, u32[]{:S(2)}) collective-permute-start(f32[32,512]{1,0:T(8,128)} %refs_0_.1), channel_id=1, source_target_pairs={{0,16},{4,20},{8,24},{12,28},{16,0},{20,4},{24,8},{28,12},{1,17},{... | collective-permute-start | bytes 196616 | tf_op jit(solution)/shard_map/ppermute | solution.py:167
  5.8 5.8 %collective-permute-start = (f32[32,512]{1,0:T(8,128)}, f32[32,512]{1,0:T(8,128)S(1)}, u32[]{:S(2)}, u32[]{:S(2)}) collective-permute-start(f32[32,512]{1,0:T(8,128)} %refs_0_.1), channel_id=1, source_target_pairs={{0,8},{4,12},{8,0},{12,4},{16,24},{20,28},{24,16},{28,20},{1,9},{5... | collective-permute-start | bytes 196616 | tf_op jit(solution)/shard_map/ppermute | solution.py:167
  6.4 6.4 %collective-permute-start.3 = (f32[32,512]{1,0:T(8,128)}, f32[32,512]{1,0:T(8,128)S(1)}, u32[]{:S(2)}, u32[]{:S(2)}) collective-permute-start(f32[32,512]{1,0:T(8,128)} %refs_0_.1), channel_id=1, source_target_pairs={{0,4},{4,0},{8,12},{12,8},{16,20},{20,16},{24,28},{28,24},{1,5},{5... | collective-permute-start | bytes 196616 | tf_op jit(solution)/shard_map/ppermute | solution.py:167
  11.6 1.3 %collective-permute-start.4 = (f32[32,512]{1,0:T(8,128)S(1)}, f32[32,512]{1,0:T(8,128)S(1)}, u32[]{:S(2)}, u32[]{:S(2)}) collective-permute-start(f32[32,512]{1,0:T(8,128)S(1)} %collective-permute-done.refs_2_), channel_id=1, source_target_pairs={{0,4},{4,0},{8,12},{12,8},{16,20},{20,16},{24,28},{28,24},{1,5},{5... | collective-permute-start | bytes 196616 | tf_op jit(solution)/shard_map/ppermute | solution.py:167
  11.6 1.4 %collective-permute-start.5 = (f32[32,512]{1,0:T(8,128)S(1)}, f32[32,512]{1,0:T(8,128)S(1)}, u32[]{:S(2)}, u32[]{:S(2)}) collective-permute-start(f32[32,512]{1,0:T(8,128)S(1)} %collective-permute-done.1.refs_4_), channel_id=1, source_target_pairs={{0,4},{4,0},{8,12},{12,8},{16,20},{20,16},{24,28},{28,24},{1,5},{5... | collective-permute-start | bytes 196616 | tf_op jit(solution)/shard_map/ppermute | solution.py:167
  12.1 1.3 %collective-permute-start.6 = (f32[32,512]{1,0:T(8,128)S(1)}, f32[32,512]{1,0:T(8,128)S(1)}, u32[]{:S(2)}, u32[]{:S(2)}) collective-permute-start(f32[32,512]{1,0:T(8,128)S(1)} %collective-permute-done.2.refs_6_), channel_id=1, source_target_pairs={{0,4},{4,0},{8,12},{12,8},{16,20},{20,16},{24,28},{28,24},{1,5},{5... | collective-permute-start | bytes 196616 | tf_op jit(solution)/shard_map/ppermute | solution.py:167
  14.8 5.3 %collective-permute-start.7 = (f32[32,512]{1,0:T(8,128)S(1)}, f32[32,512]{1,0:T(8,128)S(1)}, u32[]{:S(2)}, u32[]{:S(2)}) collective-permute-start(f32[32,512]{1,0:T(8,128)S(1)} %get-tuple-element.47), channel_id=1, source_target_pairs={{0,3},{1,2},{2,1},{3,0},{4,7},{5,6},{6,5},{7,4},{8,11},{9,10},{10,... | collective-permute-start | bytes 196616 | tf_op jit(solution)/shard_map/ppermute | solution.py:167
  17.3 4.3 %collective-permute-start.8 = (f32[32,512]{1,0:T(8,128)S(1)}, f32[32,512]{1,0:T(8,128)S(1)}, u32[]{:S(2)}, u32[]{:S(2)}) collective-permute-start(f32[32,512]{1,0:T(8,128)S(1)} %get-tuple-element.48), channel_id=1, source_target_pairs={{0,2},{1,3},{2,0},{3,1},{4,6},{5,7},{6,4},{7,5},{8,10},{9,11},{10,... | collective-permute-start | bytes 196616 | tf_op jit(solution)/shard_map/ppermute | solution.py:167
  17.8 4.3 %collective-permute-start.9 = (f32[32,512]{1,0:T(8,128)S(1)}, f32[32,512]{1,0:T(8,128)S(1)}, u32[]{:S(2)}, u32[]{:S(2)}) collective-permute-start(f32[32,512]{1,0:T(8,128)S(1)} %get-tuple-element.49), channel_id=1, source_target_pairs={{0,1},{1,0},{2,3},{3,2},{4,5},{5,4},{6,7},{7,6},{8,9},{9,8},{10,11... | collective-permute-start | bytes 196616 | tf_op jit(solution)/shard_map/ppermute | solution.py:167
  22.1 6.2 %collective-permute-start.15 = (f32[32,512]{1,0:T(8,128)S(1)}, f32[32,512]{1,0:T(8,128)S(1)}, u32[]{:S(2)}, u32[]{:S(2)}) collective-permute-start(f32[32,512]{1,0:T(8,128)S(1)} %get-tuple-element.72.refs_0_), channel_id=1, source_target_pairs={{0,24},{4,28},{8,16},{12,20},{16,8},{20,12},{24,0},{28,4},{1,25},{... | collective-permute-start | bytes 196616 | tf_op jit(solution)/shard_map/ppermute | solution.py:167
  25.1 5.3 %collective-permute-start.13 = (f32[32,512]{1,0:T(8,128)S(1)}, f32[32,512]{1,0:T(8,128)S(1)}, u32[]{:S(2)}, u32[]{:S(2)}) collective-permute-start(f32[32,512]{1,0:T(8,128)S(1)} %get-tuple-element.72.refs_0_), channel_id=1, source_target_pairs={{0,16},{4,20},{8,24},{12,28},{16,0},{20,4},{24,8},{28,12},{1,17},{... | collective-permute-start | bytes 196616 | tf_op jit(solution)/shard_map/ppermute | solution.py:167
  25.1 5.3 %collective-permute-start.11 = (f32[32,512]{1,0:T(8,128)S(1)}, f32[32,512]{1,0:T(8,128)S(1)}, u32[]{:S(2)}, u32[]{:S(2)}) collective-permute-start(f32[32,512]{1,0:T(8,128)S(1)} %get-tuple-element.72.refs_0_), channel_id=1, source_target_pairs={{0,8},{4,12},{8,0},{12,4},{16,24},{20,28},{24,16},{28,20},{1,9},{5... | collective-permute-start | bytes 196616 | tf_op jit(solution)/shard_map/ppermute | solution.py:167
  26.6 4.3 %collective-permute-start.10 = (f32[32,512]{1,0:T(8,128)S(1)}, f32[32,512]{1,0:T(8,128)S(1)}, u32[]{:S(2)}, u32[]{:S(2)}) collective-permute-start(f32[32,512]{1,0:T(8,128)S(1)} %get-tuple-element.72.refs_0_), channel_id=1, source_target_pairs={{0,4},{4,0},{8,12},{12,8},{16,20},{20,16},{24,28},{28,24},{1,5},{5... | collective-permute-start | bytes 196616 | tf_op jit(solution)/shard_map/ppermute | solution.py:167
  28.4 2.5 %collective-permute-start.16 = (f32[32,512]{1,0:T(8,128)S(1)}, f32[32,512]{1,0:T(8,128)S(1)}, u32[]{:S(2)}, u32[]{:S(2)}) collective-permute-start(f32[32,512]{1,0:T(8,128)S(1)} %collective-permute-done.15.refs_6_), channel_id=1, source_target_pairs={{0,4},{4,0},{8,12},{12,8},{16,20},{20,16},{24,28},{28,24},{1,5},{5... | collective-permute-start | bytes 196616 | tf_op jit(solution)/shard_map/ppermute | solution.py:167
  30.4 1.3 %collective-permute-start.14 = (f32[32,512]{1,0:T(8,128)S(1)}, f32[32,512]{1,0:T(8,128)S(1)}, u32[]{:S(2)}, u32[]{:S(2)}) collective-permute-start(f32[32,512]{1,0:T(8,128)S(1)} %collective-permute-done.13.refs_4_), channel_id=1, source_target_pairs={{0,4},{4,0},{8,12},{12,8},{16,20},{20,16},{24,28},{28,24},{1,5},{5... | collective-permute-start | bytes 196616 | tf_op jit(solution)/shard_map/ppermute | solution.py:167
  30.4 1.4 %collective-permute-start.12 = (f32[32,512]{1,0:T(8,128)S(1)}, f32[32,512]{1,0:T(8,128)S(1)}, u32[]{:S(2)}, u32[]{:S(2)}) collective-permute-start(f32[32,512]{1,0:T(8,128)S(1)} %collective-permute-done.11.refs_2_), channel_id=1, source_target_pairs={{0,4},{4,0},{8,12},{12,8},{16,20},{20,16},{24,28},{28,24},{1,5},{5... | collective-permute-start | bytes 196616 | tf_op jit(solution)/shard_map/ppermute | solution.py:167
  33.2 5.4 %collective-permute-start.17 = (f32[32,512]{1,0:T(8,128)S(1)}, f32[32,512]{1,0:T(8,128)S(1)}, u32[]{:S(2)}, u32[]{:S(2)}) collective-permute-start(f32[32,512]{1,0:T(8,128)S(1)} %get-tuple-element.51), channel_id=1, source_target_pairs={{0,3},{1,2},{2,1},{3,0},{4,7},{5,6},{6,5},{7,4},{8,11},{9,10},{10,... | collective-permute-start | bytes 196616 | tf_op jit(solution)/shard_map/ppermute | solution.py:167
  34.8 5.1 %collective-permute-start.18 = (f32[32,512]{1,0:T(8,128)S(1)}, f32[32,512]{1,0:T(8,128)S(1)}, u32[]{:S(2)}, u32[]{:S(2)}) collective-permute-start(f32[32,512]{1,0:T(8,128)S(1)} %get-tuple-element.52), channel_id=1, source_target_pairs={{0,2},{1,3},{2,0},{3,1},{4,6},{5,7},{6,4},{7,5},{8,10},{9,11},{10,... | collective-permute-start | bytes 196616 | tf_op jit(solution)/shard_map/ppermute | solution.py:167
  36.4 4.3 %collective-permute-start.19 = (f32[32,512]{1,0:T(8,128)S(1)}, f32[32,512]{1,0:T(8,128)S(1)}, u32[]{:S(2)}, u32[]{:S(2)}) collective-permute-start(f32[32,512]{1,0:T(8,128)S(1)} %get-tuple-element.53), channel_id=1, source_target_pairs={{0,1},{1,0},{2,3},{3,2},{4,5},{5,4},{6,7},{7,6},{8,9},{9,8},{10,11... | collective-permute-start | bytes 196616 | tf_op jit(solution)/shard_map/ppermute | solution.py:167
  40.7 6.2 %collective-permute-start.25 = (f32[32,512]{1,0:T(8,128)S(1)}, f32[32,512]{1,0:T(8,128)S(1)}, u32[]{:S(2)}, u32[]{:S(2)}) collective-permute-start(f32[32,512]{1,0:T(8,128)S(1)} %multiply_subtract_fusion.1.refs_0_), channel_id=1, source_target_pairs={{0,24},{4,28},{8,16},{12,20},{16,8},{20,12},{24,0},{28,4},{1,25},{... | collective-permute-start | bytes 196616 | tf_op jit(solution)/shard_map/ppermute | solution.py:167
  42.9 6.5 %collective-permute-start.23 = (f32[32,512]{1,0:T(8,128)S(1)}, f32[32,512]{1,0:T(8,128)S(1)}, u32[]{:S(2)}, u32[]{:S(2)}) collective-permute-start(f32[32,512]{1,0:T(8,128)S(1)} %multiply_subtract_fusion.1.refs_0_), channel_id=1, source_target_pairs={{0,16},{4,20},{8,24},{12,28},{16,0},{20,4},{24,8},{28,12},{1,17},{... | collective-permute-start | bytes 196616 | tf_op jit(solution)/shard_map/ppermute | solution.py:167
  43.0 6.4 %collective-permute-start.21 = (f32[32,512]{1,0:T(8,128)S(1)}, f32[32,512]{1,0:T(8,128)S(1)}, u32[]{:S(2)}, u32[]{:S(2)}) collective-permute-start(f32[32,512]{1,0:T(8,128)S(1)} %multiply_subtract_fusion.1.refs_0_), channel_id=1, source_target_pairs={{0,8},{4,12},{8,0},{12,4},{16,24},{20,28},{24,16},{28,20},{1,9},{5... | collective-permute-start | bytes 196616 | tf_op jit(solution)/shard_map/ppermute | solution.py:167
  45.1 4.8 %collective-permute-start.20 = (f32[32,512]{1,0:T(8,128)S(1)}, f32[32,512]{1,0:T(8,128)S(1)}, u32[]{:S(2)}, u32[]{:S(2)}) collective-permute-start(f32[32,512]{1,0:T(8,128)S(1)} %multiply_subtract_fusion.1.refs_0_), channel_id=1, source_target_pairs={{0,4},{4,0},{8,12},{12,8},{16,20},{20,16},{24,28},{28,24},{1,5},{5... | collective-permute-start | bytes 196616 | tf_op jit(solution)/shard_map/ppermute | solution.py:167
  46.8 3.1 %collective-permute-start.26 = (f32[32,512]{1,0:T(8,128)S(1)}, f32[32,512]{1,0:T(8,128)S(1)}, u32[]{:S(2)}, u32[]{:S(2)}) collective-permute-start(f32[32,512]{1,0:T(8,128)S(1)} %collective-permute-done.25.refs_6_), channel_id=1, source_target_pairs={{0,4},{4,0},{8,12},{12,8},{16,20},{20,16},{24,28},{28,24},{1,5},{5... | collective-permute-start | bytes 196616 | tf_op jit(solution)/shard_map/ppermute | solution.py:167
  49.4 1.3 %collective-permute-start.24 = (f32[32,512]{1,0:T(8,128)S(1)}, f32[32,512]{1,0:T(8,128)S(1)}, u32[]{:S(2)}, u32[]{:S(2)}) collective-permute-start(f32[32,512]{1,0:T(8,128)S(1)} %collective-permute-done.23.refs_4_), channel_id=1, source_target_pairs={{0,4},{4,0},{8,12},{12,8},{16,20},{20,16},{24,28},{28,24},{1,5},{5... | collective-permute-start | bytes 196616 | tf_op jit(solution)/shard_map/ppermute | solution.py:167
  49.4 1.4 %collective-permute-start.22 = (f32[32,512]{1,0:T(8,128)S(1)}, f32[32,512]{1,0:T(8,128)S(1)}, u32[]{:S(2)}, u32[]{:S(2)}) collective-permute-start(f32[32,512]{1,0:T(8,128)S(1)} %collective-permute-done.21.refs_2_), channel_id=1, source_target_pairs={{0,4},{4,0},{8,12},{12,8},{16,20},{20,16},{24,28},{28,24},{1,5},{5... | collective-permute-start | bytes 196616 | tf_op jit(solution)/shard_map/ppermute | solution.py:167
  52.2 5.4 %collective-permute-start.27 = (f32[32,512]{1,0:T(8,128)S(1)}, f32[32,512]{1,0:T(8,128)S(1)}, u32[]{:S(2)}, u32[]{:S(2)}) collective-permute-start(f32[32,512]{1,0:T(8,128)S(1)} %get-tuple-element.55), channel_id=1, source_target_pairs={{0,3},{1,2},{2,1},{3,0},{4,7},{5,6},{6,5},{7,4},{8,11},{9,10},{10,... | collective-permute-start | bytes 196616 | tf_op jit(solution)/shard_map/ppermute | solution.py:167
  53.8 5.2 %collective-permute-start.28 = (f32[32,512]{1,0:T(8,128)S(1)}, f32[32,512]{1,0:T(8,128)S(1)}, u32[]{:S(2)}, u32[]{:S(2)}) collective-permute-start(f32[32,512]{1,0:T(8,128)S(1)} %get-tuple-element.56), channel_id=1, source_target_pairs={{0,2},{1,3},{2,0},{3,1},{4,6},{5,7},{6,4},{7,5},{8,10},{9,11},{10,... | collective-permute-start | bytes 196616 | tf_op jit(solution)/shard_map/ppermute | solution.py:167
  54.6 4.3 %collective-permute-start.29 = (f32[32,512]{1,0:T(8,128)S(1)}, f32[32,512]{1,0:T(8,128)S(1)}, u32[]{:S(2)}, u32[]{:S(2)}) collective-permute-start(f32[32,512]{1,0:T(8,128)S(1)} %get-tuple-element.57), channel_id=1, source_target_pairs={{0,1},{1,0},{2,3},{3,2},{4,5},{5,4},{6,7},{7,6},{8,9},{9,8},{10,11... | collective-permute-start | bytes 196616 | tf_op jit(solution)/shard_map/ppermute | solution.py:167
  59.0 5.8 %collective-permute-start.34 = (f32[32,512]{1,0:T(8,128)S(1)}, f32[32,512]{1,0:T(8,128)S(1)}, u32[]{:S(2)}, u32[]{:S(2)}) collective-permute-start(f32[32,512]{1,0:T(8,128)S(1)} %multiply_subtract_fusion.refs_0_.filtered), channel_id=1, source_target_pairs={{0,1},{1,0},{2,3},{3,2},{4,5},{5,4},{6,7},{7,6},{8,9},{9,8},{10,11... | collective-permute-start | bytes 196616 | tf_op jit(solution)/shard_map/ppermute | solution.py:167
  60.2 7.4 %collective-permute-start.33 = (f32[32,512]{1,0:T(8,128)S(1)}, f32[32,512]{1,0:T(8,128)S(1)}, u32[]{:S(2)}, u32[]{:S(2)}) collective-permute-start(f32[32,512]{1,0:T(8,128)S(1)} %multiply_subtract_fusion.refs_0_.filtered), channel_id=1, source_target_pairs={{0,16},{4,20},{8,24},{12,28},{16,0},{20,4},{24,8},{28,12},{1,17},{... | collective-permute-start | bytes 196616 | tf_op jit(solution)/shard_map/ppermute | solution.py:167
  60.7 6.9 %collective-permute-start.38 = (f32[32,512]{1,0:T(8,128)S(1)}, f32[32,512]{1,0:T(8,128)S(1)}, u32[]{:S(2)}, u32[]{:S(2)}) collective-permute-start(f32[32,512]{1,0:T(8,128)S(1)} %multiply_subtract_fusion.refs_0_.filtered), channel_id=1, source_target_pairs={{0,24},{4,28},{8,16},{12,20},{16,8},{20,12},{24,0},{28,4},{1,25},{... | collective-permute-start | bytes 196616 | tf_op jit(solution)/shard_map/ppermute | solution.py:167
  62.6 5.4 %collective-permute-start.35 = (f32[32,512]{1,0:T(8,128)S(1)}, f32[32,512]{1,0:T(8,128)S(1)}, u32[]{:S(2)}, u32[]{:S(2)}) collective-permute-start(f32[32,512]{1,0:T(8,128)S(1)} %multiply_subtract_fusion.refs_0_.filtered), channel_id=1, source_target_pairs={{0,2},{1,3},{2,0},{3,1},{4,6},{5,7},{6,4},{7,5},{8,10},{9,11},{10,... | collective-permute-start | bytes 196616 | tf_op jit(solution)/shard_map/ppermute | solution.py:167
  63.6 4.6 %collective-permute-start.31 = (f32[32,512]{1,0:T(8,128)S(1)}, f32[32,512]{1,0:T(8,128)S(1)}, u32[]{:S(2)}, u32[]{:S(2)}) collective-permute-start(f32[32,512]{1,0:T(8,128)S(1)} %multiply_subtract_fusion.refs_0_.filtered), channel_id=1, source_target_pairs={{0,8},{4,12},{8,0},{12,4},{16,24},{20,28},{24,16},{28,20},{1,9},{5... | collective-permute-start | bytes 196616 | tf_op jit(solution)/shard_map/ppermute | solution.py:167
  64.8 4.3 %collective-permute-start.36 = (f32[32,512]{1,0:T(8,128)S(1)}, f32[32,512]{1,0:T(8,128)S(1)}, u32[]{:S(2)}, u32[]{:S(2)}) collective-permute-start(f32[32,512]{1,0:T(8,128)S(1)} %collective-permute-done.34.refs_8_), channel_id=1, source_target_pairs={{0,2},{1,3},{2,0},{3,1},{4,6},{5,7},{6,4},{7,5},{8,10},{9,11},{10,... | collective-permute-start | bytes 196616 | tf_op jit(solution)/shard_map/ppermute | solution.py:167
  67.6 1.5 %collective-permute-start.37 = (f32[32,512]{1,0:T(8,128)S(1)}, f32[32,512]{1,0:T(8,128)S(1)}, u32[]{:S(2)}, u32[]{:S(2)}) collective-permute-start(f32[32,512]{1,0:T(8,128)S(1)} %collective-permute-done.33.refs_4_), channel_id=1, source_target_pairs={{0,4},{4,0},{8,12},{12,8},{16,20},{20,16},{24,28},{28,24},{1,5},{5... | collective-permute-start | bytes 196616 | tf_op jit(solution)/shard_map/ppermute | solution.py:167
  67.6 1.5 %collective-permute-start.30 = (f32[32,512]{1,0:T(8,128)S(1)}, f32[32,512]{1,0:T(8,128)S(1)}, u32[]{:S(2)}, u32[]{:S(2)}) collective-permute-start(f32[32,512]{1,0:T(8,128)S(1)} %multiply_subtract_fusion.refs_0_.filtered), channel_id=1, source_target_pairs={{0,4},{4,0},{8,12},{12,8},{16,20},{20,16},{24,28},{28,24},{1,5},{5... | collective-permute-start | bytes 196616 | tf_op jit(solution)/shard_map/ppermute | solution.py:167
  68.1 1.3 %collective-permute-start.39 = (f32[32,512]{1,0:T(8,128)S(1)}, f32[32,512]{1,0:T(8,128)S(1)}, u32[]{:S(2)}, u32[]{:S(2)}) collective-permute-start(f32[32,512]{1,0:T(8,128)S(1)} %collective-permute-done.38.refs_6_), channel_id=1, source_target_pairs={{0,4},{4,0},{8,12},{12,8},{16,20},{20,16},{24,28},{28,24},{1,5},{5... | collective-permute-start | bytes 196616 | tf_op jit(solution)/shard_map/ppermute | solution.py:167
  68.2 1.3 %collective-permute-start.32 = (f32[32,512]{1,0:T(8,128)S(1)}, f32[32,512]{1,0:T(8,128)S(1)}, u32[]{:S(2)}, u32[]{:S(2)}) collective-permute-start(f32[32,512]{1,0:T(8,128)S(1)} %collective-permute-done.31.refs_2_), channel_id=1, source_target_pairs={{0,4},{4,0},{8,12},{12,8},{16,20},{20,16},{24,28},{28,24},{1,5},{5... | collective-permute-start | bytes 196616 | tf_op jit(solution)/shard_map/ppermute | solution.py:167
  71.5 4.7 %collective-permute-start.42 = (f32[32,64]{1,0:T(8,128)S(1)}, f32[32,64]{1,0:T(8,128)S(1)}, u32[]{:S(2)}, u32[]{:S(2)}) collective-permute-start(f32[32,64]{1,0:T(8,128)S(1)} %moment.1), channel_id=1, source_target_pairs={{0,3},{1,2},{2,1},{3,0},{4,7},{5,6},{6,5},{7,4},{8,11},{9,10},{10,... | collective-permute-start | bytes 24584 | tf_op jit(solution)/shard_map/ppermute | solution.py:167
  73.2 3.7 %collective-permute-start.41 = (f32[32,64]{1,0:T(8,128)S(1)}, f32[32,64]{1,0:T(8,128)S(1)}, u32[]{:S(2)}, u32[]{:S(2)}) collective-permute-start(f32[32,64]{1,0:T(8,128)S(1)} %moment.1), channel_id=1, source_target_pairs={{0,2},{1,3},{2,0},{3,1},{4,6},{5,7},{6,4},{7,5},{8,10},{9,11},{10,... | collective-permute-start | bytes 24584 | tf_op jit(solution)/shard_map/ppermute | solution.py:167
  74.0 3.7 %collective-permute-start.40 = (f32[32,64]{1,0:T(8,128)S(1)}, f32[32,64]{1,0:T(8,128)S(1)}, u32[]{:S(2)}, u32[]{:S(2)}) collective-permute-start(f32[32,64]{1,0:T(8,128)S(1)} %moment.1), channel_id=1, source_target_pairs={{0,1},{1,0},{2,3},{3,2},{4,5},{5,4},{6,7},{7,6},{8,9},{9,8},{10,11... | collective-permute-start | bytes 24584 | tf_op jit(solution)/shard_map/ppermute | solution.py:167
  77.7 6.1 %collective-permute-start.45 = (f32[32,64]{1,0:T(8,128)S(1)}, f32[32,64]{1,0:T(8,128)S(1)}, u32[]{:S(2)}, u32[]{:S(2)}) collective-permute-start(f32[32,64]{1,0:T(8,128)S(1)} %add_add_fusion.1.sums), channel_id=1, source_target_pairs={{0,24},{4,28},{8,16},{12,20},{16,8},{20,12},{24,0},{28,4},{1,25},{... | collective-permute-start | bytes 24584 | tf_op jit(solution)/shard_map/ppermute | solution.py:167
  79.9 4.6 %collective-permute-start.44 = (f32[32,64]{1,0:T(8,128)S(1)}, f32[32,64]{1,0:T(8,128)S(1)}, u32[]{:S(2)}, u32[]{:S(2)}) collective-permute-start(f32[32,64]{1,0:T(8,128)S(1)} %add_add_fusion.1.sums), channel_id=1, source_target_pairs={{0,16},{4,20},{8,24},{12,28},{16,0},{20,4},{24,8},{28,12},{1,17},{... | collective-permute-start | bytes 24584 | tf_op jit(solution)/shard_map/ppermute | solution.py:167
  80.3 4.2 %collective-permute-start.43 = (f32[32,64]{1,0:T(8,128)S(1)}, f32[32,64]{1,0:T(8,128)S(1)}, u32[]{:S(2)}, u32[]{:S(2)}) collective-permute-start(f32[32,64]{1,0:T(8,128)S(1)} %add_add_fusion.1.sums), channel_id=1, source_target_pairs={{0,8},{4,12},{8,0},{12,4},{16,24},{20,28},{24,16},{28,20},{1,9},{5... | collective-permute-start | bytes 24584 | tf_op jit(solution)/shard_map/ppermute | solution.py:167
  84.5 1.2 %collective-permute-start.46 = (f32[32,64]{1,0:T(8,128)S(1)}, f32[32,64]{1,0:T(8,128)S(1)}, u32[]{:S(2)}, u32[]{:S(2)}) collective-permute-start(f32[32,64]{1,0:T(8,128)S(1)} %add_add_fusion), channel_id=1, source_target_pairs={{0,4},{4,0},{8,12},{12,8},{16,20},{20,16},{24,28},{28,24},{1,5},{5... | collective-permute-start | bytes 24584 | tf_op jit(solution)/shard_map/ppermute | solution.py:167
  (3 other events, 29.7 us)

commit v7 on v6

--- a/solution.py
+++ b/solution.py
@@ -99,7 +99,9 @@
         return both[:, :subspace] + both[:, subspace:]
 
     own = parts[0][...]
-    moment = dot_rows(own, own * degrees[...], lax.Precision.HIGHEST)
+    moment = quarters(
+        jnp.concatenate(split(own), 0), jnp.concatenate(split(own * degrees[...]), 0)
+    )
     gram = jnp.zeros_like(moment)
     for part in parts:
         both = jnp.concatenate(split(part[...]), 0)

time: 87.1 us -> 87.1 us (level)
  transfers between devices with their start and end apart: 47 -> 47, of which waited for: 29 -> 28; matrix products, arithmetic and copies ran while one was open for 0% -> 0% of each run, Pallas kernels for 7% -> 7%
where the time goes in v7:
time: 87.1 us; the launch traced here: 86.9 us
  starting transfers between devices  42.5 us (49%)
  waiting for transfers between devices  29.5 us (34%)
  Pallas kernels  13.3 us (15%)
  between operations  1.44 us (2%)
    ppermute x47, starting transfers between devices, swap(): return lax.ppermute(value, axis, [(i, i ^ distance) for i in range(size)])  42.5 us
    ppermute x47, waiting for transfers between devices, swap(): return lax.ppermute(value, axis, [(i, i ^ distance) for i in range(size)])  29.5 us
    pallas_call x4, Pallas kernels, products(): pl.pallas_call(functools.partial(product_kernel, n_row, n_col), out_shape...  5.72 us
    pallas_call x1, Pallas kernels, body(): pl.pallas_call(stage_kernel, out_shape=[jax.ShapeDtypeStruct(tiles.shape,...  4.1 us
  transfers between devices with their start and end apart: 47, of which 28 were waited for; matrix products, arithmetic and copies ran while one was open for 0% of the time, Pallas kernels for 7%

profile of v7, /device:TPU:0, one launch (start us, length us, event | category | flops | bytes accessed | tf_op | source)
XLA Modules:
  0.0 86.9 jit_solution(4550737984533708977)
XLA Ops:
  0.7 5.1 %collective-permute-start.2 = (f32[32,512]{1,0:T(8,128)}, f32[32,512]{1,0:T(8,128)S(1)}, u32[]{:S(2)}, u32[]{:S(2)}) collective-permute-start(f32[32,512]{1,0:T(8,128)} %refs_0_.1), channel_id=1, source_target_pairs={{0,24},{4,28},{8,16},{12,20},{16,8},{20,12},{24,0},{28,4},{1,25},{... | collective-permute-start | bytes 196616 | tf_op jit(solution)/shard_map/ppermute | solution.py:169
  5.8 0.6 collective-permute-start
  6.4 4.1 %stage.1 = (bf16[32,256,256]{2,1,0:T(8,128)(2,1)S(1)}, bf16[32,256,256]{2,1,0:T(8,128)(2,1)S(1)}) custom-call(f32[32,256,256]{2,1,0:T(8,128)} %tiles.1), custom_call_target="tpu_custom_call" | custom-call | tf_op jit(solution)/shard_map/stage/pallas_call | solution.py:198
  10.5 1.1 %collective-permute-done.1.refs_4_ = f32[32,512]{1,0:T(8,128)S(1)} collective-permute-done((f32[32,512]{1,0:T(8,128)}, f32[32,512]{1,0:T(8,128)S(1)}, u32[]{:S(2)}, u32[]{:S(2)}) %collective-permute-start.1) | collective-permute-done | bytes 65568 | tf_op jit(solution)/shard_map/ppermute | solution.py:169
  13.4 1.4 %tile_products.4 = (f32[32,512]{1,0:T(8,128)S(1)}, f32[32,512]{1,0:T(8,128)S(1)}, f32[32,512]{1,0:T(8,128)S(1)}, f32[32,512]{1,0:T(8,128)S(1)}) custom-call(s32[2,32]{1,0:T(2,128)S(1)} %places.1.slots, bf16[32,256,256]{2,1,0:T(8,128)(2,1)S(1)} %get-tuple-element.41.high, bf16[32,256,256]{2,1,0:T(8,128)(2,1)S(1)} %get-tuple-element.42.low, ...), custom_call_target="tpu_custom_call" | custom-call | tf_op jit(solution)/shard_map/tile_products/pallas_call | solution.py:223
  14.8 2.5 %collective-permute-start.7 = (f32[32,512]{1,0:T(8,128)S(1)}, f32[32,512]{1,0:T(8,128)S(1)}, u32[]{:S(2)}, u32[]{:S(2)}) collective-permute-start(f32[32,512]{1,0:T(8,128)S(1)} %get-tuple-element.47), channel_id=1, source_target_pairs={{0,3},{1,2},{2,1},{3,0},{4,7},{5,6},{6,5},{7,4},{8,11},{9,10},{10,... | collective-permute-start | bytes 196616 | tf_op jit(solution)/shard_map/ppermute | solution.py:169
  18.4 1.7 %collective-permute-done.7 = f32[32,512]{1,0:T(8,128)S(1)} collective-permute-done((f32[32,512]{1,0:T(8,128)S(1)}, f32[32,512]{1,0:T(8,128)S(1)}, u32[]{:S(2)}, u32[]{:S(2)}) %collective-permute-start.7) | collective-permute-done | bytes 65568 | tf_op jit(solution)/shard_map/ppermute | solution.py:169
  20.1 1.5 %collective-permute-done.8 = f32[32,512]{1,0:T(8,128)S(1)} collective-permute-done((f32[32,512]{1,0:T(8,128)S(1)}, f32[32,512]{1,0:T(8,128)S(1)}, u32[]{:S(2)}, u32[]{:S(2)}) %collective-permute-start.8) | collective-permute-done | bytes 65568 | tf_op jit(solution)/shard_map/ppermute | solution.py:169
  22.1 3.0 %collective-permute-start.15 = (f32[32,512]{1,0:T(8,128)S(1)}, f32[32,512]{1,0:T(8,128)S(1)}, u32[]{:S(2)}, u32[]{:S(2)}) collective-permute-start(f32[32,512]{1,0:T(8,128)S(1)} %get-tuple-element.72.refs_0_), channel_id=1, source_target_pairs={{0,24},{4,28},{8,16},{12,20},{16,8},{20,12},{24,0},{28,4},{1,25},{... | collective-permute-start | bytes 196616 | tf_op jit(solution)/shard_map/ppermute | solution.py:169
  25.1 1.5 %collective-permute-start.11 = (f32[32,512]{1,0:T(8,128)S(1)}, f32[32,512]{1,0:T(8,128)S(1)}, u32[]{:S(2)}, u32[]{:S(2)}) collective-permute-start(f32[32,512]{1,0:T(8,128)S(1)} %get-tuple-element.72.refs_0_), channel_id=1, source_target_pairs={{0,8},{4,12},{8,0},{12,4},{16,24},{20,28},{24,16},{28,20},{1,9},{5... | collective-permute-start | bytes 196616 | tf_op jit(solution)/shard_map/ppermute | solution.py:169
  26.6 1.8 %collective-permute-done.15.refs_6_ = f32[32,512]{1,0:T(8,128)S(1)} collective-permute-done((f32[32,512]{1,0:T(8,128)S(1)}, f32[32,512]{1,0:T(8,128)S(1)}, u32[]{:S(2)}, u32[]{:S(2)}) %collective-permute-start.15) | collective-permute-done | bytes 65568 | tf_op jit(solution)/shard_map/ppermute | solution.py:169
  28.4 2.0 %collective-permute-done.13.refs_4_ = f32[32,512]{1,0:T(8,128)S(1)} collective-permute-done((f32[32,512]{1,0:T(8,128)S(1)}, f32[32,512]{1,0:T(8,128)S(1)}, u32[]{:S(2)}, u32[]{:S(2)}) %collective-permute-start.13) | collective-permute-done | bytes 65568 | tf_op jit(solution)/shard_map/ppermute | solution.py:169
  30.9 0.7 collective-permute-done.14.refs_5_
  31.8 1.4 %tile_products.5 = (f32[32,512]{1,0:T(8,128)S(1)}, f32[32,512]{1,0:T(8,128)S(1)}, f32[32,512]{1,0:T(8,128)S(1)}, f32[32,512]{1,0:T(8,128)S(1)}) custom-call(s32[2,32]{1,0:T(2,128)S(1)} %places.1.slots, bf16[32,256,256]{2,1,0:T(8,128)(2,1)S(1)} %get-tuple-element.41.high, bf16[32,256,256]{2,1,0:T(8,128)(2,1)S(1)} %get-tuple-element.42.low, ...), custom_call_target="tpu_custom_call" | custom-call | tf_op jit(solution)/shard_map/tile_products/pallas_call | solution.py:223
  33.2 1.6 %collective-permute-start.17 = (f32[32,512]{1,0:T(8,128)S(1)}, f32[32,512]{1,0:T(8,128)S(1)}, u32[]{:S(2)}, u32[]{:S(2)}) collective-permute-start(f32[32,512]{1,0:T(8,128)S(1)} %get-tuple-element.51), channel_id=1, source_target_pairs={{0,3},{1,2},{2,1},{3,0},{4,7},{5,6},{6,5},{7,4},{8,11},{9,10},{10,... | collective-permute-start | bytes 196616 | tf_op jit(solution)/shard_map/ppermute | solution.py:169
  34.8 1.5 %collective-permute-start.18 = (f32[32,512]{1,0:T(8,128)S(1)}, f32[32,512]{1,0:T(8,128)S(1)}, u32[]{:S(2)}, u32[]{:S(2)}) collective-permute-start(f32[32,512]{1,0:T(8,128)S(1)} %get-tuple-element.52), channel_id=1, source_target_pairs={{0,2},{1,3},{2,0},{3,1},{4,6},{5,7},{6,4},{7,5},{8,10},{9,11},{10,... | collective-permute-start | bytes 196616 | tf_op jit(solution)/shard_map/ppermute | solution.py:169
  36.8 1.9 %collective-permute-done.17 = f32[32,512]{1,0:T(8,128)S(1)} collective-permute-done((f32[32,512]{1,0:T(8,128)S(1)}, f32[32,512]{1,0:T(8,128)S(1)}, u32[]{:S(2)}, u32[]{:S(2)}) %collective-permute-start.17) | collective-permute-done | bytes 65568 | tf_op jit(solution)/shard_map/ppermute | solution.py:169
  38.7 1.3 %collective-permute-done.18 = f32[32,512]{1,0:T(8,128)S(1)} collective-permute-done((f32[32,512]{1,0:T(8,128)S(1)}, f32[32,512]{1,0:T(8,128)S(1)}, u32[]{:S(2)}, u32[]{:S(2)}) %collective-permute-start.18) | collective-permute-done | bytes 65568 | tf_op jit(solution)/shard_map/ppermute | solution.py:169
  40.0 0.7 collective-permute-done.19
  40.7 2.2 %collective-permute-start.25 = (f32[32,512]{1,0:T(8,128)S(1)}, f32[32,512]{1,0:T(8,128)S(1)}, u32[]{:S(2)}, u32[]{:S(2)}) collective-permute-start(f32[32,512]{1,0:T(8,128)S(1)} %multiply_subtract_fusion.1.refs_0_), channel_id=1, source_target_pairs={{0,24},{4,28},{8,16},{12,20},{16,8},{20,12},{24,0},{28,4},{1,25},{... | collective-permute-start | bytes 196616 | tf_op jit(solution)/shard_map/ppermute | solution.py:169
  43.0 2.1 %collective-permute-start.21 = (f32[32,512]{1,0:T(8,128)S(1)}, f32[32,512]{1,0:T(8,128)S(1)}, u32[]{:S(2)}, u32[]{:S(2)}) collective-permute-start(f32[32,512]{1,0:T(8,128)S(1)} %multiply_subtract_fusion.1.refs_0_), channel_id=1, source_target_pairs={{0,8},{4,12},{8,0},{12,4},{16,24},{20,28},{24,16},{28,20},{1,9},{5... | collective-permute-start | bytes 196616 | tf_op jit(solution)/shard_map/ppermute | solution.py:169
  45.1 1.7 %collective-permute-done.25.refs_6_ = f32[32,512]{1,0:T(8,128)S(1)} collective-permute-done((f32[32,512]{1,0:T(8,128)S(1)}, f32[32,512]{1,0:T(8,128)S(1)}, u32[]{:S(2)}, u32[]{:S(2)}) %collective-permute-start.25) | collective-permute-done | bytes 65568 | tf_op jit(solution)/shard_map/ppermute | solution.py:169
  46.8 2.5 %collective-permute-done.23.refs_4_ = f32[32,512]{1,0:T(8,128)S(1)} collective-permute-done((f32[32,512]{1,0:T(8,128)S(1)}, f32[32,512]{1,0:T(8,128)S(1)}, u32[]{:S(2)}, u32[]{:S(2)}) %collective-permute-start.23) | collective-permute-done | bytes 65568 | tf_op jit(solution)/shard_map/ppermute | solution.py:169
  49.9 0.7 collective-permute-done.24.refs_5_
  50.8 1.4 %tile_products.6 = (f32[32,512]{1,0:T(8,128)S(1)}, f32[32,512]{1,0:T(8,128)S(1)}, f32[32,512]{1,0:T(8,128)S(1)}, f32[32,512]{1,0:T(8,128)S(1)}) custom-call(s32[2,32]{1,0:T(2,128)S(1)} %places.1.slots, bf16[32,256,256]{2,1,0:T(8,128)(2,1)S(1)} %get-tuple-element.41.high, bf16[32,256,256]{2,1,0:T(8,128)(2,1)S(1)} %get-tuple-element.42.low, ...), custom_call_target="tpu_custom_call" | custom-call | tf_op jit(solution)/shard_map/tile_products/pallas_call | solution.py:223
  52.2 1.6 %collective-permute-start.27 = (f32[32,512]{1,0:T(8,128)S(1)}, f32[32,512]{1,0:T(8,128)S(1)}, u32[]{:S(2)}, u32[]{:S(2)}) collective-permute-start(f32[32,512]{1,0:T(8,128)S(1)} %get-tuple-element.55), channel_id=1, source_target_pairs={{0,3},{1,2},{2,1},{3,0},{4,7},{5,6},{6,5},{7,4},{8,11},{9,10},{10,... | collective-permute-start | bytes 196616 | tf_op jit(solution)/shard_map/ppermute | solution.py:169
  53.8 0.8 collective-permute-start.28
  54.6 1.2 %collective-permute-start.29 = (f32[32,512]{1,0:T(8,128)S(1)}, f32[32,512]{1,0:T(8,128)S(1)}, u32[]{:S(2)}, u32[]{:S(2)}) collective-permute-start(f32[32,512]{1,0:T(8,128)S(1)} %get-tuple-element.57), channel_id=1, source_target_pairs={{0,1},{1,0},{2,3},{3,2},{4,5},{5,4},{6,7},{7,6},{8,9},{9,8},{10,11... | collective-permute-start | bytes 196616 | tf_op jit(solution)/shard_map/ppermute | solution.py:169
  55.8 1.9 %collective-permute-done.27 = f32[32,512]{1,0:T(8,128)S(1)} collective-permute-done((f32[32,512]{1,0:T(8,128)S(1)}, f32[32,512]{1,0:T(8,128)S(1)}, u32[]{:S(2)}, u32[]{:S(2)}) %collective-permute-start.27) | collective-permute-done | bytes 65568 | tf_op jit(solution)/shard_map/ppermute | solution.py:169
  57.7 1.3 %collective-permute-done.28 = f32[32,512]{1,0:T(8,128)S(1)} collective-permute-done((f32[32,512]{1,0:T(8,128)S(1)}, f32[32,512]{1,0:T(8,128)S(1)}, u32[]{:S(2)}, u32[]{:S(2)}) %collective-permute-start.28) | collective-permute-done | bytes 65568 | tf_op jit(solution)/shard_map/ppermute | solution.py:169
  59.0 1.2 %collective-permute-start.34 = (f32[32,512]{1,0:T(8,128)S(1)}, f32[32,512]{1,0:T(8,128)S(1)}, u32[]{:S(2)}, u32[]{:S(2)}) collective-permute-start(f32[32,512]{1,0:T(8,128)S(1)} %multiply_subtract_fusion.refs_0_.filtered), channel_id=1, source_target_pairs={{0,1},{1,0},{2,3},{3,2},{4,5},{5,4},{6,7},{7,6},{8,9},{9,8},{10,11... | collective-permute-start | bytes 196616 | tf_op jit(solution)/shard_map/ppermute | solution.py:169
  60.7 1.9 %collective-permute-start.38 = (f32[32,512]{1,0:T(8,128)S(1)}, f32[32,512]{1,0:T(8,128)S(1)}, u32[]{:S(2)}, u32[]{:S(2)}) collective-permute-start(f32[32,512]{1,0:T(8,128)S(1)} %multiply_subtract_fusion.refs_0_.filtered), channel_id=1, source_target_pairs={{0,24},{4,28},{8,16},{12,20},{16,8},{20,12},{24,0},{28,4},{1,25},{... | collective-permute-start | bytes 196616 | tf_op jit(solution)/shard_map/ppermute | solution.py:169
  62.6 1.0 %collective-permute-start.35 = (f32[32,512]{1,0:T(8,128)S(1)}, f32[32,512]{1,0:T(8,128)S(1)}, u32[]{:S(2)}, u32[]{:S(2)}) collective-permute-start(f32[32,512]{1,0:T(8,128)S(1)} %multiply_subtract_fusion.refs_0_.filtered), channel_id=1, source_target_pairs={{0,2},{1,3},{2,0},{3,1},{4,6},{5,7},{6,4},{7,5},{8,10},{9,11},{10,... | collective-permute-start | bytes 196616 | tf_op jit(solution)/shard_map/ppermute | solution.py:169
  63.6 1.1 %collective-permute-start.31 = (f32[32,512]{1,0:T(8,128)S(1)}, f32[32,512]{1,0:T(8,128)S(1)}, u32[]{:S(2)}, u32[]{:S(2)}) collective-permute-start(f32[32,512]{1,0:T(8,128)S(1)} %multiply_subtract_fusion.refs_0_.filtered), channel_id=1, source_target_pairs={{0,8},{4,12},{8,0},{12,4},{16,24},{20,28},{24,16},{28,20},{1,9},{5... | collective-permute-start | bytes 196616 | tf_op jit(solution)/shard_map/ppermute | solution.py:169
  64.8 0.9 %collective-permute-start.36 = (f32[32,512]{1,0:T(8,128)S(1)}, f32[32,512]{1,0:T(8,128)S(1)}, u32[]{:S(2)}, u32[]{:S(2)}) collective-permute-start(f32[32,512]{1,0:T(8,128)S(1)} %collective-permute-done.34.refs_8_), channel_id=1, source_target_pairs={{0,2},{1,3},{2,0},{3,1},{4,6},{5,7},{6,4},{7,5},{8,10},{9,11},{10,... | collective-permute-start | bytes 196616 | tf_op jit(solution)/shard_map/ppermute | solution.py:169
  65.7 1.9 %collective-permute-done.33.refs_4_ = f32[32,512]{1,0:T(8,128)S(1)} collective-permute-done((f32[32,512]{1,0:T(8,128)S(1)}, f32[32,512]{1,0:T(8,128)S(1)}, u32[]{:S(2)}, u32[]{:S(2)}) %collective-permute-start.33) | collective-permute-done | bytes 65568 | tf_op jit(solution)/shard_map/ppermute | solution.py:169
  69.5 1.4 %tile_products.7 = (f32[32,512]{1,0:T(8,128)S(1)}, f32[32,512]{1,0:T(8,128)S(1)}, f32[32,512]{1,0:T(8,128)S(1)}, f32[32,512]{1,0:T(8,128)S(1)}) custom-call(s32[2,32]{1,0:T(2,128)S(1)} %places.1.slots, bf16[32,256,256]{2,1,0:T(8,128)(2,1)S(1)} %get-tuple-element.41.high, bf16[32,256,256]{2,1,0:T(8,128)(2,1)S(1)} %get-tuple-element.42.low, ...), custom_call_target="tpu_custom_call" | custom-call | tf_op jit(solution)/shard_map/tile_products/pallas_call | solution.py:223
  71.5 1.7 %collective-permute-start.42 = (f32[32,64]{1,0:T(8,128)S(1)}, f32[32,64]{1,0:T(8,128)S(1)}, u32[]{:S(2)}, u32[]{:S(2)}) collective-permute-start(f32[32,64]{1,0:T(8,128)S(1)} %moment.1), channel_id=1, source_target_pairs={{0,3},{1,2},{2,1},{3,0},{4,7},{5,6},{6,5},{7,4},{8,11},{9,10},{10,... | collective-permute-start | bytes 24584 | tf_op jit(solution)/shard_map/ppermute | solution.py:169
  73.1 0.8 collective-permute-start.41
  74.0 1.0 %collective-permute-start.40 = (f32[32,64]{1,0:T(8,128)S(1)}, f32[32,64]{1,0:T(8,128)S(1)}, u32[]{:S(2)}, u32[]{:S(2)}) collective-permute-start(f32[32,64]{1,0:T(8,128)S(1)} %moment.1), channel_id=1, source_target_pairs={{0,1},{1,0},{2,3},{3,2},{4,5},{5,4},{6,7},{7,6},{8,9},{9,8},{10,11... | collective-permute-start | bytes 24584 | tf_op jit(solution)/shard_map/ppermute | solution.py:169
  75.0 1.1 %collective-permute-done.42 = f32[32,64]{1,0:T(8,128)S(1)} collective-permute-done((f32[32,64]{1,0:T(8,128)S(1)}, f32[32,64]{1,0:T(8,128)S(1)}, u32[]{:S(2)}, u32[]{:S(2)}) %collective-permute-start.42) | collective-permute-done | bytes 8224 | tf_op jit(solution)/shard_map/ppermute | solution.py:169
  76.2 0.7 collective-permute-done.41
  76.9 0.8 collective-permute-done.40
  77.7 2.1 %collective-permute-start.45 = (f32[32,64]{1,0:T(8,128)S(1)}, f32[32,64]{1,0:T(8,128)S(1)}, u32[]{:S(2)}, u32[]{:S(2)}) collective-permute-start(f32[32,64]{1,0:T(8,128)S(1)} %add_add_fusion.1.sums), channel_id=1, source_target_pairs={{0,24},{4,28},{8,16},{12,20},{16,8},{20,12},{24,0},{28,4},{1,25},{... | collective-permute-start | bytes 24584 | tf_op jit(solution)/shard_map/ppermute | solution.py:169
  80.3 1.8 %collective-permute-start.43 = (f32[32,64]{1,0:T(8,128)S(1)}, f32[32,64]{1,0:T(8,128)S(1)}, u32[]{:S(2)}, u32[]{:S(2)}) collective-permute-start(f32[32,64]{1,0:T(8,128)S(1)} %add_add_fusion.1.sums), channel_id=1, source_target_pairs={{0,8},{4,12},{8,0},{12,4},{16,24},{20,28},{24,16},{28,20},{1,9},{5... | collective-permute-start | bytes 24584 | tf_op jit(solution)/shard_map/ppermute | solution.py:169
  82.1 1.7 %factor.1 = (f32[32,32]{1,0:T(8,128)S(1)}, f32[32,512]{1,0:T(8,128)}) custom-call(f32[32,64]{1,0:T(8,128)S(1)} %add_add_fusion.1.sums, f32[32,512]{1,0:T(8,128)S(1)} %multiply_subtract_fusion.refs_0_.filtered), custom_call_target="tpu_custom_call" | custom-call | tf_op jit(solution)/shard_map/factor/pallas_call | solution.py:264
  84.6 1.2 %collective-permute-done.46 = f32[32,64]{1,0:T(8,128)S(1)} collective-permute-done((f32[32,64]{1,0:T(8,128)S(1)}, f32[32,64]{1,0:T(8,128)S(1)}, u32[]{:S(2)}, u32[]{:S(2)}) %collective-permute-start.46) | collective-permute-done | bytes 8224 | tf_op jit(solution)/shard_map/ppermute | solution.py:169
  85.7 1.2 %project.1 = f32[32,32]{1,0:T(8,128)} custom-call(f32[32,64]{1,0:T(8,128)S(1)} %add.65.sums, f32[32,32]{1,0:T(8,128)S(1)} %get-tuple-element.71.inverse), custom_call_target="tpu_custom_call" | custom-call | tf_op jit(solution)/shard_map/project/pallas_call | solution.py:276
  (70 shorter events, 8.8 us)
Async XLA Ops:
  0.6 12.7 %copy-start = (f32[32,512]{1,0:T(8,128)S(1)}, f32[32,512]{1,0:T(8,128)}, u32[]{:S(2)}) copy-start(f32[32,512]{1,0:T(8,128)} %refs_0_.1) | copy-start | bytes 196612
  0.7 9.9 %collective-permute-start.2 = (f32[32,512]{1,0:T(8,128)}, f32[32,512]{1,0:T(8,128)S(1)}, u32[]{:S(2)}, u32[]{:S(2)}) collective-permute-start(f32[32,512]{1,0:T(8,128)} %refs_0_.1), channel_id=1, source_target_pairs={{0,24},{4,28},{8,16},{12,20},{16,8},{20,12},{24,0},{28,4},{1,25},{... | collective-permute-start | bytes 196616 | tf_op jit(solution)/shard_map/ppermute | solution.py:169
  5.8 5.8 %collective-permute-start.1 = (f32[32,512]{1,0:T(8,128)}, f32[32,512]{1,0:T(8,128)S(1)}, u32[]{:S(2)}, u32[]{:S(2)}) collective-permute-start(f32[32,512]{1,0:T(8,128)} %refs_0_.1), channel_id=1, source_target_pairs={{0,16},{4,20},{8,24},{12,28},{16,0},{20,4},{24,8},{28,12},{1,17},{... | collective-permute-start | bytes 196616 | tf_op jit(solution)/shard_map/ppermute | solution.py:169
  5.8 5.8 %collective-permute-start = (f32[32,512]{1,0:T(8,128)}, f32[32,512]{1,0:T(8,128)S(1)}, u32[]{:S(2)}, u32[]{:S(2)}) collective-permute-start(f32[32,512]{1,0:T(8,128)} %refs_0_.1), channel_id=1, source_target_pairs={{0,8},{4,12},{8,0},{12,4},{16,24},{20,28},{24,16},{28,20},{1,9},{5... | collective-permute-start | bytes 196616 | tf_op jit(solution)/shard_map/ppermute | solution.py:169
  6.4 6.4 %collective-permute-start.3 = (f32[32,512]{1,0:T(8,128)}, f32[32,512]{1,0:T(8,128)S(1)}, u32[]{:S(2)}, u32[]{:S(2)}) collective-permute-start(f32[32,512]{1,0:T(8,128)} %refs_0_.1), channel_id=1, source_target_pairs={{0,4},{4,0},{8,12},{12,8},{16,20},{20,16},{24,28},{28,24},{1,5},{5... | collective-permute-start | bytes 196616 | tf_op jit(solution)/shard_map/ppermute | solution.py:169
  11.6 1.3 %collective-permute-start.4 = (f32[32,512]{1,0:T(8,128)S(1)}, f32[32,512]{1,0:T(8,128)S(1)}, u32[]{:S(2)}, u32[]{:S(2)}) collective-permute-start(f32[32,512]{1,0:T(8,128)S(1)} %collective-permute-done.refs_2_), channel_id=1, source_target_pairs={{0,4},{4,0},{8,12},{12,8},{16,20},{20,16},{24,28},{28,24},{1,5},{5... | collective-permute-start | bytes 196616 | tf_op jit(solution)/shard_map/ppermute | solution.py:169
  11.6 1.4 %collective-permute-start.5 = (f32[32,512]{1,0:T(8,128)S(1)}, f32[32,512]{1,0:T(8,128)S(1)}, u32[]{:S(2)}, u32[]{:S(2)}) collective-permute-start(f32[32,512]{1,0:T(8,128)S(1)} %collective-permute-done.1.refs_4_), channel_id=1, source_target_pairs={{0,4},{4,0},{8,12},{12,8},{16,20},{20,16},{24,28},{28,24},{1,5},{5... | collective-permute-start | bytes 196616 | tf_op jit(solution)/shard_map/ppermute | solution.py:169
  12.1 1.3 %collective-permute-start.6 = (f32[32,512]{1,0:T(8,128)S(1)}, f32[32,512]{1,0:T(8,128)S(1)}, u32[]{:S(2)}, u32[]{:S(2)}) collective-permute-start(f32[32,512]{1,0:T(8,128)S(1)} %collective-permute-done.2.refs_6_), channel_id=1, source_target_pairs={{0,4},{4,0},{8,12},{12,8},{16,20},{20,16},{24,28},{28,24},{1,5},{5... | collective-permute-start | bytes 196616 | tf_op jit(solution)/shard_map/ppermute | solution.py:169
  14.8 5.3 %collective-permute-start.7 = (f32[32,512]{1,0:T(8,128)S(1)}, f32[32,512]{1,0:T(8,128)S(1)}, u32[]{:S(2)}, u32[]{:S(2)}) collective-permute-start(f32[32,512]{1,0:T(8,128)S(1)} %get-tuple-element.47), channel_id=1, source_target_pairs={{0,3},{1,2},{2,1},{3,0},{4,7},{5,6},{6,5},{7,4},{8,11},{9,10},{10,... | collective-permute-start | bytes 196616 | tf_op jit(solution)/shard_map/ppermute | solution.py:169
  17.3 4.3 %collective-permute-start.8 = (f32[32,512]{1,0:T(8,128)S(1)}, f32[32,512]{1,0:T(8,128)S(1)}, u32[]{:S(2)}, u32[]{:S(2)}) collective-permute-start(f32[32,512]{1,0:T(8,128)S(1)} %get-tuple-element.48), channel_id=1, source_target_pairs={{0,2},{1,3},{2,0},{3,1},{4,6},{5,7},{6,4},{7,5},{8,10},{9,11},{10,... | collective-permute-start | bytes 196616 | tf_op jit(solution)/shard_map/ppermute | solution.py:169
  17.8 4.3 %collective-permute-start.9 = (f32[32,512]{1,0:T(8,128)S(1)}, f32[32,512]{1,0:T(8,128)S(1)}, u32[]{:S(2)}, u32[]{:S(2)}) collective-permute-start(f32[32,512]{1,0:T(8,128)S(1)} %get-tuple-element.49), channel_id=1, source_target_pairs={{0,1},{1,0},{2,3},{3,2},{4,5},{5,4},{6,7},{7,6},{8,9},{9,8},{10,11... | collective-permute-start | bytes 196616 | tf_op jit(solution)/shard_map/ppermute | solution.py:169
  22.1 6.2 %collective-permute-start.15 = (f32[32,512]{1,0:T(8,128)S(1)}, f32[32,512]{1,0:T(8,128)S(1)}, u32[]{:S(2)}, u32[]{:S(2)}) collective-permute-start(f32[32,512]{1,0:T(8,128)S(1)} %get-tuple-element.72.refs_0_), channel_id=1, source_target_pairs={{0,24},{4,28},{8,16},{12,20},{16,8},{20,12},{24,0},{28,4},{1,25},{... | collective-permute-start | bytes 196616 | tf_op jit(solution)/shard_map/ppermute | solution.py:169
  25.1 5.3 %collective-permute-start.13 = (f32[32,512]{1,0:T(8,128)S(1)}, f32[32,512]{1,0:T(8,128)S(1)}, u32[]{:S(2)}, u32[]{:S(2)}) collective-permute-start(f32[32,512]{1,0:T(8,128)S(1)} %get-tuple-element.72.refs_0_), channel_id=1, source_target_pairs={{0,16},{4,20},{8,24},{12,28},{16,0},{20,4},{24,8},{28,12},{1,17},{... | collective-permute-start | bytes 196616 | tf_op jit(solution)/shard_map/ppermute | solution.py:169
  25.1 5.3 %collective-permute-start.11 = (f32[32,512]{1,0:T(8,128)S(1)}, f32[32,512]{1,0:T(8,128)S(1)}, u32[]{:S(2)}, u32[]{:S(2)}) collective-permute-start(f32[32,512]{1,0:T(8,128)S(1)} %get-tuple-element.72.refs_0_), channel_id=1, source_target_pairs={{0,8},{4,12},{8,0},{12,4},{16,24},{20,28},{24,16},{28,20},{1,9},{5... | collective-permute-start | bytes 196616 | tf_op jit(solution)/shard_map/ppermute | solution.py:169
  26.6 4.3 %collective-permute-start.10 = (f32[32,512]{1,0:T(8,128)S(1)}, f32[32,512]{1,0:T(8,128)S(1)}, u32[]{:S(2)}, u32[]{:S(2)}) collective-permute-start(f32[32,512]{1,0:T(8,128)S(1)} %get-tuple-element.72.refs_0_), channel_id=1, source_target_pairs={{0,4},{4,0},{8,12},{12,8},{16,20},{20,16},{24,28},{28,24},{1,5},{5... | collective-permute-start | bytes 196616 | tf_op jit(solution)/shard_map/ppermute | solution.py:169
  28.4 2.5 %collective-permute-start.16 = (f32[32,512]{1,0:T(8,128)S(1)}, f32[32,512]{1,0:T(8,128)S(1)}, u32[]{:S(2)}, u32[]{:S(2)}) collective-permute-start(f32[32,512]{1,0:T(8,128)S(1)} %collective-permute-done.15.refs_6_), channel_id=1, source_target_pairs={{0,4},{4,0},{8,12},{12,8},{16,20},{20,16},{24,28},{28,24},{1,5},{5... | collective-permute-start | bytes 196616 | tf_op jit(solution)/shard_map/ppermute | solution.py:169
  30.4 1.3 %collective-permute-start.14 = (f32[32,512]{1,0:T(8,128)S(1)}, f32[32,512]{1,0:T(8,128)S(1)}, u32[]{:S(2)}, u32[]{:S(2)}) collective-permute-start(f32[32,512]{1,0:T(8,128)S(1)} %collective-permute-done.13.refs_4_), channel_id=1, source_target_pairs={{0,4},{4,0},{8,12},{12,8},{16,20},{20,16},{24,28},{28,24},{1,5},{5... | collective-permute-start | bytes 196616 | tf_op jit(solution)/shard_map/ppermute | solution.py:169
  30.4 1.4 %collective-permute-start.12 = (f32[32,512]{1,0:T(8,128)S(1)}, f32[32,512]{1,0:T(8,128)S(1)}, u32[]{:S(2)}, u32[]{:S(2)}) collective-permute-start(f32[32,512]{1,0:T(8,128)S(1)} %collective-permute-done.11.refs_2_), channel_id=1, source_target_pairs={{0,4},{4,0},{8,12},{12,8},{16,20},{20,16},{24,28},{28,24},{1,5},{5... | collective-permute-start | bytes 196616 | tf_op jit(solution)/shard_map/ppermute | solution.py:169
  33.2 5.4 %collective-permute-start.17 = (f32[32,512]{1,0:T(8,128)S(1)}, f32[32,512]{1,0:T(8,128)S(1)}, u32[]{:S(2)}, u32[]{:S(2)}) collective-permute-start(f32[32,512]{1,0:T(8,128)S(1)} %get-tuple-element.51), channel_id=1, source_target_pairs={{0,3},{1,2},{2,1},{3,0},{4,7},{5,6},{6,5},{7,4},{8,11},{9,10},{10,... | collective-permute-start | bytes 196616 | tf_op jit(solution)/shard_map/ppermute | solution.py:169
  34.8 5.1 %collective-permute-start.18 = (f32[32,512]{1,0:T(8,128)S(1)}, f32[32,512]{1,0:T(8,128)S(1)}, u32[]{:S(2)}, u32[]{:S(2)}) collective-permute-start(f32[32,512]{1,0:T(8,128)S(1)} %get-tuple-element.52), channel_id=1, source_target_pairs={{0,2},{1,3},{2,0},{3,1},{4,6},{5,7},{6,4},{7,5},{8,10},{9,11},{10,... | collective-permute-start | bytes 196616 | tf_op jit(solution)/shard_map/ppermute | solution.py:169
  36.4 4.3 %collective-permute-start.19 = (f32[32,512]{1,0:T(8,128)S(1)}, f32[32,512]{1,0:T(8,128)S(1)}, u32[]{:S(2)}, u32[]{:S(2)}) collective-permute-start(f32[32,512]{1,0:T(8,128)S(1)} %get-tuple-element.53), channel_id=1, source_target_pairs={{0,1},{1,0},{2,3},{3,2},{4,5},{5,4},{6,7},{7,6},{8,9},{9,8},{10,11... | collective-permute-start | bytes 196616 | tf_op jit(solution)/shard_map/ppermute | solution.py:169
  40.7 6.2 %collective-permute-start.25 = (f32[32,512]{1,0:T(8,128)S(1)}, f32[32,512]{1,0:T(8,128)S(1)}, u32[]{:S(2)}, u32[]{:S(2)}) collective-permute-start(f32[32,512]{1,0:T(8,128)S(1)} %multiply_subtract_fusion.1.refs_0_), channel_id=1, source_target_pairs={{0,24},{4,28},{8,16},{12,20},{16,8},{20,12},{24,0},{28,4},{1,25},{... | collective-permute-start | bytes 196616 | tf_op jit(solution)/shard_map/ppermute | solution.py:169
  42.9 6.5 %collective-permute-start.23 = (f32[32,512]{1,0:T(8,128)S(1)}, f32[32,512]{1,0:T(8,128)S(1)}, u32[]{:S(2)}, u32[]{:S(2)}) collective-permute-start(f32[32,512]{1,0:T(8,128)S(1)} %multiply_subtract_fusion.1.refs_0_), channel_id=1, source_target_pairs={{0,16},{4,20},{8,24},{12,28},{16,0},{20,4},{24,8},{28,12},{1,17},{... | collective-permute-start | bytes 196616 | tf_op jit(solution)/shard_map/ppermute | solution.py:169
  43.0 6.4 %collective-permute-start.21 = (f32[32,512]{1,0:T(8,128)S(1)}, f32[32,512]{1,0:T(8,128)S(1)}, u32[]{:S(2)}, u32[]{:S(2)}) collective-permute-start(f32[32,512]{1,0:T(8,128)S(1)} %multiply_subtract_fusion.1.refs_0_), channel_id=1, source_target_pairs={{0,8},{4,12},{8,0},{12,4},{16,24},{20,28},{24,16},{28,20},{1,9},{5... | collective-permute-start | bytes 196616 | tf_op jit(solution)/shard_map/ppermute | solution.py:169
  45.1 4.8 %collective-permute-start.20 = (f32[32,512]{1,0:T(8,128)S(1)}, f32[32,512]{1,0:T(8,128)S(1)}, u32[]{:S(2)}, u32[]{:S(2)}) collective-permute-start(f32[32,512]{1,0:T(8,128)S(1)} %multiply_subtract_fusion.1.refs_0_), channel_id=1, source_target_pairs={{0,4},{4,0},{8,12},{12,8},{16,20},{20,16},{24,28},{28,24},{1,5},{5... | collective-permute-start | bytes 196616 | tf_op jit(solution)/shard_map/ppermute | solution.py:169
  46.8 3.1 %collective-permute-start.26 = (f32[32,512]{1,0:T(8,128)S(1)}, f32[32,512]{1,0:T(8,128)S(1)}, u32[]{:S(2)}, u32[]{:S(2)}) collective-permute-start(f32[32,512]{1,0:T(8,128)S(1)} %collective-permute-done.25.refs_6_), channel_id=1, source_target_pairs={{0,4},{4,0},{8,12},{12,8},{16,20},{20,16},{24,28},{28,24},{1,5},{5... | collective-permute-start | bytes 196616 | tf_op jit(solution)/shard_map/ppermute | solution.py:169
  49.4 1.3 %collective-permute-start.24 = (f32[32,512]{1,0:T(8,128)S(1)}, f32[32,512]{1,0:T(8,128)S(1)}, u32[]{:S(2)}, u32[]{:S(2)}) collective-permute-start(f32[32,512]{1,0:T(8,128)S(1)} %collective-permute-done.23.refs_4_), channel_id=1, source_target_pairs={{0,4},{4,0},{8,12},{12,8},{16,20},{20,16},{24,28},{28,24},{1,5},{5... | collective-permute-start | bytes 196616 | tf_op jit(solution)/shard_map/ppermute | solution.py:169
  49.4 1.4 %collective-permute-start.22 = (f32[32,512]{1,0:T(8,128)S(1)}, f32[32,512]{1,0:T(8,128)S(1)}, u32[]{:S(2)}, u32[]{:S(2)}) collective-permute-start(f32[32,512]{1,0:T(8,128)S(1)} %collective-permute-done.21.refs_2_), channel_id=1, source_target_pairs={{0,4},{4,0},{8,12},{12,8},{16,20},{20,16},{24,28},{28,24},{1,5},{5... | collective-permute-start | bytes 196616 | tf_op jit(solution)/shard_map/ppermute | solution.py:169
  52.2 5.4 %collective-permute-start.27 = (f32[32,512]{1,0:T(8,128)S(1)}, f32[32,512]{1,0:T(8,128)S(1)}, u32[]{:S(2)}, u32[]{:S(2)}) collective-permute-start(f32[32,512]{1,0:T(8,128)S(1)} %get-tuple-element.55), channel_id=1, source_target_pairs={{0,3},{1,2},{2,1},{3,0},{4,7},{5,6},{6,5},{7,4},{8,11},{9,10},{10,... | collective-permute-start | bytes 196616 | tf_op jit(solution)/shard_map/ppermute | solution.py:169
  53.8 5.2 %collective-permute-start.28 = (f32[32,512]{1,0:T(8,128)S(1)}, f32[32,512]{1,0:T(8,128)S(1)}, u32[]{:S(2)}, u32[]{:S(2)}) collective-permute-start(f32[32,512]{1,0:T(8,128)S(1)} %get-tuple-element.56), channel_id=1, source_target_pairs={{0,2},{1,3},{2,0},{3,1},{4,6},{5,7},{6,4},{7,5},{8,10},{9,11},{10,... | collective-permute-start | bytes 196616 | tf_op jit(solution)/shard_map/ppermute | solution.py:169
  54.6 4.3 %collective-permute-start.29 = (f32[32,512]{1,0:T(8,128)S(1)}, f32[32,512]{1,0:T(8,128)S(1)}, u32[]{:S(2)}, u32[]{:S(2)}) collective-permute-start(f32[32,512]{1,0:T(8,128)S(1)} %get-tuple-element.57), channel_id=1, source_target_pairs={{0,1},{1,0},{2,3},{3,2},{4,5},{5,4},{6,7},{7,6},{8,9},{9,8},{10,11... | collective-permute-start | bytes 196616 | tf_op jit(solution)/shard_map/ppermute | solution.py:169
  59.0 5.8 %collective-permute-start.34 = (f32[32,512]{1,0:T(8,128)S(1)}, f32[32,512]{1,0:T(8,128)S(1)}, u32[]{:S(2)}, u32[]{:S(2)}) collective-permute-start(f32[32,512]{1,0:T(8,128)S(1)} %multiply_subtract_fusion.refs_0_.filtered), channel_id=1, source_target_pairs={{0,1},{1,0},{2,3},{3,2},{4,5},{5,4},{6,7},{7,6},{8,9},{9,8},{10,11... | collective-permute-start | bytes 196616 | tf_op jit(solution)/shard_map/ppermute | solution.py:169
  60.2 7.4 %collective-permute-start.33 = (f32[32,512]{1,0:T(8,128)S(1)}, f32[32,512]{1,0:T(8,128)S(1)}, u32[]{:S(2)}, u32[]{:S(2)}) collective-permute-start(f32[32,512]{1,0:T(8,128)S(1)} %multiply_subtract_fusion.refs_0_.filtered), channel_id=1, source_target_pairs={{0,16},{4,20},{8,24},{12,28},{16,0},{20,4},{24,8},{28,12},{1,17},{... | collective-permute-start | bytes 196616 | tf_op jit(solution)/shard_map/ppermute | solution.py:169
  60.7 6.9 %collective-permute-start.38 = (f32[32,512]{1,0:T(8,128)S(1)}, f32[32,512]{1,0:T(8,128)S(1)}, u32[]{:S(2)}, u32[]{:S(2)}) collective-permute-start(f32[32,512]{1,0:T(8,128)S(1)} %multiply_subtract_fusion.refs_0_.filtered), channel_id=1, source_target_pairs={{0,24},{4,28},{8,16},{12,20},{16,8},{20,12},{24,0},{28,4},{1,25},{... | collective-permute-start | bytes 196616 | tf_op jit(solution)/shard_map/ppermute | solution.py:169
  62.6 5.4 %collective-permute-start.35 = (f32[32,512]{1,0:T(8,128)S(1)}, f32[32,512]{1,0:T(8,128)S(1)}, u32[]{:S(2)}, u32[]{:S(2)}) collective-permute-start(f32[32,512]{1,0:T(8,128)S(1)} %multiply_subtract_fusion.refs_0_.filtered), channel_id=1, source_target_pairs={{0,2},{1,3},{2,0},{3,1},{4,6},{5,7},{6,4},{7,5},{8,10},{9,11},{10,... | collective-permute-start | bytes 196616 | tf_op jit(solution)/shard_map/ppermute | solution.py:169
  63.6 4.6 %collective-permute-start.31 = (f32[32,512]{1,0:T(8,128)S(1)}, f32[32,512]{1,0:T(8,128)S(1)}, u32[]{:S(2)}, u32[]{:S(2)}) collective-permute-start(f32[32,512]{1,0:T(8,128)S(1)} %multiply_subtract_fusion.refs_0_.filtered), channel_id=1, source_target_pairs={{0,8},{4,12},{8,0},{12,4},{16,24},{20,28},{24,16},{28,20},{1,9},{5... | collective-permute-start | bytes 196616 | tf_op jit(solution)/shard_map/ppermute | solution.py:169
  64.8 4.3 %collective-permute-start.36 = (f32[32,512]{1,0:T(8,128)S(1)}, f32[32,512]{1,0:T(8,128)S(1)}, u32[]{:S(2)}, u32[]{:S(2)}) collective-permute-start(f32[32,512]{1,0:T(8,128)S(1)} %collective-permute-done.34.refs_8_), channel_id=1, source_target_pairs={{0,2},{1,3},{2,0},{3,1},{4,6},{5,7},{6,4},{7,5},{8,10},{9,11},{10,... | collective-permute-start | bytes 196616 | tf_op jit(solution)/shard_map/ppermute | solution.py:169
  67.6 1.5 %collective-permute-start.37 = (f32[32,512]{1,0:T(8,128)S(1)}, f32[32,512]{1,0:T(8,128)S(1)}, u32[]{:S(2)}, u32[]{:S(2)}) collective-permute-start(f32[32,512]{1,0:T(8,128)S(1)} %collective-permute-done.33.refs_4_), channel_id=1, source_target_pairs={{0,4},{4,0},{8,12},{12,8},{16,20},{20,16},{24,28},{28,24},{1,5},{5... | collective-permute-start | bytes 196616 | tf_op jit(solution)/shard_map/ppermute | solution.py:169
  67.6 1.5 %collective-permute-start.30 = (f32[32,512]{1,0:T(8,128)S(1)}, f32[32,512]{1,0:T(8,128)S(1)}, u32[]{:S(2)}, u32[]{:S(2)}) collective-permute-start(f32[32,512]{1,0:T(8,128)S(1)} %multiply_subtract_fusion.refs_0_.filtered), channel_id=1, source_target_pairs={{0,4},{4,0},{8,12},{12,8},{16,20},{20,16},{24,28},{28,24},{1,5},{5... | collective-permute-start | bytes 196616 | tf_op jit(solution)/shard_map/ppermute | solution.py:169
  68.1 1.3 %collective-permute-start.39 = (f32[32,512]{1,0:T(8,128)S(1)}, f32[32,512]{1,0:T(8,128)S(1)}, u32[]{:S(2)}, u32[]{:S(2)}) collective-permute-start(f32[32,512]{1,0:T(8,128)S(1)} %collective-permute-done.38.refs_6_), channel_id=1, source_target_pairs={{0,4},{4,0},{8,12},{12,8},{16,20},{20,16},{24,28},{28,24},{1,5},{5... | collective-permute-start | bytes 196616 | tf_op jit(solution)/shard_map/ppermute | solution.py:169
  68.2 1.3 %collective-permute-start.32 = (f32[32,512]{1,0:T(8,128)S(1)}, f32[32,512]{1,0:T(8,128)S(1)}, u32[]{:S(2)}, u32[]{:S(2)}) collective-permute-start(f32[32,512]{1,0:T(8,128)S(1)} %collective-permute-done.31.refs_2_), channel_id=1, source_target_pairs={{0,4},{4,0},{8,12},{12,8},{16,20},{20,16},{24,28},{28,24},{1,5},{5... | collective-permute-start | bytes 196616 | tf_op jit(solution)/shard_map/ppermute | solution.py:169
  71.5 4.7 %collective-permute-start.42 = (f32[32,64]{1,0:T(8,128)S(1)}, f32[32,64]{1,0:T(8,128)S(1)}, u32[]{:S(2)}, u32[]{:S(2)}) collective-permute-start(f32[32,64]{1,0:T(8,128)S(1)} %moment.1), channel_id=1, source_target_pairs={{0,3},{1,2},{2,1},{3,0},{4,7},{5,6},{6,5},{7,4},{8,11},{9,10},{10,... | collective-permute-start | bytes 24584 | tf_op jit(solution)/shard_map/ppermute | solution.py:169
  73.1 3.7 %collective-permute-start.41 = (f32[32,64]{1,0:T(8,128)S(1)}, f32[32,64]{1,0:T(8,128)S(1)}, u32[]{:S(2)}, u32[]{:S(2)}) collective-permute-start(f32[32,64]{1,0:T(8,128)S(1)} %moment.1), channel_id=1, source_target_pairs={{0,2},{1,3},{2,0},{3,1},{4,6},{5,7},{6,4},{7,5},{8,10},{9,11},{10,... | collective-permute-start | bytes 24584 | tf_op jit(solution)/shard_map/ppermute | solution.py:169
  74.0 3.7 %collective-permute-start.40 = (f32[32,64]{1,0:T(8,128)S(1)}, f32[32,64]{1,0:T(8,128)S(1)}, u32[]{:S(2)}, u32[]{:S(2)}) collective-permute-start(f32[32,64]{1,0:T(8,128)S(1)} %moment.1), channel_id=1, source_target_pairs={{0,1},{1,0},{2,3},{3,2},{4,5},{5,4},{6,7},{7,6},{8,9},{9,8},{10,11... | collective-permute-start | bytes 24584 | tf_op jit(solution)/shard_map/ppermute | solution.py:169
  77.7 6.1 %collective-permute-start.45 = (f32[32,64]{1,0:T(8,128)S(1)}, f32[32,64]{1,0:T(8,128)S(1)}, u32[]{:S(2)}, u32[]{:S(2)}) collective-permute-start(f32[32,64]{1,0:T(8,128)S(1)} %add_add_fusion.1.sums), channel_id=1, source_target_pairs={{0,24},{4,28},{8,16},{12,20},{16,8},{20,12},{24,0},{28,4},{1,25},{... | collective-permute-start | bytes 24584 | tf_op jit(solution)/shard_map/ppermute | solution.py:169
  79.8 4.6 %collective-permute-start.44 = (f32[32,64]{1,0:T(8,128)S(1)}, f32[32,64]{1,0:T(8,128)S(1)}, u32[]{:S(2)}, u32[]{:S(2)}) collective-permute-start(f32[32,64]{1,0:T(8,128)S(1)} %add_add_fusion.1.sums), channel_id=1, source_target_pairs={{0,16},{4,20},{8,24},{12,28},{16,0},{20,4},{24,8},{28,12},{1,17},{... | collective-permute-start | bytes 24584 | tf_op jit(solution)/shard_map/ppermute | solution.py:169
  80.3 4.2 %collective-permute-start.43 = (f32[32,64]{1,0:T(8,128)S(1)}, f32[32,64]{1,0:T(8,128)S(1)}, u32[]{:S(2)}, u32[]{:S(2)}) collective-permute-start(f32[32,64]{1,0:T(8,128)S(1)} %add_add_fusion.1.sums), channel_id=1, source_target_pairs={{0,8},{4,12},{8,0},{12,4},{16,24},{20,28},{24,16},{28,20},{1,9},{5... | collective-permute-start | bytes 24584 | tf_op jit(solution)/shard_map/ppermute | solution.py:169
  84.5 1.2 %collective-permute-start.46 = (f32[32,64]{1,0:T(8,128)S(1)}, f32[32,64]{1,0:T(8,128)S(1)}, u32[]{:S(2)}, u32[]{:S(2)}) collective-permute-start(f32[32,64]{1,0:T(8,128)S(1)} %add_add_fusion), channel_id=1, source_target_pairs={{0,4},{4,0},{8,12},{12,8},{16,20},{20,16},{24,28},{28,24},{1,5},{5... | collective-permute-start | bytes 24584 | tf_op jit(solution)/shard_map/ppermute | solution.py:169
  (3 other events, 29.7 us)
